TPU v7x, 128 devices: a whole 4x4x4 slice. The times are simulated.
128 devices in a mesh: dp: 32 (over x, y, core), mp: 4 (over z).
Axes of the slice: x: 4, y: 4, z: 4, core: 2. Of those that a mesh axis runs over, the one named last changes fastest.
Arguments:
- tokens: bfloat16 [4096, 2048], P('dp'), may hold values from -6 to 6
- depths: int32 [4096], P('dp'), may hold values from 1 to 3
- second_slot: int32 [4096], P('dp'), may hold values from -1 to 95, as said below
- third_slot: int32 [4096], P('dp'), may hold values from -1 to 63, as said below
- w_query: bfloat16 [2048, 2048], P('dp', 'mp'), may hold values from -0.125 to 0.125
- w_key: bfloat16 [2048, 256], P('dp', 'mp'), may hold values from -0.125 to 0.125
- w_value: bfloat16 [2048, 256], P('dp', 'mp'), may hold values from -0.125 to 0.125
- w_out: bfloat16 [2048, 2048], P('mp', 'dp'), may hold values from -0.75 to 0.75
- w_gate: bfloat16 [2048, 5632], P('dp', 'mp'), may hold values from -0.125 to 0.125
- w_up: bfloat16 [2048, 5632], P('dp', 'mp'), may hold values from -0.125 to 0.125
- w_down: bfloat16 [5632, 2048], P('mp', 'dp'), may hold values from -0.078125 to 0.078125
- norm_first: bfloat16 [2048], P('dp'), may hold values from 0.5 to 1.5
- norm_second: bfloat16 [2048], P('dp'), may hold values from 0.5 to 1.5
- router: bfloat16 [2048], P('dp'), may hold values from -0.125 to 0.125
- cotangent: float32 [4096, 2048], P('dp'), may hold values from -6 to 6
Outputs:
- hidden_states: float32 [4096, 2048], P('dp')
- input_grad: float32 [4096, 2048], P('dp')
- query_grad: float32 [2048, 2048], P('dp', 'mp')
- key_grad: float32 [2048, 256], P('dp', 'mp')
- value_grad: float32 [2048, 256], P('dp', 'mp')
- out_grad: float32 [2048, 2048], P('mp', 'dp')
- gate_grad: float32 [2048, 5632], P('dp', 'mp')
- up_grad: float32 [2048, 5632], P('dp', 'mp')
- down_grad: float32 [5632, 2048], P('mp', 'dp')
- norm_first_grad: float32 [2048], P('dp')
- norm_second_grad: float32 [2048], P('dp')
- router_grad: float32 [2048], P('dp')
Inputs may be any that keep to these rules, and one draw needn't show every extreme that they name: `second_slot`: among the 128 tokens of one device the values other than -1 are distinct; -1 marks tokens of depth 1 and tokens that the capacity drops; some device uses every value. `third_slot`: among the 128 tokens of one device the values other than -1 are distinct; a token has one only if it has depth 3 and a second_slot; some device uses every value.
All inputs are finite; a program needn't handle non-finite values.
Results may differ from a plain program's by a relative error of at most 0.035.
Values may be sent and summed in bfloat16 or wider, within the bound.
A program may use at most 192 MiB of HBM per device.

v0:
```python
import math

import jax
import jax.numpy as jnp
from jax import lax
from jax.sharding import PartitionSpec as P

HD = 64
SECOND_SLOTS = 96
THIRD_SLOTS = 64


EPS = 1e-05
NEG = -1e30
ROPE_BASE = 10000.0
FAR = 1073741824


def as_sent(x):
    return jax.tree.map(lambda a: a.astype(jnp.bfloat16) if a.dtype == jnp.float32 else a, x)


def project(left, right):
    return jnp.dot(left, right, preferred_element_type=jnp.float32)


def project_back(left, right):
    return lax.dot_general(
        left, right, (((1,), (1,)), ((), ())), preferred_element_type=jnp.float32
    )


def outer_rows(left, right):
    return lax.dot_general(
        left, right, (((0,), (0,)), ((), ())), preferred_element_type=jnp.float32
    )


def norm_rows(values, gain):
    factor = lax.rsqrt(jnp.mean(values * values, axis=-1, keepdims=True) + EPS)
    unit = values * factor
    return (unit * gain, unit, factor)


def norm_back(grad, unit, factor, gain):
    shaped = grad * gain
    return (
        factor * (shaped - unit * jnp.mean(shaped * unit, axis=-1, keepdims=True)),
        jnp.sum(grad * unit, axis=0),
    )


def angles(place):
    freq = jnp.exp(jnp.arange(HD // 2, dtype=jnp.float32) * (-2.0 * math.log(ROPE_BASE) / HD))
    angle = place.astype(jnp.float32)[:, None] * freq[None, :]
    return (jnp.cos(angle)[:, None, :], jnp.sin(angle)[:, None, :])


def rotate(values, cosine, sine):
    half = values.shape[-1] // 2
    first = values[..., :half]
    second = values[..., half:]
    return jnp.concatenate(
        [first * cosine - second * sine, second * cosine + first * sine], axis=-1
    )


def group_rows(values, kv_local):
    count = values.shape[0]
    groups = values.shape[1] // kv_local
    return (
        values.reshape(count, kv_local, groups, HD)
        .transpose(1, 2, 0, 3)
        .reshape(kv_local, groups * count, HD)
    )


def ungroup_rows(values, count):
    kv_local = values.shape[0]
    groups = values.shape[1] // count
    return (
        values.reshape(kv_local, groups, count, HD)
        .transpose(2, 0, 1, 3)
        .reshape(count, kv_local * groups * HD)
    )


def scores_of(query, query_place, key_part, place_part):
    scores = jnp.einsum(
        "krd,nkd->krn", query, key_part, preferred_element_type=jnp.float32
    ) * HD ** (-0.5)
    return jnp.where(place_part[None, None, :] <= query_place[None, :, None], scores, NEG)


def key_blocks(keys, values, key_place):
    count = keys.shape[0]
    block = math.gcd(count, 512)
    blocks = count // block
    kv_local = keys.shape[1]
    return (
        keys.reshape(blocks, block, kv_local, HD),
        values.reshape(blocks, block, kv_local, HD),
        key_place.reshape(blocks, block),
    )


def attend_forward(query, keys, values, key_place, query_place):
    kv_local, width = (query.shape[0], query.shape[1])
    parts = key_blocks(keys, values, key_place)

    def gather_stats(carry, part):
        top, total = carry
        scores = scores_of(query, query_place, part[0], part[2])
        peak = jnp.maximum(top, jnp.max(scores, axis=-1))
        total = total * jnp.exp(top - peak) + jnp.sum(jnp.exp(scores - peak[..., None]), axis=-1)
        return ((peak, total), None)

    start = (
        jnp.full((kv_local, width), NEG, jnp.float32),
        jnp.zeros((kv_local, width), jnp.float32),
    )
    (top, total), unused = lax.scan(gather_stats, start, parts)
    log_total = top + jnp.log(total)

    def add_values(acc, part):
        weights = jnp.exp(
            scores_of(query, query_place, part[0], part[2]) - log_total[..., None]
        ).astype(jnp.bfloat16)
        return (
            acc + jnp.einsum("krn,nkd->krd", weights, part[1], preferred_element_type=jnp.float32),
            None,
        )

    mixed, unused = lax.scan(add_values, jnp.zeros((kv_local, width, HD), jnp.float32), parts)
    return (mixed, log_total)


def attend_backward(query, keys, values, key_place, query_place, log_total, grad_mixed, delta):
    count, kv_local = (keys.shape[0], keys.shape[1])
    parts = key_blocks(keys, values, key_place)
    scale = HD ** (-0.5)

    def one_block(grad_query, part):
        key_part, value_part, place_part = part
        weights = jnp.exp(
            scores_of(query, query_place, key_part, place_part) - log_total[..., None]
        )
        rounded = weights.astype(jnp.bfloat16)
        grad_weights = jnp.einsum(
            "krd,nkd->krn", grad_mixed, value_part, preferred_element_type=jnp.float32
        )
        grad_scores = (weights * (grad_weights - delta[..., None])).astype(jnp.bfloat16)
        grad_query = (
            grad_query
            + jnp.einsum("krn,nkd->krd", grad_scores, key_part, preferred_element_type=jnp.float32)
            * scale
        )
        grad_keys = (
            jnp.einsum("krn,krd->nkd", grad_scores, query, preferred_element_type=jnp.float32)
            * scale
        )
        grad_values = jnp.einsum(
            "krn,krd->nkd", rounded, grad_mixed, preferred_element_type=jnp.float32
        )
        return (grad_query, (grad_keys, grad_values))

    grad_query, (grad_keys, grad_values) = lax.scan(
        one_block, jnp.zeros(query.shape, jnp.float32), parts
    )
    return (
        grad_query,
        grad_keys.reshape(count, kv_local * HD),
        grad_values.reshape(count, kv_local * HD),
    )


def step_forward(rows_in, place, weights):
    w_query, w_key, w_value, w_out, w_gate, w_up, w_down, norm_first, norm_second, router = weights
    count = rows_in.shape[0]
    heads = w_query.shape[1] // HD
    kv_local = w_key.shape[1] // HD
    state = rows_in.astype(jnp.float32)
    gate = jax.nn.sigmoid(project(rows_in, router))
    normed, unused, scale_one = norm_rows(state, norm_first.astype(jnp.float32))
    normed = normed.astype(jnp.bfloat16)
    cosine, sine = angles(place)
    query = rotate(project(normed, w_query).reshape(count, heads, HD), cosine, sine).astype(
        jnp.bfloat16
    )
    key_rows = rotate(project(normed, w_key).reshape(count, kv_local, HD), cosine, sine).astype(
        jnp.bfloat16
    )
    value_rows = project(normed, w_value).astype(jnp.bfloat16).reshape(count, kv_local, HD)
    keys, values, key_place = (
        lax.all_gather(key_rows, "dp", axis=0, tiled=True),
        lax.all_gather(value_rows, "dp", axis=0, tiled=True),
        lax.all_gather(as_sent(place), "dp", axis=0, tiled=True).astype(place.dtype),
    )
    query_place = jnp.tile(place, heads // kv_local)
    mixed, log_total = attend_forward(
        group_rows(query, kv_local), keys, values, key_place, query_place
    )
    mixed = ungroup_rows(mixed, count)
    attn = lax.psum(project(mixed.astype(jnp.bfloat16), w_out).astype(jnp.bfloat16), "mp").astype(
        jnp.float32
    )
    middle = state + attn
    second, unused, scale_two = norm_rows(middle, norm_second.astype(jnp.float32))
    second = second.astype(jnp.bfloat16)
    hidden = (jax.nn.silu(project(second, w_gate)) * project(second, w_up)).astype(jnp.bfloat16)
    ffn = lax.psum(project(hidden, w_down).astype(jnp.bfloat16), "mp").astype(jnp.float32)
    update = (gate[:, None] * (attn + ffn)).astype(jnp.bfloat16)
    return (update, (rows_in, place, keys, values, key_place, log_total, mixed, attn, ffn, gate))


def step_backward(grad_update, kept, weights, totals):
    rows_in, place, keys, values, key_place, log_total, mixed, attn, ffn, gate = kept
    w_query, w_key, w_value, w_out, w_gate, w_up, w_down, norm_first, norm_second, router = weights
    count = rows_in.shape[0]
    heads = w_query.shape[1] // HD
    kv_local = w_key.shape[1] // HD
    groups = heads // kv_local
    state = rows_in.astype(jnp.float32)
    gain_first = norm_first.astype(jnp.float32)
    gain_second = norm_second.astype(jnp.float32)
    normed, unit_rows, scale_one = norm_rows(state, gain_first)
    normed = normed.astype(jnp.bfloat16)
    cosine, sine = angles(place)
    query = rotate(project(normed, w_query).reshape(count, heads, HD), cosine, sine).astype(
        jnp.bfloat16
    )
    middle = state + attn
    second, unit_mid, scale_two = norm_rows(middle, gain_second)
    second = second.astype(jnp.bfloat16)
    gate_part = project(second, w_gate)
    up_part = project(second, w_up)
    sigma = jax.nn.sigmoid(gate_part)
    active_part = gate_part * sigma
    hidden = (active_part * up_part).astype(jnp.bfloat16)
    update_float = grad_update.astype(jnp.float32)
    gate_logit_grad = jnp.sum(update_float * (attn + ffn), axis=-1) * gate * (1.0 - gate)
    grad_ffn = (gate[:, None] * update_float).astype(jnp.bfloat16)
    grad_hidden = project_back(grad_ffn, w_down)
    grad_gate_part = (grad_hidden * up_part * sigma * (1.0 + gate_part * (1.0 - sigma))).astype(
        jnp.bfloat16
    )
    grad_up_part = (grad_hidden * active_part).astype(jnp.bfloat16)
    grad_second = lax.psum(
        (project_back(grad_gate_part, w_gate) + project_back(grad_up_part, w_up)).astype(
            jnp.bfloat16
        ),
        "mp",
    ).astype(jnp.float32)
    grad_middle, norm_second_part = norm_back(grad_second, unit_mid, scale_two, gain_second)
    grad_attn = (gate[:, None] * update_float + grad_middle).astype(jnp.bfloat16)
    rounded_mixed = mixed.astype(jnp.bfloat16)
    grad_mixed = project_back(grad_attn, w_out).astype(jnp.bfloat16)
    delta = jnp.sum((grad_mixed.astype(jnp.float32) * mixed).reshape(count, heads, HD), axis=-1)
    delta = (
        delta.reshape(count, kv_local, groups).transpose(1, 2, 0).reshape(kv_local, groups * count)
    )
    query_place = jnp.tile(place, groups)
    grad_query, grad_keys, grad_values = attend_backward(
        group_rows(query, kv_local),
        keys,
        values,
        key_place,
        query_place,
        log_total,
        group_rows(grad_mixed.reshape(count, heads, HD), kv_local),
        delta,
    )
    own_keys, own_values = (
        lax.psum_scatter(
            grad_keys.astype(jnp.bfloat16), "dp", scatter_dimension=0, tiled=True
        ).astype(jnp.float32),
        lax.psum_scatter(
            grad_values.astype(jnp.bfloat16), "dp", scatter_dimension=0, tiled=True
        ).astype(jnp.float32),
    )
    grad_query = (
        rotate(ungroup_rows(grad_query, count).reshape(count, heads, HD), cosine, -sine)
        .astype(jnp.bfloat16)
        .reshape(count, heads * HD)
    )
    grad_key = (
        rotate(own_keys.reshape(count, kv_local, HD), cosine, -sine)
        .astype(jnp.bfloat16)
        .reshape(count, kv_local * HD)
    )
    grad_value = own_values.astype(jnp.bfloat16)
    grad_normed = lax.psum(
        (
            project_back(grad_query, w_query)
            + project_back(grad_key, w_key)
            + project_back(grad_value, w_value)
        ).astype(jnp.bfloat16),
        "mp",
    ).astype(jnp.float32)
    grad_rows, norm_first_part = norm_back(grad_normed, unit_rows, scale_one, gain_first)
    grad_rows = grad_rows + grad_middle + gate_logit_grad[:, None] * router.astype(jnp.float32)
    terms = (
        outer_rows(normed, grad_query),
        outer_rows(normed, grad_key),
        outer_rows(normed, grad_value),
        outer_rows(rounded_mixed, grad_attn),
        outer_rows(second, grad_gate_part),
        outer_rows(second, grad_up_part),
        outer_rows(hidden, grad_ffn),
        norm_first_part,
        norm_second_part,
        jnp.sum(state * gate_logit_grad[:, None], axis=0),
    )
    totals = tuple((total + term for total, term in zip(totals, terms)))
    return (grad_rows.astype(jnp.bfloat16), totals)


def slot_sources(index, capacity, rows):
    return (
        jnp.full((capacity,), rows, jnp.int32)
        .at[index]
        .set(jnp.arange(rows, dtype=jnp.int32), mode="drop")
    )


def move_rows(values, place, index, capacity):
    devices = lax.axis_size("dp")
    rows = values.shape[0]
    source = slot_sources(index, capacity, rows)
    taken = jnp.concatenate([values, jnp.zeros((1, values.shape[1]), values.dtype)])[source]
    taken_place = jnp.concatenate([place, jnp.full((1,), FAR, jnp.int32)])[source]
    arrived, arrived_place = (
        lax.all_to_all(
            taken.reshape(devices, capacity // devices, values.shape[1]),
            "dp",
            split_axis=0,
            concat_axis=0,
            tiled=True,
        ),
        lax.all_to_all(
            taken_place.reshape(devices, capacity // devices),
            "dp",
            split_axis=0,
            concat_axis=0,
            tiled=True,
        ),
    )
    return (arrived.reshape(capacity, values.shape[1]), arrived_place.reshape(capacity))


def return_rows(values, index, capacity):
    devices = lax.axis_size("dp")
    width = values.shape[1]
    back = lax.all_to_all(
        values.reshape(devices, capacity // devices, width),
        "dp",
        split_axis=0,
        concat_axis=0,
        tiled=True,
    ).reshape(capacity, width)
    return jnp.concatenate([back, jnp.zeros((1, width), back.dtype)])[index]


def move_grads(values, index, capacity):
    devices = lax.axis_size("dp")
    width = values.shape[1]
    source = slot_sources(index, capacity, values.shape[0])
    taken = jnp.concatenate([values, jnp.zeros((1, width), values.dtype)])[source]
    arrived = lax.all_to_all(
        taken.reshape(devices, capacity // devices, width),
        "dp",
        split_axis=0,
        concat_axis=0,
        tiled=True,
    )
    return arrived.reshape(capacity, width)


def return_grads(values, index, capacity):
    devices = lax.axis_size("dp")
    width = values.shape[1]
    back = lax.all_to_all(
        values.reshape(devices, capacity // devices, width),
        "dp",
        split_axis=0,
        concat_axis=0,
        tiled=True,
    ).reshape(capacity, width)
    return jnp.concatenate([back, jnp.zeros((1, width), back.dtype)])[index]


def local(
    tokens,
    depths,
    second_slot,
    third_slot,
    w_query,
    w_key,
    w_value,
    w_out,
    w_gate,
    w_up,
    w_down,
    norm_first,
    norm_second,
    router,
    cotangent,
):
    weights = (
        lax.all_gather(w_query, "dp", axis=0, tiled=True),
        lax.all_gather(w_key, "dp", axis=0, tiled=True),
        lax.all_gather(w_value, "dp", axis=0, tiled=True),
        lax.all_gather(w_out, "dp", axis=1, tiled=True),
        lax.all_gather(w_gate, "dp", axis=0, tiled=True),
        lax.all_gather(w_up, "dp", axis=0, tiled=True),
        lax.all_gather(w_down, "dp", axis=1, tiled=True),
        lax.all_gather(norm_first, "dp", axis=0, tiled=True),
        lax.all_gather(norm_second, "dp", axis=0, tiled=True),
        lax.all_gather(router, "dp", axis=0, tiled=True),
    )
    rows = tokens.shape[0]
    home_place = lax.axis_index("dp") * rows + jnp.arange(rows, dtype=jnp.int32)
    state = tokens.astype(jnp.float32)
    levels = (
        (jnp.ones((rows,), dtype=bool), None, 0),
        ((depths >= 2) & (second_slot >= 0), second_slot, SECOND_SLOTS),
        ((depths >= 3) & (third_slot >= 0), third_slot, THIRD_SLOTS),
    )
    records = []
    for active, slot, capacity in levels:
        rows_in = state.astype(jnp.bfloat16)
        if slot is not None:
            index = jnp.where(active, slot, capacity)
            sent_rows, sent_place = move_rows(rows_in, home_place, index, capacity)
            update, kept = step_forward(sent_rows, sent_place, weights)
            state = state + return_rows(update, index, capacity).astype(jnp.float32)
        else:
            index = None
            update, kept = step_forward(rows_in, jnp.where(active, home_place, FAR), weights)
            state = state + jnp.where(active[:, None], update.astype(jnp.float32), 0.0)
        records.append((active, index, capacity, kept))
    weights = (
        lax.all_gather(w_query, "dp", axis=0, tiled=True),
        lax.all_gather(w_key, "dp", axis=0, tiled=True),
        lax.all_gather(w_value, "dp", axis=0, tiled=True),
        lax.all_gather(w_out, "dp", axis=1, tiled=True),
        lax.all_gather(w_gate, "dp", axis=0, tiled=True),
        lax.all_gather(w_up, "dp", axis=0, tiled=True),
        lax.all_gather(w_down, "dp", axis=1, tiled=True),
        lax.all_gather(norm_first, "dp", axis=0, tiled=True),
        lax.all_gather(norm_second, "dp", axis=0, tiled=True),
        lax.all_gather(router, "dp", axis=0, tiled=True),
    )
    totals = tuple((jnp.zeros(item.shape, jnp.float32) for item in weights))
    flow = cotangent
    for active, index, capacity, kept in reversed(records):
        if index is not None:
            grad_slots = move_grads(flow.astype(jnp.bfloat16), index, capacity)
            grad_rows, totals = step_backward(grad_slots, kept, weights, totals)
            flow = flow + return_grads(grad_rows, index, capacity).astype(jnp.float32)
        else:
            grad_home = jnp.where(active[:, None], flow, 0.0).astype(jnp.bfloat16)
            grad_rows, totals = step_backward(grad_home, kept, weights, totals)
            flow = flow + jnp.where(active[:, None], grad_rows.astype(jnp.float32), 0.0)
    reduced = (
        lax.psum_scatter(
            totals[0].astype(jnp.bfloat16), "dp", scatter_dimension=0, tiled=True
        ).astype(jnp.float32),
        lax.psum_scatter(
            totals[1].astype(jnp.bfloat16), "dp", scatter_dimension=0, tiled=True
        ).astype(jnp.float32),
        lax.psum_scatter(
            totals[2].astype(jnp.bfloat16), "dp", scatter_dimension=0, tiled=True
        ).astype(jnp.float32),
        lax.psum_scatter(
            totals[3].astype(jnp.bfloat16), "dp", scatter_dimension=1, tiled=True
        ).astype(jnp.float32),
        lax.psum_scatter(
            totals[4].astype(jnp.bfloat16), "dp", scatter_dimension=0, tiled=True
        ).astype(jnp.float32),
        lax.psum_scatter(
            totals[5].astype(jnp.bfloat16), "dp", scatter_dimension=0, tiled=True
        ).astype(jnp.float32),
        lax.psum_scatter(
            totals[6].astype(jnp.bfloat16), "dp", scatter_dimension=1, tiled=True
        ).astype(jnp.float32),
        lax.psum_scatter(
            totals[7].astype(jnp.bfloat16), "dp", scatter_dimension=0, tiled=True
        ).astype(jnp.float32),
        lax.psum_scatter(
            totals[8].astype(jnp.bfloat16), "dp", scatter_dimension=0, tiled=True
        ).astype(jnp.float32),
        lax.psum_scatter(
            totals[9].astype(jnp.bfloat16), "dp", scatter_dimension=0, tiled=True
        ).astype(jnp.float32),
    )
    return (state, flow) + tuple(reduced)


def solution(mesh):
    in_specs = (
        P("dp", None),
        P("dp"),
        P("dp"),
        P("dp"),
        P("dp", "mp"),
        P("dp", "mp"),
        P("dp", "mp"),
        P("mp", "dp"),
        P("dp", "mp"),
        P("dp", "mp"),
        P("mp", "dp"),
        P("dp"),
        P("dp"),
        P("dp"),
        P("dp", None),
    )
    out_specs = (
        P("dp", None),
        P("dp", None),
        P("dp", "mp"),
        P("dp", "mp"),
        P("dp", "mp"),
        P("mp", "dp"),
        P("dp", "mp"),
        P("dp", "mp"),
        P("mp", "dp"),
        P("dp"),
        P("dp"),
        P("dp"),
    )
    return jax.shard_map(local, mesh=mesh, in_specs=in_specs, out_specs=out_specs, check_vma=False)
```

profile of v0, /device:TPU:0, one launch (start us, length us, event | category | flops | bytes accessed | tf_op | source)
XLA Modules:
  0.0 2737.6 jit_solution(6054609252661517038)
XLA Ops:
  13.4 128.8 %all-reduce.18 = (bf16[2048]{0:T(1024)(128)(2,1)S(1)}, bf16[2048]{0:T(1024)(128)(2,1)}, bf16[2048]{0:T(1024)(128)(2,1)}) all-reduce(bf16[2048]{0:T(1024)(128)(2,1)S(1)} %dynamic-update-slice.1, bf16[2048]{0:T(1024)(128)(2,1)S(1)} %dynamic-update-slice.2, bf16[2048]{0:T(1024)(128)(2,1)S(1)} %dynamic-update-slice), channel_id=1, replica_groups=mesh['dp'=32,'mp'=4] {'dp'}, use_global_device_ids=true, to_apply=%add.9 | all-reduce | flops 6144 | bytes 24576
  143.4 22.6 all_gather.70
  168.4 24.3 all_gather.71
  193.6 18.8 all-gather.3
  213.7 23.9 all_gather.73
  238.8 22.9 all-gather
  264.9 16.2 while.119
  281.1 20.5 while.120
  318.1 32.3 %all-reduce.32.cloned.1.call-done = bf16[128,2048]{1,0:T(8,128)(2,1)} async-done(((bf16[128,2048]{1,0:T(8,128)(2,1)}), bf16[128,2048]{1,0:T(8,128)(2,1)}) %all-reduce.32.cloned.1.call-update) | async-done | bytes 524304 | tf_op jit(solution)/shard_map/psum | solution.py:204
  353.0 48.1 %all-gather.15.cloned.1.call-done = bf16[2048,1408]{1,0:T(8,128)(2,1)} async-done(((bf16[64,1408]{1,0:T(8,128)(2,1)}), bf16[2048,1408]{1,0:T(8,128)(2,1)}) %all-gather.15.cloned.1.call-update) | async-done | bytes 5767184 | tf_op jit(solution)/shard_map/all_gather | solution.py:414
  404.8 45.8 %all-gather.17.cloned.1.call-done = bf16[2048,1408]{1,0:T(8,128)(2,1)} async-done(((bf16[64,1408]{1,0:T(8,128)(2,1)}), bf16[2048,1408]{1,0:T(8,128)(2,1)}) %all-gather.17.cloned.1.call-update) | async-done | bytes 5767184 | tf_op jit(solution)/shard_map/all_gather | solution.py:415
  455.1 44.8 %all-gather.19.cloned.1.call-done = bf16[1408,2048]{0,1:T(8,128)(2,1)} async-done(((bf16[1408,64]{0,1:T(8,128)(2,1)}), bf16[1408,2048]{0,1:T(8,128)(2,1)}) %all-gather.19.cloned.1.call-update) | async-done | bytes 5767184 | tf_op jit(solution)/shard_map/all_gather | solution.py:416
  512.8 35.3 %all-reduce.34.cloned.1.call-done = bf16[128,2048]{1,0:T(8,128)(2,1)} async-done(((bf16[128,2048]{1,0:T(8,128)(2,1)}), bf16[128,2048]{1,0:T(8,128)(2,1)}) %all-reduce.34.cloned.1.call-update) | async-done | bytes 524304 | tf_op jit(solution)/shard_map/psum | solution.py:211
  565.7 128.7 %all-reduce.16 = (s32[2048]{0:T(1024)}, s32[3072]{0:T(1024)S(1)}) all-reduce(s32[2048]{0:T(1024)S(1)} %dynamic-update-slice.4, s32[3072]{0:T(1024)S(1)} %dynamic-update-slice.3), channel_id=1, replica_groups=mesh['dp'=32,'mp'=4] {'dp'}, use_global_device_ids=true, to_apply=%add.12 | all-reduce | flops 5120 | bytes 40960
  702.4 22.0 all-gather.4
  737.3 25.4 all_gather.81
  763.1 18.9 while.121
  782.8 23.4 while.122
  808.5 39.9 %all-reduce.36.cloned.1.call-done = bf16[96,2048]{1,0:T(8,128)(2,1)} async-done(((bf16[96,2048]{1,0:T(8,128)(2,1)}), bf16[96,2048]{1,0:T(8,128)(2,1)}) %all-reduce.36.cloned.1.call-update) | async-done | bytes 393232 | tf_op jit(solution)/shard_map/psum | solution.py:204
  863.2 42.8 %all-reduce.38.cloned.1.call-done = bf16[96,2048]{1,0:T(8,128)(2,1)} async-done(((bf16[96,2048]{1,0:T(8,128)(2,1)}), bf16[96,2048]{1,0:T(8,128)(2,1)}) %all-reduce.38.cloned.1.call-update) | async-done | bytes 393232 | tf_op jit(solution)/shard_map/psum | solution.py:211
  955.5 27.2 all-gather.2
  988.7 24.4 all_gather.84
  1015.2 21.4 while.123
  1055.6 38.4 %all-reduce.40.cloned.1.call-done = bf16[64,2048]{1,0:T(8,128)(2,1)} async-done(((bf16[64,2048]{1,0:T(8,128)(2,1)}), bf16[64,2048]{1,0:T(8,128)(2,1)}) %all-reduce.40.cloned.1.call-update) | async-done | bytes 262160 | tf_op jit(solution)/shard_map/psum | solution.py:204
  1112.6 43.8 %all-reduce.52.cloned.1.call-done = (bf16[64,2048]{1,0:T(8,128)(2,1)}, bf16[64,2048]{1,0:T(8,128)(2,1)}) async-done(((bf16[64,2048]{1,0:T(8,128)(2,1)}, bf16[64,2048]{1,0:T(8,128)(2,1)}), (bf16[64,2048]{1,0:T(8,128)(2,1)}, bf16[64,2048]{1,0:T(8,128)(2,1)})) %all-reduce.52.cloned.1.call-update) | async-done | bytes 524304 | tf_op jit(solution)/shard_map/psum | solution.py:211
  1164.1 25.2 while.126
  1197.7 71.2 %reduce-scatter.40.cloned.1.call-done = bf16[64,64]{1,0:T(8,128)(2,1)} async-done(((bf16[2048,64]{1,0:T(8,128)(2,1)}), bf16[64,64]{1,0:T(8,128)(2,1)}) %reduce-scatter.40.cloned.1.call-update) | async-done | bytes 8208
  1271.4 77.6 %reduce-scatter.42.cloned.1.call-done = bf16[64,64]{1,0:T(8,128)(2,1)} async-done(((bf16[2048,64]{1,0:T(8,128)(2,1)}), bf16[64,64]{1,0:T(8,128)(2,1)}) %reduce-scatter.42.cloned.1.call-update) | async-done | bytes 8208
  1351.2 42.1 %all-reduce.42.cloned.1.call-done = bf16[64,2048]{1,0:T(8,128)(2,1)} async-done(((bf16[64,2048]{1,0:T(8,128)(2,1)}), bf16[64,2048]{1,0:T(8,128)(2,1)}) %all-reduce.42.cloned.1.call-update) | async-done | bytes 262160 | tf_op jit(solution)/shard_map/psum | solution.py:292
  1416.8 15.0 all_to_all.58
  1445.0 39.7 %all-reduce.44.cloned.1.call-done = bf16[96,2048]{1,0:T(8,128)(2,1)} async-done(((bf16[96,2048]{1,0:T(8,128)(2,1)}), bf16[96,2048]{1,0:T(8,128)(2,1)}) %all-reduce.44.cloned.1.call-update) | async-done | bytes 393232 | tf_op jit(solution)/shard_map/psum | solution.py:248
  1493.9 64.3 %while.127 = (s32[]{:T(128)}, f32[1,768,64]{1,2,0:T(8,128)}, bf16[6,512,1,64]{1,3,2,0:T(8,128)(2,1)}, bf16[6,512,1,64]{1,3,2,0:T(8,128)(2,1)}, s32[6,512]{1,0:T(...) while((s32[]{:T(128)}, f32[1,768,64]{1,2,0:T(8,128)}, ...), condition=%wide.wide.region_46.47_spmd.clone, body=%wide.wide.region_45.46_spmd.clone.sunk | while | flops 254984192 | bytes 9057375 | solution.py:167
  1567.5 70.7 %reduce-scatter.44.cloned.1.call-done = bf16[96,64]{1,0:T(8,128)(2,1)} async-done(((bf16[3072,64]{1,0:T(8,128)(2,1)}), bf16[96,64]{1,0:T(8,128)(2,1)}) %reduce-scatter.44.cloned.1.call-update) | async-done | bytes 12304
  1641.0 77.7 %reduce-scatter.46.cloned.1.call-done = bf16[96,64]{1,0:T(8,128)(2,1)} async-done(((bf16[3072,64]{1,0:T(8,128)(2,1)}), bf16[96,64]{1,0:T(8,128)(2,1)}) %reduce-scatter.46.cloned.1.call-update) | async-done | bytes 12304
  1720.6 42.9 %all-reduce.46.cloned.1.call-done = bf16[96,2048]{1,0:T(8,128)(2,1)} async-done(((bf16[96,2048]{1,0:T(8,128)(2,1)}), bf16[96,2048]{1,0:T(8,128)(2,1)}) %all-reduce.46.cloned.1.call-update) | async-done | bytes 393232 | tf_op jit(solution)/shard_map/psum | solution.py:292
  1805.6 37.8 %all-reduce.48.cloned.1.call-done = bf16[128,2048]{1,0:T(8,128)(2,1)} async-done(((bf16[128,2048]{1,0:T(8,128)(2,1)}), bf16[128,2048]{1,0:T(8,128)(2,1)}) %all-reduce.48.cloned.1.call-update) | async-done | bytes 524304 | tf_op jit(solution)/shard_map/psum | solution.py:248
  1850.1 82.5 %while.125 = (s32[]{:T(128)}, f32[1,1024,64]{1,2,0:T(8,128)}, bf16[8,512,1,64]{1,3,2,0:T(8,128)(2,1)}, bf16[8,512,1,64]{1,3,2,0:T(8,128)(2,1)}, s32[8,512]{1,0:T...) while((s32[]{:T(128)}, f32[1,1024,64]{1,2,0:T(8,128)}, ...), condition=%wide.region_56.57_spmd.clone, body=%wide.region_55.56_spmd.clone.sunk | while | flops 339968000 | bytes 12313867 | solution.py:167
  1944.8 68.2 %reduce-scatter.48.cloned.1.call-done = bf16[128,64]{1,0:T(8,128)(2,1)} async-done(((bf16[4096,64]{1,0:T(8,128)(2,1)}), bf16[128,64]{1,0:T(8,128)(2,1)}) %reduce-scatter.48.cloned.1.call-update) | async-done | bytes 16400
  2013.8 79.9 %reduce-scatter.50.cloned.1.call-done = bf16[128,64]{1,0:T(8,128)(2,1)} async-done(((bf16[4096,64]{1,0:T(8,128)(2,1)}), bf16[128,64]{1,0:T(8,128)(2,1)}) %reduce-scatter.50.cloned.1.call-update) | async-done | bytes 16400
  2123.0 12.0 add_convert_fusion
  2148.0 11.9 add_convert_fusion.1
  2204.6 49.2 %reduce-scatter.28.cloned.1.call-done = bf16[64,64]{1,0:T(8,128)(2,1)} async-done(((bf16[2048,64]{1,0:T(8,128)(2,1)}), bf16[64,64]{1,0:T(8,128)(2,1)}) %reduce-scatter.28.cloned.1.call-update) | async-done | bytes 8208 | tf_op jit(solution)/shard_map/reduce_scatter | solution.py:469
  2255.1 44.1 %all-reduce.50.cloned.1.call-done = bf16[128,2048]{1,0:T(8,128)(2,1)} async-done(((bf16[128,2048]{1,0:T(8,128)(2,1)}), bf16[128,2048]{1,0:T(8,128)(2,1)}) %all-reduce.50.cloned.1.call-update) | async-done | bytes 524304 | tf_op jit(solution)/shard_map/psum | solution.py:292
  2300.7 126.0 %all-reduce.17 = (bf16[2048]{0:T(1024)(128)(2,1)S(1)}, bf16[2048]{0:T(1024)(128)(2,1)S(1)}, bf16[2048]{0:T(1024)(128)(2,1)S(1)}) all-reduce(bf16[2048]{0:T(1024)(128)(2,1)S(1)} %add_convert_fusion.13, bf16[2048]{0:T(1024)(128)(2,1)S(1)} %add_convert_fusion.12, ...), channel_id=18, replica_groups=mesh['dp'=32,'mp'=4] {'dp'}, use_global_device_ids=true, to_apply=%region_72.73.clone | all-reduce | flops 6144 | bytes 24576
  2434.5 28.9 %reduce-scatter.26.cloned.1.call-done = bf16[64,512]{1,0:T(8,128)(2,1)} async-done(((bf16[2048,512]{1,0:T(8,128)(2,1)}), bf16[64,512]{1,0:T(8,128)(2,1)}) %reduce-scatter.26.cloned.1.call-update) | async-done | bytes 65552 | tf_op jit(solution)/shard_map/reduce_scatter | solution.py:466
  2465.0 86.7 %reduce-scatter.38.cloned.1.call-done = bf16[1408,64]{0,1:T(8,128)(2,1)} async-done(((bf16[1408,2048]{0,1:T(8,128)(2,1)}), bf16[1408,64]{0,1:T(8,128)(2,1)}) %reduce-scatter.38.cloned.1.call-update) | async-done | bytes 180240 | tf_op jit(solution)/shard_map/reduce_scatter | solution.py:484
  2553.4 87.2 %reduce-scatter.36.cloned.1.call-done = bf16[64,1408]{1,0:T(8,128)(2,1)} async-done(((bf16[2048,1408]{1,0:T(8,128)(2,1)}), bf16[64,1408]{1,0:T(8,128)(2,1)}) %reduce-scatter.36.cloned.1.call-update) | async-done | bytes 180240 | tf_op jit(solution)/shard_map/reduce_scatter | solution.py:481
  2642.2 86.7 %reduce-scatter.34.cloned.1.call-done = bf16[64,1408]{1,0:T(8,128)(2,1)} async-done(((bf16[2048,1408]{1,0:T(8,128)(2,1)}), bf16[64,1408]{1,0:T(8,128)(2,1)}) %reduce-scatter.34.cloned.1.call-update) | async-done | bytes 180240 | tf_op jit(solution)/shard_map/reduce_scatter | solution.py:478
  (1329 shorter events, 731.2 us)
Async XLA Ops:
  7.2 254.9 %all-gather.11.cloned.1.call-start = ((), (), s32[]{:S(2)}) async-start(), calls=%async_computation.23 | async-start | bytes 2162688 | tf_op jit(solution)/shard_map/all_gather | solution.py:410
  7.9 205.8 %copy-start.167 = (bf16[64,64]{1,0:T(8,128)(2,1)S(1)}, bf16[64,64]{1,0:T(8,128)(2,1)}, u32[]{:S(2)}) copy-start(bf16[64,64]{1,0:T(8,128)(2,1)} %param.39) | copy-start | bytes 24580
  7.9 295.1 %all-gather.13.cloned.1.call-start = ((), (), s32[]{:S(2)}) async-start(), calls=%async_computation.24 | async-start | bytes 2162688 | tf_op jit(solution)/shard_map/all_gather | solution.py:413
  8.7 341.8 %all-reduce.32.cloned.1.call-start = ((), (), s32[]{:S(2)}) async-start(), calls=%async_computation.25 | async-start | bytes 1048576 | tf_op jit(solution)/shard_map/psum | solution.py:204
  306.4 94.7 %all-gather.15.cloned.1.call-start = ((), (), s32[]{:S(2)}) async-start(), calls=%async_computation.26 | async-start | bytes 5947392 | tf_op jit(solution)/shard_map/all_gather | solution.py:414
  306.9 143.6 %all-gather.17.cloned.1.call-start = ((), (), s32[]{:S(2)}) async-start(), calls=%async_computation.27 | async-start | bytes 5947392 | tf_op jit(solution)/shard_map/all_gather | solution.py:415
  307.5 192.5 %all-gather.19.cloned.1.call-start = ((), (), s32[]{:S(2)}) async-start(), calls=%async_computation.28 | async-start | bytes 5947392 | tf_op jit(solution)/shard_map/all_gather | solution.py:416
  311.2 196.5 %all-to-all-start.4 = ((s32[32,1,2]{2,1,0:T(1,128)}), s32[32,1,2]{2,1,0:T(1,128)S(1)}, u32[]{:S(2)}, u32[]{:S(2)}) async-start(s32[32,1,2]{2,1,0:T(1,128)} %bitcast.23), calls=%async_computation.4 | async-start | bytes 32768 | tf_op jit(solution)/shard_map/all_to_all | solution.py:340
  317.0 231.1 %all-reduce.34.cloned.1.call-start = ((), (), s32[]{:S(2)}) async-start(), calls=%async_computation.29 | async-start | bytes 1048576 | tf_op jit(solution)/shard_map/psum | solution.py:211
  507.8 46.2 %all-to-all-start.1 = ((s32[32,1,3]{2,1,0:T(1,128)}), s32[32,1,3]{2,1,0:T(1,128)S(1)}, u32[]{:S(2)}, u32[]{:S(2)}) async-start(s32[32,1,3]{2,1,0:T(1,128)} %bitcast.11), calls=%async_computation.1 | async-start | bytes 32768 | tf_op jit(solution)/shard_map/all_to_all | solution.py:340
  554.0 144.3 %all-to-all-start = ((bf16[32,3,2048]{2,1,0:T(4,128)(2,1)}), bf16[32,3,2048]{2,1,0:T(4,128)(2,1)S(1)}, u32[]{:S(2)}, u32[]{:S(2)}) async-start(bf16[32,3,2048]{2,1,0:T(4,128)(2,1)} %reshape.1429), calls=%async_computation | async-start | bytes 1048576 | tf_op jit(solution)/shard_map/all_to_all | solution.py:333
  561.1 287.4 %all-reduce.36.cloned.1.call-start = ((), (), s32[]{:S(2)}) async-start(), calls=%async_computation.30 | async-start | bytes 786432 | tf_op jit(solution)/shard_map/psum | solution.py:204
  808.1 98.0 %all-reduce.38.cloned.1.call-start = ((), (), s32[]{:S(2)}) async-start(), calls=%async_computation.31 | async-start | bytes 786432 | tf_op jit(solution)/shard_map/psum | solution.py:211
  908.3 18.3 all-to-all-start.2
  933.8 13.0 all-to-all-start.3
  946.8 107.4 %all-to-all-start.6 = ((bf16[32,2,2048]{2,1,0:T(2,128)(2,1)}), bf16[32,2,2048]{2,1,0:T(2,128)(2,1)}, u32[]{:S(2)}, u32[]{:S(2)}) async-start(bf16[32,2,2048]{2,1,0:T(2,128)(2,1)} %reshape.1455), calls=%async_computation.6 | async-start | bytes 524288 | tf_op jit(solution)/shard_map/all_to_all | solution.py:369
  951.5 142.4 %all-reduce.40.cloned.1.call-start = ((), (), s32[]{:S(2)}) async-start(), calls=%async_computation.32 | async-start | bytes 524288 | tf_op jit(solution)/shard_map/psum | solution.py:204
  1054.1 102.2 %all-reduce.52.cloned.1.call-start = ((), (), s32[]{:S(2)}) async-start(), calls=%async_computation.51 | async-start | bytes 1048576 | tf_op jit(solution)/shard_map/psum | solution.py:211
  1112.5 156.4 %reduce-scatter.40.cloned.1.call-start = ((), (), s32[]{:S(2)}) async-start(), calls=%async_computation.45 | async-start | bytes 540672
  1191.5 157.5 %reduce-scatter.42.cloned.1.call-start = ((), (), s32[]{:S(2)}) async-start(), calls=%async_computation.46 | async-start | bytes 540672
  1195.5 197.8 %all-reduce.42.cloned.1.call-start = ((), (), s32[]{:S(2)}) async-start(), calls=%async_computation.33 | async-start | bytes 524288 | tf_op jit(solution)/shard_map/psum | solution.py:292
  1197.7 197.3 %copy-start.69 = (bf16[64,2048]{1,0:T(8,128)(2,1)S(1)}, bf16[64,2048]{1,0:T(8,128)(2,1)}, u32[]{:S(2)}) copy-start(bf16[64,2048]{1,0:T(8,128)(2,1)} %get-tuple-element.1350) | copy-start | bytes 786436
  1197.7 197.3 %copy-start.172 = (f32[64]{0:T(128)S(1)}, f32[64]{0:T(128)}, u32[]{:S(2)}) copy-start(f32[64]{0:T(128)} %copy-done.171) | copy-start | bytes 772
  1397.4 16.0 all-to-all-start.7
  1404.5 80.3 %all-reduce.44.cloned.1.call-start = ((), (), s32[]{:S(2)}) async-start(), calls=%async_computation.34 | async-start | bytes 786432 | tf_op jit(solution)/shard_map/psum | solution.py:248
  1444.8 193.4 %reduce-scatter.44.cloned.1.call-start = ((), (), s32[]{:S(2)}) async-start(), calls=%async_computation.47 | async-start | bytes 811008
  1560.4 158.3 %reduce-scatter.46.cloned.1.call-start = ((), (), s32[]{:S(2)}) async-start(), calls=%async_computation.48 | async-start | bytes 811008
  1565.4 198.1 %all-reduce.46.cloned.1.call-start = ((), (), s32[]{:S(2)}) async-start(), calls=%async_computation.35 | async-start | bytes 786432 | tf_op jit(solution)/shard_map/psum | solution.py:292
  1768.0 18.3 all-to-all-start.9
  1775.1 68.2 %all-reduce.48.cloned.1.call-start = ((), (), s32[]{:S(2)}) async-start(), calls=%async_computation.36 | async-start | bytes 1048576 | tf_op jit(solution)/shard_map/psum | solution.py:248
  1802.7 210.3 %reduce-scatter.48.cloned.1.call-start = ((), (), s32[]{:S(2)}) async-start(), calls=%async_computation.49 | async-start | bytes 1081344
  1935.1 158.7 %reduce-scatter.50.cloned.1.call-start = ((), (), s32[]{:S(2)}) async-start(), calls=%async_computation.50 | async-start | bytes 1081344
  1942.5 260.8 %reduce-scatter.30.cloned.1.call-start = ((), (), s32[]{:S(2)}) async-start(), calls=%async_computation.40 | async-start | bytes 540672 | tf_op jit(solution)/shard_map/reduce_scatter | solution.py:472
  2096.2 157.6 %reduce-scatter.28.cloned.1.call-start = ((), (), s32[]{:S(2)}) async-start(), calls=%async_computation.39 | async-start | bytes 540672 | tf_op jit(solution)/shard_map/reduce_scatter | solution.py:469
  2097.7 201.5 %all-reduce.50.cloned.1.call-start = ((), (), s32[]{:S(2)}) async-start(), calls=%async_computation.37 | async-start | bytes 1048576 | tf_op jit(solution)/shard_map/psum | solution.py:292
  2100.1 332.9 %reduce-scatter.32.cloned.1.call-start = ((), (), s32[]{:S(2)}) async-start(), calls=%async_computation.41 | async-start | bytes 2162688 | tf_op jit(solution)/shard_map/reduce_scatter | solution.py:475
  2104.5 358.9 %reduce-scatter.26.cloned.1.call-start = ((), (), s32[]{:S(2)}) async-start(), calls=%async_computation.38 | async-start | bytes 2162688 | tf_op jit(solution)/shard_map/reduce_scatter | solution.py:466
  2109.9 441.8 %reduce-scatter.38.cloned.1.call-start = ((), (), s32[]{:S(2)}) async-start(), calls=%async_computation.44 | async-start | bytes 5947392 | tf_op jit(solution)/shard_map/reduce_scatter | solution.py:484
  2135.1 505.4 %reduce-scatter.36.cloned.1.call-start = ((), (), s32[]{:S(2)}) async-start(), calls=%async_computation.43 | async-start | bytes 5947392 | tf_op jit(solution)/shard_map/reduce_scatter | solution.py:481
  2159.9 569.0 %reduce-scatter.34.cloned.1.call-start = ((), (), s32[]{:S(2)}) async-start(), calls=%async_computation.42 | async-start | bytes 5947392 | tf_op jit(solution)/shard_map/reduce_scatter | solution.py:478
  2186.3 14.2 all-to-all-start.5
  2200.7 227.8 %copy-start.44 = (bf16[128,2048]{1,0:T(8,128)(2,1)S(1)}, bf16[128,2048]{1,0:T(8,128)(2,1)}, u32[]{:S(2)}) copy-start(bf16[128,2048]{1,0:T(8,128)(2,1)} %copy-done.43) | copy-start | bytes 1572868
  2200.7 227.8 %copy-start.124 = (f32[2048]{0:T(1024)S(1)}, f32[2048]{0:T(1024)}, u32[]{:S(2)}) copy-start(f32[2048]{0:T(1024)} %copy-done.122) | copy-start | bytes 24580
  2200.7 227.8 %copy-start.185 = (f32[128]{0:T(128)S(1)}, f32[128]{0:T(128)}, u32[]{:S(2)}) copy-start(f32[128]{0:T(128)} %copy-done.183) | copy-start | bytes 1540
  2200.7 227.8 %copy-start.216 = (f32[128]{0:T(128)S(1)}, f32[128]{0:T(128)}, u32[]{:S(2)}) copy-start(f32[128]{0:T(128)} %copy-done.215) | copy-start | bytes 1540
  2200.7 227.8 %copy-start.218 = (f32[128]{0:T(128)S(1)}, f32[128]{0:T(128)}, u32[]{:S(2)}) copy-start(f32[128]{0:T(128)} %copy-done.217) | copy-start | bytes 1540
  2202.7 225.8 %copy-start.15 = (bf16[128,2048]{1,0:T(8,128)(2,1)S(1)}, bf16[128,2048]{1,0:T(8,128)(2,1)}, u32[]{:S(2)}) copy-start(bf16[128,2048]{1,0:T(8,128)(2,1)} %all-reduce.32.cloned.1.call-done) | copy-start | bytes 1572868
  2202.7 225.8 %copy-start.22 = (f32[128,2048]{1,0:T(8,128)S(1)}, f32[128,2048]{1,0:T(8,128)}, u32[]{:S(2)}) copy-start(f32[128,2048]{1,0:T(8,128)} %param.47) | copy-start | bytes 3145732
  (280 other events, 7971.3 us)
Sparse Core Ops, SparseCore 0:
  10.3 46.2 all-gather.10
  58.9 43.1 all-gather.12
  306.4 43.9 all-reduce.31
  352.5 48.5 all-gather.14
  403.2 47.2 all-gather.16
  452.7 47.2 all-gather.18
  505.6 42.4 all-reduce.33
  808.2 40.2 all-reduce.35
  863.1 42.8 all-reduce.37
  1054.2 39.6 all-reduce.39
  1112.6 43.6 all-reduce.51
  1191.6 77.2 reduce-scatter.39
  1272.7 76.2 reduce-scatter.41
  1351.9 41.3 all-reduce.41
  1444.9 39.7 all-reduce.43
  1560.5 77.6 reduce-scatter.43
  1641.9 76.7 reduce-scatter.45
  1721.6 41.8 all-reduce.45
  1802.8 40.5 all-reduce.47
  1935.1 77.8 reduce-scatter.47
  2016.9 76.7 reduce-scatter.49
  2097.1 76.2 reduce-scatter.29
  2177.5 76.2 reduce-scatter.27
  2256.6 42.6 all-reduce.49
  2302.8 79.0 reduce-scatter.31
  2385.3 78.1 reduce-scatter.25
  2467.0 84.5 reduce-scatter.37
  2555.9 84.5 reduce-scatter.35
  2644.3 84.5 reduce-scatter.33
where the time goes:
time: 2760 us; the launch traced here: 2740 us
  waiting for transfers between devices  1410 us (51%)
  blocking collectives  610 us (22%)
  matrix products  393 us (14%)
  local copies, waits for them, and re-layouts  158 us (6%)
  other arithmetic  92.4 us (3%)
  starting transfers between devices  56.1 us (2%)
    unnamed x35, waiting for transfers between devices  449 us
    unnamed x3, blocking collectives  383 us
    psum x3, waiting for transfers between devices, step_backward(): lax.psum((project_back(grad_query, w_query) + project_back(grad_key, w_ke...  129 us
    psum x3, waiting for transfers between devices, step_forward(): lax.psum(project(hidden, w_down).astype(jnp.bfloat16), 'mp')  122 us
    psum x3, waiting for transfers between devices, step_forward(): lax.psum(project(mixed.astype(jnp.bfloat16), w_out).astype(jnp.bfloat16),...  111 us
    dot_general x21, matrix products, outer_rows(): lax.dot_general(left, right, (((0,), (0,)), ((), ())), preferred_element_...  90.1 us
    reduce_scatter x1, waiting for transfers between devices, local(): lax.psum_scatter(totals[5].astype(jnp.bfloat16), 'dp', scatter_dimension=...  87.2 us
    reduce_scatter x1, waiting for transfers between devices, local(): lax.psum_scatter(totals[6].astype(jnp.bfloat16), 'dp', scatter_dimension=...  86.7 us
  transfers between devices with their start and end apart: 38, of which 30 were waited for; matrix products, arithmetic and copies ran while one was open for 10% of the time, Pallas kernels for 0%

commit v1 on v0

v1 whole, which is shorter than its diff:
```python
import math

import jax
import jax.numpy as jnp
from jax import lax
from jax.sharding import PartitionSpec as P

HD = 64
SECOND_SLOTS = 96
THIRD_SLOTS = 64
EPS = 1e-05
NEG = -1e30
ROPE_BASE = 10000.0
FAR = 1073741824
BF = jnp.bfloat16
F32 = jnp.float32


def dot_nn(left, right):
    return lax.dot_general(left, right, (((1,), (0,)), ((), ())), preferred_element_type=F32)


def dot_nt(left, right):
    return lax.dot_general(left, right, (((1,), (1,)), ((), ())), preferred_element_type=F32)


def dot_tn(left, right):
    return lax.dot_general(left, right, (((0,), (0,)), ((), ())), preferred_element_type=F32)


def unit_of(values):
    factor = lax.rsqrt(jnp.mean(values * values, axis=-1, keepdims=True) + EPS)
    return values * factor, factor


def unit_back(shaped, unit, factor):
    return factor * (shaped - unit * jnp.mean(shaped * unit, axis=-1, keepdims=True))


def rotary_tables(place):
    freq = jnp.exp(jnp.arange(HD // 2, dtype=F32) * (-2.0 * math.log(ROPE_BASE) / HD))
    angle = place.astype(F32)[:, None] * freq[None, :]
    cosine, sine = jnp.cos(angle), jnp.sin(angle)
    return cosine, sine


def wide_tables(cosine, sine, heads):
    one = jnp.concatenate([cosine, cosine], axis=1)
    two = jnp.concatenate([-sine, sine], axis=1)
    rest = one.shape
    return (
        jnp.concatenate([jnp.tile(one, (1, heads + 1)), jnp.ones(rest, F32)], axis=1),
        jnp.concatenate([jnp.tile(two, (1, heads + 1)), jnp.zeros(rest, F32)], axis=1),
    )


def swap_halves(values):
    rows, width = values.shape
    parts = values.reshape(rows, width // HD, 2, HD // 2)
    return parts[:, :, ::-1, :].reshape(rows, width)


def scores_of(query, query_place, key_part, place_part):
    scores = dot_nt(query, key_part)
    return jnp.where(place_part[None, :] <= query_place[:, None], scores, NEG)


def key_blocks(packed, key_place):
    block = 512
    blocks = packed.shape[0] // block
    return packed.reshape(blocks, block, 2 * HD), key_place.reshape(blocks, block)


def attend_forward(query, packed, key_place, query_place):
    width = query.shape[0]

    def one_block(carry, part):
        top, total, acc = carry
        scores = scores_of(query, query_place, part[0][:, :HD], part[1])
        peak = jnp.maximum(top, jnp.max(scores, axis=-1))
        weights = jnp.exp(scores - peak[:, None])
        fade = jnp.exp(top - peak)
        total = total * fade + jnp.sum(weights, axis=-1)
        acc = acc * fade[:, None] + dot_nn(weights.astype(BF), part[0][:, HD:])
        return (peak, total, acc), None

    start = (jnp.full((width,), NEG, F32), jnp.zeros((width,), F32), jnp.zeros((width, HD), F32))
    (top, total, acc), unused = lax.scan(one_block, start, key_blocks(packed, key_place))
    return acc / total[:, None], top + jnp.log(total)


def attend_backward(query, packed, key_place, query_place, log_total, grad_mixed, delta):
    def one_block(grad_query, part):
        keys, values = part[0][:, :HD], part[0][:, HD:]
        weights = jnp.exp(scores_of(query, query_place, keys, part[1]) - log_total[:, None])
        grad_weights = dot_nt(grad_mixed, values)
        grad_scores = (weights * (grad_weights - delta[:, None])).astype(BF)
        grad_query = grad_query + dot_nn(grad_scores, keys)
        grad_keys = dot_tn(grad_scores, query)
        grad_values = dot_tn(weights.astype(BF), grad_mixed)
        return grad_query, jnp.concatenate([grad_keys, grad_values], axis=1)

    grad_query, grad_packed = lax.scan(
        one_block, jnp.zeros(query.shape, F32), key_blocks(packed, key_place)
    )
    return grad_query, grad_packed.reshape(packed.shape)


def stack_heads(values):
    count = values.shape[0]
    return values.reshape(count, -1, HD).transpose(1, 0, 2).reshape(-1, HD)


def unstack_heads(values, count):
    return values.reshape(-1, count, HD).transpose(1, 0, 2).reshape(count, -1)


def sum_mp(values):
    return lax.psum(values.astype(BF), "mp").astype(F32)


def split_columns(heads, hidden):
    ends, total = [], 0
    for width in (heads * HD + 2 * HD, heads * HD, hidden, hidden, hidden, 128):
        ends.append((total, total + width))
        total += width
    return ends


def local(
    tokens, depths, second_slot, third_slot, w_query, w_key, w_value, w_out, w_gate, w_up,
    w_down, norm_first, norm_second, router, cotangent,
):
    me = lax.axis_index("dp")
    devices = lax.axis_size("dp")
    rows = tokens.shape[0]
    heads = w_query.shape[1] // HD
    hidden_width = w_gate.shape[1]
    depth = w_query.shape[0]
    spans = split_columns(heads, hidden_width)

    actives = (
        (depths >= 2) & (second_slot >= 0),
        (depths >= 3) & (third_slot >= 0),
    )
    picks, marks = [], []
    for active, slot, capacity in zip(actives, (second_slot, third_slot), (SECOND_SLOTS, THIRD_SLOTS)):
        pick = (jnp.arange(capacity)[:, None] == slot[None, :]) & active[None, :]
        picks.append(pick.astype(BF))
        mark = jnp.min(jnp.where(pick, jnp.arange(rows, dtype=jnp.int32)[None, :], rows), axis=1)
        marks.append(mark)

    column = lambda a: a.reshape(depth, 1).astype(BF)
    second_mark = jnp.pad(marks[0], (0, 2 * depth - SECOND_SLOTS), constant_values=rows)
    extras = jnp.concatenate(
        [
            column(norm_first),
            column(norm_second),
            column(router),
            column(second_mark[:depth]),
            column(second_mark[depth:]),
            column(marks[1]),
            jnp.zeros((depth, 122), BF),
        ],
        axis=1,
    )
    shard = jnp.concatenate(
        [w_query, w_key, w_value, w_out.T, w_gate, w_up, w_down.T, extras], axis=1
    )
    full = lax.all_gather(shard, "dp", axis=0, tiled=True)
    w_qkv, w_o, w_g, w_u, w_d, extra = [full[:, a:b] for a, b in spans]
    extra = extra[:, :8].astype(F32)
    gain_first, gain_second, gain_router = extra[:, 0], extra[:, 1], extra[:, 2]
    marks_all = extra[:, 3:6].astype(jnp.int32).reshape(devices, depth, 3)
    second_all = jnp.concatenate([marks_all[:, :, 0], marks_all[:, : SECOND_SLOTS - depth, 1]], axis=1)
    third_all = marks_all[:, :, 2]
    base = (jnp.arange(devices, dtype=jnp.int32) * rows)[:, None]

    def place_of(mark, offset):
        return jnp.where(mark < rows, mark + offset, FAR)

    own = jnp.arange(rows, dtype=jnp.int32)
    levels = (
        (rows, None, own + me * rows, (jnp.arange(devices * rows, dtype=jnp.int32))),
        (SECOND_SLOTS, picks[0], place_of(marks[0], me * rows), place_of(second_all, base).reshape(-1)),
        (THIRD_SLOTS, picks[1], place_of(marks[1], me * rows), place_of(third_all, base).reshape(-1)),
    )
    state = tokens.astype(F32)
    kept = []
    for count, pick, place, key_place in levels:
        rows_in = state.astype(BF)
        if pick is not None:
            rows_in = dot_nn(pick, rows_in).astype(BF)
        level = rows_in.astype(F32)
        unit, factor = unit_of(level)
        normed = (unit * gain_first).astype(BF)
        tables = wide_tables(*rotary_tables(jnp.where(place == FAR, 0, place)), heads)
        qkv = dot_nn(normed, w_qkv)
        qkv = (qkv * tables[0] + swap_halves(qkv) * tables[1]).astype(BF)
        query = stack_heads(qkv[:, : heads * HD]) * BF(HD**-0.5)
        packed = lax.all_gather(qkv[:, heads * HD :], "dp", axis=0, tiled=True)
        query_place = jnp.tile(place, heads)
        mixed, log_total = attend_forward(query, packed, key_place, query_place)
        mixed_rows = unstack_heads(mixed, count).astype(BF)
        attn = sum_mp(dot_nt(mixed_rows, w_o))
        middle = level + attn
        unit_mid, factor_mid = unit_of(middle)
        second = (unit_mid * gain_second).astype(BF)
        gate_part, up_part = dot_nn(second, w_g), dot_nn(second, w_u)
        hidden = (jax.nn.silu(gate_part) * up_part).astype(BF)
        ffn = sum_mp(dot_nt(hidden, w_d))
        gate = jax.nn.sigmoid(jnp.sum(level * gain_router, axis=-1, keepdims=True))
        update = (gate * (attn + ffn)).astype(BF)
        if pick is not None:
            update = dot_tn(pick, update)
        state = state + update.astype(F32)
        kept.append(
            (pick, level, unit, factor, normed, tables, query, packed, key_place, query_place,
             mixed, log_total, mixed_rows, attn, unit_mid, factor_mid, second, gate_part, up_part, hidden, ffn, gate)
        )

    flow = cotangent
    terms = []
    for items in reversed(kept):
        (pick, level, unit, factor, normed, tables, query, packed, key_place, query_place,
         mixed, log_total, mixed_rows, attn, unit_mid, factor_mid, second, gate_part, up_part, hidden, ffn, gate) = items
        count = level.shape[0]
        grad_update = flow.astype(BF)
        if pick is not None:
            grad_update = dot_nn(pick, grad_update)
        grad_update = grad_update.astype(F32)
        gate_logit = jnp.sum(grad_update * (attn + ffn), axis=-1, keepdims=True) * gate * (1.0 - gate)
        grad_ffn = (gate * grad_update).astype(BF)
        grad_hidden = dot_nn(grad_ffn, w_d)
        sigma = jax.nn.sigmoid(gate_part)
        grad_gate_part = (grad_hidden * up_part * sigma * (1.0 + gate_part * (1.0 - sigma))).astype(BF)
        grad_up_part = (grad_hidden * gate_part * sigma).astype(BF)
        grad_second = sum_mp(dot_nt(grad_gate_part, w_g) + dot_nt(grad_up_part, w_u))
        grad_middle = unit_back(grad_second * gain_second, unit_mid, factor_mid)
        grad_attn = (gate * grad_update + grad_middle).astype(BF)
        grad_mixed = dot_nn(grad_attn, w_o).astype(BF)
        grad_heads = stack_heads(grad_mixed)
        delta = jnp.sum(grad_heads.astype(F32) * mixed, axis=-1)
        grad_query, grad_packed = attend_backward(
            query, packed, key_place, query_place, log_total, grad_heads, delta
        )
        own_packed = lax.psum_scatter(
            grad_packed.astype(BF), "dp", scatter_dimension=0, tiled=True
        ).astype(F32)
        grad_qkv = jnp.concatenate(
            [unstack_heads(grad_query, count) * HD**-0.5, own_packed], axis=1
        )
        grad_qkv = (grad_qkv * tables[0] - swap_halves(grad_qkv) * tables[1]).astype(BF)
        grad_normed = sum_mp(dot_nt(grad_qkv, w_qkv))
        grad_rows = unit_back(grad_normed * gain_first, unit, factor) + grad_middle + gate_logit * gain_router
        grad_rows = grad_rows.astype(BF)
        if pick is not None:
            grad_rows = dot_tn(pick, grad_rows)
        flow = flow + grad_rows.astype(F32)
        terms.append(
            (normed, grad_qkv, grad_attn, mixed_rows, second,
             grad_gate_part, grad_up_part, grad_ffn, hidden,
             jnp.sum(grad_normed * unit, axis=0),
             jnp.sum(grad_second * unit_mid, axis=0),
             jnp.sum(level * gate_logit, axis=0))
        )
    joined = [jnp.concatenate(list(parts), axis=0) for parts in list(zip(*terms))[:9]]
    normed, grad_qkv, grad_attn, mixed_rows, second, grad_gate_part, grad_up_part, grad_ffn, hidden = joined
    vectors = [sum(parts) for parts in list(zip(*terms))[9:]]
    totals = jnp.concatenate(
        [
            dot_tn(normed, grad_qkv).astype(BF),
            dot_tn(grad_attn, mixed_rows).astype(BF),
            dot_tn(second, grad_gate_part).astype(BF),
            dot_tn(second, grad_up_part).astype(BF),
            dot_tn(grad_ffn, hidden).astype(BF),
            jnp.pad(jnp.stack(vectors, axis=1), ((0, 0), (0, 125))).astype(BF),
        ],
        axis=1,
    )
    reduced = lax.psum_scatter(totals, "dp", scatter_dimension=0, tiled=True).astype(F32)
    qkv, out_t, gate_g, up_g, down_t, vec = [reduced[:, a:b] for a, b in spans]
    q_width = heads * HD
    return (
        state, flow,
        qkv[:, :q_width], qkv[:, q_width : q_width + HD], qkv[:, q_width + HD :],
        out_t.T, gate_g, up_g, down_t.T, vec[:, 0], vec[:, 1], vec[:, 2],
    )


def solution(mesh):
    in_specs = (
        P("dp", None), P("dp"), P("dp"), P("dp"), P("dp", "mp"), P("dp", "mp"), P("dp", "mp"),
        P("mp", "dp"), P("dp", "mp"), P("dp", "mp"), P("mp", "dp"), P("dp"), P("dp"), P("dp"),
        P("dp", None),
    )
    out_specs = (
        P("dp", None), P("dp", None), P("dp", "mp"), P("dp", "mp"), P("dp", "mp"), P("mp", "dp"),
        P("dp", "mp"), P("dp", "mp"), P("mp", "dp"), P("dp"), P("dp"), P("dp"),
    )
    return jax.shard_map(local, mesh=mesh, in_specs=in_specs, out_specs=out_specs, check_vma=False)
```

time: 2760 us -> 1430 us (0.52)
  blocking collectives: 610 us -> 52.7 us
  waiting for transfers between devices: 1410 us -> 914 us
  matrix products: 393 us -> 203 us
  starting transfers between devices: 56.1 us -> 1.56 us
    unnamed x3 -> x0, blocking collectives: 383 us -> none
    unnamed x35 -> x18, waiting for transfers between devices: 449 us -> 128 us
    dot_general x192 -> x169, matrix products: 393 us -> 203 us  [the longest x69 83.9 us: dot_nt(): lax.dot_general(left, right, (((1,), (1,)), ((), ())), preferred_element_...]
    all_gather x9 -> x2, blocking collectives: 212 us -> 52.7 us  [local(): packed = lax.all_gather(qkv[:, heads * HD:], 'dp', axis=0, tiled=True)]
    reduce_scatter x7 -> x3, waiting for transfers between devices: 339 us -> 222 us  [local(): lax.psum_scatter(grad_packed.astype(BF), 'dp', scatter_dimension=0, tiled...]
    all_to_all x9 -> x0, starting transfers between devices: 53.2 us -> none  [the longest x2 14.2 us: return_grads(): lax.all_to_all(values.reshape(devices, capacity // devices, width), 'dp',...]
    all_to_all x9 -> x0, waiting for transfers between devices: 40.9 us -> none  [the longest x2 19.1 us: return_grads(): lax.all_to_all(values.reshape(devices, capacity // devices, width), 'dp',...]
    squeeze x0 -> x38, local copies, waits for them, and re-layouts: none -> 28.2 us  [the longest x36 27.6 us: attend_forward(): lax.scan(one_block, start, key_blocks(packed, key_place))]
  transfers between devices with their start and end apart: 38 -> 17, of which waited for: 30 -> 17; matrix products, arithmetic and copies ran while one was open for 10% -> 3% of each run, Pallas kernels for 0% -> 0%
where the time goes in v1:
time: 1430 us; the launch traced here: 1420 us
  waiting for transfers between devices  914 us (64%)
  matrix products  203 us (14%)
  local copies, waits for them, and re-layouts  162 us (11%)
  other arithmetic  65.3 us (5%)
  blocking collectives  52.7 us (4%)
  between operations  16.9 us (1%)
    psum x11, waiting for transfers between devices, sum_mp(): return lax.psum(values.astype(BF), 'mp').astype(F32)  434 us
    reduce_scatter x3, waiting for transfers between devices, local(): lax.psum_scatter(grad_packed.astype(BF), 'dp', scatter_dimension=0, tiled...  222 us
    unnamed x18, waiting for transfers between devices  128 us
    all_gather x1, waiting for transfers between devices, local(): full = lax.all_gather(shard, 'dp', axis=0, tiled=True)  87.8 us
    dot_general x69, matrix products, dot_nt(): lax.dot_general(left, right, (((1,), (1,)), ((), ())), preferred_element_...  83.9 us
    dot_general x55, matrix products, dot_nn(): lax.dot_general(left, right, (((1,), (0,)), ((), ())), preferred_element_...  72.7 us
    all_gather x2, blocking collectives, local(): packed = lax.all_gather(qkv[:, heads * HD:], 'dp', axis=0, tiled=True)  52.7 us
    unnamed x355, local copies, waits for them, and re-layouts  50.9 us
  transfers between devices with their start and end apart: 17, of which 17 were waited for; matrix products, arithmetic and copies ran while one was open for 3% of the time, Pallas kernels for 0%

profile of v1, /device:TPU:0, one launch (start us, length us, event | category | flops | bytes accessed | tf_op | source)
XLA Modules:
  0.0 1416.9 jit_solution(15195786334394454379)
XLA Ops:
  15.5 87.8 %all-gather.3.cloned.1.call-done = bf16[2048,5504]{1,0:T(8,128)(2,1)} async-done(((bf16[64,5504]{1,0:T(8,128)(2,1)}), bf16[2048,5504]{1,0:T(8,128)(2,1)}) %all-gather.3.cloned.1.call-update) | async-done | bytes 22544400 | tf_op jit(solution)/shard_map/all_gather | solution.py:170
  112.7 41.7 %all-gather.5.cloned.1.call-done = bf16[4096,128]{1,0:T(8,128)(2,1)} async-done(((bf16[128,128]{1,0:T(8,128)(2,1)}), bf16[4096,128]{1,0:T(8,128)(2,1)}) %all-gather.5.cloned.1.call-update) | async-done | bytes 1048592 | tf_op jit(solution)/shard_map/all_gather | solution.py:201
  154.4 18.8 %while.84 = (s32[]{:T(128)}, f32[1024]{0:T(1024)S(1)}, f32[1024]{0:T(1024)S(1)}, f32[1024,64]{0,1:T(8,128)S(1)}, s32[8,512]{1,0:T(8,128)S(1)}, /*index=5*/bf16[8...) while((s32[]{:T(128)}, f32[1024]{0:T(1024)S(1)}, ...), condition=%wide.region_7.8_spmd.clone, body=%wide.region_4.7_spmd.clone.sunk | while | flops 138089472 | bytes 7551617 | solution.py:88
  178.9 40.5 %all-reduce.21.cloned.1.call-done = bf16[128,2048]{1,0:T(8,128)(2,1)} async-done(((bf16[128,2048]{1,0:T(8,128)(2,1)}), bf16[128,2048]{1,0:T(8,128)(2,1)}) %all-reduce.21.cloned.1.call-update) | async-done | bytes 524304 | tf_op jit(solution)/shard_map/psum | solution.py:119
  222.0 3.8 fusion.102
  225.8 4.8 multiply_convert_fusion.8
  231.4 5.4 convolution_convert_fusion.7
  241.9 38.7 %all-reduce.23.cloned.1.call-done = bf16[128,2048]{1,0:T(8,128)(2,1)} async-done(((bf16[128,2048]{1,0:T(8,128)(2,1)}), bf16[128,2048]{1,0:T(8,128)(2,1)}) %all-reduce.23.cloned.1.call-update) | async-done | bytes 524304 | tf_op jit(solution)/shard_map/psum | solution.py:119
  289.7 24.9 %all_gather.14 = bf16[3072,128]{1,0:T(8,128)(2,1)S(1)} all-gather(bf16[96,128]{1,0:T(8,128)(2,1)S(1)} %slice.211), channel_id=1, replica_groups=mesh['dp'=32,'mp'=4] {'dp'}, dimensions={0}, use_global_device_ids=true | all-gather | bytes 811008 | tf_op jit(solution)/shard_map/all_gather | solution.py:201
  314.6 7.6 while.85
  332.3 36.7 %all-reduce.25.cloned.1.call-done = bf16[96,2048]{1,0:T(8,128)(2,1)} async-done(((bf16[96,2048]{1,0:T(8,128)(2,1)}), bf16[96,2048]{1,0:T(8,128)(2,1)}) %all-reduce.25.cloned.1.call-update) | async-done | bytes 393232 | tf_op jit(solution)/shard_map/psum | solution.py:119
  371.4 3.8 fusion.100
  375.3 4.7 multiply_convert_fusion.11
  380.0 5.4 convolution_convert_fusion.8
  386.1 42.3 %all-reduce.27.cloned.1.call-done = bf16[96,2048]{1,0:T(8,128)(2,1)} async-done(((bf16[96,2048]{1,0:T(8,128)(2,1)}), bf16[96,2048]{1,0:T(8,128)(2,1)}) %all-reduce.27.cloned.1.call-update) | async-done | bytes 393232 | tf_op jit(solution)/shard_map/psum | solution.py:119
  445.1 27.8 %all_gather.15 = bf16[2048,128]{1,0:T(8,128)(2,1)} all-gather(bf16[64,128]{1,0:T(8,128)(2,1)} %slice.214), channel_id=1, replica_groups=mesh['dp'=32,'mp'=4] {'dp'}, dimensions={0}, use_global_device_ids=true | all-gather | bytes 540672 | tf_op jit(solution)/shard_map/all_gather | solution.py:201
  473.0 17.5 %while.86 = (s32[]{:T(128)}, f32[512]{0:T(512)}, f32[512]{0:T(512)}, f32[512,64]{0,1:T(8,128)S(1)}, s32[4,512]{1,0:T(4,128)}, /*index=5*/bf16[4,512,128]{2,1,0:T...) while((s32[]{:T(128)}, f32[512]{0:T(512)}, f32[512]{0:T(512)}, ...), condition=%wide.region_25.26_spmd.clone, body=%wide.region_22.25_spmd.clone.sunk | while | flops 69044736 | bytes 4069845 | solution.py:88
  497.4 40.0 %all-reduce.29.cloned.1.call-done = bf16[64,2048]{1,0:T(8,128)(2,1)} async-done(((bf16[64,2048]{1,0:T(8,128)(2,1)}), bf16[64,2048]{1,0:T(8,128)(2,1)}) %all-reduce.29.cloned.1.call-update) | async-done | bytes 262160 | tf_op jit(solution)/shard_map/psum | solution.py:119
  541.1 3.9 fusion.86
  545.0 4.5 fusion.76
  549.5 4.5 multiply_convert_fusion.18
  561.8 43.1 %all-reduce.41.cloned.1.call-done = (bf16[64,2048]{1,0:T(8,128)(2,1)}, bf16[64,2048]{1,0:T(8,128)(2,1)}) async-done(((bf16[64,2048]{1,0:T(8,128)(2,1)}, bf16[64,2048]{1,0:T(8,128)(2,1)}), (bf16[64,2048]{1,0:T(8,128)(2,1)}, bf16[64,2048]{1,0:T(8,128)(2,1)})) %all-reduce.41.cloned.1.call-update) | async-done | bytes 524304 | tf_op jit(solution)/shard_map/psum | solution.py:119
  614.8 21.3 %while.87 = (s32[]{:T(128)}, f32[512,64]{0,1:T(8,128)}, bf16[4,512,128]{1,2,0:T(8,128)(2,1)}, s32[4,512]{1,0:T(4,128)}, bf16[4,512,128]{2,1,0:T(8,128)(2,1)}, /*...) while((s32[]{:T(128)}, f32[512,64]{0,1:T(8,128)}, ...), condition=%wide.region_33.34_spmd.clone, body=%wide.region_32.33_spmd.clone.sunk | while | flops 169934848 | bytes 7367143 | solution.py:103
  642.9 72.7 %reduce-scatter.7.cloned.1.call-done = bf16[64,128]{1,0:T(8,128)(2,1)} async-done(((bf16[2048,128]{1,0:T(8,128)(2,1)}), bf16[64,128]{1,0:T(8,128)(2,1)}) %reduce-scatter.7.cloned.1.call-update) | async-done | bytes 16400 | tf_op jit(solution)/shard_map/reduce_scatter | solution.py:247
  726.6 41.4 %all-reduce.31.cloned.1.call-done = bf16[64,2048]{1,0:T(8,128)(2,1)} async-done(((bf16[64,2048]{1,0:T(8,128)(2,1)}), bf16[64,2048]{1,0:T(8,128)(2,1)}) %all-reduce.31.cloned.1.call-update) | async-done | bytes 262160 | tf_op jit(solution)/shard_map/psum | solution.py:119
  774.0 3.9 multiply_convert_fusion.9
  777.9 4.7 fusion.94
  782.7 5.3 fusion.71
  788.1 42.9 %all-reduce.33.cloned.1.call-done = bf16[96,2048]{1,0:T(8,128)(2,1)} async-done(((bf16[96,2048]{1,0:T(8,128)(2,1)}), bf16[96,2048]{1,0:T(8,128)(2,1)}) %all-reduce.33.cloned.1.call-update) | async-done | bytes 393232 | tf_op jit(solution)/shard_map/psum | solution.py:119
  837.3 25.9 %while.88 = (s32[]{:T(128)}, f32[768,64]{0,1:T(8,128)S(1)}, bf16[6,512,128]{1,2,0:T(8,128)(2,1)}, s32[6,512]{1,0:T(8,128)}, bf16[6,512,128]{2,1,0:T(8,128)(2,1)}...) while((s32[]{:T(128)}, f32[768,64]{0,1:T(8,128)S(1)}, ...), condition=%wide.region_42.43_spmd.clone, body=%wide.region_41.42_spmd.clone.sunk | while | flops 254771200 | bytes 8938003 | solution.py:103
  867.6 75.7 %reduce-scatter.9.cloned.1.call-done = bf16[96,128]{1,0:T(8,128)(2,1)} async-done(((bf16[3072,128]{1,0:T(8,128)(2,1)}), bf16[96,128]{1,0:T(8,128)(2,1)}) %reduce-scatter.9.cloned.1.call-update) | async-done | bytes 24592 | tf_op jit(solution)/shard_map/reduce_scatter | solution.py:247
  950.0 3.4 convolution_convert_fusion.11
  953.7 41.7 %all-reduce.35.cloned.1.call-done = bf16[96,2048]{1,0:T(8,128)(2,1)} async-done(((bf16[96,2048]{1,0:T(8,128)(2,1)}), bf16[96,2048]{1,0:T(8,128)(2,1)}) %all-reduce.35.cloned.1.call-update) | async-done | bytes 393232 | tf_op jit(solution)/shard_map/psum | solution.py:119
  999.8 4.0 multiply_convert_fusion.6
  1003.9 4.8 fusion.92
  1008.8 5.4 fusion.69
  1014.3 43.6 %all-reduce.37.cloned.1.call-done = bf16[128,2048]{1,0:T(8,128)(2,1)} async-done(((bf16[128,2048]{1,0:T(8,128)(2,1)}), bf16[128,2048]{1,0:T(8,128)(2,1)}) %all-reduce.37.cloned.1.call-update) | async-done | bytes 524304 | tf_op jit(solution)/shard_map/psum | solution.py:119
  1064.3 37.1 %while.89 = (s32[]{:T(128)}, f32[1024,64]{0,1:T(8,128)S(1)}, bf16[8,512,128]{1,2,0:T(8,128)(2,1)}, s32[8,512]{1,0:T(8,128)}, bf16[8,512,128]{2,1,0:T(8,128)(2,1)...) while((s32[]{:T(128)}, f32[1024,64]{0,1:T(8,128)S(1)}, ...), condition=%wide.region_51.52_spmd.clone, body=%wide.region_50.51_spmd.clone.sunk | while | flops 339607552 | bytes 11557523 | solution.py:103
  1107.7 74.0 %reduce-scatter.11.cloned.1.call-done = bf16[128,128]{1,0:T(8,128)(2,1)} async-done(((bf16[4096,128]{1,0:T(8,128)(2,1)}), bf16[128,128]{1,0:T(8,128)(2,1)}) %reduce-scatter.11.cloned.1.call-update) | async-done | bytes 32784 | tf_op jit(solution)/shard_map/reduce_scatter | solution.py:247
  1186.3 4.4 fusion.67
  1190.7 3.6 convolution_convert_fusion.5
  1194.7 3.9 fusion.68
  1198.7 5.1 fusion.66
  1203.8 5.1 fusion.65
  1209.1 5.0 fusion.64
  1214.1 23.0 %all-reduce.39.cloned.1.call-done = bf16[128,2048]{1,0:T(8,128)(2,1)} async-done(((bf16[128,2048]{1,0:T(8,128)(2,1)}), bf16[128,2048]{1,0:T(8,128)(2,1)}) %all-reduce.39.cloned.1.call-update) | async-done | bytes 524304 | tf_op jit(solution)/shard_map/psum | solution.py:119
  1239.7 28.3 %copy.300 = bf16[2048,5504]{1,0:T(8,128)(2,1)} copy(bf16[2048,5504]{0,1:T(8,128)(2,1)} %fusion.217) | data formatting | bytes 45088768
  1273.5 127.5 %reduce-scatter.13.cloned.1.call-done = bf16[64,5504]{1,0:T(8,128)(2,1)} async-done(((bf16[2048,5504]{1,0:T(8,128)(2,1)}), bf16[64,5504]{1,0:T(8,128)(2,1)}) %reduce-scatter.13.cloned.1.call-update) | async-done | bytes 704528
  (994 shorter events, 304.4 us)
Async XLA Ops:
  7.2 96.1 %all-gather.3.cloned.1.call-start = ((), (), s32[]{:S(2)}) async-start(), calls=%async_computation.4 | async-start | bytes 23248896 | tf_op jit(solution)/shard_map/all_gather | solution.py:170
  7.9 272.7 %copy-start.108 = (pred[128]{0:T(512)(128)(4,1)}, pred[128]{0:T(512)(128)(4,1)S(1)}, u32[]{:S(2)}) copy-start(pred[128]{0:T(512)(128)(4,1)S(1)} %get-tuple-element.865) | copy-start | bytes 388
  14.8 139.6 %all-gather.5.cloned.1.call-start = ((), (), s32[]{:S(2)}) async-start(), calls=%async_computation.5 | async-start | bytes 1081344 | tf_op jit(solution)/shard_map/all_gather | solution.py:201
  14.9 97.3 %copy-start.125 = (f32[32]{0:T(128)}, f32[32]{0:T(128)S(1)}, u32[]{:S(2)}) copy-start(f32[32]{0:T(128)S(1)} %multiply_exponential_fusion) | copy-start | bytes 388
  15.3 95.1 %copy-start.20 = (f32[128,576]{1,0:T(8,128)}, f32[128,576]{1,0:T(8,128)S(1)}, u32[]{:S(2)}) copy-start(f32[128,576]{1,0:T(8,128)S(1)} %copy.243) | copy-start | bytes 884740
  15.5 95.0 %copy-start.22 = (f32[128,576]{1,0:T(8,128)}, f32[128,576]{1,0:T(8,128)S(1)}, u32[]{:S(2)}) copy-start(f32[128,576]{1,0:T(8,128)S(1)} %copy.245) | copy-start | bytes 884740
  15.5 90.4 %copy-start = (bf16[128,2048]{1,0:T(8,128)(2,1)S(1)}, bf16[128,2048]{1,0:T(8,128)(2,1)}, u32[]{:S(2)}) copy-start(bf16[128,2048]{1,0:T(8,128)(2,1)} %param.27) | copy-start | bytes 1572868
  105.8 263.1 %copy-start.45 = (f32[2048]{0:T(1024)}, f32[2048]{0:T(1024)S(1)}, u32[]{:S(2)}) copy-start(f32[2048]{0:T(1024)S(1)} %get-tuple-element.694) | copy-start | bytes 24580
  106.1 135.7 %copy-start.148 = (f32[128]{0:T(128)}, f32[128]{0:T(128)S(1)}, u32[]{:S(2)}) copy-start(f32[128]{0:T(128)S(1)} %get-tuple-element.707) | copy-start | bytes 1540
  112.1 107.3 %all-reduce.21.cloned.1.call-start = ((), (), s32[]{:S(2)}) async-start(), calls=%async_computation.6 | async-start | bytes 1048576 | tf_op jit(solution)/shard_map/psum | solution.py:119
  176.6 104.0 %all-reduce.23.cloned.1.call-start = ((), (), s32[]{:S(2)}) async-start(), calls=%async_computation.7 | async-start | bytes 1048576 | tf_op jit(solution)/shard_map/psum | solution.py:119
  236.8 132.2 %all-reduce.25.cloned.1.call-start = ((), (), s32[]{:S(2)}) async-start(), calls=%async_computation.8 | async-start | bytes 786432 | tf_op jit(solution)/shard_map/psum | solution.py:119
  322.2 53.0 %copy-start.84 = (s32[96]{0:T(128)}, s32[96]{0:T(128)S(1)}, u32[]{:S(2)}) copy-start(s32[96]{0:T(128)S(1)} %get-tuple-element.1518) | copy-start | bytes 1156
  327.8 100.6 %all-reduce.27.cloned.1.call-start = ((), (), s32[]{:S(2)}) async-start(), calls=%async_computation.9 | async-start | bytes 786432 | tf_op jit(solution)/shard_map/psum | solution.py:119
  380.0 48.5 %copy-start.2 = (bf16[96,2048]{1,0:T(8,128)(2,1)S(1)}, bf16[96,2048]{1,0:T(8,128)(2,1)}, u32[]{:S(2)}) copy-start(bf16[96,2048]{1,0:T(8,128)(2,1)} %all-reduce.25.cloned.1.call-done) | copy-start | bytes 1179652
  380.0 48.5 %copy-start.15 = (bf16[128,2048]{1,0:T(8,128)(2,1)S(1)}, bf16[128,2048]{1,0:T(8,128)(2,1)}, u32[]{:S(2)}) copy-start(bf16[128,2048]{1,0:T(8,128)(2,1)} %all-reduce.23.cloned.1.call-done) | copy-start | bytes 1572868
  380.0 48.5 %copy-start.106 = (s32[128]{0:T(128)S(1)}, s32[128]{0:T(128)}, u32[]{:S(2)}) copy-start(s32[128]{0:T(128)} %param.29) | copy-start | bytes 1540
  380.0 48.5 %copy-start.109 = (pred[128]{0:T(512)(128)(4,1)S(1)}, pred[128]{0:T(512)(128)(4,1)}, u32[]{:S(2)}) copy-start(pred[128]{0:T(512)(128)(4,1)} %copy-done.108) | copy-start | bytes 388
  380.0 48.5 %copy-start.118 = (f32[128]{0:T(128)S(1)}, f32[128]{0:T(128)}, u32[]{:S(2)}) copy-start(f32[128]{0:T(128)} %copy-done.117) | copy-start | bytes 1540
  385.4 152.0 %all-reduce.29.cloned.1.call-start = ((), (), s32[]{:S(2)}) async-start(), calls=%async_computation.10 | async-start | bytes 524288 | tf_op jit(solution)/shard_map/psum | solution.py:119
  490.5 48.2 %copy-start.102 = (pred[128]{0:T(512)(128)(4,1)S(1)}, pred[128]{0:T(512)(128)(4,1)}, u32[]{:S(2)}) copy-start(pred[128]{0:T(512)(128)(4,1)} %copy-done.100) | copy-start | bytes 388
  497.3 107.6 %all-reduce.41.cloned.1.call-start = ((), (), s32[]{:S(2)}) async-start(), calls=%async_computation.20 | async-start | bytes 1048576 | tf_op jit(solution)/shard_map/psum | solution.py:119
  538.7 68.5 %copy-start.115 = (f32[64]{0:T(128)}, f32[64]{0:T(128)S(1)}, u32[]{:S(2)}) copy-start(f32[64]{0:T(128)S(1)} %add_rsqrt_fusion) | copy-start | bytes 772
  538.7 68.4 %copy-start.133 = (f32[64]{0:T(128)}, f32[64]{0:T(128)S(1)}, u32[]{:S(2)}) copy-start(f32[64]{0:T(128)S(1)} %add_divide_fusion.3) | copy-start | bytes 772
  561.1 154.5 %reduce-scatter.7.cloned.1.call-start = ((), (), s32[]{:S(2)}) async-start(), calls=%async_computation.11 | async-start | bytes 540672 | tf_op jit(solution)/shard_map/reduce_scatter | solution.py:247
  638.2 129.8 %all-reduce.31.cloned.1.call-start = ((), (), s32[]{:S(2)}) async-start(), calls=%async_computation.12 | async-start | bytes 524288 | tf_op jit(solution)/shard_map/psum | solution.py:119
  642.9 73.4 %copy-start.30 = (f32[64,512]{1,0:T(8,128)}, f32[64,512]{1,0:T(8,128)S(1)}, u32[]{:S(2)}) copy-start(f32[64,512]{1,0:T(8,128)S(1)} %mul.890) | copy-start | bytes 393220
  719.5 48.6 %copy-start.128 = (f32[64]{0:T(128)S(1)}, f32[64]{0:T(128)}, u32[]{:S(2)}) copy-start(f32[64]{0:T(128)} %copy-done.127) | copy-start | bytes 772
  721.2 48.6 %copy-start.9 = (bf16[64,2048]{1,0:T(8,128)(2,1)S(1)}, bf16[64,2048]{1,0:T(8,128)(2,1)}, u32[]{:S(2)}) copy-start(bf16[64,2048]{1,0:T(8,128)(2,1)} %all-reduce.29.cloned.1.call-done) | copy-start | bytes 786436
  721.2 48.6 %copy-start.47 = (f32[2048]{0:T(1024)S(1)}, f32[2048]{0:T(1024)}, u32[]{:S(2)}) copy-start(f32[2048]{0:T(1024)} %copy-done.45) | copy-start | bytes 24580
  721.3 48.6 %copy-start.98 = (s32[128]{0:T(128)S(1)}, s32[128]{0:T(128)}, u32[]{:S(2)}) copy-start(s32[128]{0:T(128)} %param.30) | copy-start | bytes 1540
  721.3 48.6 %copy-start.103 = (pred[128]{0:T(512)(128)(4,1)S(1)}, pred[128]{0:T(512)(128)(4,1)}, u32[]{:S(2)}) copy-start(pred[128]{0:T(512)(128)(4,1)} %copy-done.100) | copy-start | bytes 388
  721.3 48.6 %copy-start.116 = (f32[64]{0:T(128)S(1)}, f32[64]{0:T(128)}, u32[]{:S(2)}) copy-start(f32[64]{0:T(128)} %copy-done.115) | copy-start | bytes 772
  721.3 48.6 %copy-start.141 = (f32[64]{0:T(128)S(1)}, f32[64]{0:T(128)}, u32[]{:S(2)}) copy-start(f32[64]{0:T(128)} %copy-done.140) | copy-start | bytes 772
  726.5 104.5 %all-reduce.33.cloned.1.call-start = ((), (), s32[]{:S(2)}) async-start(), calls=%async_computation.13 | async-start | bytes 786432 | tf_op jit(solution)/shard_map/psum | solution.py:119
  782.7 48.3 %copy-start.121 = (f32[96]{0:T(128)S(1)}, f32[96]{0:T(128)}, u32[]{:S(2)}) copy-start(f32[96]{0:T(128)} %copy-done.120) | copy-start | bytes 1156
  788.0 155.4 %reduce-scatter.9.cloned.1.call-start = ((), (), s32[]{:S(2)}) async-start(), calls=%async_computation.14 | async-start | bytes 811008 | tf_op jit(solution)/shard_map/reduce_scatter | solution.py:247
  865.6 82.9 %copy-start.25 = (f32[96,576]{1,0:T(8,128)S(1)}, f32[96,576]{1,0:T(8,128)}, u32[]{:S(2)}) copy-start(f32[96,576]{1,0:T(8,128)} %copy.253) | copy-start | bytes 663556
  865.6 82.9 %copy-start.27 = (f32[96,576]{1,0:T(8,128)S(1)}, f32[96,576]{1,0:T(8,128)}, u32[]{:S(2)}) copy-start(f32[96,576]{1,0:T(8,128)} %copy.255) | copy-start | bytes 663556
  865.6 129.9 %all-reduce.35.cloned.1.call-start = ((), (), s32[]{:S(2)}) async-start(), calls=%async_computation.15 | async-start | bytes 786432 | tf_op jit(solution)/shard_map/psum | solution.py:119
  953.4 104.5 %all-reduce.37.cloned.1.call-start = ((), (), s32[]{:S(2)}) async-start(), calls=%async_computation.16 | async-start | bytes 1048576 | tf_op jit(solution)/shard_map/psum | solution.py:119
  1008.8 49.2 %copy-start.113 = (f32[128]{0:T(128)S(1)}, f32[128]{0:T(128)}, u32[]{:S(2)}) copy-start(f32[128]{0:T(128)} %copy-done.112) | copy-start | bytes 1540
  1014.2 167.4 %reduce-scatter.11.cloned.1.call-start = ((), (), s32[]{:S(2)}) async-start(), calls=%async_computation.17 | async-start | bytes 1081344 | tf_op jit(solution)/shard_map/reduce_scatter | solution.py:247
  1103.7 133.4 %all-reduce.39.cloned.1.call-start = ((), (), s32[]{:S(2)}) async-start(), calls=%async_computation.18 | async-start | bytes 1048576 | tf_op jit(solution)/shard_map/psum | solution.py:119
  1105.2 81.1 %copy-start.21 = (f32[128,576]{1,0:T(8,128)S(1)}, f32[128,576]{1,0:T(8,128)}, u32[]{:S(2)}) copy-start(f32[128,576]{1,0:T(8,128)} %copy-done.20) | copy-start | bytes 884740
  1105.2 81.1 %copy-start.23 = (f32[128,576]{1,0:T(8,128)S(1)}, f32[128,576]{1,0:T(8,128)}, u32[]{:S(2)}) copy-start(f32[128,576]{1,0:T(8,128)} %copy-done.22) | copy-start | bytes 884740
  1106.0 80.3 %copy-start.78 = (bf16[96,640]{1,0:T(8,128)(2,1)S(1)}, bf16[96,640]{1,0:T(8,128)(2,1)}, u32[]{:S(2)}) copy-start(bf16[96,640]{1,0:T(8,128)(2,1)} %copy-done.77) | copy-start | bytes 368644
  1194.3 206.7 %reduce-scatter.13.cloned.1.call-start = ((), (), s32[]{:S(2)}) async-start(), calls=%async_computation.19 | async-start | bytes 23248896
  (162 other events, 1441.6 us)
Sparse Core Ops, SparseCore 0:
  15.0 88.2 all-gather.2
  112.2 42.0 all-gather.4
  176.7 42.6 all-reduce.20
  236.9 43.6 all-reduce.22
  327.9 40.9 all-reduce.24
  385.6 42.8 all-reduce.26
  497.5 39.9 all-reduce.28
  561.3 43.6 all-reduce.40
  638.3 77.2 reduce-scatter.6
  726.7 41.2 all-reduce.30
  788.1 42.8 all-reduce.32
  865.7 77.6 reduce-scatter.8
  953.6 41.8 all-reduce.34
  1014.4 43.5 all-reduce.36
  1103.8 77.7 reduce-scatter.10
  1194.4 42.6 all-reduce.38
  1268.1 132.8 reduce-scatter.12

commit v2 on v1

v2 whole, which is shorter than its diff:
```python
import functools
import math

import jax
import jax.numpy as jnp
from jax import lax
from jax.experimental import pallas as pl
from jax.experimental.pallas import tpu as pltpu
from jax.sharding import PartitionSpec as P

HD = 64
SECOND_SLOTS = 96
THIRD_SLOTS = 64
EPS = 1e-05
NEG = -1e30
ROPE_BASE = 10000.0
FAR = 1073741824
BF = jnp.bfloat16
F32 = jnp.float32
MESH = pl.DeviceIdType.MESH
LANES = 128
VMEM_LIMIT = 58 * 1024 * 1024


def dot_nn(left, right):
    return lax.dot_general(left, right, (((1,), (0,)), ((), ())), preferred_element_type=F32)


def dot_nt(left, right):
    return lax.dot_general(left, right, (((1,), (1,)), ((), ())), preferred_element_type=F32)


def dot_tn(left, right):
    return lax.dot_general(left, right, (((0,), (0,)), ((), ())), preferred_element_type=F32)


def unit_of(values):
    factor = lax.rsqrt(jnp.mean(values * values, axis=-1, keepdims=True) + EPS)
    return values * factor, factor


def unit_back(shaped, unit, factor):
    return factor * (shaped - unit * jnp.mean(shaped * unit, axis=-1, keepdims=True))


def sigmoid(values):
    return 1.0 / (1.0 + jnp.exp(-values))


def lanes_of(shape):
    return lax.broadcasted_iota(jnp.int32, shape, 1)


def swap_halves(tile):
    first = lax.rem(lanes_of(tile.shape), HD) < HD // 2
    return jnp.where(first, pltpu.roll(tile, LANES - HD // 2, 1), pltpu.roll(tile, HD // 2, 1))


def tile_of(values, index):
    return values[:, index * LANES : (index + 1) * LANES]


def signal_all(group, me, axis):
    barrier = pltpu.get_barrier_semaphore()
    for k in range(1, group):
        pl.semaphore_signal(
            barrier, inc=1, device_id={axis: lax.rem(me + k, group)}, device_id_type=MESH
        )
    pl.semaphore_wait(barrier, group - 1)


def sum_over_mp(group, me, make_chunk, send, recv, full, sems):
    order = (2, 1, 3)
    copies = []
    for k in order:
        peer = lax.rem(me + k, group)
        send[k - 1] = make_chunk(peer).astype(BF)
        copy = pltpu.make_async_remote_copy(
            src_ref=send.at[k - 1], dst_ref=recv.at[k - 1],
            send_sem=sems.at[0, k - 1], recv_sem=sems.at[1, k - 1],
            device_id={"mp": peer}, device_id_type=MESH,
        )
        copy.start()
        copies.append(copy)
    total = make_chunk(me).astype(BF).astype(F32)
    for k, copy in zip(order, copies):
        copy.wait_recv()
        total = total + recv[k - 1].astype(F32)
    full[me] = total.astype(BF)
    backs = []
    for k in order:
        peer = lax.rem(me + k, group)
        copy = pltpu.make_async_remote_copy(
            src_ref=full.at[me], dst_ref=full.at[me],
            send_sem=sems.at[2, k - 1], recv_sem=sems.at[3, k - 1],
            device_id={"mp": peer}, device_id_type=MESH,
        )
        copy.start()
        backs.append(copy)
    for copy in backs:
        copy.wait_recv()
    for copy in copies + backs:
        copy.wait_send()
    return jnp.concatenate([full[c] for c in range(group)], axis=1)


def attend_kernel(n, heads, devices, group, picked, *refs):
    refs = list(refs)
    source = refs.pop(0)
    pick = refs.pop(0) if picked else None
    key_place = refs.pop(0) if picked else None
    query_place, gains, cosine, sine, w_hbm = [refs.pop(0) for _ in range(5)]
    rows_out, normed_out, packed_out, query_out, mixed_t_out, log_out, mixed_out = [
        refs.pop(0) for _ in range(7)
    ]
    w_v, packed, query_t, top, total, acc, w_sem, out_sem, send_sems, recv_sems = refs
    me = lax.axis_index("dp")
    width = heads * n
    load_w = pltpu.make_async_copy(w_hbm, w_v, w_sem)
    load_w.start()

    barrier = pltpu.get_barrier_semaphore()

    def greet(e, carry):
        pl.semaphore_signal(barrier, inc=1, device_id={"dp": e}, device_id_type=MESH)
        return carry

    lax.fori_loop(0, me, greet, 0)

    if picked:
        rows = dot_nn(pick[...], source[...].astype(BF)).astype(BF)
    else:
        rows = source[...]
    rows_out[...] = rows
    unit, unused = unit_of(rows.astype(F32))
    normed = (unit * gains[0:1, :]).astype(BF)
    normed_out[...] = normed
    load_w.wait()
    tiles = []
    for t in range(heads // 2 + 1):
        if t % 2 == 0:
            last = min((t + 2) * LANES, (heads // 2 + 1) * LANES)
            both = dot_nn(normed, w_v[:, t * LANES : last])
        part = tile_of(both, t % 2)
        cut = slice(t * LANES, (t + 1) * LANES)
        tiles.append(part * cosine[:, cut] + swap_halves(part) * sine[:, cut])
    packed[me] = tiles[-1].astype(BF)

    @pl.when(me < devices - 1)
    def _():
        pl.semaphore_wait(barrier, devices - 1 - me)

    def send_copy(e, source_index):
        return pltpu.make_async_remote_copy(
            src_ref=packed.at[me], dst_ref=packed.at[me],
            send_sem=send_sems.at[e], recv_sem=recv_sems.at[source_index],
            device_id={"dp": e}, device_id_type=MESH,
        )

    def send(e, carry):
        send_copy(e, me).start()
        return carry

    lax.fori_loop(me + 1, devices, send, 0)

    def clear(e, carry):
        packed[e] = jnp.zeros((n, 2 * HD), BF)
        return carry

    lax.fori_loop(me + 1, devices, clear, 0)

    left = lanes_of((n, LANES)) < HD
    for t in range(heads // 2):
        scaled = tiles[t].astype(BF).astype(F32) * HD**-0.5
        query_out[2 * t * n : (2 * t + 1) * n, :] = jnp.where(left, scaled, 0.0).astype(BF)
        query_out[(2 * t + 1) * n : (2 * t + 2) * n, :] = jnp.where(
            left, pltpu.roll(scaled, HD, 1), 0.0
        ).astype(BF)
    query_t[...] = query_out[...].T
    top[...] = jnp.full((1, width), NEG, F32)
    total[...] = jnp.zeros((1, width), F32)
    acc[...] = jnp.zeros((2 * HD, width), F32)

    def one_block(b, carry):
        for g in range(group):
            e = b * group + g

            @pl.when(e < me)
            def _():
                send_copy(me, e).wait_recv()

        part = packed[pl.ds(b * group, group)].reshape(group * n, 2 * HD)
        scores = dot_nn(part, query_t[...])
        if picked:
            start = pl.multiple_of(b * (group * n), group * n)
            place = key_place[pl.ds(start, group * n), :]
        else:
            place = lax.broadcasted_iota(jnp.int32, (group * n, LANES), 0) + b * (group * n)
        place = jnp.concatenate([place] * (width // LANES), axis=1)
        scores = jnp.where(place <= query_place[...], scores, NEG)
        peak = jnp.maximum(top[...], jnp.max(scores, axis=0, keepdims=True))
        weights = jnp.exp(scores - peak)
        fade = jnp.exp(top[...] - peak)
        total[...] = total[...] * fade + jnp.sum(weights, axis=0, keepdims=True)
        acc[...] = acc[...] * fade + dot_tn(part, weights.astype(BF))
        top[...] = peak
        return carry

    lax.fori_loop(0, me // group + 1, one_block, 0)
    mixed_t = acc[...] / total[...]
    mixed_t_out[...] = mixed_t
    log_out[...] = top[...] + jnp.log(total[...])
    mixed = mixed_t.T
    for t in range(heads // 2):
        even = mixed[2 * t * n : (2 * t + 1) * n, :]
        odd = mixed[(2 * t + 1) * n : (2 * t + 2) * n, :]
        mixed_out[:, t * LANES : (t + 1) * LANES] = jnp.where(
            left, pltpu.roll(even, HD, 1), odd
        ).astype(BF)
    keep = pltpu.make_async_copy(packed, packed_out, out_sem)
    keep.start()

    def sent(e, carry):
        send_copy(e, me).wait_send()
        return carry

    lax.fori_loop(me + 1, devices, sent, 0)
    keep.wait()


def vmem(count):
    return [pl.BlockSpec(memory_space=pltpu.VMEM)] * count


def attend(source, pick, key_place, query_place, gains, tables, w_qkv, heads, devices, n, ident):
    picked = pick is not None
    group = 512 // n if 512 % n == 0 else 4
    width = heads * n
    qkv_width = (heads + 2) * HD
    args = [source] + ([pick, key_place] if picked else []) + [query_place, gains, *tables, w_qkv]
    model = source.shape[1]
    return pl.pallas_call(
        functools.partial(attend_kernel, n, heads, devices, group, picked),
        out_shape=(
            jax.ShapeDtypeStruct((n, model), BF),
            jax.ShapeDtypeStruct((n, model), BF),
            jax.ShapeDtypeStruct((devices, n, 2 * HD), BF),
            jax.ShapeDtypeStruct((width, 2 * HD), BF),
            jax.ShapeDtypeStruct((2 * HD, width), F32),
            jax.ShapeDtypeStruct((1, width), F32),
            jax.ShapeDtypeStruct((n, heads * HD), BF),
        ),
        in_specs=vmem(len(args) - 1) + [pl.BlockSpec(memory_space=pl.ANY)],
        out_specs=tuple(vmem(2) + [pl.BlockSpec(memory_space=pl.ANY)] + vmem(4)),
        scratch_shapes=[
            pltpu.VMEM((model, qkv_width), BF),
            pltpu.VMEM((devices, n, 2 * HD), BF),
            pltpu.VMEM((2 * HD, width), BF),
            pltpu.VMEM((1, width), F32),
            pltpu.VMEM((1, width), F32),
            pltpu.VMEM((2 * HD, width), F32),
            pltpu.SemaphoreType.DMA(()),
            pltpu.SemaphoreType.DMA(()),
            pltpu.SemaphoreType.DMA((devices,)),
            pltpu.SemaphoreType.DMA((devices,)),
        ],
        compiler_params=pltpu.CompilerParams(
            collective_id=ident, has_side_effects=True, vmem_limit_bytes=VMEM_LIMIT
        ),
        cost_estimate=pl.CostEstimate(flops=4 * 10**9, bytes_accessed=10**7, transcendentals=0),
        name=f"attend_{n}",
    )(*args)


def attend_back_kernel(n, heads, devices, group, picked, *refs):
    refs = list(refs)
    key_place = refs.pop(0) if picked else None
    query_place, query, packed, mixed_t, log_total, grad_mixed, cosine, sine = [
        refs.pop(0) for _ in range(8)
    ]
    grad_out = refs.pop(0)
    query_t, grad_rows, grad_t, acc, delta, send_buf, recv_buf, send_sems, recv_sems = refs
    me = lax.axis_index("dp")
    barrier = pltpu.get_barrier_semaphore()

    def greet(e, carry):
        pl.semaphore_signal(barrier, inc=1, device_id={"dp": e}, device_id_type=MESH)
        return carry

    lax.fori_loop(me + 1, devices, greet, 0)

    left = lanes_of((n, LANES)) < HD
    for t in range(heads // 2):
        part = grad_mixed[:, t * LANES : (t + 1) * LANES].astype(F32)
        grad_rows[2 * t * n : (2 * t + 1) * n, :] = jnp.where(
            left, 0.0, pltpu.roll(part, HD, 1)
        ).astype(BF)
        grad_rows[(2 * t + 1) * n : (2 * t + 2) * n, :] = jnp.where(left, 0.0, part).astype(BF)
    query_t[...] = query[...].T
    grad_t[...] = grad_rows[...].T
    delta[...] = jnp.sum(grad_t[...].astype(F32) * mixed_t[...], axis=0, keepdims=True)
    acc[...] = jnp.zeros(acc.shape, F32)
    width = heads * n

    @pl.when(me > 0)
    def _():
        pl.semaphore_wait(barrier, me)

    def send_copy(e, source_index):
        return pltpu.make_async_remote_copy(
            src_ref=send_buf.at[e], dst_ref=recv_buf.at[source_index],
            send_sem=send_sems.at[e], recv_sem=recv_sems.at[source_index],
            device_id={"dp": e}, device_id_type=MESH,
        )

    def one_block(b, carry):
        part = packed[pl.ds(b * group, group)].reshape(group * n, 2 * HD)
        scores = dot_nn(part, query_t[...])
        if picked:
            start = pl.multiple_of(b * (group * n), group * n)
            place = key_place[pl.ds(start, group * n), :]
        else:
            place = lax.broadcasted_iota(jnp.int32, (group * n, LANES), 0) + b * (group * n)
        place = jnp.concatenate([place] * (width // LANES), axis=1)
        scores = jnp.where(place <= query_place[...], scores, NEG)
        weights = jnp.exp(scores - log_total[...])
        grad_weights = dot_nn(part, grad_t[...])
        grad_scores = (weights * (grad_weights - delta[...])).astype(BF)
        grad_part = dot_nn(grad_scores, query[...]) + dot_nn(weights.astype(BF), grad_rows[...])
        send_buf[pl.ds(b * group, group)] = grad_part.astype(BF).reshape(group, n, 2 * HD)
        acc[...] += dot_tn(part, grad_scores)
        for g in range(group):
            e = b * group + g

            @pl.when(e < me)
            def _():
                send_copy(e, me).start()

        return carry

    lax.fori_loop(0, me // group + 1, one_block, 0)

    grad_query = acc[...].T * HD**-0.5
    outs = []
    for t in range(heads // 2):
        even = grad_query[2 * t * n : (2 * t + 1) * n, :]
        odd = grad_query[(2 * t + 1) * n : (2 * t + 2) * n, :]
        outs.append(jnp.where(left, even, pltpu.roll(odd, HD, 1)))

    def add(e, carry):
        send_copy(me, e).wait_recv()
        return carry + recv_buf[e].astype(F32)

    outs.append(lax.fori_loop(me + 1, devices, add, send_buf[me].astype(F32)))
    for t, part in enumerate(outs):
        cut = slice(t * LANES, (t + 1) * LANES)
        grad_out[:, cut] = (part * cosine[:, cut] - swap_halves(part) * sine[:, cut]).astype(BF)

    def sent(e, carry):
        send_copy(e, me).wait_send()
        return carry

    lax.fori_loop(0, me, sent, 0)


def attend_back(key_place, query_place, query, packed, mixed_t, log_total, grad_mixed, tables, heads, devices, n, ident):
    picked = key_place is not None
    group = 512 // n if 512 % n == 0 else 4
    width = heads * n
    args = ([key_place] if picked else []) + [
        query_place, query, packed, mixed_t, log_total, grad_mixed, *tables
    ]
    return pl.pallas_call(
        functools.partial(attend_back_kernel, n, heads, devices, group, picked),
        out_shape=jax.ShapeDtypeStruct((n, (heads + 2) * HD), BF),
        in_specs=vmem(len(args)),
        out_specs=pl.BlockSpec(memory_space=pltpu.VMEM),
        scratch_shapes=[
            pltpu.VMEM((2 * HD, width), BF),
            pltpu.VMEM((width, 2 * HD), BF),
            pltpu.VMEM((2 * HD, width), BF),
            pltpu.VMEM((2 * HD, width), F32),
            pltpu.VMEM((1, width), F32),
            pltpu.VMEM((devices, n, 2 * HD), BF),
            pltpu.VMEM((devices, n, 2 * HD), BF),
            pltpu.SemaphoreType.DMA((devices,)),
            pltpu.SemaphoreType.DMA((devices,)),
        ],
        compiler_params=pltpu.CompilerParams(
            collective_id=ident, has_side_effects=True, vmem_limit_bytes=VMEM_LIMIT
        ),
        cost_estimate=pl.CostEstimate(flops=10**10, bytes_accessed=10**7, transcendentals=0),
        name=f"attend_back_{n}",
    )(*args)


def feed_kernel(n, mp, picked, *refs):
    refs = list(refs)
    state, rows_in, mixed = [refs.pop(0) for _ in range(3)]
    pick = refs.pop(0) if picked else None
    gains, w_hbm = refs.pop(0), refs.pop(0)
    attn_out, ffn_out, second_out, parts_out, state_out = [refs.pop(0) for _ in range(5)]
    w_o, w_gu, w_d, hidden, w_sems, send_a, recv_a, full_a, sems_a, send_b, recv_b, full_b, sems_b = refs
    me = lax.axis_index("mp")
    wide_o, wide_gu, wide_d = w_o.shape[1], w_gu.shape[1], w_d.shape[1]
    loads = []
    start = 0
    for index, (ref, wide) in enumerate(((w_o, wide_o), (w_gu, wide_gu), (w_d, wide_d))):
        load = pltpu.make_async_copy(w_hbm.at[:, start : start + wide], ref, w_sems.at[index])
        load.start()
        loads.append(load)
        start += wide
    signal_all(mp, me, "mp")
    chunk = w_o.shape[0] // mp
    loads[0].wait()
    mixed_now = mixed[...]

    def out_chunk(c):
        return dot_nt(mixed_now, w_o[pl.ds(pl.multiple_of(c * chunk, chunk), chunk), :])

    attn = sum_over_mp(mp, me, out_chunk, send_a, recv_a, full_a, sems_a)
    attn_out[...] = attn
    level = rows_in[...].astype(F32)
    unit, unused = unit_of(level + attn.astype(F32))
    second = (unit * gains[1:2, :]).astype(BF)
    second_out[...] = second
    loads[1].wait()
    step = 256
    for t in range(wide_gu // step):
        parts_out[:, t * step : (t + 1) * step] = dot_nn(second, w_gu[:, t * step : (t + 1) * step])
    half = wide_gu // 2
    for t in range(half // LANES):
        cut = slice(t * LANES, (t + 1) * LANES)
        gate_part = parts_out[:, cut]
        up_part = parts_out[:, half + t * LANES : half + (t + 1) * LANES]
        hidden[:, cut] = (gate_part * sigmoid(gate_part) * up_part).astype(BF)
    loads[2].wait()
    hidden_now = hidden[...]

    def down_chunk(c):
        return dot_nt(hidden_now, w_d[pl.ds(pl.multiple_of(c * chunk, chunk), chunk), :])

    ffn = sum_over_mp(mp, me, down_chunk, send_b, recv_b, full_b, sems_b)
    ffn_out[...] = ffn
    gate = sigmoid(jnp.sum(level * gains[2:3, :], axis=-1, keepdims=True))
    update = (gate * (attn.astype(F32) + ffn.astype(F32))).astype(BF)
    if picked:
        state_out[...] = state[...].astype(F32) + dot_tn(pick[...], update)
    else:
        state_out[...] = state[...].astype(F32) + update.astype(F32)


def sum_scratch(mp, n, model):
    return [
        pltpu.VMEM((mp - 1, n, model // mp), BF),
        pltpu.VMEM((mp - 1, n, model // mp), BF),
        pltpu.VMEM((mp, n, model // mp), BF),
        pltpu.SemaphoreType.DMA((4, mp - 1)),
    ]


def feed(state, rows, mixed, pick, gains, w_rest, hidden_width, mp, n, ident):
    picked = pick is not None
    model = rows.shape[1]
    args = [state, rows, mixed] + ([pick] if picked else []) + [gains, w_rest]
    return pl.pallas_call(
        functools.partial(feed_kernel, n, mp, picked),
        out_shape=(
            jax.ShapeDtypeStruct((n, model), BF),
            jax.ShapeDtypeStruct((n, model), BF),
            jax.ShapeDtypeStruct((n, model), BF),
            jax.ShapeDtypeStruct((n, 2 * hidden_width), F32),
            jax.ShapeDtypeStruct(state.shape, F32),
        ),
        in_specs=vmem(len(args) - 1) + [pl.BlockSpec(memory_space=pl.ANY)],
        out_specs=tuple(vmem(5)),
        scratch_shapes=[
            pltpu.VMEM((model, mixed.shape[1]), BF),
            pltpu.VMEM((model, 2 * hidden_width), BF),
            pltpu.VMEM((model, hidden_width), BF),
            pltpu.VMEM((n, hidden_width), BF),
            pltpu.SemaphoreType.DMA((3,)),
            *sum_scratch(mp, n, model),
            *sum_scratch(mp, n, model),
        ],
        compiler_params=pltpu.CompilerParams(
            collective_id=ident, has_side_effects=True, vmem_limit_bytes=VMEM_LIMIT
        ),
        cost_estimate=pl.CostEstimate(flops=5 * 10**9, bytes_accessed=10**8, transcendentals=0),
        name=f"feed_{n}",
    )(*args)


def feed_back_kernel(tail_n, head_n, mp, tail_picked, head_picked, *refs):
    refs = list(refs)
    flow, gains = refs.pop(0), refs.pop(0)
    if tail_n:
        grad_qkv, tail_rows, tail_middle, tail_logit = [refs.pop(0) for _ in range(4)]
        tail_pick = refs.pop(0) if tail_picked else None
    if head_n:
        rows_in, attn, ffn, second, parts = [refs.pop(0) for _ in range(5)]
        head_pick = refs.pop(0) if head_picked else None
    if tail_n:
        w_first_hbm = refs.pop(0)
    if head_n:
        w_rest_hbm = refs.pop(0)
    if tail_n:
        flow_out, first_out, router_out = [refs.pop(0) for _ in range(3)]
    if head_n:
        attn_grad_out, middle_out, logit_out, mixed_out, parts_grad_out, hidden_out, ffn_grad_out, second_vec_out = [
            refs.pop(0) for _ in range(8)
        ]
    if tail_n:
        w_qkv, w_first_sem = refs.pop(0), refs.pop(0)
        send_a, recv_a, full_a, sems_a = [refs.pop(0) for _ in range(4)]
    if head_n:
        w_o, w_gu, w_d, w_sems = [refs.pop(0) for _ in range(4)]
        send_b, recv_b, full_b, sems_b = [refs.pop(0) for _ in range(4)]
    me = lax.axis_index("mp")
    if tail_n:
        load_first = pltpu.make_async_copy(w_first_hbm, w_qkv, w_first_sem)
        load_first.start()
    if head_n:
        loads = {}
        wide_o, wide_gu, wide_d = w_o.shape[1], w_gu.shape[1], w_d.shape[1]
        for index, (name, ref, start) in enumerate(
            (("d", w_d, wide_o + wide_gu), ("gu", w_gu, wide_o), ("o", w_o, 0))
        ):
            loads[name] = pltpu.make_async_copy(
                w_rest_hbm.at[:, start : start + ref.shape[1]], ref, w_sems.at[index]
            )
            loads[name].start()
    signal_all(mp, me, "mp")

    if tail_n:
        load_first.wait()
        grad_now = grad_qkv[...]
        chunk = w_qkv.shape[0] // mp

        def first_chunk(c):
            return dot_nt(grad_now, w_qkv[pl.ds(pl.multiple_of(c * chunk, chunk), chunk), :])

        grad_normed = sum_over_mp(mp, me, first_chunk, send_a, recv_a, full_a, sems_a).astype(F32)
        level = tail_rows[...].astype(F32)
        unit, factor = unit_of(level)
        first_out[...] = jnp.sum(grad_normed * unit, axis=0, keepdims=True)
        router_out[...] = jnp.sum(level * tail_logit[...], axis=0, keepdims=True)
        grad_rows = (
            unit_back(grad_normed * gains[0:1, :], unit, factor)
            + tail_middle[...]
            + tail_logit[...] * gains[2:3, :]
        ).astype(BF)
        if tail_picked:
            flow_now = flow[...] + dot_tn(tail_pick[...], grad_rows)
        else:
            flow_now = flow[...] + grad_rows.astype(F32)
        flow_out[...] = flow_now
    else:
        flow_now = flow[...]

    if head_n:
        grad_update = flow_now.astype(BF)
        if head_picked:
            grad_update = dot_nn(head_pick[...], grad_update)
        grad_update = grad_update.astype(F32)
        level = rows_in[...].astype(F32)
        attn_now = attn[...].astype(F32)
        gate = sigmoid(jnp.sum(level * gains[2:3, :], axis=-1, keepdims=True))
        logit = jnp.sum(grad_update * (attn_now + ffn[...].astype(F32)), axis=-1, keepdims=True)
        logit_out[...] = logit * gate * (1.0 - gate)
        grad_ffn = (gate * grad_update).astype(BF)
        ffn_grad_out[...] = grad_ffn
        half = wide_d
        loads["d"].wait()
        for t in range(half // LANES):
            cut = slice(t * LANES, (t + 1) * LANES)
            up_cut = slice(half + t * LANES, half + (t + 1) * LANES)
            if t % 2 == 0:
                both = dot_nn(grad_ffn, w_d[:, t * LANES : min((t + 2) * LANES, half)])
            grad_hidden = tile_of(both, t % 2)
            gate_part = parts[:, cut]
            up_part = parts[:, up_cut]
            sigma = sigmoid(gate_part)
            active = gate_part * sigma
            hidden_out[:, cut] = (active * up_part).astype(BF)
            parts_grad_out[:, cut] = (
                grad_hidden * up_part * sigma * (1.0 + gate_part * (1.0 - sigma))
            ).astype(BF)
            parts_grad_out[:, up_cut] = (grad_hidden * active).astype(BF)
        loads["gu"].wait()
        parts_now = parts_grad_out[...]
        chunk = w_gu.shape[0] // mp

        def second_chunk(c):
            return dot_nt(parts_now, w_gu[pl.ds(pl.multiple_of(c * chunk, chunk), chunk), :])

        grad_second = sum_over_mp(mp, me, second_chunk, send_b, recv_b, full_b, sems_b).astype(F32)
        unit, factor = unit_of(level + attn_now)
        second_vec_out[...] = jnp.sum(grad_second * unit, axis=0, keepdims=True)
        grad_middle = unit_back(grad_second * gains[1:2, :], unit, factor)
        middle_out[...] = grad_middle
        grad_attn = (gate * grad_update + grad_middle).astype(BF)
        attn_grad_out[...] = grad_attn
        loads["o"].wait()
        mixed_out[...] = dot_nn(grad_attn, w_o[...]).astype(BF)


def feed_back(flow, gains, tail, head, w_qkv, w_rest, hidden_width, mp, ident):
    model = flow.shape[1]
    mix = w_qkv.shape[1] - 2 * HD
    args, outs, scratch = [flow, gains], [], []
    tail_n = head_n = 0
    tail_picked = head_picked = False
    if tail is not None:
        *items, pick = tail
        tail_n, tail_picked = items[0].shape[0], pick is not None
        args += items + ([pick] if tail_picked else [])
    if head is not None:
        *items, pick = head
        head_n, head_picked = items[0].shape[0], pick is not None
        args += items + ([pick] if head_picked else [])
    in_vmem = len(args)
    if tail_n:
        args.append(w_qkv)
        outs += [
            jax.ShapeDtypeStruct(flow.shape, F32),
            jax.ShapeDtypeStruct((1, model), F32),
            jax.ShapeDtypeStruct((1, model), F32),
        ]
        scratch += [
            pltpu.VMEM(w_qkv.shape, BF),
            pltpu.SemaphoreType.DMA(()),
            *sum_scratch(mp, tail_n, model),
        ]
    if head_n:
        args.append(w_rest)
        outs += [
            jax.ShapeDtypeStruct((head_n, model), BF),
            jax.ShapeDtypeStruct((head_n, model), F32),
            jax.ShapeDtypeStruct((head_n, 1), F32),
            jax.ShapeDtypeStruct((head_n, mix), BF),
            jax.ShapeDtypeStruct((head_n, 2 * hidden_width), BF),
            jax.ShapeDtypeStruct((head_n, hidden_width), BF),
            jax.ShapeDtypeStruct((head_n, model), BF),
            jax.ShapeDtypeStruct((1, model), F32),
        ]
        scratch += [
            pltpu.VMEM((model, mix), BF),
            pltpu.VMEM((model, 2 * hidden_width), BF),
            pltpu.VMEM((model, hidden_width), BF),
            pltpu.SemaphoreType.DMA((3,)),
            *sum_scratch(mp, head_n, model),
        ]
    return pl.pallas_call(
        functools.partial(feed_back_kernel, tail_n, head_n, mp, tail_picked, head_picked),
        out_shape=tuple(outs),
        in_specs=vmem(in_vmem) + [pl.BlockSpec(memory_space=pl.ANY)] * (len(args) - in_vmem),
        out_specs=tuple(vmem(len(outs))),
        scratch_shapes=scratch,
        compiler_params=pltpu.CompilerParams(
            collective_id=ident, has_side_effects=True, vmem_limit_bytes=VMEM_LIMIT
        ),
        cost_estimate=pl.CostEstimate(flops=5 * 10**9, bytes_accessed=10**8, transcendentals=0),
        name=f"feed_back_{tail_n}_{head_n}",
    )(*args)


def rotary_tables(place, heads):
    freq = jnp.exp(jnp.arange(HD // 2, dtype=F32) * (-2.0 * math.log(ROPE_BASE) / HD))
    angle = place.astype(F32)[:, None] * freq[None, :]
    cosine, sine = jnp.cos(angle), jnp.sin(angle)
    one = jnp.concatenate([cosine, cosine], axis=1)
    two = jnp.concatenate([-sine, sine], axis=1)
    return (
        jnp.concatenate([jnp.tile(one, (1, heads + 1)), jnp.ones(one.shape, F32)], axis=1),
        jnp.concatenate([jnp.tile(two, (1, heads + 1)), jnp.zeros(one.shape, F32)], axis=1),
    )


def local(
    tokens, depths, second_slot, third_slot, w_query, w_key, w_value, w_out, w_gate, w_up,
    w_down, norm_first, norm_second, router, cotangent,
):
    me = lax.axis_index("dp")
    devices, mp = lax.axis_size("dp"), lax.axis_size("mp")
    rows = tokens.shape[0]
    heads = w_query.shape[1] // HD
    hidden_width = w_gate.shape[1]
    depth = w_query.shape[0]
    qkv_width = (heads + 2) * HD

    picks, marks = [], []
    for active, slot, capacity in (
        ((depths >= 2) & (second_slot >= 0), second_slot, SECOND_SLOTS),
        ((depths >= 3) & (third_slot >= 0), third_slot, THIRD_SLOTS),
    ):
        pick = (jnp.arange(capacity)[:, None] == slot[None, :]) & active[None, :]
        picks.append(pick.astype(BF))
        marks.append(
            jnp.min(jnp.where(pick, jnp.arange(rows, dtype=jnp.int32)[None, :], rows), axis=1)
        )

    def column(values):
        return values.reshape(depth, 1).astype(BF)

    second_mark = jnp.pad(marks[0], (0, 2 * depth - SECOND_SLOTS), constant_values=rows)
    first_shard = jnp.concatenate(
        [
            w_query, w_key, w_value,
            column(norm_first), column(norm_second), column(router),
            column(second_mark[:depth]), column(second_mark[depth:]), column(marks[1]),
            jnp.zeros((depth, LANES - 6), BF),
        ],
        axis=1,
    )
    rest_shard = jnp.concatenate([w_out.T, w_gate, w_up, w_down.T], axis=1)
    first = lax.all_gather(first_shard, "dp", axis=0, tiled=True)
    w_rest = lax.all_gather(rest_shard, "dp", axis=0, tiled=True)
    w_qkv = first[:, :qkv_width]
    extra = first[:, qkv_width : qkv_width + 8].astype(F32)
    gains = extra.T
    marks_all = extra[:, 3:6].astype(jnp.int32).reshape(devices, depth, 3)
    second_all = jnp.concatenate(
        [marks_all[:, :, 0], marks_all[:, : SECOND_SLOTS - depth, 1]], axis=1
    )
    base = (jnp.arange(devices, dtype=jnp.int32) * rows)[:, None]

    def place_of(mark, offset):
        return jnp.where(mark < rows, mark + offset, FAR)

    def key_column(mark):
        return jnp.broadcast_to(place_of(mark, base).reshape(-1, 1), (mark.size, LANES))

    levels = (
        (rows, None, jnp.arange(rows, dtype=jnp.int32) + me * rows, None),
        (SECOND_SLOTS, picks[0], place_of(marks[0], me * rows), key_column(second_all)),
        (THIRD_SLOTS, picks[1], place_of(marks[1], me * rows), key_column(marks_all[:, :, 2])),
    )
    state = tokens
    kept = []
    for index, (count, pick, place, key_place) in enumerate(levels):
        tables = rotary_tables(jnp.where(place == FAR, 0, place), heads)
        query_place = jnp.tile(place, heads)[None, :]
        rows_in, normed, packed, query, mixed_t, log_total, mixed = attend(
            state, pick, key_place, query_place, gains, tables, w_qkv, heads, devices, count, index
        )
        attn, ffn, second, parts, state = feed(
            state, rows_in, mixed, pick, gains, w_rest, hidden_width, mp, count, 3 + index
        )
        kept.append(
            (pick, key_place, query_place, tables, rows_in, normed, packed, query, mixed_t, log_total, mixed,
             attn, ffn, second, parts)
        )

    flow = cotangent
    tail = None
    terms, vectors = [], []
    for index in (2, 1, 0, None):
        head = None
        if index is not None:
            (pick, key_place, query_place, tables, rows_in, normed, packed, query, mixed_t, log_total, mixed,
             attn, ffn, second, parts) = kept[index]
            head = (rows_in, attn, ffn, second, parts, pick)
        outs = list(
            feed_back(flow, gains, tail, head, w_qkv, w_rest, hidden_width, mp, 6 + (3 if index is None else index))
        )
        if tail is not None:
            flow, first_vec, router_vec = outs[:3]
            outs = outs[3:]
            vectors.append((first_vec, None, router_vec))
        if head is not None:
            grad_attn, grad_middle, logit, grad_mixed, parts_grad, hidden, grad_ffn, second_vec = outs
            vectors.append((None, second_vec, None))
            grad_qkv = attend_back(
                key_place, query_place, query, packed, mixed_t, log_total, grad_mixed, tables,
                heads, devices, rows_in.shape[0], 10 + index,
            )
            tail = (grad_qkv, rows_in, grad_middle, logit, pick)
            terms.append((normed, grad_qkv, grad_attn, mixed, second, parts_grad, grad_ffn, hidden))
    normed, grad_qkv, grad_attn, mixed, second, parts_grad, grad_ffn, hidden = [
        jnp.concatenate(items, axis=0) for items in zip(*terms)
    ]
    vectors = [sum(item for item in items if item is not None) for items in zip(*vectors)]
    columns = jnp.concatenate(vectors + [jnp.zeros((LANES - 3, flow.shape[1]), F32)], axis=0).T

    def scatter(parts):
        return lax.psum_scatter(
            jnp.concatenate([part.astype(BF) for part in parts], axis=1),
            "dp", scatter_dimension=0, tiled=True,
        ).astype(F32)

    rest = scatter([dot_tn(second, parts_grad), dot_tn(grad_ffn, hidden)])
    some = scatter([dot_tn(grad_attn, mixed), dot_tn(normed, grad_qkv), columns])
    mix = heads * HD
    return (
        state, flow,
        some[:, mix : 2 * mix],
        some[:, 2 * mix : 2 * mix + HD],
        some[:, 2 * mix + HD : 2 * mix + 2 * HD],
        some[:, :mix].T,
        rest[:, :hidden_width],
        rest[:, hidden_width : 2 * hidden_width],
        rest[:, 2 * hidden_width :].T,
        some[:, 2 * mix + 2 * HD],
        some[:, 2 * mix + 2 * HD + 1],
        some[:, 2 * mix + 2 * HD + 2],
    )


def solution(mesh):
    in_specs = (
        P("dp", None), P("dp"), P("dp"), P("dp"), P("dp", "mp"), P("dp", "mp"), P("dp", "mp"),
        P("mp", "dp"), P("dp", "mp"), P("dp", "mp"), P("mp", "dp"), P("dp"), P("dp"), P("dp"),
        P("dp", None),
    )
    out_specs = (
        P("dp", None), P("dp", None), P("dp", "mp"), P("dp", "mp"), P("dp", "mp"), P("mp", "dp"),
        P("dp", "mp"), P("dp", "mp"), P("mp", "dp"), P("dp"), P("dp"), P("dp"),
    )
    return jax.shard_map(local, mesh=mesh, in_specs=in_specs, out_specs=out_specs, check_vma=False)
```

time: 1430 us -> 738 us (0.52)
  waiting for transfers between devices: 914 us -> 279 us
  Pallas kernels: 0 us -> 359 us
  matrix products: 203 us -> 12.9 us
  local copies, waits for them, and re-layouts: 162 us -> 39 us
  blocking collectives: 52.7 us -> 0 us
  other arithmetic: 65.3 us -> 26.4 us
    psum x11 -> x0, waiting for transfers between devices: 434 us -> none  [sum_mp(): return lax.psum(values.astype(BF), 'mp').astype(F32)]
    pallas_call x0 -> x13, Pallas kernels: none -> 359 us  [the longest x4 129 us: feed_back(): pl.pallas_call(functools.partial(feed_back_kernel, tail_n, head_n, mp, ta...]
    dot_general x124 -> x0, matrix products: 157 us -> none  [the longest x69 83.9 us: dot_nt(): lax.dot_general(left, right, (((1,), (1,)), ((), ())), preferred_element_...]
    reduce_scatter x3 -> x1, waiting for transfers between devices: 222 us -> 116 us  [scatter(): lax.psum_scatter(jnp.concatenate([part.astype(BF) for part in parts], axi...]
    unnamed x18 -> x5, waiting for transfers between devices: 128 us -> 72.4 us
    all_gather x2 -> x0, blocking collectives: 52.7 us -> none  [local(): packed = lax.all_gather(qkv[:, heads * HD:], 'dp', axis=0, tiled=True)]
    all_gather x2, waiting for transfers between devices: 129 us -> 90.9 us  [the longest x1 54.2 us: local(): w_rest = lax.all_gather(rest_shard, 'dp', axis=0, tiled=True)]
    unnamed x355 -> x82, local copies, waits for them, and re-layouts: 50.9 us -> 15.7 us
  transfers between devices with their start and end apart: 17 -> 4, of which waited for: 17 -> 4; matrix products, arithmetic and copies ran while one was open for 3% -> 6% of each run, Pallas kernels for 0% -> 4%
where the time goes in v2:
time: 738 us; the launch traced here: 732 us
  Pallas kernels  359 us (49%)
  waiting for transfers between devices  279 us (38%)
  local copies, waits for them, and re-layouts  39 us (5%)
  other arithmetic  26.4 us (4%)
  between operations  14.8 us (2%)
  matrix products  12.9 us (2%)
    pallas_call x4, Pallas kernels, feed_back(): pl.pallas_call(functools.partial(feed_back_kernel, tail_n, head_n, mp, ta...  129 us
    reduce_scatter x1, waiting for transfers between devices, scatter(): lax.psum_scatter(jnp.concatenate([part.astype(BF) for part in parts], axi...  116 us
    pallas_call x3, Pallas kernels, feed(): pl.pallas_call(functools.partial(feed_kernel, n, mp, picked), out_shape=(...  104 us
    unnamed x5, waiting for transfers between devices  72.4 us
    pallas_call x3, Pallas kernels, attend(): pl.pallas_call(functools.partial(attend_kernel, n, heads, devices, group,...  67.2 us
    pallas_call x3, Pallas kernels, attend_back(): pl.pallas_call(functools.partial(attend_back_kernel, n, heads, devices, g...  58.9 us
    all_gather x1, waiting for transfers between devices, local(): w_rest = lax.all_gather(rest_shard, 'dp', axis=0, tiled=True)  54.2 us
    all_gather x1, waiting for transfers between devices, local(): first = lax.all_gather(first_shard, 'dp', axis=0, tiled=True)  36.8 us
  transfers between devices with their start and end apart: 4, of which 4 were waited for; matrix products, arithmetic and copies ran while one was open for 6% of the time, Pallas kernels for 4%

profile of v2, /device:TPU:0, one launch (start us, length us, event | category | flops | bytes accessed | tf_op | source)
XLA Modules:
  0.0 731.8 jit_solution(7519121581480149221)
XLA Ops:
  7.2 0.8 copy.78
  8.0 0.8 copy.79
  8.8 0.8 copy.80
  10.2 0.8 select_reduce_fusion
  11.3 0.8 select_reduce_fusion.1
  12.2 1.6 concatenate.79
  13.9 2.0 pad_maximum_fusion.2
  17.6 0.7 concatenate.81.refs_3_.refs_6_
  19.2 0.7 concatenate.83.refs_4_.refs_7_
  24.6 36.8 %all-gather.3.cloned.1.call-done = bf16[2048,768]{1,0:T(8,128)(2,1)} async-done(((bf16[64,768]{1,0:T(8,128)(2,1)}), bf16[2048,768]{1,0:T(8,128)(2,1)}) %all-gather.3.cloned.1.call-update) | async-done | bytes 3145744 | tf_op jit(solution)/shard_map/all_gather | solution.py:717
  61.4 1.2 slice_convert_fusion.1
  62.6 0.9 copy.86.refs_2_.refs_3_.refs_4_.refs_1_
  64.3 1.0 slice_reduce_fusion
  65.9 3.5 slice.76.refs_5_.refs_7_.refs_13_.refs_12_.refs_6_
  70.0 27.0 %attend_128.1 = (bf16[128,2048]{1,0:T(8,128)(2,1)}, bf16[128,2048]{1,0:T(8,128)(2,1)}, bf16[32,128,128]{2,1,0:T(8,128)(2,1)}, bf16[1024,128]{1,0:T(8,128)(2,1)},...) custom-call(bf16[128,2048]{1,0:T(8,128)(2,1)} %refs_0_.5, s32[1,1024]{1,0:T(1,128)} %bitcast.48, ...), custom_call_target="tpu_custom_call" | custom-call | flops 4000000000 | bytes 10000000 | tf_op jit(solution)/shard_map/attend_128/pallas_call | solution.py:242
  97.0 54.2 %all-gather.5.cloned.1.call-done.refs_4_.refs_5_.refs_8_.refs_14_.refs_13_ = bf16[2048,4736]{1,0:T(8,128)(2,1)} async-done(((bf16[64,4736]{1,0:T(8,128)(2,1)}), bf16[2048,4736]{1,0:T(8,128)(2,1)}) %all-gather.5.cloned.1.call-update) | async-done | bytes 19398672 | tf_op jit(solution)/shard_map/all_gather | solution.py:718
  151.2 41.9 %feed_128.1 = (bf16[128,2048]{1,0:T(8,128)(2,1)}, bf16[128,2048]{1,0:T(8,128)(2,1)}, bf16[128,2048]{1,0:T(8,128)(2,1)}, f32[128,2816]{1,0:T(8,128)}, f32[128,2048]{1,0:T(8,128)}) custom-call(bf16[128,2048]{1,0:T(8,128)(2,1)} %refs_0_.5, bf16[128,2048]{1,0:T(8,128)(2,1)} %get-tuple-element.81.refs_1_.refs_7_.refs_3_, ...), custom_call_target="tpu_custom_call" | custom-call | flops 5000000000 | bytes 100000000 | tf_op jit(solution)/shard_map/feed_128/pallas_call | solution.py:466
  193.1 2.3 broadcast_in_dim.93.refs_2_.refs_0_
  195.3 16.4 %attend_96.1 = (bf16[96,2048]{1,0:T(8,128)(2,1)}, bf16[96,2048]{1,0:T(8,128)(2,1)}, bf16[32,96,128]{2,1,0:T(8,128)(2,1)}, bf16[768,128]{1,0:T(8,128)(2,1)}, f32[...) custom-call(f32[128,2048]{1,0:T(8,128)} %get-tuple-element.83.refs_0_, ...), custom_call_target="tpu_custom_call" | custom-call | flops 4000000000 | bytes 10000000 | tf_op jit(solution)/shard_map/attend_96/pallas_call | solution.py:242
  211.7 34.4 %feed_96.1 = (bf16[96,2048]{1,0:T(8,128)(2,1)}, bf16[96,2048]{1,0:T(8,128)(2,1)}, bf16[96,2048]{1,0:T(8,128)(2,1)}, f32[96,2816]{1,0:T(8,128)}, f32[128,2048]{1,0:T(8,128)}) custom-call(f32[128,2048]{1,0:T(8,128)} %get-tuple-element.83.refs_0_, bf16[96,2048]{1,0:T(8,128)(2,1)} %get-tuple-element.84.refs_1_.refs_7_.refs_3_, ...), custom_call_target="tpu_custom_call" | custom-call | flops 5000000000 | bytes 100000000 | tf_op jit(solution)/shard_map/feed_96/pallas_call | solution.py:466
  246.1 1.3 broadcast_in_dim.97.refs_2_.refs_0_
  247.4 23.8 %attend_64.1 = (bf16[64,2048]{1,0:T(8,128)(2,1)}, bf16[64,2048]{1,0:T(8,128)(2,1)}, bf16[32,64,128]{2,1,0:T(8,128)(2,1)}, bf16[512,128]{1,0:T(8,128)(2,1)}, f32[...) custom-call(f32[128,2048]{1,0:T(8,128)} %get-tuple-element.86.refs_0_, ...), custom_call_target="tpu_custom_call" | custom-call | flops 4000000000 | bytes 10000000 | tf_op jit(solution)/shard_map/attend_64/pallas_call | solution.py:242
  271.2 27.4 %feed_64.1 = (bf16[64,2048]{1,0:T(8,128)(2,1)}, bf16[64,2048]{1,0:T(8,128)(2,1)}, bf16[64,2048]{1,0:T(8,128)(2,1)}, f32[64,2816]{1,0:T(8,128)}, f32[128,2048]{1,0:T(8,128)}) custom-call(f32[128,2048]{1,0:T(8,128)} %get-tuple-element.86.refs_0_, bf16[64,2048]{1,0:T(8,128)(2,1)} %get-tuple-element.87.refs_1_.refs_2_.refs_3_, ...), custom_call_target="tpu_custom_call" | custom-call | flops 5000000000 | bytes 100000000 | tf_op jit(solution)/shard_map/feed_64/pallas_call | solution.py:466
  298.7 21.1 %feed_back_0_64.1 = (bf16[64,2048]{1,0:T(8,128)(2,1)}, f32[64,2048]{1,0:T(8,128)}, f32[64,1]{1,0:T(8,128)}, bf16[64,512]{1,0:T(8,128)(2,1)}, bf16[64,2816]{1,0:T...) custom-call(f32[128,2048]{1,0:T(8,128)} %refs_0_.7, ...), custom_call_target="tpu_custom_call" | custom-call | flops 5000000000 | bytes 100000000 | tf_op jit(solution)/shard_map/feed_back_0_64/pallas_call | solution.py:654
  319.8 18.5 %attend_back_64.1.refs_2_ = bf16[64,640]{1,0:T(8,128)(2,1)} custom-call(s32[2048,128]{1,0:T(8,128)} %broadcast_in_dim.97.refs_2_.refs_0_, s32[1,512]{1,0:T(1,128)} %broadcast_in_dim_tile.11.refs_3_.refs_1_, bf16[512,128]{1,0:T(8,128)(2,1)} %get-tuple-element.90.refs_2_, bf16[32,64,128]{2,1,0:T(8,128)(2,1)} %get-tuple-element.91.refs_3_, ...), custom_call_target="tpu_custom_call" | custom-call | flops 10000000000 | bytes 10000000 | tf_op jit(solution)/shard_map/attend_back_64/pallas_call | solution.py:373
  338.3 38.9 %feed_back_64_96.1 = (f32[128,2048]{1,0:T(8,128)}, f32[1,2048]{1,0:T(1,128)}, f32[1,2048]{1,0:T(1,128)}, bf16[96,2048]{1,0:T(8,128)(2,1)}, f32[96,2048]{1,0:T(8,...) custom-call(f32[128,2048]{1,0:T(8,128)} %refs_0_.7, ...), custom_call_target="tpu_custom_call" | custom-call | flops 5000000000 | bytes 100000000 | tf_op jit(solution)/shard_map/feed_back_64_96/pallas_call | solution.py:654
  377.2 18.0 %attend_back_96.1.refs_2_ = bf16[96,640]{1,0:T(8,128)(2,1)} custom-call(s32[3072,128]{1,0:T(8,128)} %broadcast_in_dim.93.refs_2_.refs_0_, s32[1,768]{1,0:T(1,128)} %broadcast_in_dim_tile.10.refs_3_.refs_1_, bf16[768,128]{1,0:T(8,128)(2,1)} %get-tuple-element.106.refs_2_, bf16[32,96,128]{2,1,0:T(8,128)(2,1)} %get-tuple-element.107.refs_3_, ...), custom_call_target="tpu_custom_call" | custom-call | flops 10000000000 | bytes 10000000 | tf_op jit(solution)/shard_map/attend_back_96/pallas_call | solution.py:373
  395.3 46.4 %feed_back_96_128.1 = (f32[128,2048]{1,0:T(8,128)}, f32[1,2048]{1,0:T(1,128)}, f32[1,2048]{1,0:T(1,128)}, bf16[128,2048]{1,0:T(8,128)(2,1)}, f32[128,2048]{1,0:T...) custom-call(f32[128,2048]{1,0:T(8,128)} %get-tuple-element.105.refs_, ...), custom_call_target="tpu_custom_call" | custom-call | flops 5000000000 | bytes 100000000 | tf_op jit(solution)/shard_map/feed_back_96_128/pallas_call | solution.py:654
  441.7 22.3 %attend_back_128.1.refs_2_ = bf16[128,640]{1,0:T(8,128)(2,1)} custom-call(s32[1,1024]{1,0:T(1,128)} %bitcast.49, bf16[1024,128]{1,0:T(8,128)(2,1)} %get-tuple-element.118.refs_1_, bf16[32,128,128]{2,1,0:T(8,128)(2,1)} %get-tuple-element.119.refs_2_, f32[128,1024]{1,0:T(8,128)} %get-tuple-element.120.refs_3_, f32[1,1024]{1,0:T(1,128)} %get-tuple-element.121.refs_4_, ...), custom_call_target="tpu_custom_call" | custom-call | flops 10000000000 | bytes 10000000 | tf_op jit(solution)/shard_map/attend_back_128/pallas_call | solution.py:373
  464.2 22.5 %feed_back_128_0.1 = (f32[128,2048]{1,0:T(8,128)}, f32[1,2048]{1,0:T(1,128)}, f32[1,2048]{1,0:T(1,128)}) custom-call(f32[128,2048]{1,0:T(8,128)} %get-tuple-element.117.refs_0_, f32[8,2048]{1,0:T(8,128)} %copy.86.refs_2_.refs_3_.refs_4_.refs_1_, bf16[128,640]{1,0:T(8,128)(2,1)} %attend_back_128.1.refs_2_, ...), custom_call_target="tpu_custom_call" | custom-call | flops 5000000000 | bytes 100000000 | tf_op jit(solution)/shard_map/feed_back_128_0/pallas_call | solution.py:654
  486.7 0.7 add_convert_fusion
  488.4 1.6 convolution_convert_fusion.2
  490.0 1.3 convolution_convert_fusion.3
  491.4 9.2 %pad_maximum_fusion.1 = bf16[2048,1280]{0,1:T(8,128)(2,1)} fusion(bf16[2048,128]{0,1:T(8,128)(2,1)S(1)} %maximum_bitcast_fusion, bf16[2048,640]{0,1:T(8,128)(2,1)S(1)} %convolution_convert_fusion.2, bf16[2048,512]{0,1:T(8,128)(2,1)S(1)} %convolution_convert_fusion.3), kind=kLoop, calls=%fused_computation.3 | loop fusion | flops 15728640 | bytes 10485760 | tf_op jit(solution)/shard_map/concatenate | solution.py:788
  500.7 7.9 %copy.109 = bf16[2048,1280]{1,0:T(8,128)(2,1)} copy(bf16[2048,1280]{0,1:T(8,128)(2,1)} %pad_maximum_fusion.1) | data formatting | bytes 10485760
  510.0 3.6 convolution_convert_fusion.1
  513.7 6.4 convolution_convert_fusion
  520.1 6.8 pad_maximum_fusion
  527.0 72.3 %reduce-scatter.7.cloned.1.call-done = bf16[64,1280]{1,0:T(8,128)(2,1)} async-done(((bf16[2048,1280]{1,0:T(8,128)(2,1)}), bf16[64,1280]{1,0:T(8,128)(2,1)}) %reduce-scatter.7.cloned.1.call-update) | async-done | bytes 163856
  599.3 1.1 copy.110
  600.5 0.8 copy.104
  602.7 0.8 copy.107
  604.0 116.1 %reduce-scatter.5.cloned.1.call-done = bf16[64,4224]{1,0:T(8,128)(2,1)} async-done(((bf16[2048,4224]{1,0:T(8,128)(2,1)}), bf16[64,4224]{1,0:T(8,128)(2,1)}) %reduce-scatter.5.cloned.1.call-update) | async-done | bytes 540688 | tf_op jit(solution)/shard_map/reduce_scatter | solution.py:787
  720.1 1.2 convert_element_type.94
  721.3 0.8 slice_bitcast_fusion
  722.1 0.9 fusion.55
  723.0 1.0 copy.116
  724.0 1.0 copy.117
  (143 shorter events, 14.7 us)
Async XLA Ops:
  7.2 54.2 %all-gather.3.cloned.1.call-start = ((), (), s32[]{:S(2)}) async-start(), calls=%async_computation.2 | async-start | bytes 3244032 | tf_op jit(solution)/shard_map/all_gather | solution.py:717
  13.9 137.3 %all-gather.5.cloned.1.call-start = ((), (), s32[]{:S(2)}) async-start(), calls=%async_computation.3 | async-start | bytes 20004864 | tf_op jit(solution)/shard_map/all_gather | solution.py:718
  15.9 583.4 %reduce-scatter.7.cloned.1.call-start = ((), (), s32[]{:S(2)}) async-start(), calls=%async_computation.5 | async-start | bytes 5406720
  19.0 4.4 copy-start.18
  19.0 5.0 copy-start.19
  464.0 22.7 %copy-start.14 = (f32[1,2048]{1,0:T(1,128)S(1)}, f32[1,2048]{1,0:T(1,128)}, u32[]{:S(2)}) copy-start(f32[1,2048]{1,0:T(1,128)} %get-tuple-element.138) | copy-start | bytes 24580
  464.0 22.7 %copy-start.17 = (f32[1,2048]{1,0:T(1,128)S(1)}, f32[1,2048]{1,0:T(1,128)}, u32[]{:S(2)}) copy-start(f32[1,2048]{1,0:T(1,128)} %get-tuple-element.139) | copy-start | bytes 24580
  464.1 23.4 %copy-start.11 = (f32[1,2048]{1,0:T(1,128)S(1)}, f32[1,2048]{1,0:T(1,128)}, u32[]{:S(2)}) copy-start(f32[1,2048]{1,0:T(1,128)} %get-tuple-element.135) | copy-start | bytes 24580
  464.1 23.4 %copy-start.13 = (f32[1,2048]{1,0:T(1,128)S(1)}, f32[1,2048]{1,0:T(1,128)}, u32[]{:S(2)}) copy-start(f32[1,2048]{1,0:T(1,128)} %get-tuple-element.136) | copy-start | bytes 24580
  464.1 23.4 %copy-start.16 = (f32[1,2048]{1,0:T(1,128)S(1)}, f32[1,2048]{1,0:T(1,128)}, u32[]{:S(2)}) copy-start(f32[1,2048]{1,0:T(1,128)} %get-tuple-element.137) | copy-start | bytes 24580
  464.1 23.4 %copy-start.12 = (f32[1,2048]{1,0:T(1,128)S(1)}, f32[1,2048]{1,0:T(1,128)}, u32[]{:S(2)}) copy-start(f32[1,2048]{1,0:T(1,128)} %get-tuple-element.132) | copy-start | bytes 24580
  464.1 23.4 %copy-start.15 = (f32[1,2048]{1,0:T(1,128)S(1)}, f32[1,2048]{1,0:T(1,128)}, u32[]{:S(2)}) copy-start(f32[1,2048]{1,0:T(1,128)} %get-tuple-element.133) | copy-start | bytes 24580
  464.1 24.1 %copy-start.7 = (bf16[96,640]{1,0:T(8,128)(2,1)S(1)}, bf16[96,640]{1,0:T(8,128)(2,1)}, u32[]{:S(2)}) copy-start(bf16[96,640]{1,0:T(8,128)(2,1)} %attend_back_96.1.refs_2_) | copy-start | bytes 368644
  464.1 24.1 %copy-start.9 = (bf16[64,640]{1,0:T(8,128)(2,1)S(1)}, bf16[64,640]{1,0:T(8,128)(2,1)}, u32[]{:S(2)}) copy-start(bf16[64,640]{1,0:T(8,128)(2,1)} %attend_back_64.1.refs_2_) | copy-start | bytes 245764
  464.1 24.1 %copy-start.32 = (bf16[128,2048]{1,0:T(8,128)(2,1)S(1)}, bf16[128,2048]{1,0:T(8,128)(2,1)}, u32[]{:S(2)}) copy-start(bf16[128,2048]{1,0:T(8,128)(2,1)} %get-tuple-element.131) | copy-start | bytes 1572868
  464.1 24.1 %copy-start.33 = (bf16[96,2048]{1,0:T(8,128)(2,1)S(1)}, bf16[96,2048]{1,0:T(8,128)(2,1)}, u32[]{:S(2)}) copy-start(bf16[96,2048]{1,0:T(8,128)(2,1)} %get-tuple-element.130) | copy-start | bytes 1179652
  464.1 24.1 %copy-start.34 = (bf16[64,2048]{1,0:T(8,128)(2,1)S(1)}, bf16[64,2048]{1,0:T(8,128)(2,1)}, u32[]{:S(2)}) copy-start(bf16[64,2048]{1,0:T(8,128)(2,1)} %get-tuple-element.129) | copy-start | bytes 786436
  464.2 24.1 %copy-start.35 = (bf16[128,640]{1,0:T(8,128)(2,1)S(1)}, bf16[128,640]{1,0:T(8,128)(2,1)}, u32[]{:S(2)}) copy-start(bf16[128,640]{1,0:T(8,128)(2,1)} %attend_back_128.1.refs_2_) | copy-start | bytes 491524
  488.3 1.6 copy-start.6
  488.3 1.6 copy-start.8
  488.3 1.6 copy-start.10
  488.3 1.6 copy-start.23
  488.3 1.6 copy-start.25
  488.3 1.6 copy-start.30
  508.5 1.0 copy-start.22
  508.5 1.2 copy-start.24
  508.5 1.3 copy-start.27
  508.5 1.3 copy-start.28
  508.5 1.4 copy-start.29
  508.5 1.4 copy-start.31
  508.6 211.6 %reduce-scatter.5.cloned.1.call-start = ((), (), s32[]{:S(2)}) async-start(), calls=%async_computation.4 | async-start | bytes 17842176 | tf_op jit(solution)/shard_map/reduce_scatter | solution.py:787
  510.0 3.6 copy-start.3
  510.0 3.6 copy-start.4
  510.0 3.6 copy-start.5
  510.0 3.7 copy-start.20
  510.0 3.7 copy-start.21
  510.0 3.7 copy-start.26
  602.7 120.3 %copy-start.1 = (f32[128,2048]{1,0:T(8,128)S(1)}, f32[128,2048]{1,0:T(8,128)}, u32[]{:S(2)}) copy-start(f32[128,2048]{1,0:T(8,128)} %get-tuple-element.234) | copy-start | bytes 3145732
  720.1 2.0 copy-start
  721.3 2.7 copy-start.2
Sparse Core Ops, SparseCore 0:
  14.0 47.3 all-gather.2
  64.2 86.8 all-gather.4
  508.7 90.5 reduce-scatter.6
  603.6 116.4 reduce-scatter.4

commit v3 on v2

--- a/solution.py
+++ b/solution.py
@@ -116,7 +116,7 @@
     w_v, packed, query_t, top, total, acc, w_sem, out_sem, send_sems, recv_sems = refs
     me = lax.axis_index("dp")
     width = heads * n
-    load_w = pltpu.make_async_copy(w_hbm, w_v, w_sem)
+    load_w = pltpu.make_async_copy(w_hbm.at[:, : w_v.shape[1]], w_v, w_sem)
     load_w.start()
 
     barrier = pltpu.get_barrier_semaphore()
@@ -404,7 +404,7 @@
     me = lax.axis_index("mp")
     wide_o, wide_gu, wide_d = w_o.shape[1], w_gu.shape[1], w_d.shape[1]
     loads = []
-    start = 0
+    start = wide_o + 2 * LANES
     for index, (ref, wide) in enumerate(((w_o, wide_o), (w_gu, wide_gu), (w_d, wide_d))):
         load = pltpu.make_async_copy(w_hbm.at[:, start : start + wide], ref, w_sems.at[index])
         load.start()
@@ -518,7 +518,7 @@
         send_b, recv_b, full_b, sems_b = [refs.pop(0) for _ in range(4)]
     me = lax.axis_index("mp")
     if tail_n:
-        load_first = pltpu.make_async_copy(w_first_hbm, w_qkv, w_first_sem)
+        load_first = pltpu.make_async_copy(w_first_hbm.at[:, : w_qkv.shape[1]], w_qkv, w_first_sem)
         load_first.start()
     if head_n:
         loads = {}
@@ -526,6 +526,7 @@
         for index, (name, ref, start) in enumerate(
             (("d", w_d, wide_o + wide_gu), ("gu", w_gu, wide_o), ("o", w_o, 0))
         ):
+            start += wide_o + 2 * LANES
             loads[name] = pltpu.make_async_copy(
                 w_rest_hbm.at[:, start : start + ref.shape[1]], ref, w_sems.at[index]
             )
@@ -605,9 +606,8 @@
         mixed_out[...] = dot_nn(grad_attn, w_o[...]).astype(BF)
 
 
-def feed_back(flow, gains, tail, head, w_qkv, w_rest, hidden_width, mp, ident):
+def feed_back(flow, gains, tail, head, weights, hidden_width, mix, mp, ident):
     model = flow.shape[1]
-    mix = w_qkv.shape[1] - 2 * HD
     args, outs, scratch = [flow, gains], [], []
     tail_n = head_n = 0
     tail_picked = head_picked = False
@@ -621,19 +621,19 @@
         args += items + ([pick] if head_picked else [])
     in_vmem = len(args)
     if tail_n:
-        args.append(w_qkv)
+        args.append(weights)
         outs += [
             jax.ShapeDtypeStruct(flow.shape, F32),
             jax.ShapeDtypeStruct((1, model), F32),
             jax.ShapeDtypeStruct((1, model), F32),
         ]
         scratch += [
-            pltpu.VMEM(w_qkv.shape, BF),
+            pltpu.VMEM((model, mix + 2 * HD), BF),
             pltpu.SemaphoreType.DMA(()),
             *sum_scratch(mp, tail_n, model),
         ]
     if head_n:
-        args.append(w_rest)
+        args.append(weights)
         outs += [
             jax.ShapeDtypeStruct((head_n, model), BF),
             jax.ShapeDtypeStruct((head_n, model), F32),
@@ -665,6 +665,411 @@
     )(*args)
 
 
+def plane(me):
+    return me // 8, lax.rem(me // 2, 4), lax.rem(me, 2)
+
+
+def peer(x, y, core):
+    return {"dp": (lax.rem(x, 4) * 4 + lax.rem(y, 4)) * 2 + core}
+
+
+def shifted(x, y, core, axis, k):
+    return peer(x + k, y, core) if axis == 0 else peer(x, y + k, core)
+
+
+def meet(me, partners):
+    barrier = pltpu.get_barrier_semaphore()
+    for device in partners:
+        pl.semaphore_signal(barrier, inc=1, device_id=device, device_id_type=MESH)
+    pl.semaphore_wait(barrier, len(partners))
+
+
+def plane_partners(x, y, core):
+    return (
+        [peer(x, y, 1 - core)]
+        + [shifted(x, y, core, 0, k) for k in (1, 2, 3)]
+        + [shifted(x, y, core, 1, k) for k in (1, 2, 3)]
+    )
+
+
+def spread_kernel(
+    groups, w_query, w_key, w_value, w_out, w_gate, w_up, w_down, extras, full, gains,
+    shard, columns, own_sem, column_sem, send_sems, recv_sems,
+):
+    me = lax.axis_index("dp")
+    x, y, core = plane(me)
+    start = 0
+    pair = jnp.concatenate([w_key[...].astype(F32), w_value[...].astype(F32)], axis=1).astype(BF)
+    for part in (
+        w_query[...], pair, extras[...],
+        w_out[...].T, w_gate[...], w_up[...], w_down[...].T,
+    ):
+        shard[:, start : start + part.shape[1]] = part
+        start += part.shape[1]
+    own = pltpu.make_async_copy(shard, full.at[x, y, core], own_sem)
+    own.start()
+    meet(me, plane_partners(x, y, core))
+    started = []
+
+    def remote(g, index, source, target, device):
+        copy = pltpu.make_async_remote_copy(
+            src_ref=source, dst_ref=target, send_sem=send_sems.at[g, index],
+            recv_sem=recv_sems.at[g, index], device_id=device, device_id_type=MESH,
+        )
+        copy.start()
+        started.append(copy)
+        return copy
+
+    def line(axis, at, first, count, cut):
+        if axis == 0:
+            return full.at[pl.ds(first, count), at, core, :, cut]
+        return full.at[at, pl.ds(first, count), core, :, cut]
+
+    waits = [{} for _ in groups]
+
+    def one(g):
+        low, high, axis = groups[g]
+        cut = slice(low, high)
+        waits[g][1] = [
+            remote(
+                g, k - 1, shard.at[:, cut], full.at[x, y, core, :, cut],
+                shifted(x, y, core, axis, k),
+            )
+            for k in (2, 1, 3)
+        ]
+
+    def two(g):
+        low, high, axis = groups[g]
+        cut = slice(low, high)
+        for copy in waits[g][1]:
+            copy.wait_recv()
+        mine = line(axis, y if axis == 0 else x, 0, 4, cut)
+        waits[g][2] = [
+            remote(g, 3 + i, mine, mine, shifted(x, y, core, 1 - axis, k))
+            for i, k in enumerate((1, 3))
+        ]
+
+    def three(g):
+        low, high, axis = groups[g]
+        cut = slice(low, high)
+        at = y if axis == 0 else x
+        waits[g][3] = []
+        for i, k in enumerate((1, 3)):
+            waits[g][2][i].wait_recv()
+            piece = line(axis, lax.rem(at + 4 - k, 4), 2 * i, 2, cut)
+            waits[g][3].append(
+                remote(g, 5 + i, piece, piece, shifted(x, y, core, 1 - axis, k))
+            )
+
+    def four(g):
+        low, high, axis = groups[g]
+        for copy in waits[g][3]:
+            copy.wait_recv()
+        mine = full.at[:, :, core, :, slice(low, high)]
+        waits[g][4] = [remote(g, 7, mine, mine, peer(x, y, 1 - core))]
+
+    def five(g):
+        waits[g][4][0].wait_recv()
+
+    count = len(groups)
+    one(0)
+    one(1)
+    own.wait()
+    for i in range(count + 3):
+        if i < count:
+            two(i)
+        if i + 2 < count:
+            one(i + 2)
+        if 0 <= i - 1 < count:
+            three(i - 1)
+        if 0 <= i - 2 < count:
+            four(i - 2)
+        if 0 <= i - 3 < count:
+            five(i - 3)
+            if i == 3:
+                low = w_query.shape[1] + LANES
+                load = pltpu.make_async_copy(
+                    full.at[:, :, :, :, low : low + LANES], columns, column_sem
+                )
+                load.start()
+                load.wait()
+                flat = columns[...].reshape(gains.shape[1], LANES).astype(F32)
+                gains[...] = flat.T[: gains.shape[0], :]
+    for copy in started:
+        copy.wait_send()
+
+
+def spread(w_query, w_key, w_value, w_out, w_gate, w_up, w_down, extras, ident):
+    depth, mix = w_query.shape
+    hidden = w_gate.shape[1]
+    total = 2 * mix + 2 * LANES + 3 * hidden
+    cuts = [0, mix + 2 * LANES]
+    while cuts[-1] < total:
+        cuts.append(min(cuts[-1] + 512, total))
+    if cuts[-1] - cuts[-2] < 256:
+        cuts.pop(-2)
+    groups = [(a, b, i % 2) for i, (a, b) in enumerate(zip(cuts[:-1], cuts[1:]))]
+    return pl.pallas_call(
+        functools.partial(spread_kernel, groups),
+        out_shape=(
+            jax.ShapeDtypeStruct((4, 4, 2, depth, total), BF),
+            jax.ShapeDtypeStruct((8, 32 * depth), F32),
+        ),
+        in_specs=vmem(8),
+        out_specs=(pl.BlockSpec(memory_space=pl.ANY), pl.BlockSpec(memory_space=pltpu.VMEM)),
+        scratch_shapes=[
+            pltpu.VMEM((depth, total), BF),
+            pltpu.VMEM((4, 4, 2, depth, LANES), BF),
+            pltpu.SemaphoreType.DMA(()),
+            pltpu.SemaphoreType.DMA(()),
+            pltpu.SemaphoreType.DMA((len(groups), 8)),
+            pltpu.SemaphoreType.DMA((len(groups), 8)),
+        ],
+        compiler_params=pltpu.CompilerParams(
+            collective_id=ident, has_side_effects=True, vmem_limit_bytes=VMEM_LIMIT
+        ),
+        name="spread",
+    )(w_query, w_key, w_value, w_out, w_gate, w_up, w_down, extras)
+
+
+SLOTS = 4
+GROUP = 512
+
+
+def collect_kernel(levels, spans, groups, *refs):
+    refs = list(refs)
+    sources = [[refs.pop(0) for _ in range(8)] for _ in levels]
+    vectors = refs.pop(0)
+    q_out, k_out, v_out, out_out, gate_out, up_out, down_out, vec_out = [refs.pop(0) for _ in range(8)]
+    lefts, turned, rights, final, slots, core_recv, relay_recv, first_recv, mid, last_recv, loads, send_sems, recv_sems = refs
+    me = lax.axis_index("dp")
+    x, y, core = plane(me)
+    copies = []
+    row = 0
+    for level, count in enumerate(levels):
+        for s in range(4):
+            low, high = spans[s]
+            for side, ref in enumerate((lefts.at[s, row : row + count], rights.at[row : row + count, low:high])):
+                copy = pltpu.make_async_copy(sources[level][2 * s + side], ref, loads.at[level, 2 * s + side])
+                copy.start()
+                copies.append(copy)
+        row += count
+    meet(me, plane_partners(x, y, core))
+    for copy in copies:
+        copy.wait()
+    started = []
+
+    def remote(g, index, source, target, device):
+        copy = pltpu.make_async_remote_copy(
+            src_ref=source, dst_ref=target, send_sem=send_sems.at[g, index],
+            recv_sem=recv_sems.at[g, index], device_id=device, device_id_type=MESH,
+        )
+        copy.start()
+        return copy
+
+    waits = [{} for _ in groups]
+    done = set()
+
+    def held(slot, axis, at, first, count):
+        if axis == 0:
+            return slots.at[slot, at, pl.ds(first, count), core]
+        return slots.at[slot, pl.ds(first, count), at, core]
+
+    def zero(g):
+        slot = g % SLOTS
+        if g >= SLOTS:
+            for copy in waits[g - SLOTS][0] + waits[g - SLOTS][1] + waits[g - SLOTS][2]:
+                copy.wait_send()
+        column = 0
+        for section, low, high in groups[g][1]:
+            wide = high - low
+            if section < 4:
+                if section not in done:
+                    done.add(section)
+                    turned[section] = lefts[section].T
+                base = spans[section][0]
+
+            def rows_of(m, carry, section=section, low=low, high=high, column=column, wide=wide):
+                start = pl.multiple_of(m * 256, 256)
+                if section < 4:
+                    value = dot_nn(turned[section, pl.ds(start, 256), :], rights[:, base + low : base + high])
+                else:
+                    value = vectors[:, pl.ds(start, 256)].T
+                slots[slot, m // 2, pl.ds(lax.rem(m, 2) * 2, 2), :, :, column : column + wide] = (
+                    value.astype(BF).reshape(2, 2, 64, wide)
+                )
+                return carry
+
+            lax.fori_loop(0, 8, rows_of, 0)
+            column += wide
+        waits[g][0] = [
+            remote(g, 0, slots.at[slot, :, :, 1 - core, :, :column], core_recv.at[g, :, :, :, :column], peer(x, y, 1 - core))
+        ]
+
+    def first(g):
+        slot, (width, _, axis) = g % SLOTS, groups[g]
+        waits[g][0][0].wait_recv()
+
+        def add(i, carry):
+            a, b = i // 4, lax.rem(i, 4)
+            slots[slot, a, b, core, :, :width] = (
+                slots[slot, a, b, core, :, :width].astype(F32) + core_recv[g, a, b, :, :width].astype(F32)
+            ).astype(BF)
+            return carry
+
+        lax.fori_loop(0, 16, add, 0)
+        at = x if axis == 0 else y
+        waits[g][1] = [
+            remote(
+                g, 1 + i, held(slot, axis, lax.rem(at + 2, 4), 2 * i, 2).at[:, :, :width],
+                relay_recv.at[g, i, :, :, :width], shifted(x, y, core, axis, k),
+            )
+            for i, k in enumerate((1, 3))
+        ]
+
+    def second(g):
+        slot, (width, _, axis) = g % SLOTS, groups[g]
+        at = x if axis == 0 else y
+        waits[g][2] = []
+        for i, k in enumerate((1, 3)):
+            waits[g][1][i].wait_recv()
+            there = lax.rem(at + k, 4)
+            for j in range(2):
+                b = 2 * i + j
+                where = (slot, there, b, core) if axis == 0 else (slot, b, there, core)
+                slots[where + (slice(None), slice(0, width))] = (
+                    slots[where + (slice(None), slice(0, width))].astype(F32)
+                    + relay_recv[g, i, j, :, :width].astype(F32)
+                ).astype(BF)
+            waits[g][2].append(
+                remote(
+                    g, 3 + i, held(slot, axis, there, 0, 4).at[:, :, :width],
+                    first_recv.at[g, i, :, :, :width], shifted(x, y, core, axis, k),
+                )
+            )
+
+    def third(g):
+        slot, (width, _, axis) = g % SLOTS, groups[g]
+        at, other = (x, y) if axis == 0 else (y, x)
+        for copy in waits[g][2]:
+            copy.wait_recv()
+        for b in range(4):
+            where = (slot, at, b, core) if axis == 0 else (slot, b, at, core)
+            mid[g, b, :, :width] = (
+                slots[where + (slice(None), slice(0, width))].astype(F32)
+                + first_recv[g, 0, b, :, :width].astype(F32)
+                + first_recv[g, 1, b, :, :width].astype(F32)
+            ).astype(BF)
+        waits[g][3] = [
+            remote(
+                g, 4 + k, mid.at[g, lax.rem(other + k, 4), :, :width], last_recv.at[g, k - 1, :, :width],
+                shifted(x, y, core, 1 - axis, k),
+            )
+            for k in (2, 1, 3)
+        ]
+
+    def fourth(g):
+        width, pieces, axis = groups[g]
+        other = y if axis == 0 else x
+        value = mid[g, other, :, :width].astype(F32)
+        for i, copy in enumerate(waits[g][3]):
+            copy.wait_recv()
+        for k in range(3):
+            value = value + last_recv[g, k, :, :width].astype(F32)
+        column = 0
+        for section, low, high in pieces:
+            base = spans[section][0]
+            final[:, base + low : base + high] = value[:, column : column + high - low]
+            column += high - low
+
+    count = len(groups)
+    for i in range(count + 4):
+        for stage, step in enumerate((zero, first, second, third, fourth)):
+            if 0 <= i - stage < count:
+                step(i - stage)
+    hidden = gate_out.shape[1]
+    mix = q_out.shape[1]
+    gate_out[...] = final[:, :hidden]
+    up_out[...] = final[:, hidden : 2 * hidden]
+    down_out[...] = final[:, spans[1][0] : spans[1][1]].T
+    out_out[...] = final[:, spans[2][0] : spans[2][1]].T
+    low = spans[3][0]
+    q_out[...] = final[:, low : low + mix]
+    k_out[...] = final[:, low + mix : low + mix + HD]
+    v_out[...] = final[:, low + mix + HD : low + mix + 2 * HD]
+    vec_out[...] = final[:, spans[4][0] : spans[4][1]]
+    for g in range(count):
+        for stage in range(4):
+            if stage == 3 or g >= count - SLOTS:
+                for copy in waits[g][stage]:
+                    copy.wait_send()
+
+
+def collect(levels, vectors, depth, ident):
+    widths = [levels[0][i].shape[1] for i in (1, 3, 5, 7)] + [LANES]
+    spans, total = [], 0
+    for width in widths:
+        spans.append((total, total + width))
+        total += width
+    pieces = []
+    for section, width in enumerate(widths):
+        low = 0
+        while low < width:
+            pieces.append((section, low, low + LANES))
+            low += LANES
+    groups = []
+    per = GROUP // LANES
+    for index in range(0, len(pieces), per):
+        merged = []
+        for section, low, high in pieces[index : index + per]:
+            if merged and merged[-1][0] == section:
+                merged[-1] = (section, merged[-1][1], high)
+            else:
+                merged.append((section, low, high))
+        width = sum(high - low for _, low, high in merged)
+        groups.append((width, merged, (index // per) % 2))
+    counts = [level[0].shape[0] for level in levels]
+    rows = sum(counts)
+    model = levels[0][0].shape[1]
+    hidden, mix = widths[1], widths[2]
+    many = len(groups)
+    args = [item for level in levels for item in level] + [vectors]
+    return pl.pallas_call(
+        functools.partial(collect_kernel, counts, spans, groups),
+        out_shape=(
+            jax.ShapeDtypeStruct((depth, mix), F32),
+            jax.ShapeDtypeStruct((depth, HD), F32),
+            jax.ShapeDtypeStruct((depth, HD), F32),
+            jax.ShapeDtypeStruct((mix, depth), F32),
+            jax.ShapeDtypeStruct((depth, hidden), F32),
+            jax.ShapeDtypeStruct((depth, hidden), F32),
+            jax.ShapeDtypeStruct((hidden, depth), F32),
+            jax.ShapeDtypeStruct((depth, LANES), F32),
+        ),
+        in_specs=[pl.BlockSpec(memory_space=pl.ANY)] * (len(args) - 1) + vmem(1),
+        out_specs=tuple(vmem(8)),
+        scratch_shapes=[
+            pltpu.VMEM((4, rows, model), BF),
+            pltpu.VMEM((4, model, rows), BF),
+            pltpu.VMEM((rows, spans[3][1]), BF),
+            pltpu.VMEM((depth, total), F32),
+            pltpu.VMEM((SLOTS, 4, 4, 2, depth, GROUP), BF),
+            pltpu.VMEM((many, 4, 4, depth, GROUP), BF),
+            pltpu.VMEM((many, 2, 2, depth, GROUP), BF),
+            pltpu.VMEM((many, 2, 4, depth, GROUP), BF),
+            pltpu.VMEM((many, 4, depth, GROUP), BF),
+            pltpu.VMEM((many, 3, depth, GROUP), BF),
+            pltpu.SemaphoreType.DMA((len(levels), 8)),
+            pltpu.SemaphoreType.DMA((many, 8)),
+            pltpu.SemaphoreType.DMA((many, 8)),
+        ],
+        compiler_params=pltpu.CompilerParams(
+            collective_id=ident, has_side_effects=True, vmem_limit_bytes=VMEM_LIMIT
+        ),
+        name="collect",
+    )(*args)
+
+
 def rotary_tables(place, heads):
     freq = jnp.exp(jnp.arange(HD // 2, dtype=F32) * (-2.0 * math.log(ROPE_BASE) / HD))
     angle = place.astype(F32)[:, None] * freq[None, :]
@@ -687,7 +1092,6 @@
     heads = w_query.shape[1] // HD
     hidden_width = w_gate.shape[1]
     depth = w_query.shape[0]
-    qkv_width = (heads + 2) * HD
 
     picks, marks = [], []
     for active, slot, capacity in (
@@ -704,24 +1108,19 @@
         return values.reshape(depth, 1).astype(BF)
 
     second_mark = jnp.pad(marks[0], (0, 2 * depth - SECOND_SLOTS), constant_values=rows)
-    first_shard = jnp.concatenate(
+    extras = jnp.concatenate(
         [
-            w_query, w_key, w_value,
             column(norm_first), column(norm_second), column(router),
             column(second_mark[:depth]), column(second_mark[depth:]), column(marks[1]),
             jnp.zeros((depth, LANES - 6), BF),
         ],
         axis=1,
     )
-    rest_shard = jnp.concatenate([w_out.T, w_gate, w_up, w_down.T], axis=1)
-    first = lax.all_gather(first_shard, "dp", axis=0, tiled=True)
-    w_rest = lax.all_gather(rest_shard, "dp", axis=0, tiled=True)
-    w_qkv = first[:, :qkv_width]
-    extra = first[:, qkv_width : qkv_width + 8].astype(F32)
-    gains = extra.T
-    marks_all = extra[:, 3:6].astype(jnp.int32).reshape(devices, depth, 3)
+    weights, gains = spread(w_query, w_key, w_value, w_out, w_gate, w_up, w_down, extras, 13)
+    weights = weights.reshape(devices * depth, -1)
+    marks_all = gains[3:6].astype(jnp.int32).reshape(3, devices, depth)
     second_all = jnp.concatenate(
-        [marks_all[:, :, 0], marks_all[:, : SECOND_SLOTS - depth, 1]], axis=1
+        [marks_all[0], marks_all[1, :, : SECOND_SLOTS - depth]], axis=1
     )
     base = (jnp.arange(devices, dtype=jnp.int32) * rows)[:, None]
 
@@ -734,7 +1133,7 @@
     levels = (
         (rows, None, jnp.arange(rows, dtype=jnp.int32) + me * rows, None),
         (SECOND_SLOTS, picks[0], place_of(marks[0], me * rows), key_column(second_all)),
-        (THIRD_SLOTS, picks[1], place_of(marks[1], me * rows), key_column(marks_all[:, :, 2])),
+        (THIRD_SLOTS, picks[1], place_of(marks[1], me * rows), key_column(marks_all[2])),
     )
     state = tokens
     kept = []
@@ -742,10 +1141,10 @@
         tables = rotary_tables(jnp.where(place == FAR, 0, place), heads)
         query_place = jnp.tile(place, heads)[None, :]
         rows_in, normed, packed, query, mixed_t, log_total, mixed = attend(
-            state, pick, key_place, query_place, gains, tables, w_qkv, heads, devices, count, index
+            state, pick, key_place, query_place, gains, tables, weights, heads, devices, count, index
         )
         attn, ffn, second, parts, state = feed(
-            state, rows_in, mixed, pick, gains, w_rest, hidden_width, mp, count, 3 + index
+            state, rows_in, mixed, pick, gains, weights, hidden_width, mp, count, 3 + index
         )
         kept.append(
             (pick, key_place, query_place, tables, rows_in, normed, packed, query, mixed_t, log_total, mixed,
@@ -762,7 +1161,7 @@
              attn, ffn, second, parts) = kept[index]
             head = (rows_in, attn, ffn, second, parts, pick)
         outs = list(
-            feed_back(flow, gains, tail, head, w_qkv, w_rest, hidden_width, mp, 6 + (3 if index is None else index))
+            feed_back(flow, gains, tail, head, weights, hidden_width, heads * HD, mp, 6 + (3 if index is None else index))
         )
         if tail is not None:
             flow, first_vec, router_vec = outs[:3]
@@ -776,34 +1175,15 @@
                 heads, devices, rows_in.shape[0], 10 + index,
             )
             tail = (grad_qkv, rows_in, grad_middle, logit, pick)
-            terms.append((normed, grad_qkv, grad_attn, mixed, second, parts_grad, grad_ffn, hidden))
-    normed, grad_qkv, grad_attn, mixed, second, parts_grad, grad_ffn, hidden = [
-        jnp.concatenate(items, axis=0) for items in zip(*terms)
-    ]
+            terms.append((second, parts_grad, grad_ffn, hidden, grad_attn, mixed, normed, grad_qkv))
     vectors = [sum(item for item in items if item is not None) for items in zip(*vectors)]
-    columns = jnp.concatenate(vectors + [jnp.zeros((LANES - 3, flow.shape[1]), F32)], axis=0).T
-
-    def scatter(parts):
-        return lax.psum_scatter(
-            jnp.concatenate([part.astype(BF) for part in parts], axis=1),
-            "dp", scatter_dimension=0, tiled=True,
-        ).astype(F32)
-
-    rest = scatter([dot_tn(second, parts_grad), dot_tn(grad_ffn, hidden)])
-    some = scatter([dot_tn(grad_attn, mixed), dot_tn(normed, grad_qkv), columns])
-    mix = heads * HD
+    vectors = jnp.concatenate(vectors + [jnp.zeros((LANES - 3, flow.shape[1]), F32)], axis=0)
+    query_grad, key_grad, value_grad, out_grad, gate_grad, up_grad, down_grad, vec = collect(
+        terms[::-1], vectors, depth, 14
+    )
     return (
-        state, flow,
-        some[:, mix : 2 * mix],
-        some[:, 2 * mix : 2 * mix + HD],
-        some[:, 2 * mix + HD : 2 * mix + 2 * HD],
-        some[:, :mix].T,
-        rest[:, :hidden_width],
-        rest[:, hidden_width : 2 * hidden_width],
-        rest[:, 2 * hidden_width :].T,
-        some[:, 2 * mix + 2 * HD],
-        some[:, 2 * mix + 2 * HD + 1],
-        some[:, 2 * mix + 2 * HD + 2],
+        state, flow, query_grad, key_grad, value_grad, out_grad, gate_grad, up_grad, down_grad,
+        vec[:, 0], vec[:, 1], vec[:, 2],
     )
 
 

time: 738 us -> 595 us (0.81)
  waiting for transfers between devices: 279 us -> 0 us
  Pallas kernels: 359 us -> 549 us
  other arithmetic: 26.4 us -> 6.61 us
  between operations: 14.8 us -> 1.62 us
  matrix products: 12.9 us -> 0 us
  local copies, waits for them, and re-layouts: 39 us -> 29.1 us
    pallas_call x0 -> x2, Pallas kernels: none -> 184 us  [the longest x1 99.6 us: collect(): pl.pallas_call(functools.partial(collect_kernel, counts, spans, groups),...]
    reduce_scatter x1 -> x0, waiting for transfers between devices: 116 us -> none  [scatter(): lax.psum_scatter(jnp.concatenate([part.astype(BF) for part in parts], axi...]
    all_gather x2 -> x0, waiting for transfers between devices: 90.9 us -> none  [the longest x1 54.2 us: local(): w_rest = lax.all_gather(rest_shard, 'dp', axis=0, tiled=True)]
    unnamed x5 -> x0, waiting for transfers between devices: 72.4 us -> none
    concatenate x3 -> x1, other arithmetic: 18 us -> 1.11 us  [local(): jnp.concatenate(vectors + [jnp.zeros((LANES - 3, flow.shape[1]), F32)], a...]
    dot_general x4 -> x0, matrix products: 12.9 us -> none  [dot_tn(): lax.dot_general(left, right, (((0,), (0,)), ((), ())), preferred_element_...]
    unnamed x82 -> x45, local copies, waits for them, and re-layouts: 15.7 us -> 12.8 us
  transfers between devices with their start and end apart: 4 -> 0, of which waited for: 4 -> 0; matrix products, arithmetic and copies ran while one was open for 6% -> 0% of each run, Pallas kernels for 4% -> 0%
where the time goes in v3:
time: 595 us; the launch traced here: 586 us
  Pallas kernels  549 us (92%)
  local copies, waits for them, and re-layouts  29.1 us (5%)
  other arithmetic  6.61 us (1%)
    pallas_call x4, Pallas kernels, feed_back(): pl.pallas_call(functools.partial(feed_back_kernel, tail_n, head_n, mp, ta...  128 us
    pallas_call x3, Pallas kernels, feed(): pl.pallas_call(functools.partial(feed_kernel, n, mp, picked), out_shape=(...  104 us
    pallas_call x1, Pallas kernels, collect(): pl.pallas_call(functools.partial(collect_kernel, counts, spans, groups),...  99.6 us
    pallas_call x1, Pallas kernels, spread(): pl.pallas_call(functools.partial(spread_kernel, groups), out_shape=(jax.S...  84.6 us
    pallas_call x3, Pallas kernels, attend(): pl.pallas_call(functools.partial(attend_kernel, n, heads, devices, group,...  74.2 us
    pallas_call x3, Pallas kernels, attend_back(): pl.pallas_call(functools.partial(attend_back_kernel, n, heads, devices, g...  58.8 us
    unnamed x45, local copies, waits for them, and re-layouts  12.8 us

profile of v3, /device:TPU:0, one launch (start us, length us, event | category | flops | bytes accessed | tf_op | source)
XLA Modules:
  0.0 586.1 jit_solution(8335809278046227552)
XLA Ops:
  1.3 1.6 copy.43.w_out
  2.9 1.8 copy.44.w_down
  4.7 0.8 copy.37
  5.4 0.8 copy.38
  6.2 0.8 copy.39
  7.0 0.7 compare_and_fusion
  7.7 0.8 select_reduce_fusion
  8.8 0.8 select_reduce_fusion.1
  9.7 0.7 concatenate.45.extras
  10.4 84.6 %spread.1 = (bf16[4,4,2,64,5504]{4,3,2,1,0:T(8,128)(2,1)}, f32[8,2048]{1,0:T(8,128)}) custom-call(bf16[64,512]{1,0:T(8,128)(2,1)} %w_query.1, bf16[64,64]{1,0:T(8,128)(2,1)} %w_key.1, bf16[64,64]{1,0:T(8,128)(2,1)} %w_value.1, bf16[512,64]{1,0:T(8,128)(2,1)} %copy.43.w_out, bf16[64,1408]{1,0:T(8,128)(2,1)} %w_gate.1, bf16[64,1408]{1,0:T(8,128)(2,1)} %w_up.1, ...), custom_call_target="tpu_custom_call" | custom-call | tf_op jit(solution)/shard_map/spread/pallas_call | solution.py:812
  95.3 0.8 concatenate.47.refs_3_.refs_6_
  96.3 0.8 concatenate.49.refs_4_.refs_7_
  97.0 20.2 %attend_128.1 = (bf16[128,2048]{1,0:T(8,128)(2,1)}, bf16[128,2048]{1,0:T(8,128)(2,1)}, bf16[32,128,128]{2,1,0:T(8,128)(2,1)}, bf16[1024,128]{1,0:T(8,128)(2,1)},...) custom-call(bf16[128,2048]{1,0:T(8,128)(2,1)} %refs_0_.5, s32[1,1024]{1,0:T(1,128)} %bitcast.39, ...), custom_call_target="tpu_custom_call" | custom-call | flops 4000000000 | bytes 10000000 | tf_op jit(solution)/shard_map/attend_128/pallas_call | solution.py:242
  117.3 41.9 %feed_128.1 = (bf16[128,2048]{1,0:T(8,128)(2,1)}, bf16[128,2048]{1,0:T(8,128)(2,1)}, bf16[128,2048]{1,0:T(8,128)(2,1)}, f32[128,2816]{1,0:T(8,128)}, f32[128,2048]{1,0:T(8,128)}) custom-call(bf16[128,2048]{1,0:T(8,128)(2,1)} %refs_0_.5, bf16[128,2048]{1,0:T(8,128)(2,1)} %get-tuple-element.93.refs_1_.refs_7_.refs_3_, ...), custom_call_target="tpu_custom_call" | custom-call | flops 5000000000 | bytes 100000000 | tf_op jit(solution)/shard_map/feed_128/pallas_call | solution.py:466
  159.2 0.6 fusion.1.refs_1_.refs_3_.refs_12_.refs_6_
  160.2 2.2 broadcast_in_dim.93.refs_2_.refs_0_
  162.4 0.7 broadcast_in_dim_tile.10.refs_3_.refs_1_
  163.4 0.7 concatenate.52.refs_5_.refs_7_
  164.3 0.7 concatenate.54.refs_6_.refs_8_
  165.0 29.9 %attend_96.1 = (bf16[96,2048]{1,0:T(8,128)(2,1)}, bf16[96,2048]{1,0:T(8,128)(2,1)}, bf16[32,96,128]{2,1,0:T(8,128)(2,1)}, bf16[768,128]{1,0:T(8,128)(2,1)}, f32[...) custom-call(f32[128,2048]{1,0:T(8,128)} %get-tuple-element.95.refs_0_, ...), custom_call_target="tpu_custom_call" | custom-call | flops 4000000000 | bytes 10000000 | tf_op jit(solution)/shard_map/attend_96/pallas_call | solution.py:242
  195.0 34.1 %feed_96.1 = (bf16[96,2048]{1,0:T(8,128)(2,1)}, bf16[96,2048]{1,0:T(8,128)(2,1)}, bf16[96,2048]{1,0:T(8,128)(2,1)}, f32[96,2816]{1,0:T(8,128)}, f32[128,2048]{1,0:T(8,128)}) custom-call(f32[128,2048]{1,0:T(8,128)} %get-tuple-element.95.refs_0_, bf16[96,2048]{1,0:T(8,128)(2,1)} %get-tuple-element.96.refs_1_.refs_7_.refs_3_, ...), custom_call_target="tpu_custom_call" | custom-call | flops 5000000000 | bytes 100000000 | tf_op jit(solution)/shard_map/feed_96/pallas_call | solution.py:466
  229.2 0.6 fusion.3.refs_1_.refs_3_.refs_7_.refs_6_
  229.9 1.3 broadcast_in_dim.97.refs_2_.refs_0_
  231.2 0.7 broadcast_in_dim_tile.11.refs_3_.refs_1_
  232.2 0.7 concatenate.56.refs_5_.refs_7_
  233.1 0.7 concatenate.58.refs_6_.refs_8_
  233.8 24.1 %attend_64.1 = (bf16[64,2048]{1,0:T(8,128)(2,1)}, bf16[64,2048]{1,0:T(8,128)(2,1)}, bf16[32,64,128]{2,1,0:T(8,128)(2,1)}, bf16[512,128]{1,0:T(8,128)(2,1)}, f32[...) custom-call(f32[128,2048]{1,0:T(8,128)} %get-tuple-element.98.refs_0_, ...), custom_call_target="tpu_custom_call" | custom-call | flops 4000000000 | bytes 10000000 | tf_op jit(solution)/shard_map/attend_64/pallas_call | solution.py:242
  257.8 27.5 %feed_64.1 = (bf16[64,2048]{1,0:T(8,128)(2,1)}, bf16[64,2048]{1,0:T(8,128)(2,1)}, bf16[64,2048]{1,0:T(8,128)(2,1)}, f32[64,2816]{1,0:T(8,128)}, f32[128,2048]{1,0:T(8,128)}) custom-call(f32[128,2048]{1,0:T(8,128)} %get-tuple-element.98.refs_0_, bf16[64,2048]{1,0:T(8,128)(2,1)} %get-tuple-element.99.refs_1_.refs_2_.refs_3_, ...), custom_call_target="tpu_custom_call" | custom-call | flops 5000000000 | bytes 100000000 | tf_op jit(solution)/shard_map/feed_64/pallas_call | solution.py:466
  285.4 21.1 %feed_back_0_64.1 = (bf16[64,2048]{1,0:T(8,128)(2,1)}, f32[64,2048]{1,0:T(8,128)}, f32[64,1]{1,0:T(8,128)}, bf16[64,512]{1,0:T(8,128)(2,1)}, bf16[64,2816]{1,0:T...) custom-call(f32[128,2048]{1,0:T(8,128)} %refs_0_.7, ...), custom_call_target="tpu_custom_call" | custom-call | flops 5000000000 | bytes 100000000 | tf_op jit(solution)/shard_map/feed_back_0_64/pallas_call | solution.py:654
  306.5 18.3 %attend_back_64.1.refs_2_.refs_23_ = bf16[64,640]{1,0:T(8,128)(2,1)} custom-call(s32[2048,128]{1,0:T(8,128)} %broadcast_in_dim.97.refs_2_.refs_0_, s32[1,512]{1,0:T(1,128)} %broadcast_in_dim_tile.11.refs_3_.refs_1_, bf16[512,128]{1,0:T(8,128)(2,1)} %get-tuple-element.102.refs_2_, bf16[32,64,128]{2,1,0:T(8,128)(2,1)} %get-tuple-element.103.refs_3_, ...), custom_call_target="tpu_custom_call" | custom-call | flops 10000000000 | bytes 10000000 | tf_op jit(solution)/shard_map/attend_back_64/pallas_call | solution.py:373
  324.8 37.9 %feed_back_64_96.1 = (f32[128,2048]{1,0:T(8,128)}, f32[1,2048]{1,0:T(1,128)}, f32[1,2048]{1,0:T(1,128)}, bf16[96,2048]{1,0:T(8,128)(2,1)}, f32[96,2048]{1,0:T(8,...) custom-call(f32[128,2048]{1,0:T(8,128)} %refs_0_.7, ...), custom_call_target="tpu_custom_call" | custom-call | flops 5000000000 | bytes 100000000 | tf_op jit(solution)/shard_map/feed_back_64_96/pallas_call | solution.py:654
  362.7 18.6 %attend_back_96.1.refs_2_.refs_15_ = bf16[96,640]{1,0:T(8,128)(2,1)} custom-call(s32[3072,128]{1,0:T(8,128)} %broadcast_in_dim.93.refs_2_.refs_0_, s32[1,768]{1,0:T(1,128)} %broadcast_in_dim_tile.10.refs_3_.refs_1_, bf16[768,128]{1,0:T(8,128)(2,1)} %get-tuple-element.118.refs_2_, bf16[32,96,128]{2,1,0:T(8,128)(2,1)} %get-tuple-element.119.refs_3_, ...), custom_call_target="tpu_custom_call" | custom-call | flops 10000000000 | bytes 10000000 | tf_op jit(solution)/shard_map/attend_back_96/pallas_call | solution.py:373
  381.3 46.4 %feed_back_96_128.1 = (f32[128,2048]{1,0:T(8,128)}, f32[1,2048]{1,0:T(1,128)}, f32[1,2048]{1,0:T(1,128)}, bf16[128,2048]{1,0:T(8,128)(2,1)}, f32[128,2048]{1,0:T...) custom-call(f32[128,2048]{1,0:T(8,128)} %get-tuple-element.117.refs_, ...), custom_call_target="tpu_custom_call" | custom-call | flops 5000000000 | bytes 100000000 | tf_op jit(solution)/shard_map/feed_back_96_128/pallas_call | solution.py:654
  427.7 21.9 %attend_back_128.1.refs_2_.refs_7_ = bf16[128,640]{1,0:T(8,128)(2,1)} custom-call(s32[1,1024]{1,0:T(1,128)} %bitcast.40, bf16[1024,128]{1,0:T(8,128)(2,1)} %get-tuple-element.130.refs_1_, bf16[32,128,128]{2,1,0:T(8,128)(2,1)} %get-tuple-element.131.refs_2_, f32[128,1024]{1,0:T(8,128)} %get-tuple-element.132.refs_3_, f32[1,1024]{1,0:T(1,128)} %get-tuple-element.133.refs_4_, ...), custom_call_target="tpu_custom_call" | custom-call | flops 10000000000 | bytes 10000000 | tf_op jit(solution)/shard_map/attend_back_128/pallas_call | solution.py:373
  449.6 22.7 %feed_back_128_0.1 = (f32[128,2048]{1,0:T(8,128)}, f32[1,2048]{1,0:T(1,128)}, f32[1,2048]{1,0:T(1,128)}) custom-call(f32[128,2048]{1,0:T(8,128)} %get-tuple-element.129.refs_0_, f32[8,2048]{1,0:T(8,128)} %get-tuple-element.91.refs_2_.refs_3_.refs_4_.refs_1_, bf16[128,640]{1,0:T(8,128)(2,1)} %attend_back_128.1.refs_2_.refs_7_, ...), custom_call_target="tpu_custom_call" | custom-call | flops 5000000000 | bytes 100000000 | tf_op jit(solution)/shard_map/feed_back_128_0/pallas_call | solution.py:654
  472.4 0.7 add_add_fusion
  473.1 0.7 add_add_fusion.2
  473.9 1.1 maximum_maximum_fusion.refs_24_
  475.0 99.6 %collect.1 = (f32[64,512]{1,0:T(8,128)}, f32[64,64]{1,0:T(8,128)}, f32[64,64]{1,0:T(8,128)}, f32[512,64]{1,0:T(8,128)}, f32[64,1408]{1,0:T(8,128)}, /*index=5*/f...) custom-call(bf16[128,2048]{1,0:T(8,128)(2,1)} %get-tuple-element.127.refs_10_.refs_0_, ...), custom_call_target="tpu_custom_call" | custom-call | tf_op jit(solution)/shard_map/collect/pallas_call | solution.py:1037
  574.6 1.8 copy.51
  576.4 2.2 copy.52
  578.6 1.6 slice_reduce_fusion
  580.2 1.0 copy.60
  581.3 1.0 copy.61
  582.2 0.7 copy.62
  582.9 0.6 copy.63
  584.1 0.7 copy.65
  584.9 0.7 copy.66
  (80 shorter events, 3.8 us)
Async XLA Ops:
  117.3 41.9 %copy-start.15 = (s32[128]{0:T(128)S(1)}, s32[128]{0:T(128)}, u32[]{:S(2)}) copy-start(s32[128]{0:T(128)} %param.17) | copy-start | bytes 1540
  117.3 42.6 %copy-start = (f32[8,2048]{1,0:T(8,128)S(1)}, f32[8,2048]{1,0:T(8,128)}, u32[]{:S(2)}) copy-start(f32[8,2048]{1,0:T(8,128)} %get-tuple-element.91.refs_2_.refs_3_.refs_4_.refs_1_) | copy-start | bytes 196612
  195.0 34.2 %copy-start.16 = (s32[128]{0:T(128)S(1)}, s32[128]{0:T(128)}, u32[]{:S(2)}) copy-start(s32[128]{0:T(128)} %param.18) | copy-start | bytes 1540
  449.5 22.8 %copy-start.11 = (f32[1,2048]{1,0:T(1,128)S(1)}, f32[1,2048]{1,0:T(1,128)}, u32[]{:S(2)}) copy-start(f32[1,2048]{1,0:T(1,128)} %get-tuple-element.159) | copy-start | bytes 24580
  449.6 22.8 %copy-start.14 = (f32[1,2048]{1,0:T(1,128)S(1)}, f32[1,2048]{1,0:T(1,128)}, u32[]{:S(2)}) copy-start(f32[1,2048]{1,0:T(1,128)} %get-tuple-element.160) | copy-start | bytes 24580
  449.6 23.5 %copy-start.8 = (f32[1,2048]{1,0:T(1,128)S(1)}, f32[1,2048]{1,0:T(1,128)}, u32[]{:S(2)}) copy-start(f32[1,2048]{1,0:T(1,128)} %get-tuple-element.156) | copy-start | bytes 24580
  449.6 23.5 %copy-start.10 = (f32[1,2048]{1,0:T(1,128)S(1)}, f32[1,2048]{1,0:T(1,128)}, u32[]{:S(2)}) copy-start(f32[1,2048]{1,0:T(1,128)} %get-tuple-element.157) | copy-start | bytes 24580
  449.6 23.5 %copy-start.13 = (f32[1,2048]{1,0:T(1,128)S(1)}, f32[1,2048]{1,0:T(1,128)}, u32[]{:S(2)}) copy-start(f32[1,2048]{1,0:T(1,128)} %get-tuple-element.158) | copy-start | bytes 24580
  449.6 23.5 %copy-start.9 = (f32[1,2048]{1,0:T(1,128)S(1)}, f32[1,2048]{1,0:T(1,128)}, u32[]{:S(2)}) copy-start(f32[1,2048]{1,0:T(1,128)} %get-tuple-element.153) | copy-start | bytes 24580
  449.6 23.5 %copy-start.12 = (f32[1,2048]{1,0:T(1,128)S(1)}, f32[1,2048]{1,0:T(1,128)}, u32[]{:S(2)}) copy-start(f32[1,2048]{1,0:T(1,128)} %get-tuple-element.154) | copy-start | bytes 24580
  574.6 5.6 copy-start.1
  576.4 4.8 copy-start.2
  581.2 1.0 copy-start.5
  581.2 1.7 copy-start.7
  581.2 2.3 copy-start.6
  581.2 2.9 copy-start.4
  581.2 3.6 copy-start.3

commit v4 on v3

--- a/solution.py
+++ b/solution.py
@@ -832,191 +832,398 @@
     )(w_query, w_key, w_value, w_out, w_gate, w_up, w_down, extras)
 
 
-SLOTS = 4
+SLOTS = 6
 GROUP = 512
 
 
-def collect_kernel(levels, spans, groups, *refs):
-    refs = list(refs)
-    sources = [[refs.pop(0) for _ in range(8)] for _ in levels]
-    vectors = refs.pop(0)
-    q_out, k_out, v_out, out_out, gate_out, up_out, down_out, vec_out = [refs.pop(0) for _ in range(8)]
-    lefts, turned, rights, final, slots, core_recv, relay_recv, first_recv, mid, last_recv, loads, send_sems, recv_sems = refs
-    me = lax.axis_index("dp")
-    x, y, core = plane(me)
-    copies = []
-    row = 0
-    for level, count in enumerate(levels):
-        for s in range(4):
-            low, high = spans[s]
-            for side, ref in enumerate((lefts.at[s, row : row + count], rights.at[row : row + count, low:high])):
-                copy = pltpu.make_async_copy(sources[level][2 * s + side], ref, loads.at[level, 2 * s + side])
-                copy.start()
-                copies.append(copy)
-        row += count
-    meet(me, plane_partners(x, y, core))
-    for copy in copies:
-        copy.wait()
-    started = []
-
-    def remote(g, index, source, target, device):
+class Collect:
+    def __init__(self, spans, groups, x, y, core, turned, rights, vectors, store, slots, core_recv, relay_recv, first_recv, last_recv, send_sems, recv_sems, turn):
+        self.spans, self.groups = spans, groups
+        self.x, self.y, self.core = x, y, core
+        self.turned, self.rights, self.vectors, self.store, self.slots = turned, rights, vectors, store, slots
+        self.core_recv, self.relay_recv, self.first_recv = core_recv, relay_recv, first_recv
+        self.last_recv = last_recv
+        self.send_sems, self.recv_sems = send_sems, recv_sems
+        self.turn = turn
+        self.waits = [{} for _ in groups]
+        self.done = set()
+
+    def remote(self, g, index, source, target, device):
         copy = pltpu.make_async_remote_copy(
-            src_ref=source, dst_ref=target, send_sem=send_sems.at[g, index],
-            recv_sem=recv_sems.at[g, index], device_id=device, device_id_type=MESH,
+            src_ref=source, dst_ref=target, send_sem=self.send_sems.at[g, index],
+            recv_sem=self.recv_sems.at[g, index], device_id=device, device_id_type=MESH,
         )
         copy.start()
         return copy
 
-    waits = [{} for _ in groups]
-    done = set()
-
-    def held(slot, axis, at, first, count):
+    def held(self, slot, axis, at, first, count):
         if axis == 0:
-            return slots.at[slot, at, pl.ds(first, count), core]
-        return slots.at[slot, pl.ds(first, count), at, core]
-
-    def zero(g):
-        slot = g % SLOTS
+            return self.slots.at[slot, at, pl.ds(first, count), self.core]
+        return self.slots.at[slot, pl.ds(first, count), at, self.core]
+
+    def zero(self, g):
+        slot, waits = g % SLOTS, self.waits
         if g >= SLOTS:
-            for copy in waits[g - SLOTS][0] + waits[g - SLOTS][1] + waits[g - SLOTS][2]:
-                copy.wait_send()
+            for stage in range(3):
+                for copy in waits[g - SLOTS][stage]:
+                    copy.wait_send()
         column = 0
-        for section, low, high in groups[g][1]:
+        for section, low, high in self.groups[g][1]:
             wide = high - low
             if section < 4:
-                if section not in done:
-                    done.add(section)
-                    turned[section] = lefts[section].T
-                base = spans[section][0]
+                if section not in self.done:
+                    self.done.add(section)
+                    self.turn(section)
+                base = self.spans[section][0]
 
             def rows_of(m, carry, section=section, low=low, high=high, column=column, wide=wide):
-                start = pl.multiple_of(m * 256, 256)
+                start = pl.multiple_of(m * 1024, 1024)
                 if section < 4:
-                    value = dot_nn(turned[section, pl.ds(start, 256), :], rights[:, base + low : base + high])
+                    value = dot_nn(
+                        self.turned[section % 2, pl.ds(start, 1024), :], self.rights[:, base + low : base + high]
+                    )
                 else:
-                    value = vectors[:, pl.ds(start, 256)].T
-                slots[slot, m // 2, pl.ds(lax.rem(m, 2) * 2, 2), :, :, column : column + wide] = (
-                    value.astype(BF).reshape(2, 2, 64, wide)
+                    value = self.vectors[:, pl.ds(start, 1024)].T
+                self.slots[slot, pl.ds(m * 2, 2), :, :, :, column : column + wide] = (
+                    value.astype(BF).reshape(2, 4, 2, 64, wide)
                 )
                 return carry
 
-            lax.fori_loop(0, 8, rows_of, 0)
+            lax.fori_loop(0, 2, rows_of, 0)
             column += wide
         waits[g][0] = [
-            remote(g, 0, slots.at[slot, :, :, 1 - core, :, :column], core_recv.at[g, :, :, :, :column], peer(x, y, 1 - core))
+            self.remote(
+                g, 0, self.slots.at[slot, :, :, 1 - self.core, :, :column],
+                self.core_recv.at[g, :, :, :, :column], peer(self.x, self.y, 1 - self.core),
+            )
         ]
 
-    def first(g):
-        slot, (width, _, axis) = g % SLOTS, groups[g]
+    def first(self, g):
+        slot, (width, _, axis) = g % SLOTS, self.groups[g]
+        waits, slots = self.waits, self.slots
         waits[g][0][0].wait_recv()
 
         def add(i, carry):
-            a, b = i // 4, lax.rem(i, 4)
-            slots[slot, a, b, core, :, :width] = (
-                slots[slot, a, b, core, :, :width].astype(F32) + core_recv[g, a, b, :, :width].astype(F32)
-            ).astype(BF)
+            slots[slot, i, :, self.core, :, :width] = (
+                slots[slot, i, :, self.core, :, :width] + self.core_recv[g, i, :, :, :width]
+            )
             return carry
 
-        lax.fori_loop(0, 16, add, 0)
-        at = x if axis == 0 else y
+        lax.fori_loop(0, 4, add, 0)
+        at = self.x if axis == 0 else self.y
         waits[g][1] = [
-            remote(
-                g, 1 + i, held(slot, axis, lax.rem(at + 2, 4), 2 * i, 2).at[:, :, :width],
-                relay_recv.at[g, i, :, :, :width], shifted(x, y, core, axis, k),
+            self.remote(
+                g, 1 + i, self.held(slot, axis, lax.rem(at + 2, 4), 2 * i, 2).at[:, :, :width],
+                self.relay_recv.at[g, i, :, :, :width], shifted(self.x, self.y, self.core, axis, k),
             )
             for i, k in enumerate((1, 3))
         ]
 
-    def second(g):
-        slot, (width, _, axis) = g % SLOTS, groups[g]
-        at = x if axis == 0 else y
+    def second(self, g):
+        slot, (width, _, axis) = g % SLOTS, self.groups[g]
+        waits, slots = self.waits, self.slots
+        at = self.x if axis == 0 else self.y
         waits[g][2] = []
         for i, k in enumerate((1, 3)):
             waits[g][1][i].wait_recv()
             there = lax.rem(at + k, 4)
             for j in range(2):
                 b = 2 * i + j
-                where = (slot, there, b, core) if axis == 0 else (slot, b, there, core)
-                slots[where + (slice(None), slice(0, width))] = (
-                    slots[where + (slice(None), slice(0, width))].astype(F32)
-                    + relay_recv[g, i, j, :, :width].astype(F32)
-                ).astype(BF)
+                where = (slot, there, b, self.core) if axis == 0 else (slot, b, there, self.core)
+                where = where + (slice(None), slice(0, width))
+                slots[where] = slots[where] + self.relay_recv[g, i, j, :, :width]
             waits[g][2].append(
-                remote(
-                    g, 3 + i, held(slot, axis, there, 0, 4).at[:, :, :width],
-                    first_recv.at[g, i, :, :, :width], shifted(x, y, core, axis, k),
+                self.remote(
+                    g, 3 + i, self.held(slot, axis, there, 0, 4).at[:, :, :width],
+                    self.first_recv.at[g, i, :, :, :width], shifted(self.x, self.y, self.core, axis, k),
                 )
             )
 
-    def third(g):
-        slot, (width, _, axis) = g % SLOTS, groups[g]
-        at, other = (x, y) if axis == 0 else (y, x)
+    def third(self, g):
+        slot, (width, _, axis) = g % SLOTS, self.groups[g]
+        waits, slots = self.waits, self.slots
+        at, other = (self.x, self.y) if axis == 0 else (self.y, self.x)
         for copy in waits[g][2]:
             copy.wait_recv()
         for b in range(4):
-            where = (slot, at, b, core) if axis == 0 else (slot, b, at, core)
-            mid[g, b, :, :width] = (
+            where = (slot, at, b, self.core) if axis == 0 else (slot, b, at, self.core)
+            self.core_recv[g, 0, b, :, :width] = (
                 slots[where + (slice(None), slice(0, width))].astype(F32)
-                + first_recv[g, 0, b, :, :width].astype(F32)
-                + first_recv[g, 1, b, :, :width].astype(F32)
+                + self.first_recv[g, 0, b, :, :width].astype(F32)
+                + self.first_recv[g, 1, b, :, :width].astype(F32)
             ).astype(BF)
         waits[g][3] = [
-            remote(
-                g, 4 + k, mid.at[g, lax.rem(other + k, 4), :, :width], last_recv.at[g, k - 1, :, :width],
-                shifted(x, y, core, 1 - axis, k),
+            self.remote(
+                g, 4 + k, self.core_recv.at[g, 0, lax.rem(other + k, 4), :, :width],
+                self.last_recv.at[g, k - 1, :, :width],
+                shifted(self.x, self.y, self.core, 1 - axis, k),
             )
             for k in (2, 1, 3)
         ]
 
-    def fourth(g):
-        width, pieces, axis = groups[g]
-        other = y if axis == 0 else x
-        value = mid[g, other, :, :width].astype(F32)
-        for i, copy in enumerate(waits[g][3]):
+    def fourth(self, g):
+        width, pieces, axis = self.groups[g]
+        other = self.y if axis == 0 else self.x
+        value = self.core_recv[g, 0, other, :, :width].astype(F32)
+        for copy in self.waits[g][3]:
             copy.wait_recv()
         for k in range(3):
-            value = value + last_recv[g, k, :, :width].astype(F32)
+            value = value + self.last_recv[g, k, :, :width].astype(F32)
         column = 0
         for section, low, high in pieces:
-            base = spans[section][0]
-            final[:, base + low : base + high] = value[:, column : column + high - low]
+            self.store(section, low, value[:, column : column + high - low])
             column += high - low
 
-    count = len(groups)
-    for i in range(count + 4):
-        for stage, step in enumerate((zero, first, second, third, fourth)):
-            if 0 <= i - stage < count:
-                step(i - stage)
+    def step(self, i):
+        for back, work in ((0, self.zero), (1, self.first), (3, self.second), (5, self.third), (6, self.fourth)):
+            if 0 <= i - back < len(self.groups):
+                work(i - back)
+
+    def drain(self):
+        count = len(self.groups)
+        for g in range(count):
+            for stage in range(4):
+                if stage == 3 or g >= count - SLOTS:
+                    for copy in self.waits[g][stage]:
+                        copy.wait_send()
+
+
+def finish_kernel(n, heads, devices, mp, group, levels, spans, groups, *refs):
+    refs = list(refs)
+    flow, gains, query_place, query, packed, mixed_t, log_total, grad_mixed, cosine, sine = [refs.pop(0) for _ in range(10)]
+    rows_in, middle, logit, second_vecs, first_vecs, router_vecs = [refs.pop(0) for _ in range(6)]
+    w_hbm = refs.pop(0)
+    sources = [[refs.pop(0) for _ in range(8 if level else 7)] for level in range(len(levels))]
+    flow_out, q_out, k_out, v_out, out_out, gate_out, up_out, down_out, vec_out = [refs.pop(0) for _ in range(9)]
+    query_t, grad_rows, grad_t, acc, delta, send_buf, recv_buf, kv_send, kv_recv = [refs.pop(0) for _ in range(9)]
+    w_qkv, w_sem, send_a, recv_a, full_a, sems_a = [refs.pop(0) for _ in range(6)]
+    (lefts, turned, rights, vectors, slots, core_recv, relay_recv, first_recv, last_recv,
+     loads, send_sems, recv_sems) = refs
+    me, mp_me = lax.axis_index("dp"), lax.axis_index("mp")
+    x, y, core = plane(me)
+    load_w = pltpu.make_async_copy(w_hbm.at[:, : w_qkv.shape[1]], w_qkv, w_sem)
+    load_w.start()
+    fetches = [[] for _ in range(4)]
+
+    def fetch(s, side):
+        row = 0
+        for level, count in enumerate(levels):
+            low, high = spans[s]
+            target = (lefts.at[s % 2, row : row + count], rights.at[row : row + count, low:high])[side]
+            if 2 * s + side < len(sources[level]):
+                copy = pltpu.make_async_copy(
+                    sources[level][2 * s + side], target, loads.at[level, 2 * s + side]
+                )
+                copy.start()
+                fetches[s].append(copy)
+            row += count
+
+    for s in range(4):
+        if s < 2:
+            fetch(s, 0)
+        fetch(s, 1)
+
+    barrier = pltpu.get_barrier_semaphore()
+
+    def greet(k, carry):
+        pl.semaphore_signal(
+            barrier, inc=1, device_id={"dp": lax.rem(me + k, devices)}, device_id_type=MESH
+        )
+        return carry
+
+    lax.fori_loop(1, devices, greet, 0)
+    for k in range(1, mp):
+        pl.semaphore_signal(
+            barrier, inc=1, device_id={"mp": lax.rem(mp_me + k, mp)}, device_id_type=MESH
+        )
+
+    def turn(section):
+        for copy in fetches[section]:
+            copy.wait()
+        turned[section % 2] = lefts[section % 2].T
+        if section < 2:
+            fetch(section + 2, 0)
+
     hidden = gate_out.shape[1]
     mix = q_out.shape[1]
-    gate_out[...] = final[:, :hidden]
-    up_out[...] = final[:, hidden : 2 * hidden]
-    down_out[...] = final[:, spans[1][0] : spans[1][1]].T
-    out_out[...] = final[:, spans[2][0] : spans[2][1]].T
+
+    def store(section, low, value):
+        high = low + value.shape[1]
+        if section == 0:
+            middle_cut = min(max(hidden - low, 0), high - low)
+            if middle_cut:
+                gate_out[:, low : low + middle_cut] = value[:, :middle_cut]
+            if low + middle_cut < high:
+                up_out[:, low + middle_cut - hidden : high - hidden] = value[:, middle_cut:]
+        elif section == 1:
+            down_out[low:high, :] = value.T
+        elif section == 2:
+            out_out[low:high, :] = value.T
+        elif section == 3:
+            if low < mix:
+                q_out[:, low : min(high, mix)] = value[:, : min(high, mix) - low]
+            if high > mix:
+                k_out[...] = value[:, mix - low : mix - low + HD]
+                v_out[...] = value[:, mix - low + HD :]
+        else:
+            vec_out[...] = value
+
+    work = Collect(
+        spans, groups, x, y, core, turned, rights, vectors, store, slots, core_recv, relay_recv,
+        first_recv, last_recv, send_sems, recv_sems, turn,
+    )
+    left = lanes_of((n, LANES)) < HD
+    for t in range(heads // 2):
+        part = grad_mixed[:, t * LANES : (t + 1) * LANES].astype(F32)
+        grad_rows[2 * t * n : (2 * t + 1) * n, :] = jnp.where(
+            left, 0.0, pltpu.roll(part, HD, 1)
+        ).astype(BF)
+        grad_rows[(2 * t + 1) * n : (2 * t + 2) * n, :] = jnp.where(left, 0.0, part).astype(BF)
+    query_t[...] = query[...].T
+    grad_t[...] = grad_rows[...].T
+    delta[...] = jnp.sum(grad_t[...].astype(F32) * mixed_t[...], axis=0, keepdims=True)
+    acc[...] = jnp.zeros(acc.shape, F32)
+    width = heads * n
+    pl.semaphore_wait(barrier, devices - 1 + mp - 1)
+
+    def send_copy(e, source_index):
+        return pltpu.make_async_remote_copy(
+            src_ref=send_buf.at[e], dst_ref=recv_buf.at[source_index],
+            send_sem=kv_send.at[e], recv_sem=kv_recv.at[source_index],
+            device_id={"dp": e}, device_id_type=MESH,
+        )
+
+    def one_block(b):
+        part = packed[b * group : (b + 1) * group].reshape(group * n, 2 * HD)
+        scores = dot_nn(part, query_t[...])
+        place = lax.broadcasted_iota(jnp.int32, (group * n, LANES), 0) + b * (group * n)
+        place = jnp.concatenate([place] * (width // LANES), axis=1)
+        scores = jnp.where(place <= query_place[...], scores, NEG)
+        weights = jnp.exp(scores - log_total[...])
+        grad_weights = dot_nn(part, grad_t[...])
+        grad_scores = (weights * (grad_weights - delta[...])).astype(BF)
+        grad_part = dot_nn(grad_scores, query[...]) + dot_nn(weights.astype(BF), grad_rows[...])
+        send_buf[b * group : (b + 1) * group] = grad_part.astype(BF).reshape(group, n, 2 * HD)
+        acc[...] += dot_tn(part, grad_scores)
+        for e in range(b * group, (b + 1) * group):
+
+            @pl.when(e < me)
+            def _(e=e):
+                send_copy(e, me).start()
+
+    blocks = devices // group
+    for b in range(blocks):
+        work.step(b)
+
+        @pl.when(b * group <= me)
+        def _(b=b):
+            one_block(b)
+
+    grad_query = acc[...].T * HD**-0.5
+    outs = []
+    for t in range(heads // 2):
+        even = grad_query[2 * t * n : (2 * t + 1) * n, :]
+        odd = grad_query[(2 * t + 1) * n : (2 * t + 2) * n, :]
+        outs.append(jnp.where(left, even, pltpu.roll(odd, HD, 1)))
+
+    def add(e, carry):
+        send_copy(me, e).wait_recv()
+        return carry + recv_buf[e].astype(F32)
+
+    outs.append(lax.fori_loop(me + 1, devices, add, send_buf[me].astype(F32)))
     low = spans[3][0]
-    q_out[...] = final[:, low : low + mix]
-    k_out[...] = final[:, low + mix : low + mix + HD]
-    v_out[...] = final[:, low + mix + HD : low + mix + 2 * HD]
-    vec_out[...] = final[:, spans[4][0] : spans[4][1]]
-    for g in range(count):
-        for stage in range(4):
-            if stage == 3 or g >= count - SLOTS:
-                for copy in waits[g][stage]:
-                    copy.wait_send()
-
-
-def collect(levels, vectors, depth, ident):
-    widths = [levels[0][i].shape[1] for i in (1, 3, 5, 7)] + [LANES]
+    for t, part in enumerate(outs):
+        cut = slice(t * LANES, (t + 1) * LANES)
+        rights[0:n, low + t * LANES : low + (t + 1) * LANES] = (
+            part * cosine[:, cut] - swap_halves(part) * sine[:, cut]
+        ).astype(BF)
+    load_w.wait()
+    grad_now = rights[0:n, low : spans[3][1]]
+    chunk = w_qkv.shape[0] // mp
+
+    def first_chunk(c):
+        return dot_nt(grad_now, w_qkv[pl.ds(pl.multiple_of(c * chunk, chunk), chunk), :])
+
+    total = Sum(mp, mp_me, send_a, recv_a, full_a, sems_a)
+    total.start(first_chunk)
+    work.step(blocks)
+    total.middle()
+    work.step(blocks + 1)
+    grad_normed = total.finish().astype(F32)
+    level = rows_in[...].astype(F32)
+    unit, factor = unit_of(level)
+    vectors[...] = jnp.zeros(vectors.shape, F32)
+    vectors[0:1, :] = jnp.sum(grad_normed * unit, axis=0, keepdims=True) + first_vecs[0:1, :] + first_vecs[1:2, :]
+    vectors[1:2, :] = second_vecs[0:1, :] + second_vecs[1:2, :] + second_vecs[2:3, :]
+    vectors[2:3, :] = jnp.sum(level * logit[...], axis=0, keepdims=True) + router_vecs[0:1, :] + router_vecs[1:2, :]
+    flow_out[...] = flow[...] + (
+        unit_back(grad_normed * gains[0:1, :], unit, factor) + middle[...] + logit[...] * gains[2:3, :]
+    ).astype(BF).astype(F32)
+    for i in range(blocks + 2, len(groups) + 6):
+        work.step(i)
+    work.drain()
+    total.drain()
+
+    def sent(e, carry):
+        send_copy(e, me).wait_send()
+        return carry
+
+    lax.fori_loop(0, me, sent, 0)
+
+
+class Sum:
+    order = (2, 1, 3)
+
+    def __init__(self, group, me, send, recv, full, sems):
+        self.group, self.me, self.send, self.recv, self.full, self.sems = group, me, send, recv, full, sems
+
+    def remote(self, source, target, stage, k):
+        copy = pltpu.make_async_remote_copy(
+            src_ref=source, dst_ref=target, send_sem=self.sems.at[stage, k - 1],
+            recv_sem=self.sems.at[stage + 1, k - 1],
+            device_id={"mp": lax.rem(self.me + k, self.group)}, device_id_type=MESH,
+        )
+        copy.start()
+        return copy
+
+    def start(self, make_chunk):
+        self.out = []
+        for k in self.order:
+            self.send[k - 1] = make_chunk(lax.rem(self.me + k, self.group)).astype(BF)
+            self.out.append(self.remote(self.send.at[k - 1], self.recv.at[k - 1], 0, k))
+        self.own = make_chunk(self.me).astype(BF).astype(F32)
+
+    def middle(self):
+        total = self.own
+        for k, copy in zip(self.order, self.out):
+            copy.wait_recv()
+            total = total + self.recv[k - 1].astype(F32)
+        self.full[self.me] = total.astype(BF)
+        self.back = [self.remote(self.full.at[self.me], self.full.at[self.me], 2, k) for k in self.order]
+
+    def finish(self):
+        for copy in self.back:
+            copy.wait_recv()
+        return jnp.concatenate([self.full[c] for c in range(self.group)], axis=1)
+
+    def drain(self):
+        for copy in self.out + self.back:
+            copy.wait_send()
+
+
+def finish(flow, gains, attention, tail, vecs, weights, levels, heads, devices, mp, depth, ident):
+    n, model = levels[0][0].shape
+    width = heads * n
+    group = 512 // n
+    mix = heads * HD
+    widths = [levels[1][i].shape[1] for i in (1, 3, 5, 7)] + [LANES]
     spans, total = [], 0
-    for width in widths:
-        spans.append((total, total + width))
-        total += width
+    for wide in widths:
+        spans.append((total, total + wide))
+        total += wide
     pieces = []
-    for section, width in enumerate(widths):
-        low = 0
-        while low < width:
-            pieces.append((section, low, low + LANES))
-            low += LANES
+    for section, wide in enumerate(widths):
+        pieces += [(section, low, low + LANES) for low in range(0, wide, LANES)]
     groups = []
     per = GROUP // LANES
     for index in range(0, len(pieces), per):
@@ -1026,17 +1233,18 @@
                 merged[-1] = (section, merged[-1][1], high)
             else:
                 merged.append((section, low, high))
-        width = sum(high - low for _, low, high in merged)
-        groups.append((width, merged, (index // per) % 2))
+        wide = sum(high - low for _, low, high in merged)
+        groups.append((wide, merged, (index // per) % 2))
     counts = [level[0].shape[0] for level in levels]
     rows = sum(counts)
-    model = levels[0][0].shape[1]
-    hidden, mix = widths[1], widths[2]
+    hidden = widths[1]
     many = len(groups)
-    args = [item for level in levels for item in level] + [vectors]
+    whole = [flow, gains, *attention, *tail, *vecs]
+    args = whole + [weights] + [item for level in levels for item in level]
     return pl.pallas_call(
-        functools.partial(collect_kernel, counts, spans, groups),
+        functools.partial(finish_kernel, n, heads, devices, mp, group, counts, spans, groups),
         out_shape=(
+            jax.ShapeDtypeStruct(flow.shape, F32),
             jax.ShapeDtypeStruct((depth, mix), F32),
             jax.ShapeDtypeStruct((depth, HD), F32),
             jax.ShapeDtypeStruct((depth, HD), F32),
@@ -1046,27 +1254,38 @@
             jax.ShapeDtypeStruct((hidden, depth), F32),
             jax.ShapeDtypeStruct((depth, LANES), F32),
         ),
-        in_specs=[pl.BlockSpec(memory_space=pl.ANY)] * (len(args) - 1) + vmem(1),
-        out_specs=tuple(vmem(8)),
+        in_specs=vmem(len(whole)) + [pl.BlockSpec(memory_space=pl.ANY)] * (len(args) - len(whole)),
+        out_specs=tuple(vmem(9)),
         scratch_shapes=[
-            pltpu.VMEM((4, rows, model), BF),
-            pltpu.VMEM((4, model, rows), BF),
+            pltpu.VMEM((2 * HD, width), BF),
+            pltpu.VMEM((width, 2 * HD), BF),
+            pltpu.VMEM((2 * HD, width), BF),
+            pltpu.VMEM((2 * HD, width), F32),
+            pltpu.VMEM((1, width), F32),
+            pltpu.VMEM((devices, n, 2 * HD), BF),
+            pltpu.VMEM((devices, n, 2 * HD), BF),
+            pltpu.SemaphoreType.DMA((devices,)),
+            pltpu.SemaphoreType.DMA((devices,)),
+            pltpu.VMEM((model, mix + 2 * HD), BF),
+            pltpu.SemaphoreType.DMA(()),
+            *sum_scratch(mp, n, model),
+            pltpu.VMEM((2, rows, model), BF),
+            pltpu.VMEM((2, model, rows), BF),
             pltpu.VMEM((rows, spans[3][1]), BF),
-            pltpu.VMEM((depth, total), F32),
+            pltpu.VMEM((LANES, model), F32),
             pltpu.VMEM((SLOTS, 4, 4, 2, depth, GROUP), BF),
             pltpu.VMEM((many, 4, 4, depth, GROUP), BF),
             pltpu.VMEM((many, 2, 2, depth, GROUP), BF),
             pltpu.VMEM((many, 2, 4, depth, GROUP), BF),
-            pltpu.VMEM((many, 4, depth, GROUP), BF),
             pltpu.VMEM((many, 3, depth, GROUP), BF),
             pltpu.SemaphoreType.DMA((len(levels), 8)),
             pltpu.SemaphoreType.DMA((many, 8)),
             pltpu.SemaphoreType.DMA((many, 8)),
         ],
         compiler_params=pltpu.CompilerParams(
-            collective_id=ident, has_side_effects=True, vmem_limit_bytes=VMEM_LIMIT
+            collective_id=ident, has_side_effects=True, vmem_limit_bytes=63 * 1024 * 1024
         ),
-        name="collect",
+        name="finish",
     )(*args)
 
 
@@ -1153,33 +1372,34 @@
 
     flow = cotangent
     tail = None
-    terms, vectors = [], []
-    for index in (2, 1, 0, None):
-        head = None
-        if index is not None:
-            (pick, key_place, query_place, tables, rows_in, normed, packed, query, mixed_t, log_total, mixed,
-             attn, ffn, second, parts) = kept[index]
-            head = (rows_in, attn, ffn, second, parts, pick)
+    terms, vectors, second_vecs = [], [], []
+    for index in (2, 1, 0):
+        (pick, key_place, query_place, tables, rows_in, normed, packed, query, mixed_t, log_total, mixed,
+         attn, ffn, second, parts) = kept[index]
+        head = (rows_in, attn, ffn, second, parts, pick)
         outs = list(
-            feed_back(flow, gains, tail, head, weights, hidden_width, heads * HD, mp, 6 + (3 if index is None else index))
+            feed_back(flow, gains, tail, head, weights, hidden_width, heads * HD, mp, 6 + index)
         )
         if tail is not None:
             flow, first_vec, router_vec = outs[:3]
             outs = outs[3:]
-            vectors.append((first_vec, None, router_vec))
-        if head is not None:
-            grad_attn, grad_middle, logit, grad_mixed, parts_grad, hidden, grad_ffn, second_vec = outs
-            vectors.append((None, second_vec, None))
+            vectors.append((first_vec, router_vec))
+        grad_attn, grad_middle, logit, grad_mixed, parts_grad, hidden, grad_ffn, second_vec = outs
+        second_vecs.append(second_vec)
+        items = (second, parts_grad, grad_ffn, hidden, grad_attn, mixed, normed)
+        if index:
             grad_qkv = attend_back(
                 key_place, query_place, query, packed, mixed_t, log_total, grad_mixed, tables,
                 heads, devices, rows_in.shape[0], 10 + index,
             )
             tail = (grad_qkv, rows_in, grad_middle, logit, pick)
-            terms.append((second, parts_grad, grad_ffn, hidden, grad_attn, mixed, normed, grad_qkv))
-    vectors = [sum(item for item in items if item is not None) for items in zip(*vectors)]
-    vectors = jnp.concatenate(vectors + [jnp.zeros((LANES - 3, flow.shape[1]), F32)], axis=0)
-    query_grad, key_grad, value_grad, out_grad, gate_grad, up_grad, down_grad, vec = collect(
-        terms[::-1], vectors, depth, 14
+            items = items + (grad_qkv,)
+        terms.append(items)
+    attention = (query_place, query, packed, mixed_t, log_total, grad_mixed, *tables)
+    vecs = [jnp.concatenate(list(part), axis=0) for part in (second_vecs, *zip(*vectors))]
+    flow, query_grad, key_grad, value_grad, out_grad, gate_grad, up_grad, down_grad, vec = finish(
+        flow, gains, attention, (rows_in, grad_middle, logit), vecs, weights, terms[::-1],
+        heads, devices, mp, depth, 14,
     )
     return (
         state, flow, query_grad, key_grad, value_grad, out_grad, gate_grad, up_grad, down_grad,

time: 595 us -> 559 us (0.939)
  Pallas kernels: 549 us -> 510 us
    pallas_call x3 -> x2, Pallas kernels: 58.8 us -> 35.7 us  [attend_back(): pl.pallas_call(functools.partial(attend_back_kernel, n, heads, devices, g...]
    pallas_call x4 -> x3, Pallas kernels: 128 us -> 107 us  [feed_back(): pl.pallas_call(functools.partial(feed_back_kernel, tail_n, head_n, mp, ta...]
    unnamed x45 -> x35, local copies, waits for them, and re-layouts: 12.8 us -> 11.8 us
where the time goes in v4:
time: 559 us; the launch traced here: 550 us
  Pallas kernels  510 us (91%)
  local copies, waits for them, and re-layouts  28 us (5%)
  other arithmetic  10.2 us (2%)
    pallas_call x3, Pallas kernels, feed_back(): pl.pallas_call(functools.partial(feed_back_kernel, tail_n, head_n, mp, ta...  107 us
    pallas_call x1, Pallas kernels, finish(): pl.pallas_call(functools.partial(finish_kernel, n, heads, devices, mp, gr...  105 us
    pallas_call x3, Pallas kernels, feed(): pl.pallas_call(functools.partial(feed_kernel, n, mp, picked), out_shape=(...  103 us
    pallas_call x1, Pallas kernels, spread(): pl.pallas_call(functools.partial(spread_kernel, groups), out_shape=(jax.S...  84.6 us
    pallas_call x3, Pallas kernels, attend(): pl.pallas_call(functools.partial(attend_kernel, n, heads, devices, group,...  74.5 us
    pallas_call x2, Pallas kernels, attend_back(): pl.pallas_call(functools.partial(attend_back_kernel, n, heads, devices, g...  35.7 us
    unnamed x35, local copies, waits for them, and re-layouts  11.8 us

profile of v4, /device:TPU:0, one launch (start us, length us, event | category | flops | bytes accessed | tf_op | source)
XLA Modules:
  0.0 550.0 jit_solution(16613271901481324546)
XLA Ops:
  0.7 0.7 compare_and_fusion
  1.4 0.8 select_reduce_fusion.1
  2.1 0.8 select_reduce_fusion
  3.6 0.6 broadcast_in_dim_tile.11.refs_3_.refs_1_
  4.3 0.7 broadcast_in_dim_tile.10.refs_3_.refs_1_
  4.9 1.3 fusion.3.refs_1_.refs_3_.refs_7_.refs_6_
  6.7 0.8 copy.37
  7.4 0.8 copy.38
  8.2 0.8 copy.39
  9.0 0.7 concatenate.51.extras
  9.7 1.3 fusion.1.refs_1_.refs_3_.refs_12_.refs_6_
  11.5 1.6 copy.43.w_out
  13.2 0.7 concatenate.58.refs_5_.refs_7_
  14.1 0.7 concatenate.62.refs_5_.refs_7_
  15.0 0.8 concatenate.53.refs_3_.refs_8_
  16.0 0.7 concatenate.55.refs_4_.refs_9_
  16.9 0.7 concatenate.60.refs_6_.refs_8_
  17.8 0.7 concatenate.64.refs_6_.refs_8_
  18.5 0.9 copy.44.w_down
  19.4 84.6 %spread.1 = (bf16[4,4,2,64,5504]{4,3,2,1,0:T(8,128)(2,1)}, f32[8,2048]{1,0:T(8,128)}) custom-call(bf16[64,512]{1,0:T(8,128)(2,1)} %w_query.1, bf16[64,64]{1,0:T(8,128)(2,1)} %w_key.1, bf16[64,64]{1,0:T(8,128)(2,1)} %w_value.1, bf16[512,64]{1,0:T(8,128)(2,1)} %copy.43.w_out, bf16[64,1408]{1,0:T(8,128)(2,1)} %w_gate.1, bf16[64,1408]{1,0:T(8,128)(2,1)} %w_up.1, ...), custom_call_target="tpu_custom_call" | custom-call | tf_op jit(solution)/shard_map/spread/pallas_call | solution.py:812
  104.0 0.9 slice_convert_fusion
  105.2 1.3 broadcast_in_dim.94.refs_2_.refs_0_
  106.5 2.2 broadcast_in_dim.90.refs_2_.refs_0_
  108.8 20.2 %attend_128.1 = (bf16[128,2048]{1,0:T(8,128)(2,1)}, bf16[128,2048]{1,0:T(8,128)(2,1)}, bf16[32,128,128]{2,1,0:T(8,128)(2,1)}, bf16[1024,128]{1,0:T(8,128)(2,1)},...) custom-call(bf16[128,2048]{1,0:T(8,128)(2,1)} %refs_0_.5, s32[1,1024]{1,0:T(1,128)} %bitcast.38, ...), custom_call_target="tpu_custom_call" | custom-call | flops 4000000000 | bytes 10000000 | tf_op jit(solution)/shard_map/attend_128/pallas_call | solution.py:242
  129.0 41.9 %feed_128.1 = (bf16[128,2048]{1,0:T(8,128)(2,1)}, bf16[128,2048]{1,0:T(8,128)(2,1)}, bf16[128,2048]{1,0:T(8,128)(2,1)}, f32[128,2816]{1,0:T(8,128)}, f32[128,2048]{1,0:T(8,128)}) custom-call(bf16[128,2048]{1,0:T(8,128)(2,1)} %refs_0_.5, bf16[128,2048]{1,0:T(8,128)(2,1)} %get-tuple-element.91.refs_1_.refs_7_.refs_10_, ...), custom_call_target="tpu_custom_call" | custom-call | flops 5000000000 | bytes 100000000 | tf_op jit(solution)/shard_map/feed_128/pallas_call | solution.py:466
  170.9 30.0 %attend_96.1 = (bf16[96,2048]{1,0:T(8,128)(2,1)}, bf16[96,2048]{1,0:T(8,128)(2,1)}, bf16[32,96,128]{2,1,0:T(8,128)(2,1)}, bf16[768,128]{1,0:T(8,128)(2,1)}, f32[...) custom-call(f32[128,2048]{1,0:T(8,128)} %get-tuple-element.93.refs_0_, ...), custom_call_target="tpu_custom_call" | custom-call | flops 4000000000 | bytes 10000000 | tf_op jit(solution)/shard_map/attend_96/pallas_call | solution.py:242
  201.0 34.1 %feed_96.1 = (bf16[96,2048]{1,0:T(8,128)(2,1)}, bf16[96,2048]{1,0:T(8,128)(2,1)}, bf16[96,2048]{1,0:T(8,128)(2,1)}, f32[96,2816]{1,0:T(8,128)}, f32[128,2048]{1,0:T(8,128)}) custom-call(f32[128,2048]{1,0:T(8,128)} %get-tuple-element.93.refs_0_, bf16[96,2048]{1,0:T(8,128)(2,1)} %get-tuple-element.94.refs_1_.refs_7_.refs_3_, ...), custom_call_target="tpu_custom_call" | custom-call | flops 5000000000 | bytes 100000000 | tf_op jit(solution)/shard_map/feed_96/pallas_call | solution.py:466
  235.1 24.2 %attend_64.1 = (bf16[64,2048]{1,0:T(8,128)(2,1)}, bf16[64,2048]{1,0:T(8,128)(2,1)}, bf16[32,64,128]{2,1,0:T(8,128)(2,1)}, bf16[512,128]{1,0:T(8,128)(2,1)}, f32[...) custom-call(f32[128,2048]{1,0:T(8,128)} %get-tuple-element.96.refs_0_, ...), custom_call_target="tpu_custom_call" | custom-call | flops 4000000000 | bytes 10000000 | tf_op jit(solution)/shard_map/attend_64/pallas_call | solution.py:242
  259.3 27.4 %feed_64.1 = (bf16[64,2048]{1,0:T(8,128)(2,1)}, bf16[64,2048]{1,0:T(8,128)(2,1)}, bf16[64,2048]{1,0:T(8,128)(2,1)}, f32[64,2816]{1,0:T(8,128)}, f32[128,2048]{1,0:T(8,128)}) custom-call(f32[128,2048]{1,0:T(8,128)} %get-tuple-element.96.refs_0_, bf16[64,2048]{1,0:T(8,128)(2,1)} %get-tuple-element.97.refs_1_.refs_2_.refs_3_, ...), custom_call_target="tpu_custom_call" | custom-call | flops 5000000000 | bytes 100000000 | tf_op jit(solution)/shard_map/feed_64/pallas_call | solution.py:466
  286.7 21.4 %feed_back_0_64.1 = (bf16[64,2048]{1,0:T(8,128)(2,1)}, f32[64,2048]{1,0:T(8,128)}, f32[64,1]{1,0:T(8,128)}, bf16[64,512]{1,0:T(8,128)(2,1)}, bf16[64,2816]{1,0:T...) custom-call(f32[128,2048]{1,0:T(8,128)} %refs_0_.7, ...), custom_call_target="tpu_custom_call" | custom-call | flops 5000000000 | bytes 100000000 | tf_op jit(solution)/shard_map/feed_back_0_64/pallas_call | solution.py:654
  308.1 17.9 %attend_back_64.1.refs_2_.refs_39_ = bf16[64,640]{1,0:T(8,128)(2,1)} custom-call(s32[2048,128]{1,0:T(8,128)} %broadcast_in_dim.94.refs_2_.refs_0_, s32[1,512]{1,0:T(1,128)} %broadcast_in_dim_tile.11.refs_3_.refs_1_, bf16[512,128]{1,0:T(8,128)(2,1)} %get-tuple-element.100.refs_2_, bf16[32,64,128]{2,1,0:T(8,128)(2,1)} %get-tuple-element.101.refs_3_, ...), custom_call_target="tpu_custom_call" | custom-call | flops 10000000000 | bytes 10000000 | tf_op jit(solution)/shard_map/attend_back_64/pallas_call | solution.py:373
  326.0 39.2 %feed_back_64_96.1 = (f32[128,2048]{1,0:T(8,128)}, f32[1,2048]{1,0:T(1,128)}, f32[1,2048]{1,0:T(1,128)}, bf16[96,2048]{1,0:T(8,128)(2,1)}, f32[96,2048]{1,0:T(8,...) custom-call(f32[128,2048]{1,0:T(8,128)} %refs_0_.7, ...), custom_call_target="tpu_custom_call" | custom-call | flops 5000000000 | bytes 100000000 | tf_op jit(solution)/shard_map/feed_back_64_96/pallas_call | solution.py:654
  365.3 17.8 %attend_back_96.1.refs_2_.refs_31_ = bf16[96,640]{1,0:T(8,128)(2,1)} custom-call(s32[3072,128]{1,0:T(8,128)} %broadcast_in_dim.90.refs_2_.refs_0_, s32[1,768]{1,0:T(1,128)} %broadcast_in_dim_tile.10.refs_3_.refs_1_, bf16[768,128]{1,0:T(8,128)(2,1)} %get-tuple-element.116.refs_2_, bf16[32,96,128]{2,1,0:T(8,128)(2,1)} %get-tuple-element.117.refs_3_, ...), custom_call_target="tpu_custom_call" | custom-call | flops 10000000000 | bytes 10000000 | tf_op jit(solution)/shard_map/attend_back_96/pallas_call | solution.py:373
  383.1 46.4 %feed_back_96_128.1 = (f32[128,2048]{1,0:T(8,128)}, f32[1,2048]{1,0:T(1,128)}, f32[1,2048]{1,0:T(1,128)}, bf16[128,2048]{1,0:T(8,128)(2,1)}, f32[128,2048]{1,0:T...) custom-call(f32[128,2048]{1,0:T(8,128)} %get-tuple-element.115.refs_, ...), custom_call_target="tpu_custom_call" | custom-call | flops 5000000000 | bytes 100000000 | tf_op jit(solution)/shard_map/feed_back_96_128/pallas_call | solution.py:654
  429.6 1.3 pad_maximum_fusion.7.refs_14_
  430.9 1.3 pad_maximum_fusion.8.refs_15_
  432.2 1.3 pad_maximum_fusion.6.refs_13_
  433.5 105.1 %finish.1 = (f32[128,2048]{1,0:T(8,128)}, f32[64,512]{1,0:T(8,128)}, f32[64,64]{1,0:T(8,128)}, f32[64,64]{1,0:T(8,128)}, f32[512,64]{1,0:T(8,128)}, /*index=5*/f...) custom-call(f32[128,2048]{1,0:T(8,128)} %get-tuple-element.127.refs_0_, ...), custom_call_target="tpu_custom_call" | custom-call | tf_op jit(solution)/shard_map/finish/pallas_call | solution.py:1244
  538.7 1.6 slice_reduce_fusion
  540.3 1.7 copy.51
  542.0 2.2 copy.52
  544.2 1.0 copy.60
  545.2 1.0 copy.61
  546.2 0.7 copy.62
  546.8 0.6 copy.63
  547.5 0.6 copy.64
  548.1 0.7 copy.65
  548.8 0.7 copy.66
  (65 shorter events, 3.1 us)
Async XLA Ops:
  16.0 2.5 copy-start.4
  383.1 46.4 %copy-start.11 = (f32[1,2048]{1,0:T(1,128)S(1)}, f32[1,2048]{1,0:T(1,128)}, u32[]{:S(2)}) copy-start(f32[1,2048]{1,0:T(1,128)} %get-tuple-element.138) | copy-start | bytes 24580
  383.1 47.8 %copy-start.10 = (f32[1,2048]{1,0:T(1,128)S(1)}, f32[1,2048]{1,0:T(1,128)}, u32[]{:S(2)}) copy-start(f32[1,2048]{1,0:T(1,128)} %get-tuple-element.140) | copy-start | bytes 24580
  383.1 49.1 %copy-start.8 = (f32[1,2048]{1,0:T(1,128)S(1)}, f32[1,2048]{1,0:T(1,128)}, u32[]{:S(2)}) copy-start(f32[1,2048]{1,0:T(1,128)} %get-tuple-element.135) | copy-start | bytes 24580
  383.1 49.1 %copy-start.9 = (f32[1,2048]{1,0:T(1,128)S(1)}, f32[1,2048]{1,0:T(1,128)}, u32[]{:S(2)}) copy-start(f32[1,2048]{1,0:T(1,128)} %get-tuple-element.136) | copy-start | bytes 24580
  538.7 5.5 %copy-start = (f32[128,2048]{1,0:T(8,128)S(1)}, f32[128,2048]{1,0:T(8,128)}, u32[]{:S(2)}) copy-start(f32[128,2048]{1,0:T(8,128)} %get-tuple-element.232) | copy-start | bytes 3145732
  542.0 3.2 copy-start.1
  545.2 1.0 copy-start.5
  545.2 1.7 copy-start.7
  545.2 2.3 copy-start.6
  545.2 2.9 copy-start.3
  545.2 3.6 copy-start.2

commit v5 on v4

--- a/solution.py
+++ b/solution.py
@@ -14,12 +14,12 @@
 EPS = 1e-05
 NEG = -1e30
 ROPE_BASE = 10000.0
-FAR = 1073741824
+FAR = 1e9
 BF = jnp.bfloat16
 F32 = jnp.float32
 MESH = pl.DeviceIdType.MESH
 LANES = 128
-VMEM_LIMIT = 58 * 1024 * 1024
+VMEM_LIMIT = 63 * 1024 * 1024
 
 
 def dot_nn(left, right):
@@ -54,6 +54,13 @@
 def swap_halves(tile):
     first = lax.rem(lanes_of(tile.shape), HD) < HD // 2
     return jnp.where(first, pltpu.roll(tile, LANES - HD // 2, 1), pltpu.roll(tile, HD // 2, 1))
+
+
+def turn_back(part, cosine, sine, packed):
+    if packed:
+        left = lanes_of(part.shape) < HD
+        cosine, sine = jnp.where(left, cosine, 1.0), jnp.where(left, sine, 0.0)
+    return (part * cosine - swap_halves(part) * sine).astype(BF)
 
 
 def tile_of(values, index):
@@ -104,172 +111,8 @@
     return jnp.concatenate([full[c] for c in range(group)], axis=1)
 
 
-def attend_kernel(n, heads, devices, group, picked, *refs):
-    refs = list(refs)
-    source = refs.pop(0)
-    pick = refs.pop(0) if picked else None
-    key_place = refs.pop(0) if picked else None
-    query_place, gains, cosine, sine, w_hbm = [refs.pop(0) for _ in range(5)]
-    rows_out, normed_out, packed_out, query_out, mixed_t_out, log_out, mixed_out = [
-        refs.pop(0) for _ in range(7)
-    ]
-    w_v, packed, query_t, top, total, acc, w_sem, out_sem, send_sems, recv_sems = refs
-    me = lax.axis_index("dp")
-    width = heads * n
-    load_w = pltpu.make_async_copy(w_hbm.at[:, : w_v.shape[1]], w_v, w_sem)
-    load_w.start()
-
-    barrier = pltpu.get_barrier_semaphore()
-
-    def greet(e, carry):
-        pl.semaphore_signal(barrier, inc=1, device_id={"dp": e}, device_id_type=MESH)
-        return carry
-
-    lax.fori_loop(0, me, greet, 0)
-
-    if picked:
-        rows = dot_nn(pick[...], source[...].astype(BF)).astype(BF)
-    else:
-        rows = source[...]
-    rows_out[...] = rows
-    unit, unused = unit_of(rows.astype(F32))
-    normed = (unit * gains[0:1, :]).astype(BF)
-    normed_out[...] = normed
-    load_w.wait()
-    tiles = []
-    for t in range(heads // 2 + 1):
-        if t % 2 == 0:
-            last = min((t + 2) * LANES, (heads // 2 + 1) * LANES)
-            both = dot_nn(normed, w_v[:, t * LANES : last])
-        part = tile_of(both, t % 2)
-        cut = slice(t * LANES, (t + 1) * LANES)
-        tiles.append(part * cosine[:, cut] + swap_halves(part) * sine[:, cut])
-    packed[me] = tiles[-1].astype(BF)
-
-    @pl.when(me < devices - 1)
-    def _():
-        pl.semaphore_wait(barrier, devices - 1 - me)
-
-    def send_copy(e, source_index):
-        return pltpu.make_async_remote_copy(
-            src_ref=packed.at[me], dst_ref=packed.at[me],
-            send_sem=send_sems.at[e], recv_sem=recv_sems.at[source_index],
-            device_id={"dp": e}, device_id_type=MESH,
-        )
-
-    def send(e, carry):
-        send_copy(e, me).start()
-        return carry
-
-    lax.fori_loop(me + 1, devices, send, 0)
-
-    def clear(e, carry):
-        packed[e] = jnp.zeros((n, 2 * HD), BF)
-        return carry
-
-    lax.fori_loop(me + 1, devices, clear, 0)
-
-    left = lanes_of((n, LANES)) < HD
-    for t in range(heads // 2):
-        scaled = tiles[t].astype(BF).astype(F32) * HD**-0.5
-        query_out[2 * t * n : (2 * t + 1) * n, :] = jnp.where(left, scaled, 0.0).astype(BF)
-        query_out[(2 * t + 1) * n : (2 * t + 2) * n, :] = jnp.where(
-            left, pltpu.roll(scaled, HD, 1), 0.0
-        ).astype(BF)
-    query_t[...] = query_out[...].T
-    top[...] = jnp.full((1, width), NEG, F32)
-    total[...] = jnp.zeros((1, width), F32)
-    acc[...] = jnp.zeros((2 * HD, width), F32)
-
-    def one_block(b, carry):
-        for g in range(group):
-            e = b * group + g
-
-            @pl.when(e < me)
-            def _():
-                send_copy(me, e).wait_recv()
-
-        part = packed[pl.ds(b * group, group)].reshape(group * n, 2 * HD)
-        scores = dot_nn(part, query_t[...])
-        if picked:
-            start = pl.multiple_of(b * (group * n), group * n)
-            place = key_place[pl.ds(start, group * n), :]
-        else:
-            place = lax.broadcasted_iota(jnp.int32, (group * n, LANES), 0) + b * (group * n)
-        place = jnp.concatenate([place] * (width // LANES), axis=1)
-        scores = jnp.where(place <= query_place[...], scores, NEG)
-        peak = jnp.maximum(top[...], jnp.max(scores, axis=0, keepdims=True))
-        weights = jnp.exp(scores - peak)
-        fade = jnp.exp(top[...] - peak)
-        total[...] = total[...] * fade + jnp.sum(weights, axis=0, keepdims=True)
-        acc[...] = acc[...] * fade + dot_tn(part, weights.astype(BF))
-        top[...] = peak
-        return carry
-
-    lax.fori_loop(0, me // group + 1, one_block, 0)
-    mixed_t = acc[...] / total[...]
-    mixed_t_out[...] = mixed_t
-    log_out[...] = top[...] + jnp.log(total[...])
-    mixed = mixed_t.T
-    for t in range(heads // 2):
-        even = mixed[2 * t * n : (2 * t + 1) * n, :]
-        odd = mixed[(2 * t + 1) * n : (2 * t + 2) * n, :]
-        mixed_out[:, t * LANES : (t + 1) * LANES] = jnp.where(
-            left, pltpu.roll(even, HD, 1), odd
-        ).astype(BF)
-    keep = pltpu.make_async_copy(packed, packed_out, out_sem)
-    keep.start()
-
-    def sent(e, carry):
-        send_copy(e, me).wait_send()
-        return carry
-
-    lax.fori_loop(me + 1, devices, sent, 0)
-    keep.wait()
-
-
 def vmem(count):
     return [pl.BlockSpec(memory_space=pltpu.VMEM)] * count
-
-
-def attend(source, pick, key_place, query_place, gains, tables, w_qkv, heads, devices, n, ident):
-    picked = pick is not None
-    group = 512 // n if 512 % n == 0 else 4
-    width = heads * n
-    qkv_width = (heads + 2) * HD
-    args = [source] + ([pick, key_place] if picked else []) + [query_place, gains, *tables, w_qkv]
-    model = source.shape[1]
-    return pl.pallas_call(
-        functools.partial(attend_kernel, n, heads, devices, group, picked),
-        out_shape=(
-            jax.ShapeDtypeStruct((n, model), BF),
-            jax.ShapeDtypeStruct((n, model), BF),
-            jax.ShapeDtypeStruct((devices, n, 2 * HD), BF),
-            jax.ShapeDtypeStruct((width, 2 * HD), BF),
-            jax.ShapeDtypeStruct((2 * HD, width), F32),
-            jax.ShapeDtypeStruct((1, width), F32),
-            jax.ShapeDtypeStruct((n, heads * HD), BF),
-        ),
-        in_specs=vmem(len(args) - 1) + [pl.BlockSpec(memory_space=pl.ANY)],
-        out_specs=tuple(vmem(2) + [pl.BlockSpec(memory_space=pl.ANY)] + vmem(4)),
-        scratch_shapes=[
-            pltpu.VMEM((model, qkv_width), BF),
-            pltpu.VMEM((devices, n, 2 * HD), BF),
-            pltpu.VMEM((2 * HD, width), BF),
-            pltpu.VMEM((1, width), F32),
-            pltpu.VMEM((1, width), F32),
-            pltpu.VMEM((2 * HD, width), F32),
-            pltpu.SemaphoreType.DMA(()),
-            pltpu.SemaphoreType.DMA(()),
-            pltpu.SemaphoreType.DMA((devices,)),
-            pltpu.SemaphoreType.DMA((devices,)),
-        ],
-        compiler_params=pltpu.CompilerParams(
-            collective_id=ident, has_side_effects=True, vmem_limit_bytes=VMEM_LIMIT
-        ),
-        cost_estimate=pl.CostEstimate(flops=4 * 10**9, bytes_accessed=10**7, transcendentals=0),
-        name=f"attend_{n}",
-    )(*args)
 
 
 def attend_back_kernel(n, heads, devices, group, picked, *refs):
@@ -320,7 +163,7 @@
             start = pl.multiple_of(b * (group * n), group * n)
             place = key_place[pl.ds(start, group * n), :]
         else:
-            place = lax.broadcasted_iota(jnp.int32, (group * n, LANES), 0) + b * (group * n)
+            place = (lax.broadcasted_iota(jnp.int32, (group * n, LANES), 0) + b * (group * n)).astype(F32)
         place = jnp.concatenate([place] * (width // LANES), axis=1)
         scores = jnp.where(place <= query_place[...], scores, NEG)
         weights = jnp.exp(scores - log_total[...])
@@ -353,8 +196,9 @@
 
     outs.append(lax.fori_loop(me + 1, devices, add, send_buf[me].astype(F32)))
     for t, part in enumerate(outs):
-        cut = slice(t * LANES, (t + 1) * LANES)
-        grad_out[:, cut] = (part * cosine[:, cut] - swap_halves(part) * sine[:, cut]).astype(BF)
+        grad_out[:, t * LANES : (t + 1) * LANES] = turn_back(
+            part, cosine[...], sine[...], t == heads // 2
+        )
 
     def sent(e, carry):
         send_copy(e, me).wait_send()
@@ -394,62 +238,6 @@
     )(*args)
 
 
-def feed_kernel(n, mp, picked, *refs):
-    refs = list(refs)
-    state, rows_in, mixed = [refs.pop(0) for _ in range(3)]
-    pick = refs.pop(0) if picked else None
-    gains, w_hbm = refs.pop(0), refs.pop(0)
-    attn_out, ffn_out, second_out, parts_out, state_out = [refs.pop(0) for _ in range(5)]
-    w_o, w_gu, w_d, hidden, w_sems, send_a, recv_a, full_a, sems_a, send_b, recv_b, full_b, sems_b = refs
-    me = lax.axis_index("mp")
-    wide_o, wide_gu, wide_d = w_o.shape[1], w_gu.shape[1], w_d.shape[1]
-    loads = []
-    start = wide_o + 2 * LANES
-    for index, (ref, wide) in enumerate(((w_o, wide_o), (w_gu, wide_gu), (w_d, wide_d))):
-        load = pltpu.make_async_copy(w_hbm.at[:, start : start + wide], ref, w_sems.at[index])
-        load.start()
-        loads.append(load)
-        start += wide
-    signal_all(mp, me, "mp")
-    chunk = w_o.shape[0] // mp
-    loads[0].wait()
-    mixed_now = mixed[...]
-
-    def out_chunk(c):
-        return dot_nt(mixed_now, w_o[pl.ds(pl.multiple_of(c * chunk, chunk), chunk), :])
-
-    attn = sum_over_mp(mp, me, out_chunk, send_a, recv_a, full_a, sems_a)
-    attn_out[...] = attn
-    level = rows_in[...].astype(F32)
-    unit, unused = unit_of(level + attn.astype(F32))
-    second = (unit * gains[1:2, :]).astype(BF)
-    second_out[...] = second
-    loads[1].wait()
-    step = 256
-    for t in range(wide_gu // step):
-        parts_out[:, t * step : (t + 1) * step] = dot_nn(second, w_gu[:, t * step : (t + 1) * step])
-    half = wide_gu // 2
-    for t in range(half // LANES):
-        cut = slice(t * LANES, (t + 1) * LANES)
-        gate_part = parts_out[:, cut]
-        up_part = parts_out[:, half + t * LANES : half + (t + 1) * LANES]
-        hidden[:, cut] = (gate_part * sigmoid(gate_part) * up_part).astype(BF)
-    loads[2].wait()
-    hidden_now = hidden[...]
-
-    def down_chunk(c):
-        return dot_nt(hidden_now, w_d[pl.ds(pl.multiple_of(c * chunk, chunk), chunk), :])
-
-    ffn = sum_over_mp(mp, me, down_chunk, send_b, recv_b, full_b, sems_b)
-    ffn_out[...] = ffn
-    gate = sigmoid(jnp.sum(level * gains[2:3, :], axis=-1, keepdims=True))
-    update = (gate * (attn.astype(F32) + ffn.astype(F32))).astype(BF)
-    if picked:
-        state_out[...] = state[...].astype(F32) + dot_tn(pick[...], update)
-    else:
-        state_out[...] = state[...].astype(F32) + update.astype(F32)
-
-
 def sum_scratch(mp, n, model):
     return [
         pltpu.VMEM((mp - 1, n, model // mp), BF),
@@ -457,38 +245,6 @@
         pltpu.VMEM((mp, n, model // mp), BF),
         pltpu.SemaphoreType.DMA((4, mp - 1)),
     ]
-
-
-def feed(state, rows, mixed, pick, gains, w_rest, hidden_width, mp, n, ident):
-    picked = pick is not None
-    model = rows.shape[1]
-    args = [state, rows, mixed] + ([pick] if picked else []) + [gains, w_rest]
-    return pl.pallas_call(
-        functools.partial(feed_kernel, n, mp, picked),
-        out_shape=(
-            jax.ShapeDtypeStruct((n, model), BF),
-            jax.ShapeDtypeStruct((n, model), BF),
-            jax.ShapeDtypeStruct((n, model), BF),
-            jax.ShapeDtypeStruct((n, 2 * hidden_width), F32),
-            jax.ShapeDtypeStruct(state.shape, F32),
-        ),
-        in_specs=vmem(len(args) - 1) + [pl.BlockSpec(memory_space=pl.ANY)],
-        out_specs=tuple(vmem(5)),
-        scratch_shapes=[
-            pltpu.VMEM((model, mixed.shape[1]), BF),
-            pltpu.VMEM((model, 2 * hidden_width), BF),
-            pltpu.VMEM((model, hidden_width), BF),
-            pltpu.VMEM((n, hidden_width), BF),
-            pltpu.SemaphoreType.DMA((3,)),
-            *sum_scratch(mp, n, model),
-            *sum_scratch(mp, n, model),
-        ],
-        compiler_params=pltpu.CompilerParams(
-            collective_id=ident, has_side_effects=True, vmem_limit_bytes=VMEM_LIMIT
-        ),
-        cost_estimate=pl.CostEstimate(flops=5 * 10**9, bytes_accessed=10**8, transcendentals=0),
-        name=f"feed_{n}",
-    )(*args)
 
 
 def feed_back_kernel(tail_n, head_n, mp, tail_picked, head_picked, *refs):
@@ -692,116 +448,405 @@
     )
 
 
-def spread_kernel(
-    groups, w_query, w_key, w_value, w_out, w_gate, w_up, w_down, extras, full, gains,
-    shard, columns, own_sem, column_sem, send_sems, recv_sems,
-):
-    me = lax.axis_index("dp")
+class Spread:
+    def __init__(self, groups, x, y, core, shard, full, send_sems, recv_sems):
+        self.groups, self.x, self.y, self.core = groups, x, y, core
+        self.shard, self.full = shard, full
+        self.send_sems, self.recv_sems = send_sems, recv_sems
+        self.started = []
+        self.waits = [{} for _ in groups]
+
+    def remote(self, g, index, source, target, device):
+        copy = pltpu.make_async_remote_copy(
+            src_ref=source, dst_ref=target, send_sem=self.send_sems.at[g, index],
+            recv_sem=self.recv_sems.at[g, index], device_id=device, device_id_type=MESH,
+        )
+        copy.start()
+        self.started.append(copy)
+        return copy
+
+    def line(self, axis, at, first, count, cut):
+        if axis == 0:
+            return self.full.at[pl.ds(first, count), at, self.core, :, cut]
+        return self.full.at[at, pl.ds(first, count), self.core, :, cut]
+
+    def one(self, g):
+        low, high, axis = self.groups[g]
+        cut = slice(low, high)
+        self.waits[g][1] = [
+            self.remote(
+                g, k - 1, self.shard.at[:, cut], self.full.at[self.x, self.y, self.core, :, cut],
+                shifted(self.x, self.y, self.core, axis, k),
+            )
+            for k in (2, 1, 3)
+        ]
+
+    def two(self, g):
+        low, high, axis = self.groups[g]
+        for copy in self.waits[g][1]:
+            copy.wait_recv()
+        mine = self.line(axis, self.y if axis == 0 else self.x, 0, 4, slice(low, high))
+        self.waits[g][2] = [
+            self.remote(g, 3 + i, mine, mine, shifted(self.x, self.y, self.core, 1 - axis, k))
+            for i, k in enumerate((1, 3))
+        ]
+
+    def three(self, g):
+        low, high, axis = self.groups[g]
+        at = self.y if axis == 0 else self.x
+        self.waits[g][3] = []
+        for i, k in enumerate((1, 3)):
+            self.waits[g][2][i].wait_recv()
+            piece = self.line(axis, lax.rem(at + 4 - k, 4), 2 * i, 2, slice(low, high))
+            self.waits[g][3].append(
+                self.remote(g, 5 + i, piece, piece, shifted(self.x, self.y, self.core, 1 - axis, k))
+            )
+
+    def four(self, g):
+        low, high, axis = self.groups[g]
+        for copy in self.waits[g][3]:
+            copy.wait_recv()
+        mine = self.full.at[:, :, self.core, :, slice(low, high)]
+        self.waits[g][4] = [self.remote(g, 7, mine, mine, peer(self.x, self.y, 1 - self.core))]
+
+    def five(self, g):
+        self.waits[g][4][0].wait_recv()
+
+    def step(self, i):
+        for back, work in ((0, self.one), (2, self.two), (4, self.three), (5, self.four), (6, self.five)):
+            if 1 <= i - back < len(self.groups):
+                work(i - back)
+
+    def drain(self):
+        for copy in self.started:
+            copy.wait_send()
+
+
+def advance_kernel(counts, heads, devices, mp, hidden, groups, names, *refs):
+    refs = list(refs)
+    (tokens, depths, second_slot, third_slot, w_query, w_key, w_value, w_out, w_gate, w_up, w_down,
+     norm_first, norm_second, router, cosine_in, sine_in) = [refs.pop(0) for _ in range(16)]
+    outs = {name: refs.pop(0) for name in names}
+    held = {name: refs.pop(0) for name in names}
+    shard, own_sem, send_sems, recv_sems, query_t, top, total, acc, hidden_v, keep_sems, kv_send, kv_recv = [
+        refs.pop(0) for _ in range(12)
+    ]
+    sum_refs = refs
+    me, mp_me = lax.axis_index("dp"), lax.axis_index("mp")
     x, y, core = plane(me)
+    weights = held["weights"]
+    rows, model = tokens.shape
+    mix = heads * HD
+    lanes = lanes_of((rows, LANES))
+    left = lanes < HD
+    keeps = []
+
+    def keep(name):
+        copy = pltpu.make_async_copy(held[name], outs[name], keep_sems.at[len(keeps)])
+        copy.start()
+        keeps.append(copy)
+
+    barrier = pltpu.get_barrier_semaphore()
+
+    def greet(k, carry):
+        pl.semaphore_signal(
+            barrier, inc=1, device_id={"dp": lax.rem(me + k, devices)}, device_id_type=MESH
+        )
+        return carry
+
+    lax.fori_loop(1, devices, greet, 0)
+    for k in range(1, mp):
+        pl.semaphore_signal(
+            barrier, inc=1, device_id={"mp": lax.rem(mp_me + k, mp)}, device_id_type=MESH
+        )
+
+    token = lanes_of((1, rows)).astype(F32)
+    picks, marks, query_places = [None], [None], []
+    query_places.append(
+        (lax.rem(lanes_of((1, heads * rows)), rows) + me * rows).astype(F32)
+    )
+    held["place_0"][...] = query_places[0]
+    for level, slot, deep in ((1, second_slot, 2), (2, third_slot, 3)):
+        count = counts[level]
+        slots = lax.broadcasted_iota(jnp.int32, (count, rows), 0)
+        active = (depths[...] >= deep) & (slot[...] >= 0)
+        chosen = jnp.where(active, slot[...], -1) == slots
+        pick = jnp.where(chosen, 1.0, 0.0).astype(BF)
+        held[f"pick_{level}"][...] = pick
+        picks.append(pick)
+        marks.append(
+            jnp.min(jnp.where(chosen, token, float(rows)), axis=1, keepdims=True)
+        )
+        sublane = lax.broadcasted_iota(jnp.int32, (16, rows), 0)
+        probe = jnp.where(sublane == 0, token, 1.0).astype(BF)
+        found = dot_nt(probe, jnp.concatenate([pick] * heads, axis=0))
+        place = jnp.where(found[1:2, :] > 0.5, found[0:1, :] + (me * rows).astype(F32), FAR)
+        held[f"place_{level}"][...] = place
+        query_places.append(place)
+        table = jnp.concatenate([cosine_in[...], sine_in[...]], axis=1)
+        turned = lax.dot_general(
+            pick.astype(F32), table, (((1,), (0,)), ((), ())),
+            preferred_element_type=F32, precision=lax.Precision.HIGHEST,
+        )
+        held[f"cosine_{level}"][...] = turned[:, :LANES]
+        held[f"sine_{level}"][...] = turned[:, LANES:]
+    depth = w_query.shape[0]
+    wide = jnp.zeros((1, LANES - depth), F32)
+    gain_rows = jnp.concatenate(
+        [jnp.concatenate([ref[...].astype(F32), wide], axis=1) for ref in (norm_first, norm_second, router)]
+        + [jnp.zeros((LANES - 3, LANES), F32)],
+        axis=0,
+    )
+    extra = gain_rows.T[:depth, :]
+    rest = counts[1] - depth
+    lane = lanes_of((depth, LANES))
+    over = jnp.concatenate([marks[1][depth:, :], jnp.full((depth - rest, 1), float(rows), F32)], axis=0)
+    extra = jnp.where(lane == 3, marks[1][:depth, :], extra)
+    extra = jnp.where(lane == 4, over, extra)
+    extra = jnp.where(lane == 5, marks[2], extra)
+    pair = jnp.concatenate([w_key[...].astype(F32), w_value[...].astype(F32)], axis=1).astype(BF)
     start = 0
-    pair = jnp.concatenate([w_key[...].astype(F32), w_value[...].astype(F32)], axis=1).astype(BF)
     for part in (
-        w_query[...], pair, extras[...],
-        w_out[...].T, w_gate[...], w_up[...], w_down[...].T,
+        w_query[...], pair, extra.astype(BF), w_out[...], w_gate[...], w_up[...], w_down[...],
     ):
         shard[:, start : start + part.shape[1]] = part
         start += part.shape[1]
-    own = pltpu.make_async_copy(shard, full.at[x, y, core], own_sem)
+    own = pltpu.make_async_copy(shard, weights.at[x, y, core], own_sem)
     own.start()
-    meet(me, plane_partners(x, y, core))
-    started = []
-
-    def remote(g, index, source, target, device):
-        copy = pltpu.make_async_remote_copy(
-            src_ref=source, dst_ref=target, send_sem=send_sems.at[g, index],
-            recv_sem=recv_sems.at[g, index], device_id=device, device_id_type=MESH,
-        )
-        copy.start()
-        started.append(copy)
-        return copy
-
-    def line(axis, at, first, count, cut):
-        if axis == 0:
-            return full.at[pl.ds(first, count), at, core, :, cut]
-        return full.at[at, pl.ds(first, count), core, :, cut]
-
-    waits = [{} for _ in groups]
-
-    def one(g):
-        low, high, axis = groups[g]
-        cut = slice(low, high)
-        waits[g][1] = [
-            remote(
-                g, k - 1, shard.at[:, cut], full.at[x, y, core, :, cut],
-                shifted(x, y, core, axis, k),
+    spread = Spread(groups, x, y, core, shard, weights, send_sems, recv_sems)
+    pl.semaphore_wait(barrier, devices - 1 + mp - 1)
+    spread.one(0)
+    own.wait()
+    spread.step(1)
+    spread.two(0)
+    spread.step(2)
+    spread.three(0)
+    spread.four(0)
+    spread.step(3)
+    spread.five(0)
+    upto = 4
+
+    gains = held["gains"]
+    columns = weights[:, :, :, :, mix + LANES : mix + 2 * LANES].reshape(model, LANES).astype(F32)
+    gains[...] = columns.T[: gains.shape[0], :]
+    keep("gains")
+
+    def key_places(e, carry):
+        for level, lanes_at in ((1, (3, 4)), (2, (5,))):
+            tile = weights[e // 8, lax.rem(e // 2, 4), lax.rem(e, 2), :, mix + LANES : mix + 2 * LANES].astype(F32)
+            value = jnp.concatenate(
+                [jnp.broadcast_to(tile[:, at : at + 1], (depth, LANES)) for at in lanes_at], axis=0
+            )[: counts[level], :]
+            held[f"keys_{level}"][e] = jnp.where(
+                value < rows, value + (e * rows).astype(F32), FAR
             )
-            for k in (2, 1, 3)
-        ]
-
-    def two(g):
-        low, high, axis = groups[g]
-        cut = slice(low, high)
-        for copy in waits[g][1]:
-            copy.wait_recv()
-        mine = line(axis, y if axis == 0 else x, 0, 4, cut)
-        waits[g][2] = [
-            remote(g, 3 + i, mine, mine, shifted(x, y, core, 1 - axis, k))
-            for i, k in enumerate((1, 3))
-        ]
-
-    def three(g):
-        low, high, axis = groups[g]
-        cut = slice(low, high)
-        at = y if axis == 0 else x
-        waits[g][3] = []
-        for i, k in enumerate((1, 3)):
-            waits[g][2][i].wait_recv()
-            piece = line(axis, lax.rem(at + 4 - k, 4), 2 * i, 2, cut)
-            waits[g][3].append(
-                remote(g, 5 + i, piece, piece, shifted(x, y, core, 1 - axis, k))
+        return carry
+
+    lax.fori_loop(0, devices, key_places, 0)
+
+    def kv_copy(level, e, source_index):
+        packed = held[f"packed_{level}"]
+        return pltpu.make_async_remote_copy(
+            src_ref=packed.at[me], dst_ref=packed.at[me],
+            send_sem=kv_send.at[level, e], recv_sem=kv_recv.at[level, source_index],
+            device_id={"dp": e}, device_id_type=MESH,
+        )
+
+    def project(level, now):
+        n = counts[level]
+        name = lambda base: held[f"{base}_{level}"]
+        name("rows")[...] = now
+        unit, unused = unit_of(now.astype(F32))
+        normed = (unit * gains[0:1, :]).astype(BF)
+        name("normed")[...] = normed
+        cosine, sine = (cosine_in[...], sine_in[...]) if level == 0 else (name("cosine")[...], name("sine")[...])
+        here = left[:n]
+        tiles = [None] * (heads // 2 + 1)
+        for t in range(heads // 2, -1, -2):
+            low = max(t - 1, 0)
+            both = dot_nn(normed, weights[:, :, :, :, low * LANES : (t + 1) * LANES].reshape(model, (t + 1 - low) * LANES))
+            for j in range(low, t + 1):
+                part = tile_of(both, j - low)
+                if j == heads // 2:
+                    part = part * jnp.where(here, cosine, 1.0) + swap_halves(part) * jnp.where(here, sine, 0.0)
+                    name("packed")[me] = part.astype(BF)
+
+                    def send(e, carry):
+                        kv_copy(level, e, me).start()
+                        return carry
+
+                    lax.fori_loop(me + 1, devices, send, 0)
+                else:
+                    tiles[j] = part * cosine + swap_halves(part) * sine
+
+        def clear(e, carry):
+            name("packed")[e] = jnp.zeros((n, 2 * HD), BF)
+            return carry
+
+        lax.fori_loop(me + 1, devices, clear, 0)
+        for t in range(heads // 2):
+            scaled = tiles[t].astype(BF).astype(F32) * HD**-0.5
+            name("query")[2 * t * n : (2 * t + 1) * n, :] = jnp.where(here, scaled, 0.0).astype(BF)
+            name("query")[(2 * t + 1) * n : (2 * t + 2) * n, :] = jnp.where(
+                here, pltpu.roll(scaled, HD, 1), 0.0
+            ).astype(BF)
+        width = heads * n
+        query_t[:, :width] = name("query")[...].T
+        top[:, :width] = jnp.full((1, width), NEG, F32)
+        total[:, :width] = jnp.zeros((1, width), F32)
+        acc[:, :width] = jnp.zeros((2 * HD, width), F32)
+        for base in ("rows", "normed", "query"):
+            keep(f"{base}_{level}")
+
+    def group_of(level):
+        return 512 // counts[level] if 512 % counts[level] == 0 else 4
+
+    def block(level, b):
+        n, group = counts[level], group_of(level)
+        width = heads * n
+        for g in range(group):
+            e = b * group + g
+
+            @pl.when(e < me)
+            def _(e=e):
+                kv_copy(level, me, e).wait_recv()
+
+        part = held[f"packed_{level}"][pl.ds(b * group, group)].reshape(group * n, 2 * HD)
+        scores = dot_nn(part, query_t[:, :width])
+        if level:
+            place = held[f"keys_{level}"][pl.ds(b * group, group)].reshape(group * n, LANES)
+        else:
+            place = (lax.broadcasted_iota(jnp.int32, (group * n, LANES), 0) + b * (group * n)).astype(F32)
+        place = jnp.concatenate([place] * (width // LANES), axis=1)
+        scores = jnp.where(place <= held[f"place_{level}"][...], scores, NEG)
+        before = top[:, :width]
+        peak = jnp.maximum(before, jnp.max(scores, axis=0, keepdims=True))
+        soft = jnp.exp(scores - peak)
+        fade = jnp.exp(before - peak)
+        total[:, :width] = total[:, :width] * fade + jnp.sum(soft, axis=0, keepdims=True)
+        acc[:, :width] = acc[:, :width] * fade + dot_tn(part, soft.astype(BF))
+        top[:, :width] = peak
+
+    def mix_heads(level):
+        n = counts[level]
+        width = heads * n
+        mixed_t = acc[:, :width] / total[:, :width]
+        held[f"mixed_t_{level}"][...] = mixed_t
+        held[f"log_{level}"][...] = top[:, :width] + jnp.log(total[:, :width])
+        mixed = mixed_t.T
+        for t in range(heads // 2):
+            even = mixed[2 * t * n : (2 * t + 1) * n, :]
+            odd = mixed[(2 * t + 1) * n : (2 * t + 2) * n, :]
+            held[f"mixed_{level}"][:, t * LANES : (t + 1) * LANES] = jnp.where(
+                left[:n], pltpu.roll(even, HD, 1), odd
+            ).astype(BF)
+        for base in ("mixed_t", "log", "mixed", "packed"):
+            keep(f"{base}_{level}")
+
+    sums = [Sum(mp, mp_me, *sum_refs[4 * i : 4 * i + 4]) for i in range(2 * len(counts))]
+    chunk = model // mp
+    base_o = mix + 2 * LANES
+    base_gu = base_o + mix
+    base_d = base_gu + 2 * hidden
+
+    def chunk_of(c, low, high):
+        return weights[c, :, :, :, low:high].reshape(chunk, high - low)
+
+    def feed(level, beside):
+        name = lambda base: held[f"{base}_{level}"]
+        mixed_now = name("mixed")[...]
+        first, last = sums[2 * level], sums[2 * level + 1]
+        first.start(lambda c: dot_nt(mixed_now, chunk_of(c, base_o, base_gu)))
+        beside(1)
+        first.middle()
+        beside(1)
+        attn = first.finish()
+        name("attn")[...] = attn
+        level_rows = name("rows")[...].astype(F32)
+        unit, unused = unit_of(level_rows + attn.astype(F32))
+        second = (unit * gains[1:2, :]).astype(BF)
+        name("second")[...] = second
+        beside(100)
+        parts = name("parts")
+        for t in range(2 * hidden // 256):
+            low = base_gu + t * 256
+            parts[:, t * 256 : (t + 1) * 256] = dot_nn(
+                second, weights[:, :, :, :, low : low + 256].reshape(model, 256)
             )
-
-    def four(g):
-        low, high, axis = groups[g]
-        for copy in waits[g][3]:
-            copy.wait_recv()
-        mine = full.at[:, :, core, :, slice(low, high)]
-        waits[g][4] = [remote(g, 7, mine, mine, peer(x, y, 1 - core))]
-
-    def five(g):
-        waits[g][4][0].wait_recv()
-
-    count = len(groups)
-    one(0)
-    one(1)
-    own.wait()
-    for i in range(count + 3):
-        if i < count:
-            two(i)
-        if i + 2 < count:
-            one(i + 2)
-        if 0 <= i - 1 < count:
-            three(i - 1)
-        if 0 <= i - 2 < count:
-            four(i - 2)
-        if 0 <= i - 3 < count:
-            five(i - 3)
-            if i == 3:
-                low = w_query.shape[1] + LANES
-                load = pltpu.make_async_copy(
-                    full.at[:, :, :, :, low : low + LANES], columns, column_sem
-                )
-                load.start()
-                load.wait()
-                flat = columns[...].reshape(gains.shape[1], LANES).astype(F32)
-                gains[...] = flat.T[: gains.shape[0], :]
-    for copy in started:
-        copy.wait_send()
-
-
-def spread(w_query, w_key, w_value, w_out, w_gate, w_up, w_down, extras, ident):
-    depth, mix = w_query.shape
-    hidden = w_gate.shape[1]
+        n = counts[level]
+        for t in range(hidden // LANES):
+            cut = slice(t * LANES, (t + 1) * LANES)
+            gate_part = parts[:, cut]
+            up_part = parts[:, hidden + t * LANES : hidden + (t + 1) * LANES]
+            hidden_v[:n, cut] = (gate_part * sigmoid(gate_part) * up_part).astype(BF)
+        hidden_now = hidden_v[:n, :]
+        last.start(lambda c: dot_nt(hidden_now, chunk_of(c, base_d, base_d + hidden)))
+        for base in ("attn", "second", "parts"):
+            keep(f"{base}_{level}")
+        gate = sigmoid(jnp.sum(level_rows * gains[2:3, :], axis=-1, keepdims=True))
+        last.middle()
+        ffn = last.finish()
+        name("ffn")[...] = ffn
+        keep(f"ffn_{level}")
+        update = (gate * (attn.astype(F32) + ffn.astype(F32))).astype(BF)
+        if level:
+            update = dot_tn(held[f"pick_{level}"][...], update)
+        held["state"][...] = held["state"][...] + update.astype(F32)
+
+    steps = len(groups) + 6
+    done = [upto]
+
+    def beside(count):
+        for _ in range(count):
+            if done[0] < steps:
+                spread.step(done[0])
+                done[0] += 1
+
+    project(0, tokens[...])
+    held["state"][...] = tokens[...].astype(F32)
+    for name in ("place_0", "pick_1", "pick_2", "place_1", "place_2", "cosine_1", "sine_1", "cosine_2", "sine_2", "keys_1", "keys_2"):
+        keep(name)
+    for b in range(devices // group_of(0)):
+        beside(1)
+
+        @pl.when(b * group_of(0) <= me)
+        def _(b=b):
+            block(0, b)
+
+    mix_heads(0)
+    feed(0, beside)
+    keep("weights")
+    for level in range(1, len(counts)):
+        now = dot_nn(held[f"pick_{level}"][...], held["state"][...].astype(BF)).astype(BF)
+        project(level, now)
+
+        def one_block(b, carry, level=level):
+            block(level, b)
+            return carry
+
+        lax.fori_loop(0, me // group_of(level) + 1, one_block, 0)
+        mix_heads(level)
+        feed(level, lambda count: None)
+    keep("state")
+    spread.drain()
+    for item in sums:
+        item.drain()
+    for level in range(len(counts)):
+
+        def sent(e, carry, level=level):
+            kv_copy(level, e, me).wait_send()
+            return carry
+
+        lax.fori_loop(me + 1, devices, sent, 0)
+    for copy in keeps:
+        copy.wait()
+
+
+def advance(tokens, depths, second_slot, third_slot, matrices, vectors, tables, heads, devices, mp, ident):
+    counts = (tokens.shape[0], SECOND_SLOTS, THIRD_SLOTS)
+    rows, model = tokens.shape
+    depth, mix = matrices[0].shape
+    hidden = matrices[4].shape[1]
     total = 2 * mix + 2 * LANES + 3 * hidden
     cuts = [0, mix + 2 * LANES]
     while cuts[-1] < total:
@@ -809,27 +854,57 @@
     if cuts[-1] - cuts[-2] < 256:
         cuts.pop(-2)
     groups = [(a, b, i % 2) for i, (a, b) in enumerate(zip(cuts[:-1], cuts[1:]))]
-    return pl.pallas_call(
-        functools.partial(spread_kernel, groups),
-        out_shape=(
-            jax.ShapeDtypeStruct((4, 4, 2, depth, total), BF),
-            jax.ShapeDtypeStruct((8, 32 * depth), F32),
-        ),
-        in_specs=vmem(8),
-        out_specs=(pl.BlockSpec(memory_space=pl.ANY), pl.BlockSpec(memory_space=pltpu.VMEM)),
-        scratch_shapes=[
+    shapes = {
+        "state": ((rows, model), F32),
+        "weights": ((4, 4, 2, depth, total), BF),
+        "gains": ((8, model), F32),
+    }
+    for level, n in enumerate(counts):
+        width = heads * n
+        shapes[f"place_{level}"] = ((1, width), F32)
+        if level:
+            shapes[f"pick_{level}"] = ((n, rows), BF)
+            shapes[f"cosine_{level}"] = ((n, LANES), F32)
+            shapes[f"sine_{level}"] = ((n, LANES), F32)
+            shapes[f"keys_{level}"] = ((devices, n, LANES), F32)
+        for base in ("rows", "normed", "attn", "ffn", "second"):
+            shapes[f"{base}_{level}"] = ((n, model), BF)
+        shapes[f"parts_{level}"] = ((n, 2 * hidden), F32)
+        shapes[f"packed_{level}"] = ((devices, n, 2 * HD), BF)
+        shapes[f"query_{level}"] = ((width, 2 * HD), BF)
+        shapes[f"mixed_t_{level}"] = ((2 * HD, width), F32)
+        shapes[f"log_{level}"] = ((1, width), F32)
+        shapes[f"mixed_{level}"] = ((n, mix), BF)
+    names = tuple(shapes)
+    args = (tokens, depths, second_slot, third_slot, *matrices, *vectors, *tables)
+    width = heads * rows
+    outs = pl.pallas_call(
+        functools.partial(advance_kernel, counts, heads, devices, mp, hidden, groups, names),
+        out_shape=tuple(jax.ShapeDtypeStruct(*shapes[name]) for name in names),
+        in_specs=vmem(len(args)),
+        out_specs=tuple([pl.BlockSpec(memory_space=pl.ANY)] * len(names)),
+        scratch_shapes=[pltpu.VMEM(*shapes[name]) for name in names]
+        + [
             pltpu.VMEM((depth, total), BF),
-            pltpu.VMEM((4, 4, 2, depth, LANES), BF),
-            pltpu.SemaphoreType.DMA(()),
             pltpu.SemaphoreType.DMA(()),
             pltpu.SemaphoreType.DMA((len(groups), 8)),
             pltpu.SemaphoreType.DMA((len(groups), 8)),
-        ],
+            pltpu.VMEM((2 * HD, width), BF),
+            pltpu.VMEM((1, width), F32),
+            pltpu.VMEM((1, width), F32),
+            pltpu.VMEM((2 * HD, width), F32),
+            pltpu.VMEM((rows, hidden), BF),
+            pltpu.SemaphoreType.DMA((len(names),)),
+            pltpu.SemaphoreType.DMA((len(counts), devices)),
+            pltpu.SemaphoreType.DMA((len(counts), devices)),
+        ]
+        + [item for n in counts for _ in range(2) for item in sum_scratch(mp, n, model)],
         compiler_params=pltpu.CompilerParams(
             collective_id=ident, has_side_effects=True, vmem_limit_bytes=VMEM_LIMIT
         ),
-        name="spread",
-    )(w_query, w_key, w_value, w_out, w_gate, w_up, w_down, extras)
+        name="advance",
+    )(*args)
+    return dict(zip(names, outs))
 
 
 SLOTS = 6
@@ -1056,9 +1131,9 @@
             if low + middle_cut < high:
                 up_out[:, low + middle_cut - hidden : high - hidden] = value[:, middle_cut:]
         elif section == 1:
-            down_out[low:high, :] = value.T
+            down_out[:, low:high] = value
         elif section == 2:
-            out_out[low:high, :] = value.T
+            out_out[:, low:high] = value
         elif section == 3:
             if low < mix:
                 q_out[:, low : min(high, mix)] = value[:, : min(high, mix) - low]
@@ -1096,7 +1171,7 @@
     def one_block(b):
         part = packed[b * group : (b + 1) * group].reshape(group * n, 2 * HD)
         scores = dot_nn(part, query_t[...])
-        place = lax.broadcasted_iota(jnp.int32, (group * n, LANES), 0) + b * (group * n)
+        place = (lax.broadcasted_iota(jnp.int32, (group * n, LANES), 0) + b * (group * n)).astype(F32)
         place = jnp.concatenate([place] * (width // LANES), axis=1)
         scores = jnp.where(place <= query_place[...], scores, NEG)
         weights = jnp.exp(scores - log_total[...])
@@ -1133,10 +1208,9 @@
     outs.append(lax.fori_loop(me + 1, devices, add, send_buf[me].astype(F32)))
     low = spans[3][0]
     for t, part in enumerate(outs):
-        cut = slice(t * LANES, (t + 1) * LANES)
-        rights[0:n, low + t * LANES : low + (t + 1) * LANES] = (
-            part * cosine[:, cut] - swap_halves(part) * sine[:, cut]
-        ).astype(BF)
+        rights[0:n, low + t * LANES : low + (t + 1) * LANES] = turn_back(
+            part, cosine[...], sine[...], t == heads // 2
+        )
     load_w.wait()
     grad_now = rights[0:n, low : spans[3][1]]
     chunk = w_qkv.shape[0] // mp
@@ -1248,10 +1322,10 @@
             jax.ShapeDtypeStruct((depth, mix), F32),
             jax.ShapeDtypeStruct((depth, HD), F32),
             jax.ShapeDtypeStruct((depth, HD), F32),
-            jax.ShapeDtypeStruct((mix, depth), F32),
+            jax.ShapeDtypeStruct((depth, mix), F32),
             jax.ShapeDtypeStruct((depth, hidden), F32),
             jax.ShapeDtypeStruct((depth, hidden), F32),
-            jax.ShapeDtypeStruct((hidden, depth), F32),
+            jax.ShapeDtypeStruct((depth, hidden), F32),
             jax.ShapeDtypeStruct((depth, LANES), F32),
         ),
         in_specs=vmem(len(whole)) + [pl.BlockSpec(memory_space=pl.ANY)] * (len(args) - len(whole)),
@@ -1289,15 +1363,13 @@
     )(*args)
 
 
-def rotary_tables(place, heads):
+def rotary_tables(place):
     freq = jnp.exp(jnp.arange(HD // 2, dtype=F32) * (-2.0 * math.log(ROPE_BASE) / HD))
     angle = place.astype(F32)[:, None] * freq[None, :]
     cosine, sine = jnp.cos(angle), jnp.sin(angle)
-    one = jnp.concatenate([cosine, cosine], axis=1)
-    two = jnp.concatenate([-sine, sine], axis=1)
     return (
-        jnp.concatenate([jnp.tile(one, (1, heads + 1)), jnp.ones(one.shape, F32)], axis=1),
-        jnp.concatenate([jnp.tile(two, (1, heads + 1)), jnp.zeros(one.shape, F32)], axis=1),
+        jnp.concatenate([cosine] * 4, axis=1),
+        jnp.concatenate([-sine, sine, -sine, sine], axis=1),
     )
 
 
@@ -1311,71 +1383,29 @@
     heads = w_query.shape[1] // HD
     hidden_width = w_gate.shape[1]
     depth = w_query.shape[0]
-
-    picks, marks = [], []
-    for active, slot, capacity in (
-        ((depths >= 2) & (second_slot >= 0), second_slot, SECOND_SLOTS),
-        ((depths >= 3) & (third_slot >= 0), third_slot, THIRD_SLOTS),
-    ):
-        pick = (jnp.arange(capacity)[:, None] == slot[None, :]) & active[None, :]
-        picks.append(pick.astype(BF))
-        marks.append(
-            jnp.min(jnp.where(pick, jnp.arange(rows, dtype=jnp.int32)[None, :], rows), axis=1)
-        )
-
-    def column(values):
-        return values.reshape(depth, 1).astype(BF)
-
-    second_mark = jnp.pad(marks[0], (0, 2 * depth - SECOND_SLOTS), constant_values=rows)
-    extras = jnp.concatenate(
-        [
-            column(norm_first), column(norm_second), column(router),
-            column(second_mark[:depth]), column(second_mark[depth:]), column(marks[1]),
-            jnp.zeros((depth, LANES - 6), BF),
-        ],
-        axis=1,
+    home = rotary_tables(jnp.arange(rows, dtype=jnp.int32) + me * rows)
+
+    def row(values):
+        return values.reshape(1, -1)
+
+    kept = advance(
+        tokens, row(depths), row(second_slot), row(third_slot),
+        (w_query, w_key, w_value, w_out.T, w_gate, w_up, w_down.T),
+        (row(norm_first), row(norm_second), row(router)), home, heads, devices, mp, 0,
     )
-    weights, gains = spread(w_query, w_key, w_value, w_out, w_gate, w_up, w_down, extras, 13)
-    weights = weights.reshape(devices * depth, -1)
-    marks_all = gains[3:6].astype(jnp.int32).reshape(3, devices, depth)
-    second_all = jnp.concatenate(
-        [marks_all[0], marks_all[1, :, : SECOND_SLOTS - depth]], axis=1
-    )
-    base = (jnp.arange(devices, dtype=jnp.int32) * rows)[:, None]
-
-    def place_of(mark, offset):
-        return jnp.where(mark < rows, mark + offset, FAR)
-
-    def key_column(mark):
-        return jnp.broadcast_to(place_of(mark, base).reshape(-1, 1), (mark.size, LANES))
-
-    levels = (
-        (rows, None, jnp.arange(rows, dtype=jnp.int32) + me * rows, None),
-        (SECOND_SLOTS, picks[0], place_of(marks[0], me * rows), key_column(second_all)),
-        (THIRD_SLOTS, picks[1], place_of(marks[1], me * rows), key_column(marks_all[2])),
-    )
-    state = tokens
-    kept = []
-    for index, (count, pick, place, key_place) in enumerate(levels):
-        tables = rotary_tables(jnp.where(place == FAR, 0, place), heads)
-        query_place = jnp.tile(place, heads)[None, :]
-        rows_in, normed, packed, query, mixed_t, log_total, mixed = attend(
-            state, pick, key_place, query_place, gains, tables, weights, heads, devices, count, index
-        )
-        attn, ffn, second, parts, state = feed(
-            state, rows_in, mixed, pick, gains, weights, hidden_width, mp, count, 3 + index
-        )
-        kept.append(
-            (pick, key_place, query_place, tables, rows_in, normed, packed, query, mixed_t, log_total, mixed,
-             attn, ffn, second, parts)
-        )
-
+    weights = kept["weights"].reshape(devices * depth, -1)
+    gains = kept["gains"]
     flow = cotangent
     tail = None
     terms, vectors, second_vecs = [], [], []
     for index in (2, 1, 0):
-        (pick, key_place, query_place, tables, rows_in, normed, packed, query, mixed_t, log_total, mixed,
-         attn, ffn, second, parts) = kept[index]
+        query_place, rows_in, normed, packed, query, mixed_t, log_total, mixed, attn, ffn, second, parts = [
+            kept[f"{base}_{index}"]
+            for base in (
+                "place", "rows", "normed", "packed", "query", "mixed_t", "log", "mixed", "attn", "ffn", "second", "parts"
+            )
+        ]
+        pick = kept[f"pick_{index}"] if index else None
         head = (rows_in, attn, ffn, second, parts, pick)
         outs = list(
             feed_back(flow, gains, tail, head, weights, hidden_width, heads * HD, mp, 6 + index)
@@ -1389,20 +1419,21 @@
         items = (second, parts_grad, grad_ffn, hidden, grad_attn, mixed, normed)
         if index:
             grad_qkv = attend_back(
-                key_place, query_place, query, packed, mixed_t, log_total, grad_mixed, tables,
+                kept[f"keys_{index}"].reshape(-1, LANES), query_place, query, packed, mixed_t, log_total,
+                grad_mixed, (kept[f"cosine_{index}"], kept[f"sine_{index}"]),
                 heads, devices, rows_in.shape[0], 10 + index,
             )
             tail = (grad_qkv, rows_in, grad_middle, logit, pick)
             items = items + (grad_qkv,)
         terms.append(items)
-    attention = (query_place, query, packed, mixed_t, log_total, grad_mixed, *tables)
+    attention = (query_place, query, packed, mixed_t, log_total, grad_mixed, *home)
     vecs = [jnp.concatenate(list(part), axis=0) for part in (second_vecs, *zip(*vectors))]
     flow, query_grad, key_grad, value_grad, out_grad, gate_grad, up_grad, down_grad, vec = finish(
         flow, gains, attention, (rows_in, grad_middle, logit), vecs, weights, terms[::-1],
         heads, devices, mp, depth, 14,
     )
     return (
-        state, flow, query_grad, key_grad, value_grad, out_grad, gate_grad, up_grad, down_grad,
+        kept["state"], flow, query_grad, key_grad, value_grad, out_grad.T, gate_grad, up_grad, down_grad.T,
         vec[:, 0], vec[:, 1], vec[:, 2],
     )
 

time: 559 us -> 485 us (0.87); the launches traced: 550 us -> 482 us
  Pallas kernels: 510 us -> 467 us
  local copies, waits for them, and re-layouts: 28 us -> 9.68 us
    pallas_call x7 -> x1, Pallas kernels: 262 us -> 207 us  [advance(): pl.pallas_call(functools.partial(advance_kernel, counts, heads, devices,...]
    pallas_call x2, Pallas kernels: 35.7 us -> 49.1 us  [attend_back(): pl.pallas_call(functools.partial(attend_back_kernel, n, heads, devices, g...]
    unnamed x35 -> x33, local copies, waits for them, and re-layouts: 11.8 us -> 8.06 us
where the time goes in v5:
time: 485 us; the launch traced here: 482 us
  Pallas kernels  467 us (96%)
  local copies, waits for them, and re-layouts  9.68 us (2%)
  other arithmetic  5.13 us (1%)
    pallas_call x1, Pallas kernels, advance(): pl.pallas_call(functools.partial(advance_kernel, counts, heads, devices,...  207 us
    pallas_call x3, Pallas kernels, feed_back(): pl.pallas_call(functools.partial(feed_back_kernel, tail_n, head_n, mp, ta...  106 us
    pallas_call x1, Pallas kernels, finish(): pl.pallas_call(functools.partial(finish_kernel, n, heads, devices, mp, gr...  104 us
    pallas_call x2, Pallas kernels, attend_back(): pl.pallas_call(functools.partial(attend_back_kernel, n, heads, devices, g...  49.1 us

profile of v5, /device:TPU:0, one launch (start us, length us, event | category | flops | bytes accessed | tf_op | source)
XLA Modules:
  0.0 482.4 jit_solution(5535974706980240470)
XLA Ops:
  0.7 0.3 fusion
  1.0 0.8 pad_maximum_fusion
  1.8 207.2 %advance.1 = (f32[128,2048]{1,0:T(8,128)}, bf16[4,4,2,64,5504]{4,3,2,1,0:T(8,128)(2,1)}, f32[8,2048]{1,0:T(8,128)}, f32[1,1024]{1,0:T(1,128)}, bf16[128,2048]{1,...) custom-call(bf16[128,2048]{1,0:T(8,128)(2,1)} %refs_0_.3, ...), custom_call_target="tpu_custom_call" | custom-call | tf_op jit(solution)/shard_map/advance/pallas_call | solution.py:881
  209.0 20.9 %feed_back_0_64.1 = (bf16[64,2048]{1,0:T(8,128)(2,1)}, f32[64,2048]{1,0:T(8,128)}, f32[64,1]{1,0:T(8,128)}, bf16[64,512]{1,0:T(8,128)(2,1)}, bf16[64,2816]{1,0:T...) custom-call(f32[128,2048]{1,0:T(8,128)} %refs_0_.5, ...), custom_call_target="tpu_custom_call" | custom-call | flops 5000000000 | bytes 100000000 | tf_op jit(solution)/shard_map/feed_back_0_64/pallas_call | solution.py:410
  230.0 29.5 %attend_back_64.1.refs_2_.refs_39_ = bf16[64,640]{1,0:T(8,128)(2,1)} custom-call(f32[2048,128]{1,0:T(8,128)} %bitcast.30, f32[1,512]{1,0:T(1,128)} %get-tuple-element.101.refs_1_, bf16[512,128]{1,0:T(8,128)(2,1)} %get-tuple-element.102.refs_2_, bf16[32,64,128]{2,1,0:T(8,128)(2,1)} %get-tuple-element.103.refs_3_, f32[128,512]{1,0:T(8,128)} %get-tuple-element.104.refs_4_, ...), custom_call_target="tpu_custom_call" | custom-call | flops 10000000000 | bytes 10000000 | tf_op jit(solution)/shard_map/attend_back_64/pallas_call | solution.py:217
  259.5 38.7 %feed_back_64_96.1 = (f32[128,2048]{1,0:T(8,128)}, f32[1,2048]{1,0:T(1,128)}, f32[1,2048]{1,0:T(1,128)}, bf16[96,2048]{1,0:T(8,128)(2,1)}, f32[96,2048]{1,0:T(8,...) custom-call(f32[128,2048]{1,0:T(8,128)} %refs_0_.5, ...), custom_call_target="tpu_custom_call" | custom-call | flops 5000000000 | bytes 100000000 | tf_op jit(solution)/shard_map/feed_back_64_96/pallas_call | solution.py:410
  298.2 19.6 %attend_back_96.1.refs_2_.refs_31_ = bf16[96,640]{1,0:T(8,128)(2,1)} custom-call(f32[3072,128]{1,0:T(8,128)} %bitcast.29, f32[1,768]{1,0:T(1,128)} %get-tuple-element.126.refs_1_, bf16[768,128]{1,0:T(8,128)(2,1)} %get-tuple-element.127.refs_2_, bf16[32,96,128]{2,1,0:T(8,128)(2,1)} %get-tuple-element.128.refs_3_, f32[128,768]{1,0:T(8,128)} %get-tuple-element.129.refs_4_, ...), custom_call_target="tpu_custom_call" | custom-call | flops 10000000000 | bytes 10000000 | tf_op jit(solution)/shard_map/attend_back_96/pallas_call | solution.py:217
  317.7 0.0 copy-start.11
  317.8 0.0 copy-start.10
  317.8 0.0 copy-start.8
  317.8 0.0 copy-start.9
  317.8 46.4 %feed_back_96_128.1 = (f32[128,2048]{1,0:T(8,128)}, f32[1,2048]{1,0:T(1,128)}, f32[1,2048]{1,0:T(1,128)}, bf16[128,2048]{1,0:T(8,128)(2,1)}, f32[128,2048]{1,0:T...) custom-call(f32[128,2048]{1,0:T(8,128)} %get-tuple-element.124.refs_, ...), custom_call_target="tpu_custom_call" | custom-call | flops 5000000000 | bytes 100000000 | tf_op jit(solution)/shard_map/feed_back_96_128/pallas_call | solution.py:410
  364.2 0.0 copy-done.11
  364.2 1.3 pad_maximum_fusion.3.refs_14_
  365.6 0.0 copy-done.10
  365.6 1.3 pad_maximum_fusion.4.refs_15_
  366.9 0.0 copy-done.8
  366.9 0.0 copy-done.9
  366.9 1.3 pad_maximum_fusion.2.refs_13_
  368.2 104.2 %finish.1 = (f32[128,2048]{1,0:T(8,128)}, f32[64,512]{1,0:T(8,128)}, f32[64,64]{1,0:T(8,128)}, f32[64,64]{1,0:T(8,128)}, f32[64,512]{1,0:T(8,128)}, /*index=5*/f...) custom-call(f32[128,2048]{1,0:T(8,128)} %get-tuple-element.141.refs_0_, ...), custom_call_target="tpu_custom_call" | custom-call | tf_op jit(solution)/shard_map/finish/pallas_call | solution.py:1318
  472.4 0.0 copy-start
  472.4 1.6 slice_reduce_fusion
  474.0 2.3 copy.37
  476.3 0.0 copy-done
  476.3 0.0 copy-start.5
  476.3 0.0 copy-start.7
  476.4 0.0 copy-start.6
  476.4 0.0 copy-start.4
  476.4 0.0 copy-start.3
  476.4 0.0 copy-start.2
  476.4 1.0 copy.38
  477.4 0.0 copy-done.5
  477.4 0.0 copy-start.1
  477.4 0.7 copy.39
  478.0 0.0 copy-done.7
  478.0 0.6 copy.40
  478.6 0.0 copy-done.6
  478.6 0.6 copy.41
  479.3 0.0 copy-done.4
  479.3 0.7 copy.42
  479.9 0.0 copy-done.3
  479.9 0.7 copy.43
  480.7 0.0 copy-done.2
  480.7 0.7 copy.44
  481.4 0.0 copy-done.1
  481.4 0.7 copy.45
  (2 shorter events, 0.0 us)
Async XLA Ops:
  317.7 46.5 %copy-start.11 = (f32[1,2048]{1,0:T(1,128)S(1)}, f32[1,2048]{1,0:T(1,128)}, u32[]{:S(2)}) copy-start(f32[1,2048]{1,0:T(1,128)} %get-tuple-element.153) | copy-start | bytes 24580
  317.8 47.8 %copy-start.10 = (f32[1,2048]{1,0:T(1,128)S(1)}, f32[1,2048]{1,0:T(1,128)}, u32[]{:S(2)}) copy-start(f32[1,2048]{1,0:T(1,128)} %get-tuple-element.155) | copy-start | bytes 24580
  317.8 49.1 %copy-start.8 = (f32[1,2048]{1,0:T(1,128)S(1)}, f32[1,2048]{1,0:T(1,128)}, u32[]{:S(2)}) copy-start(f32[1,2048]{1,0:T(1,128)} %get-tuple-element.150) | copy-start | bytes 24580
  317.8 49.1 %copy-start.9 = (f32[1,2048]{1,0:T(1,128)S(1)}, f32[1,2048]{1,0:T(1,128)}, u32[]{:S(2)}) copy-start(f32[1,2048]{1,0:T(1,128)} %get-tuple-element.151) | copy-start | bytes 24580
  472.4 3.9 copy-start
  476.3 1.0 copy-start.5
  476.3 1.7 copy-start.7
  476.4 2.3 copy-start.6
  476.4 2.9 copy-start.4
  476.4 3.5 copy-start.3
  476.4 4.3 copy-start.2
  477.4 4.0 copy-start.1

commit v6 on v5

--- a/solution.py
+++ b/solution.py
@@ -76,349 +76,373 @@
     pl.semaphore_wait(barrier, group - 1)
 
 
-def sum_over_mp(group, me, make_chunk, send, recv, full, sems):
+PIECES = 2
+
+
+class Sum:
     order = (2, 1, 3)
-    copies = []
-    for k in order:
-        peer = lax.rem(me + k, group)
-        send[k - 1] = make_chunk(peer).astype(BF)
+
+    def __init__(self, group, me, send, recv, full, sems):
+        self.group, self.me, self.send, self.recv, self.full, self.sems = group, me, send, recv, full, sems
+        self.wide = send.shape[-1]
+
+    def remote(self, source, target, stage, k, piece):
         copy = pltpu.make_async_remote_copy(
-            src_ref=send.at[k - 1], dst_ref=recv.at[k - 1],
-            send_sem=sems.at[0, k - 1], recv_sem=sems.at[1, k - 1],
-            device_id={"mp": peer}, device_id_type=MESH,
+            src_ref=source, dst_ref=target, send_sem=self.sems.at[stage, k - 1, piece],
+            recv_sem=self.sems.at[stage + 1, k - 1, piece],
+            device_id={"mp": lax.rem(self.me + k, self.group)}, device_id_type=MESH,
         )
         copy.start()
-        copies.append(copy)
-    total = make_chunk(me).astype(BF).astype(F32)
-    for k, copy in zip(order, copies):
-        copy.wait_recv()
-        total = total + recv[k - 1].astype(F32)
-    full[me] = total.astype(BF)
-    backs = []
-    for k in order:
-        peer = lax.rem(me + k, group)
-        copy = pltpu.make_async_remote_copy(
-            src_ref=full.at[me], dst_ref=full.at[me],
-            send_sem=sems.at[2, k - 1], recv_sem=sems.at[3, k - 1],
-            device_id={"mp": peer}, device_id_type=MESH,
-        )
-        copy.start()
-        backs.append(copy)
-    for copy in backs:
-        copy.wait_recv()
-    for copy in copies + backs:
-        copy.wait_send()
-    return jnp.concatenate([full[c] for c in range(group)], axis=1)
+        return copy
+
+    def start(self, make_piece):
+        self.make, self.out, self.back = make_piece, [], []
+        for piece in range(PIECES):
+            copies = []
+            for k in self.order:
+                at = (k - 1, piece)
+                self.send[at] = self.part(lax.rem(self.me + k, self.group), piece).astype(BF)
+                copies.append(self.remote(self.send.at[at], self.recv.at[at], 0, k, piece))
+            self.out.append(copies)
+
+    def part(self, c, piece):
+        start = c * (PIECES * self.wide) + piece * self.wide
+        return self.make(pl.multiple_of(start, self.wide), self.wide)
+
+    def middle(self):
+        for piece in range(PIECES):
+            total = self.part(self.me, piece).astype(BF).astype(F32)
+            for k, copy in zip(self.order, self.out[piece]):
+                copy.wait_recv()
+                total = total + self.recv[k - 1, piece].astype(F32)
+            self.full[self.me, piece] = total.astype(BF)
+            where = self.full.at[self.me, piece]
+            self.back.append([self.remote(where, where, 2, k, piece) for k in self.order])
+
+    def finish(self):
+        for copies in self.back:
+            for copy in copies:
+                copy.wait_recv()
+        return jnp.concatenate(
+            [self.full[c, piece] for c in range(self.group) for piece in range(PIECES)], axis=1
+        )
+
+    def drain(self):
+        for copies in self.out + self.back:
+            for copy in copies:
+                copy.wait_send()
 
 
 def vmem(count):
     return [pl.BlockSpec(memory_space=pltpu.VMEM)] * count
 
 
-def attend_back_kernel(n, heads, devices, group, picked, *refs):
+def sum_scratch(mp, n, model):
+    wide = model // mp // PIECES
+    return [
+        pltpu.VMEM((mp - 1, PIECES, n, wide), BF),
+        pltpu.VMEM((mp - 1, PIECES, n, wide), BF),
+        pltpu.VMEM((mp, PIECES, n, wide), BF),
+        pltpu.SemaphoreType.DMA((4, mp - 1, PIECES)),
+    ]
+
+
+def retreat_kernel(counts, heads, devices, mp, hidden, ins, names, *refs):
     refs = list(refs)
-    key_place = refs.pop(0) if picked else None
-    query_place, query, packed, mixed_t, log_total, grad_mixed, cosine, sine = [
-        refs.pop(0) for _ in range(8)
-    ]
-    grad_out = refs.pop(0)
-    query_t, grad_rows, grad_t, acc, delta, send_buf, recv_buf, send_sems, recv_sems = refs
-    me = lax.axis_index("dp")
+    sources = {name: refs.pop(0) for name in ins}
+    w_hbm = refs.pop(0)
+    outs = {name: refs.pop(0) for name in names}
+    held = {name: refs.pop(0) for name in ins}
+    held.update({name: refs.pop(0) for name in names})
+    w_qkv, w_o, w_gu, w_d, fetch_sems, w_sems, keep_sems = [refs.pop(0) for _ in range(7)]
+    query_t, grad_rows, grad_t, acc, delta = [refs.pop(0) for _ in range(5)]
+    buffers = {level: [refs.pop(0) for _ in range(4)] for level in (1, 2)}
+    sum_refs = {key: [refs.pop(0) for _ in range(4)] for key in ("head_2", "tail_2", "head_1", "tail_1", "head_0")}
+    me, mp_me = lax.axis_index("dp"), lax.axis_index("mp")
+    model = w_o.shape[0]
+    mix = heads * HD
+    loads, keeps = {}, []
+
+    def fetch(name):
+        loads[name] = pltpu.make_async_copy(sources[name], held[name], fetch_sems.at[ins.index(name)])
+        loads[name].start()
+
+    def load(name, ref, start, index):
+        loads[name] = pltpu.make_async_copy(w_hbm.at[:, start : start + ref.shape[1]], ref, w_sems.at[index])
+        loads[name].start()
+
+    def get(name):
+        if name in loads:
+            loads.pop(name).wait()
+        return held[name]
+
+    def need(name):
+        if name in loads:
+            loads.pop(name).wait()
+
+    def keep(name):
+        copy = pltpu.make_async_copy(held[name], outs[name], keep_sems.at[len(keeps)])
+        copy.start()
+        keeps.append(copy)
+
+    base_o = mix + 2 * LANES
+    for name in ("flow", "gains", "pick_2", "rows_2", "attn_2", "ffn_2", "parts_2"):
+        fetch(name)
+    load("d", w_d, base_o + mix + 2 * hidden, 0)
+    load("gu", w_gu, base_o + mix, 1)
+    load("o", w_o, base_o, 2)
+    load("qkv", w_qkv, 0, 3)
+    for name in ins:
+        if name not in loads:
+            fetch(name)
+
     barrier = pltpu.get_barrier_semaphore()
 
-    def greet(e, carry):
-        pl.semaphore_signal(barrier, inc=1, device_id={"dp": e}, device_id_type=MESH)
+    def greet(k, carry):
+        pl.semaphore_signal(
+            barrier, inc=1, device_id={"dp": lax.rem(me + k, devices)}, device_id_type=MESH
+        )
         return carry
 
-    lax.fori_loop(me + 1, devices, greet, 0)
-
-    left = lanes_of((n, LANES)) < HD
-    for t in range(heads // 2):
-        part = grad_mixed[:, t * LANES : (t + 1) * LANES].astype(F32)
-        grad_rows[2 * t * n : (2 * t + 1) * n, :] = jnp.where(
-            left, 0.0, pltpu.roll(part, HD, 1)
-        ).astype(BF)
-        grad_rows[(2 * t + 1) * n : (2 * t + 2) * n, :] = jnp.where(left, 0.0, part).astype(BF)
-    query_t[...] = query[...].T
-    grad_t[...] = grad_rows[...].T
-    delta[...] = jnp.sum(grad_t[...].astype(F32) * mixed_t[...], axis=0, keepdims=True)
-    acc[...] = jnp.zeros(acc.shape, F32)
-    width = heads * n
-
-    @pl.when(me > 0)
-    def _():
-        pl.semaphore_wait(barrier, me)
-
-    def send_copy(e, source_index):
-        return pltpu.make_async_remote_copy(
-            src_ref=send_buf.at[e], dst_ref=recv_buf.at[source_index],
-            send_sem=send_sems.at[e], recv_sem=recv_sems.at[source_index],
-            device_id={"dp": e}, device_id_type=MESH,
-        )
-
-    def one_block(b, carry):
-        part = packed[pl.ds(b * group, group)].reshape(group * n, 2 * HD)
-        scores = dot_nn(part, query_t[...])
-        if picked:
-            start = pl.multiple_of(b * (group * n), group * n)
-            place = key_place[pl.ds(start, group * n), :]
-        else:
-            place = (lax.broadcasted_iota(jnp.int32, (group * n, LANES), 0) + b * (group * n)).astype(F32)
-        place = jnp.concatenate([place] * (width // LANES), axis=1)
-        scores = jnp.where(place <= query_place[...], scores, NEG)
-        weights = jnp.exp(scores - log_total[...])
-        grad_weights = dot_nn(part, grad_t[...])
-        grad_scores = (weights * (grad_weights - delta[...])).astype(BF)
-        grad_part = dot_nn(grad_scores, query[...]) + dot_nn(weights.astype(BF), grad_rows[...])
-        send_buf[pl.ds(b * group, group)] = grad_part.astype(BF).reshape(group, n, 2 * HD)
-        acc[...] += dot_tn(part, grad_scores)
-        for g in range(group):
-            e = b * group + g
-
-            @pl.when(e < me)
-            def _():
-                send_copy(e, me).start()
-
-        return carry
-
-    lax.fori_loop(0, me // group + 1, one_block, 0)
-
-    grad_query = acc[...].T * HD**-0.5
-    outs = []
-    for t in range(heads // 2):
-        even = grad_query[2 * t * n : (2 * t + 1) * n, :]
-        odd = grad_query[(2 * t + 1) * n : (2 * t + 2) * n, :]
-        outs.append(jnp.where(left, even, pltpu.roll(odd, HD, 1)))
-
-    def add(e, carry):
-        send_copy(me, e).wait_recv()
-        return carry + recv_buf[e].astype(F32)
-
-    outs.append(lax.fori_loop(me + 1, devices, add, send_buf[me].astype(F32)))
-    for t, part in enumerate(outs):
-        grad_out[:, t * LANES : (t + 1) * LANES] = turn_back(
-            part, cosine[...], sine[...], t == heads // 2
-        )
-
-    def sent(e, carry):
-        send_copy(e, me).wait_send()
-        return carry
-
-    lax.fori_loop(0, me, sent, 0)
-
-
-def attend_back(key_place, query_place, query, packed, mixed_t, log_total, grad_mixed, tables, heads, devices, n, ident):
-    picked = key_place is not None
-    group = 512 // n if 512 % n == 0 else 4
-    width = heads * n
-    args = ([key_place] if picked else []) + [
-        query_place, query, packed, mixed_t, log_total, grad_mixed, *tables
-    ]
-    return pl.pallas_call(
-        functools.partial(attend_back_kernel, n, heads, devices, group, picked),
-        out_shape=jax.ShapeDtypeStruct((n, (heads + 2) * HD), BF),
-        in_specs=vmem(len(args)),
-        out_specs=pl.BlockSpec(memory_space=pltpu.VMEM),
-        scratch_shapes=[
-            pltpu.VMEM((2 * HD, width), BF),
-            pltpu.VMEM((width, 2 * HD), BF),
-            pltpu.VMEM((2 * HD, width), BF),
-            pltpu.VMEM((2 * HD, width), F32),
-            pltpu.VMEM((1, width), F32),
-            pltpu.VMEM((devices, n, 2 * HD), BF),
-            pltpu.VMEM((devices, n, 2 * HD), BF),
-            pltpu.SemaphoreType.DMA((devices,)),
-            pltpu.SemaphoreType.DMA((devices,)),
-        ],
-        compiler_params=pltpu.CompilerParams(
-            collective_id=ident, has_side_effects=True, vmem_limit_bytes=VMEM_LIMIT
-        ),
-        cost_estimate=pl.CostEstimate(flops=10**10, bytes_accessed=10**7, transcendentals=0),
-        name=f"attend_back_{n}",
-    )(*args)
-
-
-def sum_scratch(mp, n, model):
-    return [
-        pltpu.VMEM((mp - 1, n, model // mp), BF),
-        pltpu.VMEM((mp - 1, n, model // mp), BF),
-        pltpu.VMEM((mp, n, model // mp), BF),
-        pltpu.SemaphoreType.DMA((4, mp - 1)),
-    ]
-
-
-def feed_back_kernel(tail_n, head_n, mp, tail_picked, head_picked, *refs):
-    refs = list(refs)
-    flow, gains = refs.pop(0), refs.pop(0)
-    if tail_n:
-        grad_qkv, tail_rows, tail_middle, tail_logit = [refs.pop(0) for _ in range(4)]
-        tail_pick = refs.pop(0) if tail_picked else None
-    if head_n:
-        rows_in, attn, ffn, second, parts = [refs.pop(0) for _ in range(5)]
-        head_pick = refs.pop(0) if head_picked else None
-    if tail_n:
-        w_first_hbm = refs.pop(0)
-    if head_n:
-        w_rest_hbm = refs.pop(0)
-    if tail_n:
-        flow_out, first_out, router_out = [refs.pop(0) for _ in range(3)]
-    if head_n:
-        attn_grad_out, middle_out, logit_out, mixed_out, parts_grad_out, hidden_out, ffn_grad_out, second_vec_out = [
-            refs.pop(0) for _ in range(8)
-        ]
-    if tail_n:
-        w_qkv, w_first_sem = refs.pop(0), refs.pop(0)
-        send_a, recv_a, full_a, sems_a = [refs.pop(0) for _ in range(4)]
-    if head_n:
-        w_o, w_gu, w_d, w_sems = [refs.pop(0) for _ in range(4)]
-        send_b, recv_b, full_b, sems_b = [refs.pop(0) for _ in range(4)]
-    me = lax.axis_index("mp")
-    if tail_n:
-        load_first = pltpu.make_async_copy(w_first_hbm.at[:, : w_qkv.shape[1]], w_qkv, w_first_sem)
-        load_first.start()
-    if head_n:
-        loads = {}
-        wide_o, wide_gu, wide_d = w_o.shape[1], w_gu.shape[1], w_d.shape[1]
-        for index, (name, ref, start) in enumerate(
-            (("d", w_d, wide_o + wide_gu), ("gu", w_gu, wide_o), ("o", w_o, 0))
-        ):
-            start += wide_o + 2 * LANES
-            loads[name] = pltpu.make_async_copy(
-                w_rest_hbm.at[:, start : start + ref.shape[1]], ref, w_sems.at[index]
-            )
-            loads[name].start()
-    signal_all(mp, me, "mp")
-
-    if tail_n:
-        load_first.wait()
-        grad_now = grad_qkv[...]
-        chunk = w_qkv.shape[0] // mp
-
-        def first_chunk(c):
-            return dot_nt(grad_now, w_qkv[pl.ds(pl.multiple_of(c * chunk, chunk), chunk), :])
-
-        grad_normed = sum_over_mp(mp, me, first_chunk, send_a, recv_a, full_a, sems_a).astype(F32)
-        level = tail_rows[...].astype(F32)
-        unit, factor = unit_of(level)
-        first_out[...] = jnp.sum(grad_normed * unit, axis=0, keepdims=True)
-        router_out[...] = jnp.sum(level * tail_logit[...], axis=0, keepdims=True)
-        grad_rows = (
-            unit_back(grad_normed * gains[0:1, :], unit, factor)
-            + tail_middle[...]
-            + tail_logit[...] * gains[2:3, :]
-        ).astype(BF)
-        if tail_picked:
-            flow_now = flow[...] + dot_tn(tail_pick[...], grad_rows)
-        else:
-            flow_now = flow[...] + grad_rows.astype(F32)
-        flow_out[...] = flow_now
-    else:
-        flow_now = flow[...]
-
-    if head_n:
-        grad_update = flow_now.astype(BF)
-        if head_picked:
-            grad_update = dot_nn(head_pick[...], grad_update)
+    lax.fori_loop(1, devices, greet, 0)
+    for k in range(1, mp):
+        pl.semaphore_signal(
+            barrier, inc=1, device_id={"mp": lax.rem(mp_me + k, mp)}, device_id_type=MESH
+        )
+    sums = {key: Sum(mp, mp_me, *items) for key, items in sum_refs.items()}
+    vecs = held["vecs"]
+    vecs[...] = jnp.zeros(vecs.shape, F32)
+    gate_of = {}
+
+    def head(level):
+        n = counts[level]
+        name = lambda base: held[f"{base}_{level}"]
+        grad_update = get("flow")[...].astype(BF)
+        if level:
+            grad_update = dot_nn(get(f"pick_{level}")[...], grad_update)
         grad_update = grad_update.astype(F32)
-        level = rows_in[...].astype(F32)
-        attn_now = attn[...].astype(F32)
-        gate = sigmoid(jnp.sum(level * gains[2:3, :], axis=-1, keepdims=True))
-        logit = jnp.sum(grad_update * (attn_now + ffn[...].astype(F32)), axis=-1, keepdims=True)
-        logit_out[...] = logit * gate * (1.0 - gate)
+        rows_now = get(f"rows_{level}")[...].astype(F32)
+        attn_now = get(f"attn_{level}")[...].astype(F32)
+        gains = get("gains")
+        gate = sigmoid(jnp.sum(rows_now * gains[2:3, :], axis=-1, keepdims=True))
+        logit = jnp.sum(
+            grad_update * (attn_now + get(f"ffn_{level}")[...].astype(F32)), axis=-1, keepdims=True
+        )
+        name("logit")[...] = logit * gate * (1.0 - gate)
         grad_ffn = (gate * grad_update).astype(BF)
-        ffn_grad_out[...] = grad_ffn
-        half = wide_d
-        loads["d"].wait()
-        for t in range(half // LANES):
+        name("grad_ffn")[...] = grad_ffn
+        parts, parts_grad, hidden_out = get(f"parts_{level}"), name("parts_grad"), name("hidden")
+        need("d")
+        for t in range(hidden // LANES):
             cut = slice(t * LANES, (t + 1) * LANES)
-            up_cut = slice(half + t * LANES, half + (t + 1) * LANES)
+            up_cut = slice(hidden + t * LANES, hidden + (t + 1) * LANES)
             if t % 2 == 0:
-                both = dot_nn(grad_ffn, w_d[:, t * LANES : min((t + 2) * LANES, half)])
+                both = dot_nn(grad_ffn, w_d[:, t * LANES : min((t + 2) * LANES, hidden)])
             grad_hidden = tile_of(both, t % 2)
             gate_part = parts[:, cut]
             up_part = parts[:, up_cut]
             sigma = sigmoid(gate_part)
             active = gate_part * sigma
             hidden_out[:, cut] = (active * up_part).astype(BF)
-            parts_grad_out[:, cut] = (
+            parts_grad[:, cut] = (
                 grad_hidden * up_part * sigma * (1.0 + gate_part * (1.0 - sigma))
             ).astype(BF)
-            parts_grad_out[:, up_cut] = (grad_hidden * active).astype(BF)
-        loads["gu"].wait()
-        parts_now = parts_grad_out[...]
-        chunk = w_gu.shape[0] // mp
-
-        def second_chunk(c):
-            return dot_nt(parts_now, w_gu[pl.ds(pl.multiple_of(c * chunk, chunk), chunk), :])
-
-        grad_second = sum_over_mp(mp, me, second_chunk, send_b, recv_b, full_b, sems_b).astype(F32)
-        unit, factor = unit_of(level + attn_now)
-        second_vec_out[...] = jnp.sum(grad_second * unit, axis=0, keepdims=True)
+            parts_grad[:, up_cut] = (grad_hidden * active).astype(BF)
+        need("gu")
+        if level == 2:
+            pl.semaphore_wait(barrier, devices - 1 + mp - 1)
+        parts_now = parts_grad[...]
+        total = sums[f"head_{level}"]
+        total.start(lambda start, wide: dot_nt(parts_now, w_gu[pl.ds(start, wide), :]))
+        for base in ("grad_ffn", "hidden", "parts_grad", "logit"):
+            keep(f"{base}_{level}")
+        unit, factor = unit_of(rows_now + attn_now)
+        total.middle()
+        grad_second = total.finish().astype(F32)
+        vecs[2 - level : 3 - level, :] = jnp.sum(grad_second * unit, axis=0, keepdims=True)
         grad_middle = unit_back(grad_second * gains[1:2, :], unit, factor)
-        middle_out[...] = grad_middle
+        name("middle")[...] = grad_middle
         grad_attn = (gate * grad_update + grad_middle).astype(BF)
-        attn_grad_out[...] = grad_attn
-        loads["o"].wait()
-        mixed_out[...] = dot_nn(grad_attn, w_o[...]).astype(BF)
-
-
-def feed_back(flow, gains, tail, head, weights, hidden_width, mix, mp, ident):
-    model = flow.shape[1]
-    args, outs, scratch = [flow, gains], [], []
-    tail_n = head_n = 0
-    tail_picked = head_picked = False
-    if tail is not None:
-        *items, pick = tail
-        tail_n, tail_picked = items[0].shape[0], pick is not None
-        args += items + ([pick] if tail_picked else [])
-    if head is not None:
-        *items, pick = head
-        head_n, head_picked = items[0].shape[0], pick is not None
-        args += items + ([pick] if head_picked else [])
-    in_vmem = len(args)
-    if tail_n:
-        args.append(weights)
-        outs += [
-            jax.ShapeDtypeStruct(flow.shape, F32),
-            jax.ShapeDtypeStruct((1, model), F32),
-            jax.ShapeDtypeStruct((1, model), F32),
+        name("grad_attn")[...] = grad_attn
+        need("o")
+        name("grad_mixed")[...] = dot_nn(grad_attn, w_o[...]).astype(BF)
+        for base in ("grad_attn", "middle", "grad_mixed"):
+            keep(f"{base}_{level}")
+
+    def attention(level):
+        n = counts[level]
+        group = 512 // n if 512 % n == 0 else 4
+        width = heads * n
+        send_buf, recv_buf, send_sems, recv_sems = buffers[level]
+        query, packed = get(f"query_{level}"), get(f"packed_{level}")
+        mixed_t, log_total = get(f"mixed_t_{level}"), get(f"log_{level}")
+        keys, query_place = get(f"keys_{level}"), get(f"place_{level}")
+        cosine, sine = get(f"cosine_{level}"), get(f"sine_{level}")
+        grad_mixed, grad_qkv = held[f"grad_mixed_{level}"], held[f"grad_qkv_{level}"]
+        left = lanes_of((n, LANES)) < HD
+        for t in range(heads // 2):
+            part = grad_mixed[:, t * LANES : (t + 1) * LANES].astype(F32)
+            grad_rows[2 * t * n : (2 * t + 1) * n, :] = jnp.where(
+                left, 0.0, pltpu.roll(part, HD, 1)
+            ).astype(BF)
+            grad_rows[(2 * t + 1) * n : (2 * t + 2) * n, :] = jnp.where(left, 0.0, part).astype(BF)
+        query_t[:, :width] = query[...].T
+        grad_t[:, :width] = grad_rows[:width, :].T
+        delta[:, :width] = jnp.sum(grad_t[:, :width].astype(F32) * mixed_t[...], axis=0, keepdims=True)
+        acc[:, :width] = jnp.zeros((2 * HD, width), F32)
+
+        def send_copy(e, source_index):
+            return pltpu.make_async_remote_copy(
+                src_ref=send_buf.at[e], dst_ref=recv_buf.at[source_index],
+                send_sem=send_sems.at[e], recv_sem=recv_sems.at[source_index],
+                device_id={"dp": e}, device_id_type=MESH,
+            )
+
+        def one_block(b, carry):
+            part = packed[pl.ds(b * group, group)].reshape(group * n, 2 * HD)
+            scores = dot_nn(part, query_t[:, :width])
+            place = keys[pl.ds(b * group, group)].reshape(group * n, LANES)
+            place = jnp.concatenate([place] * (width // LANES), axis=1)
+            scores = jnp.where(place <= query_place[...], scores, NEG)
+            soft = jnp.exp(scores - log_total[...])
+            grad_soft = dot_nn(part, grad_t[:, :width])
+            grad_scores = (soft * (grad_soft - delta[:, :width])).astype(BF)
+            grad_part = dot_nn(grad_scores, query[...]) + dot_nn(soft.astype(BF), grad_rows[:width, :])
+            send_buf[pl.ds(b * group, group)] = grad_part.astype(BF).reshape(group, n, 2 * HD)
+            acc[:, :width] += dot_tn(part, grad_scores)
+            for g in range(group):
+                e = b * group + g
+
+                @pl.when(e < me)
+                def _(e=e):
+                    send_copy(e, me).start()
+
+            return carry
+
+        lax.fori_loop(0, me // group + 1, one_block, 0)
+        grad_query = acc[:, :width].T * HD**-0.5
+        for t in range(heads // 2):
+            even = grad_query[2 * t * n : (2 * t + 1) * n, :]
+            odd = grad_query[(2 * t + 1) * n : (2 * t + 2) * n, :]
+            part = jnp.where(left, even, pltpu.roll(odd, HD, 1))
+            grad_qkv[:, t * LANES : (t + 1) * LANES] = turn_back(part, cosine[...], sine[...], False)
+
+        def add(e, carry):
+            send_copy(me, e).wait_recv()
+            return carry + recv_buf[e].astype(F32)
+
+        part = lax.fori_loop(me + 1, devices, add, send_buf[me].astype(F32))
+        grad_qkv[:, mix:] = turn_back(part, cosine[...], sine[...], True)
+
+        def drain():
+            def sent(e, carry):
+                send_copy(e, me).wait_send()
+                return carry
+
+            lax.fori_loop(0, me, sent, 0)
+
+        return drain
+
+    def tail(level):
+        gains, flow = held["gains"], held["flow"]
+        grad_now = held[f"grad_qkv_{level}"][...]
+        need("qkv")
+        total = sums[f"tail_{level}"]
+        total.start(lambda start, wide: dot_nt(grad_now, w_qkv[pl.ds(start, wide), :]))
+        keep(f"grad_qkv_{level}")
+        rows_now = held[f"rows_{level}"][...].astype(F32)
+        unit, factor = unit_of(rows_now)
+        logit = held[f"logit_{level}"][...]
+        vecs[7 - level : 8 - level, :] = jnp.sum(rows_now * logit, axis=0, keepdims=True)
+        total.middle()
+        grad_normed = total.finish().astype(F32)
+        vecs[5 - level : 6 - level, :] = jnp.sum(grad_normed * unit, axis=0, keepdims=True)
+        grad_rows_now = (
+            unit_back(grad_normed * gains[0:1, :], unit, factor)
+            + held[f"middle_{level}"][...]
+            + logit * gains[2:3, :]
+        ).astype(BF)
+        flow[...] = flow[...] + dot_tn(held[f"pick_{level}"][...], grad_rows_now)
+
+    drains = []
+    for level in (2, 1):
+        head(level)
+        drains.append(attention(level))
+        tail(level)
+    held["flow_out"][...] = held["flow"][...]
+    keep("flow_out")
+    head(0)
+    keep("vecs")
+    for drain in drains:
+        drain()
+    for item in sums.values():
+        item.drain()
+    for copy in keeps:
+        copy.wait()
+
+
+def retreat(cotangent, kept, weights, heads, devices, mp, ident):
+    counts = tuple(kept[f"rows_{level}"].shape[0] for level in range(3))
+    model = cotangent.shape[1]
+    mix = heads * HD
+    hidden = kept["parts_0"].shape[1] // 2
+    ins = {"flow": cotangent, "gains": kept["gains"]}
+    shapes = {"flow_out": (cotangent.shape, F32), "vecs": ((8, model), F32)}
+    for level, n in enumerate(counts):
+        for base in ("rows", "attn", "ffn", "parts"):
+            ins[f"{base}_{level}"] = kept[f"{base}_{level}"]
+        if level:
+            for base in ("pick", "query", "packed", "mixed_t", "log", "keys", "place", "cosine", "sine"):
+                ins[f"{base}_{level}"] = kept[f"{base}_{level}"]
+            shapes[f"grad_qkv_{level}"] = ((n, mix + 2 * HD), BF)
+        shapes[f"grad_attn_{level}"] = ((n, model), BF)
+        shapes[f"grad_ffn_{level}"] = ((n, model), BF)
+        shapes[f"hidden_{level}"] = ((n, hidden), BF)
+        shapes[f"parts_grad_{level}"] = ((n, 2 * hidden), BF)
+        shapes[f"grad_mixed_{level}"] = ((n, mix), BF)
+        shapes[f"middle_{level}"] = ((n, model), F32)
+        shapes[f"logit_{level}"] = ((n, 1), F32)
+    names = tuple(shapes)
+    most = heads * max(counts[1:])
+    anywhere = pl.BlockSpec(memory_space=pl.ANY)
+    outs = pl.pallas_call(
+        functools.partial(retreat_kernel, counts, heads, devices, mp, hidden, tuple(ins), names),
+        out_shape=tuple(jax.ShapeDtypeStruct(*shapes[name]) for name in names),
+        in_specs=[anywhere] * (len(ins) + 1),
+        out_specs=tuple([anywhere] * len(names)),
+        scratch_shapes=[pltpu.VMEM(item.shape, item.dtype) for item in ins.values()]
+        + [pltpu.VMEM(*shapes[name]) for name in names]
+        + [
+            pltpu.VMEM((model, mix + 2 * HD), BF),
+            pltpu.VMEM((model, mix), BF),
+            pltpu.VMEM((model, 2 * hidden), BF),
+            pltpu.VMEM((model, hidden), BF),
+            pltpu.SemaphoreType.DMA((len(ins),)),
+            pltpu.SemaphoreType.DMA((4,)),
+            pltpu.SemaphoreType.DMA((len(names),)),
+            pltpu.VMEM((2 * HD, most), BF),
+            pltpu.VMEM((most, 2 * HD), BF),
+            pltpu.VMEM((2 * HD, most), BF),
+            pltpu.VMEM((2 * HD, most), F32),
+            pltpu.VMEM((1, most), F32),
         ]
-        scratch += [
-            pltpu.VMEM((model, mix + 2 * HD), BF),
-            pltpu.SemaphoreType.DMA(()),
-            *sum_scratch(mp, tail_n, model),
+        + [
+            item
+            for level in (1, 2)
+            for item in (
+                pltpu.VMEM((devices, counts[level], 2 * HD), BF),
+                pltpu.VMEM((devices, counts[level], 2 * HD), BF),
+                pltpu.SemaphoreType.DMA((devices,)),
+                pltpu.SemaphoreType.DMA((devices,)),
+            )
         ]
-    if head_n:
-        args.append(weights)
-        outs += [
-            jax.ShapeDtypeStruct((head_n, model), BF),
-            jax.ShapeDtypeStruct((head_n, model), F32),
-            jax.ShapeDtypeStruct((head_n, 1), F32),
-            jax.ShapeDtypeStruct((head_n, mix), BF),
-            jax.ShapeDtypeStruct((head_n, 2 * hidden_width), BF),
-            jax.ShapeDtypeStruct((head_n, hidden_width), BF),
-            jax.ShapeDtypeStruct((head_n, model), BF),
-            jax.ShapeDtypeStruct((1, model), F32),
-        ]
-        scratch += [
-            pltpu.VMEM((model, mix), BF),
-            pltpu.VMEM((model, 2 * hidden_width), BF),
-            pltpu.VMEM((model, hidden_width), BF),
-            pltpu.SemaphoreType.DMA((3,)),
-            *sum_scratch(mp, head_n, model),
-        ]
-    return pl.pallas_call(
-        functools.partial(feed_back_kernel, tail_n, head_n, mp, tail_picked, head_picked),
-        out_shape=tuple(outs),
-        in_specs=vmem(in_vmem) + [pl.BlockSpec(memory_space=pl.ANY)] * (len(args) - in_vmem),
-        out_specs=tuple(vmem(len(outs))),
-        scratch_shapes=scratch,
+        + [item for level in (2, 2, 1, 1, 0) for item in sum_scratch(mp, counts[level], model)],
         compiler_params=pltpu.CompilerParams(
             collective_id=ident, has_side_effects=True, vmem_limit_bytes=VMEM_LIMIT
         ),
-        cost_estimate=pl.CostEstimate(flops=5 * 10**9, bytes_accessed=10**8, transcendentals=0),
-        name=f"feed_back_{tail_n}_{head_n}",
-    )(*args)
+        name="retreat",
+    )(*ins.values(), weights)
+    return dict(zip(names, outs))
 
 
 def plane(me):
@@ -749,14 +773,16 @@
     base_gu = base_o + mix
     base_d = base_gu + 2 * hidden
 
-    def chunk_of(c, low, high):
-        return weights[c, :, :, :, low:high].reshape(chunk, high - low)
+    def rows_of(start, wide, low, high):
+        return weights[start // chunk, pl.ds(lax.rem(start, chunk) // LANES, wide // LANES), :, :, low:high].reshape(
+            wide, high - low
+        )
 
     def feed(level, beside):
         name = lambda base: held[f"{base}_{level}"]
         mixed_now = name("mixed")[...]
         first, last = sums[2 * level], sums[2 * level + 1]
-        first.start(lambda c: dot_nt(mixed_now, chunk_of(c, base_o, base_gu)))
+        first.start(lambda start, wide: dot_nt(mixed_now, rows_of(start, wide, base_o, base_gu)))
         beside(1)
         first.middle()
         beside(1)
@@ -780,7 +806,7 @@
             up_part = parts[:, hidden + t * LANES : hidden + (t + 1) * LANES]
             hidden_v[:n, cut] = (gate_part * sigmoid(gate_part) * up_part).astype(BF)
         hidden_now = hidden_v[:n, :]
-        last.start(lambda c: dot_nt(hidden_now, chunk_of(c, base_d, base_d + hidden)))
+        last.start(lambda start, wide: dot_nt(hidden_now, rows_of(start, wide, base_d, base_d + hidden)))
         for base in ("attn", "second", "parts"):
             keep(f"{base}_{level}")
         gate = sigmoid(jnp.sum(level_rows * gains[2:3, :], axis=-1, keepdims=True))
@@ -1066,7 +1092,7 @@
 def finish_kernel(n, heads, devices, mp, group, levels, spans, groups, *refs):
     refs = list(refs)
     flow, gains, query_place, query, packed, mixed_t, log_total, grad_mixed, cosine, sine = [refs.pop(0) for _ in range(10)]
-    rows_in, middle, logit, second_vecs, first_vecs, router_vecs = [refs.pop(0) for _ in range(6)]
+    rows_in, middle, logit, vecs = [refs.pop(0) for _ in range(4)]
     w_hbm = refs.pop(0)
     sources = [[refs.pop(0) for _ in range(8 if level else 7)] for level in range(len(levels))]
     flow_out, q_out, k_out, v_out, out_out, gate_out, up_out, down_out, vec_out = [refs.pop(0) for _ in range(9)]
@@ -1213,13 +1239,12 @@
         )
     load_w.wait()
     grad_now = rights[0:n, low : spans[3][1]]
-    chunk = w_qkv.shape[0] // mp
-
-    def first_chunk(c):
-        return dot_nt(grad_now, w_qkv[pl.ds(pl.multiple_of(c * chunk, chunk), chunk), :])
+
+    def first_piece(start, wide):
+        return dot_nt(grad_now, w_qkv[pl.ds(start, wide), :])
 
     total = Sum(mp, mp_me, send_a, recv_a, full_a, sems_a)
-    total.start(first_chunk)
+    total.start(first_piece)
     work.step(blocks)
     total.middle()
     work.step(blocks + 1)
@@ -1227,9 +1252,9 @@
     level = rows_in[...].astype(F32)
     unit, factor = unit_of(level)
     vectors[...] = jnp.zeros(vectors.shape, F32)
-    vectors[0:1, :] = jnp.sum(grad_normed * unit, axis=0, keepdims=True) + first_vecs[0:1, :] + first_vecs[1:2, :]
-    vectors[1:2, :] = second_vecs[0:1, :] + second_vecs[1:2, :] + second_vecs[2:3, :]
-    vectors[2:3, :] = jnp.sum(level * logit[...], axis=0, keepdims=True) + router_vecs[0:1, :] + router_vecs[1:2, :]
+    vectors[0:1, :] = jnp.sum(grad_normed * unit, axis=0, keepdims=True) + vecs[3:4, :] + vecs[4:5, :]
+    vectors[1:2, :] = vecs[0:1, :] + vecs[1:2, :] + vecs[2:3, :]
+    vectors[2:3, :] = jnp.sum(level * logit[...], axis=0, keepdims=True) + vecs[5:6, :] + vecs[6:7, :]
     flow_out[...] = flow[...] + (
         unit_back(grad_normed * gains[0:1, :], unit, factor) + middle[...] + logit[...] * gains[2:3, :]
     ).astype(BF).astype(F32)
@@ -1243,46 +1268,6 @@
         return carry
 
     lax.fori_loop(0, me, sent, 0)
-
-
-class Sum:
-    order = (2, 1, 3)
-
-    def __init__(self, group, me, send, recv, full, sems):
-        self.group, self.me, self.send, self.recv, self.full, self.sems = group, me, send, recv, full, sems
-
-    def remote(self, source, target, stage, k):
-        copy = pltpu.make_async_remote_copy(
-            src_ref=source, dst_ref=target, send_sem=self.sems.at[stage, k - 1],
-            recv_sem=self.sems.at[stage + 1, k - 1],
-            device_id={"mp": lax.rem(self.me + k, self.group)}, device_id_type=MESH,
-        )
-        copy.start()
-        return copy
-
-    def start(self, make_chunk):
-        self.out = []
-        for k in self.order:
-            self.send[k - 1] = make_chunk(lax.rem(self.me + k, self.group)).astype(BF)
-            self.out.append(self.remote(self.send.at[k - 1], self.recv.at[k - 1], 0, k))
-        self.own = make_chunk(self.me).astype(BF).astype(F32)
-
-    def middle(self):
-        total = self.own
-        for k, copy in zip(self.order, self.out):
-            copy.wait_recv()
-            total = total + self.recv[k - 1].astype(F32)
-        self.full[self.me] = total.astype(BF)
-        self.back = [self.remote(self.full.at[self.me], self.full.at[self.me], 2, k) for k in self.order]
-
-    def finish(self):
-        for copy in self.back:
-            copy.wait_recv()
-        return jnp.concatenate([self.full[c] for c in range(self.group)], axis=1)
-
-    def drain(self):
-        for copy in self.out + self.back:
-            copy.wait_send()
 
 
 def finish(flow, gains, attention, tail, vecs, weights, levels, heads, devices, mp, depth, ident):
@@ -1313,7 +1298,7 @@
     rows = sum(counts)
     hidden = widths[1]
     many = len(groups)
-    whole = [flow, gains, *attention, *tail, *vecs]
+    whole = [flow, gains, *attention, *tail, vecs]
     args = whole + [weights] + [item for level in levels for item in level]
     return pl.pallas_call(
         functools.partial(finish_kernel, n, heads, devices, mp, group, counts, spans, groups),
@@ -1381,7 +1366,6 @@
     devices, mp = lax.axis_size("dp"), lax.axis_size("mp")
     rows = tokens.shape[0]
     heads = w_query.shape[1] // HD
-    hidden_width = w_gate.shape[1]
     depth = w_query.shape[0]
     home = rotary_tables(jnp.arange(rows, dtype=jnp.int32) + me * rows)
 
@@ -1395,42 +1379,19 @@
     )
     weights = kept["weights"].reshape(devices * depth, -1)
     gains = kept["gains"]
-    flow = cotangent
-    tail = None
-    terms, vectors, second_vecs = [], [], []
-    for index in (2, 1, 0):
-        query_place, rows_in, normed, packed, query, mixed_t, log_total, mixed, attn, ffn, second, parts = [
-            kept[f"{base}_{index}"]
-            for base in (
-                "place", "rows", "normed", "packed", "query", "mixed_t", "log", "mixed", "attn", "ffn", "second", "parts"
-            )
-        ]
-        pick = kept[f"pick_{index}"] if index else None
-        head = (rows_in, attn, ffn, second, parts, pick)
-        outs = list(
-            feed_back(flow, gains, tail, head, weights, hidden_width, heads * HD, mp, 6 + index)
-        )
-        if tail is not None:
-            flow, first_vec, router_vec = outs[:3]
-            outs = outs[3:]
-            vectors.append((first_vec, router_vec))
-        grad_attn, grad_middle, logit, grad_mixed, parts_grad, hidden, grad_ffn, second_vec = outs
-        second_vecs.append(second_vec)
-        items = (second, parts_grad, grad_ffn, hidden, grad_attn, mixed, normed)
-        if index:
-            grad_qkv = attend_back(
-                kept[f"keys_{index}"].reshape(-1, LANES), query_place, query, packed, mixed_t, log_total,
-                grad_mixed, (kept[f"cosine_{index}"], kept[f"sine_{index}"]),
-                heads, devices, rows_in.shape[0], 10 + index,
-            )
-            tail = (grad_qkv, rows_in, grad_middle, logit, pick)
-            items = items + (grad_qkv,)
-        terms.append(items)
-    attention = (query_place, query, packed, mixed_t, log_total, grad_mixed, *home)
-    vecs = [jnp.concatenate(list(part), axis=0) for part in (second_vecs, *zip(*vectors))]
+    back = retreat(cotangent, kept, weights, heads, devices, mp, 1)
+    terms = []
+    for level in range(3):
+        terms.append(
+            tuple(back.get(f"{base}_{level}", kept.get(f"{base}_{level}")) for base in (
+                "second", "parts_grad", "grad_ffn", "hidden", "grad_attn", "mixed", "normed", "grad_qkv"
+            )[: 8 if level else 7])
+        )
+    attention = [kept[f"{base}_0"] for base in ("place", "query", "packed", "mixed_t", "log")]
     flow, query_grad, key_grad, value_grad, out_grad, gate_grad, up_grad, down_grad, vec = finish(
-        flow, gains, attention, (rows_in, grad_middle, logit), vecs, weights, terms[::-1],
-        heads, devices, mp, depth, 14,
+        back["flow_out"], gains, (*attention, back["grad_mixed_0"], *home),
+        (kept["rows_0"], back["middle_0"], back["logit_0"]), back["vecs"], weights, terms,
+        heads, devices, mp, depth, 2,
     )
     return (
         kept["state"], flow, query_grad, key_grad, value_grad, out_grad.T, gate_grad, up_grad, down_grad.T,

time: 485 us -> 434 us (0.89); the launches traced: 482 us -> 426 us
  Pallas kernels: 467 us -> 414 us
    pallas_call x5 -> x1, Pallas kernels: 155 us -> 120 us  [retreat(): pl.pallas_call(functools.partial(retreat_kernel, counts, heads, devices,...]
    pallas_call x1, Pallas kernels: 207 us -> 190 us  [advance(): pl.pallas_call(functools.partial(advance_kernel, counts, heads, devices,...]
where the time goes in v6:
time: 434 us; the launch traced here: 426 us
  Pallas kernels  414 us (95%)
  local copies, waits for them, and re-layouts  9.67 us (2%)
    pallas_call x1, Pallas kernels, advance(): pl.pallas_call(functools.partial(advance_kernel, counts, heads, devices,...  190 us
    pallas_call x1, Pallas kernels, retreat(): pl.pallas_call(functools.partial(retreat_kernel, counts, heads, devices,...  120 us
    pallas_call x1, Pallas kernels, finish(): pl.pallas_call(functools.partial(finish_kernel, n, heads, devices, mp, gr...  103 us

profile of v6, /device:TPU:0, one launch (start us, length us, event | category | flops | bytes accessed | tf_op | source)
XLA Modules:
  0.0 425.6 jit_solution(7312345516778484968)
XLA Ops:
  0.7 0.3 fusion
  1.0 0.8 pad_maximum_fusion
  1.8 190.0 %advance.1 = (f32[128,2048]{1,0:T(8,128)}, bf16[4,4,2,64,5504]{4,3,2,1,0:T(8,128)(2,1)}, f32[8,2048]{1,0:T(8,128)}, f32[1,1024]{1,0:T(1,128)}, bf16[128,2048]{1,...) custom-call(bf16[128,2048]{1,0:T(8,128)(2,1)} %refs_0_.2, ...), custom_call_target="tpu_custom_call" | custom-call | tf_op jit(solution)/shard_map/advance/pallas_call | solution.py:907
  191.9 120.2 %retreat.1 = (f32[128,2048]{1,0:T(8,128)}, f32[8,2048]{1,0:T(8,128)}, bf16[128,2048]{1,0:T(8,128)(2,1)}, bf16[128,2048]{1,0:T(8,128)(2,1)}, bf16[128,1408]{1,0:T...) custom-call(f32[128,2048]{1,0:T(8,128)} %refs_0_.3, ...), custom_call_target="tpu_custom_call" | custom-call | tf_op jit(solution)/shard_map/retreat/pallas_call | solution.py:408
  312.1 103.4 %finish.1 = (f32[128,2048]{1,0:T(8,128)}, f32[64,512]{1,0:T(8,128)}, f32[64,64]{1,0:T(8,128)}, f32[64,64]{1,0:T(8,128)}, f32[64,512]{1,0:T(8,128)}, /*index=5*/f...) custom-call(f32[128,2048]{1,0:T(8,128)} %get-tuple-element.120.refs_0_, ...), custom_call_target="tpu_custom_call" | custom-call | tf_op jit(solution)/shard_map/finish/pallas_call | solution.py:1303
  415.5 0.0 copy-start
  415.5 1.6 slice_reduce_fusion
  417.1 2.3 copy.37
  419.4 0.0 copy-done
  419.4 0.0 copy-start.5
  419.4 0.0 copy-start.7
  419.4 0.0 copy-start.6
  419.4 0.0 copy-start.4
  419.4 0.0 copy-start.3
  419.4 0.0 copy-start.2
  419.5 0.0 copy-start.1
  419.5 1.0 copy.38
  420.4 0.0 copy-done.5
  420.4 0.7 copy.39
  421.1 0.0 copy-done.7
  421.1 0.6 copy.40
  421.7 0.0 copy-done.6
  421.7 0.6 copy.41
  422.3 0.0 copy-done.4
  422.3 0.7 copy.42
  423.0 0.0 copy-done.3
  423.0 0.7 copy.43
  423.7 0.0 copy-done.2
  423.7 0.7 copy.44
  424.5 0.0 copy-done.1
  424.5 0.7 copy.45
  (2 shorter events, 0.0 us)
Async XLA Ops:
  415.5 3.9 copy-start
  419.4 1.0 copy-start.5
  419.4 1.7 copy-start.7
  419.4 2.3 copy-start.6
  419.4 2.9 copy-start.4
  419.4 3.6 copy-start.3
  419.4 4.3 %copy-start.2 = (f32[64,1408]{1,0:T(8,128)S(1)}, f32[64,1408]{1,0:T(8,128)}, u32[]{:S(2)}) copy-start(f32[64,1408]{1,0:T(8,128)} %get-tuple-element.189) | copy-start | bytes 1081348
  419.5 5.0 %copy-start.1 = (f32[64,1408]{1,0:T(8,128)S(1)}, f32[64,1408]{1,0:T(8,128)}, u32[]{:S(2)}) copy-start(f32[64,1408]{1,0:T(8,128)} %get-tuple-element.160) | copy-start | bytes 1081348

commit v7 on v6

--- a/solution.py
+++ b/solution.py
@@ -18,6 +18,9 @@
 BF = jnp.bfloat16
 F32 = jnp.float32
 MESH = pl.DeviceIdType.MESH
+
+(K_ROWS, K_NORMED, K_ATTN, K_FFN, K_SECOND, K_PARTS, K_PACKED, K_QUERY, K_MIXED_T, K_LOG, K_MIXED, K_PLACE, K_PICK, K_COSINE, K_SINE, K_KEYS, K_STATE, K_WEIGHTS, K_GAINS, K_FLOW, K_FLOW_OUT, K_VECS, K_GRAD_QKV, K_GRAD_FFN, K_HIDDEN, K_PARTS_GRAD, K_GRAD_ATTN, K_GRAD_MIXED, K_MIDDLE, K_LOGIT, K_HEAD, K_TAIL, K_D, K_GU, K_O, K_QKV) = range(36)
+
 LANES = 128
 VMEM_LIMIT = 63 * 1024 * 1024
 
@@ -147,17 +150,17 @@
     ]
 
 
-def retreat_kernel(counts, heads, devices, mp, hidden, ins, names, *refs):
+def retreat_kernel(counts, heads, devices, mp, hidden, ins, names, inner, *refs):
     refs = list(refs)
     sources = {name: refs.pop(0) for name in ins}
     w_hbm = refs.pop(0)
     outs = {name: refs.pop(0) for name in names}
     held = {name: refs.pop(0) for name in ins}
-    held.update({name: refs.pop(0) for name in names})
+    held.update({name: refs.pop(0) for name in names + inner})
     w_qkv, w_o, w_gu, w_d, fetch_sems, w_sems, keep_sems = [refs.pop(0) for _ in range(7)]
     query_t, grad_rows, grad_t, acc, delta = [refs.pop(0) for _ in range(5)]
     buffers = {level: [refs.pop(0) for _ in range(4)] for level in (1, 2)}
-    sum_refs = {key: [refs.pop(0) for _ in range(4)] for key in ("head_2", "tail_2", "head_1", "tail_1", "head_0")}
+    sum_refs = {key: [refs.pop(0) for _ in range(4)] for key in ((K_HEAD, 2), (K_TAIL, 2), (K_HEAD, 1), (K_TAIL, 1))}
     me, mp_me = lax.axis_index("dp"), lax.axis_index("mp")
     model = w_o.shape[0]
     mix = heads * HD
@@ -186,12 +189,12 @@
         keeps.append(copy)
 
     base_o = mix + 2 * LANES
-    for name in ("flow", "gains", "pick_2", "rows_2", "attn_2", "ffn_2", "parts_2"):
+    for name in (K_FLOW, K_GAINS, (K_PICK, 2), (K_ROWS, 2), (K_ATTN, 2), (K_FFN, 2), (K_PARTS, 2)):
         fetch(name)
-    load("d", w_d, base_o + mix + 2 * hidden, 0)
-    load("gu", w_gu, base_o + mix, 1)
-    load("o", w_o, base_o, 2)
-    load("qkv", w_qkv, 0, 3)
+    load(K_D, w_d, base_o + mix + 2 * hidden, 0)
+    load(K_GU, w_gu, base_o + mix, 1)
+    load(K_O, w_o, base_o, 2)
+    load(K_QKV, w_qkv, 0, 3)
     for name in ins:
         if name not in loads:
             fetch(name)
@@ -210,29 +213,29 @@
             barrier, inc=1, device_id={"mp": lax.rem(mp_me + k, mp)}, device_id_type=MESH
         )
     sums = {key: Sum(mp, mp_me, *items) for key, items in sum_refs.items()}
-    vecs = held["vecs"]
+    vecs = held[K_VECS]
     vecs[...] = jnp.zeros(vecs.shape, F32)
     gate_of = {}
 
     def head(level):
         n = counts[level]
-        name = lambda base: held[f"{base}_{level}"]
-        grad_update = get("flow")[...].astype(BF)
+        name = lambda base: held[(base, level)]
+        grad_update = get(K_FLOW)[...].astype(BF)
         if level:
-            grad_update = dot_nn(get(f"pick_{level}")[...], grad_update)
+            grad_update = dot_nn(get((K_PICK, level))[...], grad_update)
         grad_update = grad_update.astype(F32)
-        rows_now = get(f"rows_{level}")[...].astype(F32)
-        attn_now = get(f"attn_{level}")[...].astype(F32)
-        gains = get("gains")
+        rows_now = get((K_ROWS, level))[...].astype(F32)
+        attn_now = get((K_ATTN, level))[...].astype(F32)
+        gains = get(K_GAINS)
         gate = sigmoid(jnp.sum(rows_now * gains[2:3, :], axis=-1, keepdims=True))
         logit = jnp.sum(
-            grad_update * (attn_now + get(f"ffn_{level}")[...].astype(F32)), axis=-1, keepdims=True
-        )
-        name("logit")[...] = logit * gate * (1.0 - gate)
+            grad_update * (attn_now + get((K_FFN, level))[...].astype(F32)), axis=-1, keepdims=True
+        )
+        name(K_LOGIT)[...] = logit * gate * (1.0 - gate)
         grad_ffn = (gate * grad_update).astype(BF)
-        name("grad_ffn")[...] = grad_ffn
-        parts, parts_grad, hidden_out = get(f"parts_{level}"), name("parts_grad"), name("hidden")
-        need("d")
+        name(K_GRAD_FFN)[...] = grad_ffn
+        parts, parts_grad, hidden_out = get((K_PARTS, level)), name(K_PARTS_GRAD), name(K_HIDDEN)
+        need(K_D)
         for t in range(hidden // LANES):
             cut = slice(t * LANES, (t + 1) * LANES)
             up_cut = slice(hidden + t * LANES, hidden + (t + 1) * LANES)
@@ -248,37 +251,41 @@
                 grad_hidden * up_part * sigma * (1.0 + gate_part * (1.0 - sigma))
             ).astype(BF)
             parts_grad[:, up_cut] = (grad_hidden * active).astype(BF)
-        need("gu")
+        for base in (K_GRAD_FFN, K_HIDDEN, K_PARTS_GRAD, K_LOGIT):
+            keep((base, level))
+        return grad_update, rows_now, attn_now, gate
+
+    def head_end(level, grad_update, rows_now, attn_now, gate):
+        name = lambda base: held[(base, level)]
+        gains = held[K_GAINS]
+        need(K_GU)
         if level == 2:
             pl.semaphore_wait(barrier, devices - 1 + mp - 1)
-        parts_now = parts_grad[...]
-        total = sums[f"head_{level}"]
+        parts_now = name(K_PARTS_GRAD)[...]
+        total = sums[(K_HEAD, level)]
         total.start(lambda start, wide: dot_nt(parts_now, w_gu[pl.ds(start, wide), :]))
-        for base in ("grad_ffn", "hidden", "parts_grad", "logit"):
-            keep(f"{base}_{level}")
         unit, factor = unit_of(rows_now + attn_now)
         total.middle()
         grad_second = total.finish().astype(F32)
         vecs[2 - level : 3 - level, :] = jnp.sum(grad_second * unit, axis=0, keepdims=True)
         grad_middle = unit_back(grad_second * gains[1:2, :], unit, factor)
-        name("middle")[...] = grad_middle
+        name(K_MIDDLE)[...] = grad_middle
         grad_attn = (gate * grad_update + grad_middle).astype(BF)
-        name("grad_attn")[...] = grad_attn
-        need("o")
-        name("grad_mixed")[...] = dot_nn(grad_attn, w_o[...]).astype(BF)
-        for base in ("grad_attn", "middle", "grad_mixed"):
-            keep(f"{base}_{level}")
+        name(K_GRAD_ATTN)[...] = grad_attn
+        need(K_O)
+        name(K_GRAD_MIXED)[...] = dot_nn(grad_attn, w_o[...]).astype(BF)
+        keep((K_GRAD_ATTN, level))
 
     def attention(level):
         n = counts[level]
-        group = 512 // n if 512 % n == 0 else 4
+        group = 8
         width = heads * n
         send_buf, recv_buf, send_sems, recv_sems = buffers[level]
-        query, packed = get(f"query_{level}"), get(f"packed_{level}")
-        mixed_t, log_total = get(f"mixed_t_{level}"), get(f"log_{level}")
-        keys, query_place = get(f"keys_{level}"), get(f"place_{level}")
-        cosine, sine = get(f"cosine_{level}"), get(f"sine_{level}")
-        grad_mixed, grad_qkv = held[f"grad_mixed_{level}"], held[f"grad_qkv_{level}"]
+        query, packed = get((K_QUERY, level)), get((K_PACKED, level))
+        mixed_t, log_total = get((K_MIXED_T, level)), get((K_LOG, level))
+        keys, query_place = get((K_KEYS, level)), get((K_PLACE, level))
+        cosine, sine = get((K_COSINE, level)), get((K_SINE, level))
+        grad_mixed, grad_qkv = held[(K_GRAD_MIXED, level)], held[(K_GRAD_QKV, level)]
         left = lanes_of((n, LANES)) < HD
         for t in range(heads // 2):
             part = grad_mixed[:, t * LANES : (t + 1) * LANES].astype(F32)
@@ -344,35 +351,35 @@
         return drain
 
     def tail(level):
-        gains, flow = held["gains"], held["flow"]
-        grad_now = held[f"grad_qkv_{level}"][...]
-        need("qkv")
-        total = sums[f"tail_{level}"]
+        gains, flow = held[K_GAINS], held[K_FLOW]
+        grad_now = held[(K_GRAD_QKV, level)][...]
+        need(K_QKV)
+        total = sums[(K_TAIL, level)]
         total.start(lambda start, wide: dot_nt(grad_now, w_qkv[pl.ds(start, wide), :]))
-        keep(f"grad_qkv_{level}")
-        rows_now = held[f"rows_{level}"][...].astype(F32)
+        keep((K_GRAD_QKV, level))
+        rows_now = held[(K_ROWS, level)][...].astype(F32)
         unit, factor = unit_of(rows_now)
-        logit = held[f"logit_{level}"][...]
+        logit = held[(K_LOGIT, level)][...]
         vecs[7 - level : 8 - level, :] = jnp.sum(rows_now * logit, axis=0, keepdims=True)
         total.middle()
         grad_normed = total.finish().astype(F32)
         vecs[5 - level : 6 - level, :] = jnp.sum(grad_normed * unit, axis=0, keepdims=True)
         grad_rows_now = (
             unit_back(grad_normed * gains[0:1, :], unit, factor)
-            + held[f"middle_{level}"][...]
+            + held[(K_MIDDLE, level)][...]
             + logit * gains[2:3, :]
         ).astype(BF)
-        flow[...] = flow[...] + dot_tn(held[f"pick_{level}"][...], grad_rows_now)
+        flow[...] = flow[...] + dot_tn(held[(K_PICK, level)][...], grad_rows_now)
 
     drains = []
     for level in (2, 1):
-        head(level)
+        head_end(level, *head(level))
         drains.append(attention(level))
         tail(level)
-    held["flow_out"][...] = held["flow"][...]
-    keep("flow_out")
+    held[K_FLOW_OUT][...] = held[K_FLOW][...]
+    keep(K_FLOW_OUT)
     head(0)
-    keep("vecs")
+    keep(K_VECS)
     for drain in drains:
         drain()
     for item in sums.values():
@@ -382,36 +389,37 @@
 
 
 def retreat(cotangent, kept, weights, heads, devices, mp, ident):
-    counts = tuple(kept[f"rows_{level}"].shape[0] for level in range(3))
+    counts = tuple(kept[(K_ROWS, level)].shape[0] for level in range(3))
     model = cotangent.shape[1]
     mix = heads * HD
-    hidden = kept["parts_0"].shape[1] // 2
-    ins = {"flow": cotangent, "gains": kept["gains"]}
-    shapes = {"flow_out": (cotangent.shape, F32), "vecs": ((8, model), F32)}
+    hidden = kept[(K_PARTS, 0)].shape[1] // 2
+    ins = {K_FLOW: cotangent, K_GAINS: kept[K_GAINS]}
+    inner = {}
+    shapes = {K_FLOW_OUT: (cotangent.shape, F32), K_VECS: ((8, model), F32)}
     for level, n in enumerate(counts):
-        for base in ("rows", "attn", "ffn", "parts"):
-            ins[f"{base}_{level}"] = kept[f"{base}_{level}"]
+        for base in (K_ROWS, K_ATTN, K_FFN, K_PARTS):
+            ins[(base, level)] = kept[(base, level)]
         if level:
-            for base in ("pick", "query", "packed", "mixed_t", "log", "keys", "place", "cosine", "sine"):
-                ins[f"{base}_{level}"] = kept[f"{base}_{level}"]
-            shapes[f"grad_qkv_{level}"] = ((n, mix + 2 * HD), BF)
-        shapes[f"grad_attn_{level}"] = ((n, model), BF)
-        shapes[f"grad_ffn_{level}"] = ((n, model), BF)
-        shapes[f"hidden_{level}"] = ((n, hidden), BF)
-        shapes[f"parts_grad_{level}"] = ((n, 2 * hidden), BF)
-        shapes[f"grad_mixed_{level}"] = ((n, mix), BF)
-        shapes[f"middle_{level}"] = ((n, model), F32)
-        shapes[f"logit_{level}"] = ((n, 1), F32)
+            for base in (K_PICK, K_QUERY, K_PACKED, K_MIXED_T, K_LOG, K_KEYS, K_PLACE, K_COSINE, K_SINE):
+                ins[(base, level)] = kept[(base, level)]
+            shapes[(K_GRAD_QKV, level)] = ((n, mix + 2 * HD), BF)
+            shapes[(K_GRAD_ATTN, level)] = ((n, model), BF)
+            inner[(K_GRAD_MIXED, level)] = ((n, mix), BF)
+            inner[(K_MIDDLE, level)] = ((n, model), F32)
+        shapes[(K_GRAD_FFN, level)] = ((n, model), BF)
+        shapes[(K_HIDDEN, level)] = ((n, hidden), BF)
+        shapes[(K_PARTS_GRAD, level)] = ((n, 2 * hidden), BF)
+        shapes[(K_LOGIT, level)] = ((n, 1), F32)
     names = tuple(shapes)
     most = heads * max(counts[1:])
     anywhere = pl.BlockSpec(memory_space=pl.ANY)
     outs = pl.pallas_call(
-        functools.partial(retreat_kernel, counts, heads, devices, mp, hidden, tuple(ins), names),
+        functools.partial(retreat_kernel, counts, heads, devices, mp, hidden, tuple(ins), names, tuple(inner)),
         out_shape=tuple(jax.ShapeDtypeStruct(*shapes[name]) for name in names),
         in_specs=[anywhere] * (len(ins) + 1),
         out_specs=tuple([anywhere] * len(names)),
         scratch_shapes=[pltpu.VMEM(item.shape, item.dtype) for item in ins.values()]
-        + [pltpu.VMEM(*shapes[name]) for name in names]
+        + [pltpu.VMEM(*shape) for shape in (*shapes.values(), *inner.values())]
         + [
             pltpu.VMEM((model, mix + 2 * HD), BF),
             pltpu.VMEM((model, mix), BF),
@@ -436,7 +444,7 @@
                 pltpu.SemaphoreType.DMA((devices,)),
             )
         ]
-        + [item for level in (2, 2, 1, 1, 0) for item in sum_scratch(mp, counts[level], model)],
+        + [item for level in (2, 2, 1, 1) for item in sum_scratch(mp, counts[level], model)],
         compiler_params=pltpu.CompilerParams(
             collective_id=ident, has_side_effects=True, vmem_limit_bytes=VMEM_LIMIT
         ),
@@ -558,7 +566,7 @@
     sum_refs = refs
     me, mp_me = lax.axis_index("dp"), lax.axis_index("mp")
     x, y, core = plane(me)
-    weights = held["weights"]
+    weights = held[K_WEIGHTS]
     rows, model = tokens.shape
     mix = heads * HD
     lanes = lanes_of((rows, LANES))
@@ -589,14 +597,14 @@
     query_places.append(
         (lax.rem(lanes_of((1, heads * rows)), rows) + me * rows).astype(F32)
     )
-    held["place_0"][...] = query_places[0]
+    held[(K_PLACE, 0)][...] = query_places[0]
     for level, slot, deep in ((1, second_slot, 2), (2, third_slot, 3)):
         count = counts[level]
         slots = lax.broadcasted_iota(jnp.int32, (count, rows), 0)
         active = (depths[...] >= deep) & (slot[...] >= 0)
         chosen = jnp.where(active, slot[...], -1) == slots
         pick = jnp.where(chosen, 1.0, 0.0).astype(BF)
-        held[f"pick_{level}"][...] = pick
+        held[(K_PICK, level)][...] = pick
         picks.append(pick)
         marks.append(
             jnp.min(jnp.where(chosen, token, float(rows)), axis=1, keepdims=True)
@@ -605,15 +613,15 @@
         probe = jnp.where(sublane == 0, token, 1.0).astype(BF)
         found = dot_nt(probe, jnp.concatenate([pick] * heads, axis=0))
         place = jnp.where(found[1:2, :] > 0.5, found[0:1, :] + (me * rows).astype(F32), FAR)
-        held[f"place_{level}"][...] = place
+        held[(K_PLACE, level)][...] = place
         query_places.append(place)
         table = jnp.concatenate([cosine_in[...], sine_in[...]], axis=1)
         turned = lax.dot_general(
             pick.astype(F32), table, (((1,), (0,)), ((), ())),
             preferred_element_type=F32, precision=lax.Precision.HIGHEST,
         )
-        held[f"cosine_{level}"][...] = turned[:, :LANES]
-        held[f"sine_{level}"][...] = turned[:, LANES:]
+        held[(K_COSINE, level)][...] = turned[:, :LANES]
+        held[(K_SINE, level)][...] = turned[:, LANES:]
     depth = w_query.shape[0]
     wide = jnp.zeros((1, LANES - depth), F32)
     gain_rows = jnp.concatenate(
@@ -650,10 +658,10 @@
     spread.five(0)
     upto = 4
 
-    gains = held["gains"]
+    gains = held[K_GAINS]
     columns = weights[:, :, :, :, mix + LANES : mix + 2 * LANES].reshape(model, LANES).astype(F32)
     gains[...] = columns.T[: gains.shape[0], :]
-    keep("gains")
+    keep(K_GAINS)
 
     def key_places(e, carry):
         for level, lanes_at in ((1, (3, 4)), (2, (5,))):
@@ -661,7 +669,7 @@
             value = jnp.concatenate(
                 [jnp.broadcast_to(tile[:, at : at + 1], (depth, LANES)) for at in lanes_at], axis=0
             )[: counts[level], :]
-            held[f"keys_{level}"][e] = jnp.where(
+            held[(K_KEYS, level)][e] = jnp.where(
                 value < rows, value + (e * rows).astype(F32), FAR
             )
         return carry
@@ -669,7 +677,7 @@
     lax.fori_loop(0, devices, key_places, 0)
 
     def kv_copy(level, e, source_index):
-        packed = held[f"packed_{level}"]
+        packed = held[(K_PACKED, level)]
         return pltpu.make_async_remote_copy(
             src_ref=packed.at[me], dst_ref=packed.at[me],
             send_sem=kv_send.at[level, e], recv_sem=kv_recv.at[level, source_index],
@@ -678,12 +686,12 @@
 
     def project(level, now):
         n = counts[level]
-        name = lambda base: held[f"{base}_{level}"]
-        name("rows")[...] = now
+        name = lambda base: held[(base, level)]
+        name(K_ROWS)[...] = now
         unit, unused = unit_of(now.astype(F32))
         normed = (unit * gains[0:1, :]).astype(BF)
-        name("normed")[...] = normed
-        cosine, sine = (cosine_in[...], sine_in[...]) if level == 0 else (name("cosine")[...], name("sine")[...])
+        name(K_NORMED)[...] = normed
+        cosine, sine = (cosine_in[...], sine_in[...]) if level == 0 else (name(K_COSINE)[...], name(K_SINE)[...])
         here = left[:n]
         tiles = [None] * (heads // 2 + 1)
         for t in range(heads // 2, -1, -2):
@@ -693,37 +701,37 @@
                 part = tile_of(both, j - low)
                 if j == heads // 2:
                     part = part * jnp.where(here, cosine, 1.0) + swap_halves(part) * jnp.where(here, sine, 0.0)
-                    name("packed")[me] = part.astype(BF)
-
-                    def send(e, carry):
-                        kv_copy(level, e, me).start()
+                    name(K_PACKED)[me] = part.astype(BF)
+
+                    def send(k, carry):
+                        kv_copy(level, devices - 1 - k, me).start()
                         return carry
 
-                    lax.fori_loop(me + 1, devices, send, 0)
+                    lax.fori_loop(0, devices - 1 - me, send, 0)
                 else:
                     tiles[j] = part * cosine + swap_halves(part) * sine
 
         def clear(e, carry):
-            name("packed")[e] = jnp.zeros((n, 2 * HD), BF)
+            name(K_PACKED)[e] = jnp.zeros((n, 2 * HD), BF)
             return carry
 
         lax.fori_loop(me + 1, devices, clear, 0)
         for t in range(heads // 2):
             scaled = tiles[t].astype(BF).astype(F32) * HD**-0.5
-            name("query")[2 * t * n : (2 * t + 1) * n, :] = jnp.where(here, scaled, 0.0).astype(BF)
-            name("query")[(2 * t + 1) * n : (2 * t + 2) * n, :] = jnp.where(
+            name(K_QUERY)[2 * t * n : (2 * t + 1) * n, :] = jnp.where(here, scaled, 0.0).astype(BF)
+            name(K_QUERY)[(2 * t + 1) * n : (2 * t + 2) * n, :] = jnp.where(
                 here, pltpu.roll(scaled, HD, 1), 0.0
             ).astype(BF)
         width = heads * n
-        query_t[:, :width] = name("query")[...].T
+        query_t[:, :width] = name(K_QUERY)[...].T
         top[:, :width] = jnp.full((1, width), NEG, F32)
         total[:, :width] = jnp.zeros((1, width), F32)
         acc[:, :width] = jnp.zeros((2 * HD, width), F32)
-        for base in ("rows", "normed", "query"):
-            keep(f"{base}_{level}")
+        for base in (K_ROWS, K_NORMED, K_QUERY):
+            keep((base, level))
 
     def group_of(level):
-        return 512 // counts[level] if 512 % counts[level] == 0 else 4
+        return (4, 8, 16)[level]
 
     def block(level, b):
         n, group = counts[level], group_of(level)
@@ -735,14 +743,14 @@
             def _(e=e):
                 kv_copy(level, me, e).wait_recv()
 
-        part = held[f"packed_{level}"][pl.ds(b * group, group)].reshape(group * n, 2 * HD)
+        part = held[(K_PACKED, level)][pl.ds(b * group, group)].reshape(group * n, 2 * HD)
         scores = dot_nn(part, query_t[:, :width])
         if level:
-            place = held[f"keys_{level}"][pl.ds(b * group, group)].reshape(group * n, LANES)
+            place = held[(K_KEYS, level)][pl.ds(b * group, group)].reshape(group * n, LANES)
         else:
             place = (lax.broadcasted_iota(jnp.int32, (group * n, LANES), 0) + b * (group * n)).astype(F32)
         place = jnp.concatenate([place] * (width // LANES), axis=1)
-        scores = jnp.where(place <= held[f"place_{level}"][...], scores, NEG)
+        scores = jnp.where(place <= held[(K_PLACE, level)][...], scores, NEG)
         before = top[:, :width]
         peak = jnp.maximum(before, jnp.max(scores, axis=0, keepdims=True))
         soft = jnp.exp(scores - peak)
@@ -755,17 +763,17 @@
         n = counts[level]
         width = heads * n
         mixed_t = acc[:, :width] / total[:, :width]
-        held[f"mixed_t_{level}"][...] = mixed_t
-        held[f"log_{level}"][...] = top[:, :width] + jnp.log(total[:, :width])
+        held[(K_MIXED_T, level)][...] = mixed_t
+        held[(K_LOG, level)][...] = top[:, :width] + jnp.log(total[:, :width])
         mixed = mixed_t.T
         for t in range(heads // 2):
             even = mixed[2 * t * n : (2 * t + 1) * n, :]
             odd = mixed[(2 * t + 1) * n : (2 * t + 2) * n, :]
-            held[f"mixed_{level}"][:, t * LANES : (t + 1) * LANES] = jnp.where(
+            held[(K_MIXED, level)][:, t * LANES : (t + 1) * LANES] = jnp.where(
                 left[:n], pltpu.roll(even, HD, 1), odd
             ).astype(BF)
-        for base in ("mixed_t", "log", "mixed", "packed"):
-            keep(f"{base}_{level}")
+        for base in (K_MIXED_T, K_LOG, K_MIXED, K_PACKED):
+            keep((base, level))
 
     sums = [Sum(mp, mp_me, *sum_refs[4 * i : 4 * i + 4]) for i in range(2 * len(counts))]
     chunk = model // mp
@@ -779,21 +787,21 @@
         )
 
     def feed(level, beside):
-        name = lambda base: held[f"{base}_{level}"]
-        mixed_now = name("mixed")[...]
+        name = lambda base: held[(base, level)]
+        mixed_now = name(K_MIXED)[...]
         first, last = sums[2 * level], sums[2 * level + 1]
         first.start(lambda start, wide: dot_nt(mixed_now, rows_of(start, wide, base_o, base_gu)))
         beside(1)
         first.middle()
         beside(1)
         attn = first.finish()
-        name("attn")[...] = attn
-        level_rows = name("rows")[...].astype(F32)
+        name(K_ATTN)[...] = attn
+        level_rows = name(K_ROWS)[...].astype(F32)
         unit, unused = unit_of(level_rows + attn.astype(F32))
         second = (unit * gains[1:2, :]).astype(BF)
-        name("second")[...] = second
+        name(K_SECOND)[...] = second
         beside(100)
-        parts = name("parts")
+        parts = name(K_PARTS)
         for t in range(2 * hidden // 256):
             low = base_gu + t * 256
             parts[:, t * 256 : (t + 1) * 256] = dot_nn(
@@ -807,17 +815,17 @@
             hidden_v[:n, cut] = (gate_part * sigmoid(gate_part) * up_part).astype(BF)
         hidden_now = hidden_v[:n, :]
         last.start(lambda start, wide: dot_nt(hidden_now, rows_of(start, wide, base_d, base_d + hidden)))
-        for base in ("attn", "second", "parts"):
-            keep(f"{base}_{level}")
+        for base in (K_ATTN, K_SECOND, K_PARTS):
+            keep((base, level))
         gate = sigmoid(jnp.sum(level_rows * gains[2:3, :], axis=-1, keepdims=True))
         last.middle()
         ffn = last.finish()
-        name("ffn")[...] = ffn
-        keep(f"ffn_{level}")
+        name(K_FFN)[...] = ffn
+        keep((K_FFN, level))
         update = (gate * (attn.astype(F32) + ffn.astype(F32))).astype(BF)
         if level:
-            update = dot_tn(held[f"pick_{level}"][...], update)
-        held["state"][...] = held["state"][...] + update.astype(F32)
+            update = dot_tn(held[(K_PICK, level)][...], update)
+        held[K_STATE][...] = held[K_STATE][...] + update.astype(F32)
 
     steps = len(groups) + 6
     done = [upto]
@@ -829,8 +837,8 @@
                 done[0] += 1
 
     project(0, tokens[...])
-    held["state"][...] = tokens[...].astype(F32)
-    for name in ("place_0", "pick_1", "pick_2", "place_1", "place_2", "cosine_1", "sine_1", "cosine_2", "sine_2", "keys_1", "keys_2"):
+    held[K_STATE][...] = tokens[...].astype(F32)
+    for name in ((K_PLACE, 0), (K_PICK, 1), (K_PICK, 2), (K_PLACE, 1), (K_PLACE, 2), (K_COSINE, 1), (K_SINE, 1), (K_COSINE, 2), (K_SINE, 2), (K_KEYS, 1), (K_KEYS, 2)):
         keep(name)
     for b in range(devices // group_of(0)):
         beside(1)
@@ -841,9 +849,9 @@
 
     mix_heads(0)
     feed(0, beside)
-    keep("weights")
+    keep(K_WEIGHTS)
     for level in range(1, len(counts)):
-        now = dot_nn(held[f"pick_{level}"][...], held["state"][...].astype(BF)).astype(BF)
+        now = dot_nn(held[(K_PICK, level)][...], held[K_STATE][...].astype(BF)).astype(BF)
         project(level, now)
 
         def one_block(b, carry, level=level):
@@ -853,7 +861,7 @@
         lax.fori_loop(0, me // group_of(level) + 1, one_block, 0)
         mix_heads(level)
         feed(level, lambda count: None)
-    keep("state")
+    keep(K_STATE)
     spread.drain()
     for item in sums:
         item.drain()
@@ -881,26 +889,26 @@
         cuts.pop(-2)
     groups = [(a, b, i % 2) for i, (a, b) in enumerate(zip(cuts[:-1], cuts[1:]))]
     shapes = {
-        "state": ((rows, model), F32),
-        "weights": ((4, 4, 2, depth, total), BF),
-        "gains": ((8, model), F32),
+        K_STATE: ((rows, model), F32),
+        K_WEIGHTS: ((4, 4, 2, depth, total), BF),
+        K_GAINS: ((8, model), F32),
     }
     for level, n in enumerate(counts):
         width = heads * n
-        shapes[f"place_{level}"] = ((1, width), F32)
+        shapes[(K_PLACE, level)] = ((1, width), F32)
         if level:
-            shapes[f"pick_{level}"] = ((n, rows), BF)
-            shapes[f"cosine_{level}"] = ((n, LANES), F32)
-            shapes[f"sine_{level}"] = ((n, LANES), F32)
-            shapes[f"keys_{level}"] = ((devices, n, LANES), F32)
-        for base in ("rows", "normed", "attn", "ffn", "second"):
-            shapes[f"{base}_{level}"] = ((n, model), BF)
-        shapes[f"parts_{level}"] = ((n, 2 * hidden), F32)
-        shapes[f"packed_{level}"] = ((devices, n, 2 * HD), BF)
-        shapes[f"query_{level}"] = ((width, 2 * HD), BF)
-        shapes[f"mixed_t_{level}"] = ((2 * HD, width), F32)
-        shapes[f"log_{level}"] = ((1, width), F32)
-        shapes[f"mixed_{level}"] = ((n, mix), BF)
+            shapes[(K_PICK, level)] = ((n, rows), BF)
+            shapes[(K_COSINE, level)] = ((n, LANES), F32)
+            shapes[(K_SINE, level)] = ((n, LANES), F32)
+            shapes[(K_KEYS, level)] = ((devices, n, LANES), F32)
+        for base in (K_ROWS, K_NORMED, K_ATTN, K_FFN, K_SECOND):
+            shapes[(base, level)] = ((n, model), BF)
+        shapes[(K_PARTS, level)] = ((n, 2 * hidden), F32)
+        shapes[(K_PACKED, level)] = ((devices, n, 2 * HD), BF)
+        shapes[(K_QUERY, level)] = ((width, 2 * HD), BF)
+        shapes[(K_MIXED_T, level)] = ((2 * HD, width), F32)
+        shapes[(K_LOG, level)] = ((1, width), F32)
+        shapes[(K_MIXED, level)] = ((n, mix), BF)
     names = tuple(shapes)
     args = (tokens, depths, second_slot, third_slot, *matrices, *vectors, *tables)
     width = heads * rows
@@ -934,16 +942,17 @@
 
 
 SLOTS = 6
+CORE_SLOTS = 3
 GROUP = 512
 
 
 class Collect:
-    def __init__(self, spans, groups, x, y, core, turned, rights, vectors, store, slots, core_recv, relay_recv, first_recv, last_recv, send_sems, recv_sems, turn):
+    def __init__(self, spans, groups, x, y, core, turned, rights, vectors, store, slots, core_recv, relay_recv, first_recv, mid, last_recv, send_sems, recv_sems, credit, turn):
         self.spans, self.groups = spans, groups
         self.x, self.y, self.core = x, y, core
         self.turned, self.rights, self.vectors, self.store, self.slots = turned, rights, vectors, store, slots
         self.core_recv, self.relay_recv, self.first_recv = core_recv, relay_recv, first_recv
-        self.last_recv = last_recv
+        self.mid, self.last_recv, self.credit = mid, last_recv, credit
         self.send_sems, self.recv_sems = send_sems, recv_sems
         self.turn = turn
         self.waits = [{} for _ in groups]
@@ -984,7 +993,8 @@
                         self.turned[section % 2, pl.ds(start, 1024), :], self.rights[:, base + low : base + high]
                     )
                 else:
-                    value = self.vectors[:, pl.ds(start, 1024)].T
+                    few = self.vectors[:, pl.ds(start, 1024)]
+                    value = jnp.concatenate([few, jnp.zeros((LANES - few.shape[0], 1024), F32)], axis=0).T
                 self.slots[slot, pl.ds(m * 2, 2), :, :, :, column : column + wide] = (
                     value.astype(BF).reshape(2, 4, 2, 64, wide)
                 )
@@ -992,10 +1002,12 @@
 
             lax.fori_loop(0, 2, rows_of, 0)
             column += wide
+        if g >= CORE_SLOTS:
+            pl.semaphore_wait(self.credit, 1)
         waits[g][0] = [
             self.remote(
                 g, 0, self.slots.at[slot, :, :, 1 - self.core, :, :column],
-                self.core_recv.at[g, :, :, :, :column], peer(self.x, self.y, 1 - self.core),
+                self.core_recv.at[g % CORE_SLOTS, :, :, :, :column], peer(self.x, self.y, 1 - self.core),
             )
         ]
 
@@ -1006,11 +1018,15 @@
 
         def add(i, carry):
             slots[slot, i, :, self.core, :, :width] = (
-                slots[slot, i, :, self.core, :, :width] + self.core_recv[g, i, :, :, :width]
+                slots[slot, i, :, self.core, :, :width] + self.core_recv[g % CORE_SLOTS, i, :, :, :width]
             )
             return carry
 
         lax.fori_loop(0, 4, add, 0)
+        if g + CORE_SLOTS < len(self.groups):
+            pl.semaphore_signal(
+                self.credit, inc=1, device_id=peer(self.x, self.y, 1 - self.core), device_id_type=MESH
+            )
         at = self.x if axis == 0 else self.y
         waits[g][1] = [
             self.remote(
@@ -1048,14 +1064,14 @@
             copy.wait_recv()
         for b in range(4):
             where = (slot, at, b, self.core) if axis == 0 else (slot, b, at, self.core)
-            self.core_recv[g, 0, b, :, :width] = (
+            self.mid[g, b, :, :width] = (
                 slots[where + (slice(None), slice(0, width))].astype(F32)
                 + self.first_recv[g, 0, b, :, :width].astype(F32)
                 + self.first_recv[g, 1, b, :, :width].astype(F32)
             ).astype(BF)
         waits[g][3] = [
             self.remote(
-                g, 4 + k, self.core_recv.at[g, 0, lax.rem(other + k, 4), :, :width],
+                g, 4 + k, self.mid.at[g, lax.rem(other + k, 4), :, :width],
                 self.last_recv.at[g, k - 1, :, :width],
                 shifted(self.x, self.y, self.core, 1 - axis, k),
             )
@@ -1065,7 +1081,7 @@
     def fourth(self, g):
         width, pieces, axis = self.groups[g]
         other = self.y if axis == 0 else self.x
-        value = self.core_recv[g, 0, other, :, :width].astype(F32)
+        value = self.mid[g, other, :, :width].astype(F32)
         for copy in self.waits[g][3]:
             copy.wait_recv()
         for k in range(3):
@@ -1075,9 +1091,9 @@
             self.store(section, low, value[:, column : column + high - low])
             column += high - low
 
-    def step(self, i):
+    def step(self, i, new=True):
         for back, work in ((0, self.zero), (1, self.first), (3, self.second), (5, self.third), (6, self.fourth)):
-            if 0 <= i - back < len(self.groups):
+            if 0 <= i - back < len(self.groups) and (back or new):
                 work(i - back)
 
     def drain(self):
@@ -1091,19 +1107,41 @@
 
 def finish_kernel(n, heads, devices, mp, group, levels, spans, groups, *refs):
     refs = list(refs)
-    flow, gains, query_place, query, packed, mixed_t, log_total, grad_mixed, cosine, sine = [refs.pop(0) for _ in range(10)]
-    rows_in, middle, logit, vecs = [refs.pop(0) for _ in range(4)]
+    flow, gains, query_place, query, packed, mixed_t, log_total, cosine, sine = [refs.pop(0) for _ in range(9)]
+    rows_in, attn_in, logit, vecs = [refs.pop(0) for _ in range(4)]
     w_hbm = refs.pop(0)
-    sources = [[refs.pop(0) for _ in range(8 if level else 7)] for level in range(len(levels))]
+    sources = [[refs.pop(0) if level or i not in (4, 7) else None for i in range(8)] for level in range(len(levels))]
     flow_out, q_out, k_out, v_out, out_out, gate_out, up_out, down_out, vec_out = [refs.pop(0) for _ in range(9)]
     query_t, grad_rows, grad_t, acc, delta, send_buf, recv_buf, kv_send, kv_recv = [refs.pop(0) for _ in range(9)]
-    w_qkv, w_sem, send_a, recv_a, full_a, sems_a = [refs.pop(0) for _ in range(6)]
-    (lefts, turned, rights, vectors, slots, core_recv, relay_recv, first_recv, last_recv,
-     loads, send_sems, recv_sems) = refs
+    w_qkv, w_sem, w_gu, gu_sems, middle = [refs.pop(0) for _ in range(5)]
+    sum_refs = [[refs.pop(0) for _ in range(4)] for _ in range(2)]
+    (lefts, turned, rights, vectors, slots, core_recv, relay_recv, first_recv, mid, last_recv,
+     loads, send_sems, recv_sems, credit) = refs
     me, mp_me = lax.axis_index("dp"), lax.axis_index("mp")
     x, y, core = plane(me)
-    load_w = pltpu.make_async_copy(w_hbm.at[:, : w_qkv.shape[1]], w_qkv, w_sem)
-    load_w.start()
+    hidden = gate_out.shape[1]
+    mix = q_out.shape[1]
+    base_o = mix + 2 * LANES
+    load_o = pltpu.make_async_copy(w_hbm.at[:, base_o : base_o + mix], w_qkv.at[:, :mix], w_sem)
+    load_o.start()
+    wide = w_gu.shape[1]
+    pieces = [(mp_me + k, piece) for piece in range(PIECES) for k in Sum.order]
+    pieces += [(mp_me, piece) for piece in range(PIECES)]
+    gu_loads = []
+
+    def load_gu():
+        i = len(gu_loads)
+        if i < len(pieces):
+            start = pl.multiple_of((lax.rem(pieces[i][0], mp) * PIECES + pieces[i][1]) * wide, wide)
+            copy = pltpu.make_async_copy(
+                w_hbm.at[pl.ds(start, wide), base_o + mix : base_o + mix + 2 * hidden],
+                w_gu.at[i % w_gu.shape[0]], gu_sems.at[i % w_gu.shape[0]],
+            )
+            copy.start()
+            gu_loads.append(copy)
+
+    for _ in range(w_gu.shape[0]):
+        load_gu()
     fetches = [[] for _ in range(4)]
 
     def fetch(s, side):
@@ -1111,7 +1149,7 @@
         for level, count in enumerate(levels):
             low, high = spans[s]
             target = (lefts.at[s % 2, row : row + count], rights.at[row : row + count, low:high])[side]
-            if 2 * s + side < len(sources[level]):
+            if sources[level][2 * s + side] is not None:
                 copy = pltpu.make_async_copy(
                     sources[level][2 * s + side], target, loads.at[level, 2 * s + side]
                 )
@@ -1144,9 +1182,6 @@
         turned[section % 2] = lefts[section % 2].T
         if section < 2:
             fetch(section + 2, 0)
-
-    hidden = gate_out.shape[1]
-    mix = q_out.shape[1]
 
     def store(section, low, value):
         high = low + value.shape[1]
@@ -1167,15 +1202,52 @@
                 k_out[...] = value[:, mix - low : mix - low + HD]
                 v_out[...] = value[:, mix - low + HD :]
         else:
-            vec_out[...] = value
+            vec_out[...] = value.T[: vec_out.shape[0], :]
 
     work = Collect(
         spans, groups, x, y, core, turned, rights, vectors, store, slots, core_recv, relay_recv,
-        first_recv, last_recv, send_sems, recv_sems, turn,
+        first_recv, mid, last_recv, send_sems, recv_sems, credit, turn,
     )
+    pl.semaphore_wait(barrier, devices - 1 + mp - 1)
+    for i in range(4):
+        work.step(i)
+
+    update = flow[...].astype(BF).astype(F32)
+    level = rows_in[...].astype(F32)
+    gate = sigmoid(jnp.sum(level * gains[2:3, :], axis=-1, keepdims=True))
+    parts_now = rights[0:n, : 2 * hidden]
+    used = []
+
+    def gu_piece(start, size):
+        i = len(used)
+        used.append(i)
+        gu_loads[i].wait()
+        value = dot_nt(parts_now, w_gu[i % w_gu.shape[0]])
+        load_gu()
+        return value
+
+    head = Sum(mp, mp_me, *sum_refs[0])
+    head.start(gu_piece)
+    work.step(4)
+    head.middle()
+    work.step(5)
+    grad_second = head.finish().astype(F32)
+    unit, factor = unit_of(level + attn_in[...].astype(F32))
+    vectors[...] = jnp.zeros(vectors.shape, F32)
+    vectors[1:2, :] = (
+        jnp.sum(grad_second * unit, axis=0, keepdims=True) + vecs[0:1, :] + vecs[1:2, :]
+    )
+    middle[...] = unit_back(grad_second * gains[1:2, :], unit, factor)
+    grad_attn = (gate * update + middle[...]).astype(BF)
+    lefts[0, 0:n, :] = grad_attn
+    load_o.wait()
+    grad_mixed = dot_nn(grad_attn, w_qkv[:, :mix]).astype(BF).astype(F32)
+    load_w = pltpu.make_async_copy(w_hbm.at[:, : w_qkv.shape[1]], w_qkv, w_sem)
+    load_w.start()
+    work.step(6)
     left = lanes_of((n, LANES)) < HD
     for t in range(heads // 2):
-        part = grad_mixed[:, t * LANES : (t + 1) * LANES].astype(F32)
+        part = grad_mixed[:, t * LANES : (t + 1) * LANES]
         grad_rows[2 * t * n : (2 * t + 1) * n, :] = jnp.where(
             left, 0.0, pltpu.roll(part, HD, 1)
         ).astype(BF)
@@ -1185,7 +1257,6 @@
     delta[...] = jnp.sum(grad_t[...].astype(F32) * mixed_t[...], axis=0, keepdims=True)
     acc[...] = jnp.zeros(acc.shape, F32)
     width = heads * n
-    pl.semaphore_wait(barrier, devices - 1 + mp - 1)
 
     def send_copy(e, source_index):
         return pltpu.make_async_remote_copy(
@@ -1214,12 +1285,14 @@
 
     blocks = devices // group
     for b in range(blocks):
-        work.step(b)
+        if b == blocks // 2:
+            work.step(7)
 
         @pl.when(b * group <= me)
         def _(b=b):
             one_block(b)
 
+    work.step(8)
     grad_query = acc[...].T * HD**-0.5
     outs = []
     for t in range(heads // 2):
@@ -1243,24 +1316,24 @@
     def first_piece(start, wide):
         return dot_nt(grad_now, w_qkv[pl.ds(start, wide), :])
 
-    total = Sum(mp, mp_me, send_a, recv_a, full_a, sems_a)
+    total = Sum(mp, mp_me, *sum_refs[1])
     total.start(first_piece)
-    work.step(blocks)
+    work.step(9)
     total.middle()
-    work.step(blocks + 1)
+    work.step(10)
+    work.step(11, False)
     grad_normed = total.finish().astype(F32)
-    level = rows_in[...].astype(F32)
     unit, factor = unit_of(level)
-    vectors[...] = jnp.zeros(vectors.shape, F32)
     vectors[0:1, :] = jnp.sum(grad_normed * unit, axis=0, keepdims=True) + vecs[3:4, :] + vecs[4:5, :]
-    vectors[1:2, :] = vecs[0:1, :] + vecs[1:2, :] + vecs[2:3, :]
     vectors[2:3, :] = jnp.sum(level * logit[...], axis=0, keepdims=True) + vecs[5:6, :] + vecs[6:7, :]
     flow_out[...] = flow[...] + (
         unit_back(grad_normed * gains[0:1, :], unit, factor) + middle[...] + logit[...] * gains[2:3, :]
     ).astype(BF).astype(F32)
-    for i in range(blocks + 2, len(groups) + 6):
+    work.zero(11)
+    for i in range(12, len(groups) + 6):
         work.step(i)
     work.drain()
+    head.drain()
     total.drain()
 
     def sent(e, carry):
@@ -1285,21 +1358,22 @@
         pieces += [(section, low, low + LANES) for low in range(0, wide, LANES)]
     groups = []
     per = GROUP // LANES
-    for index in range(0, len(pieces), per):
+    cuts = [*range(0, len(pieces) - 1, per), len(pieces) - 1, len(pieces)]
+    for index, end in zip(cuts[:-1], cuts[1:]):
         merged = []
-        for section, low, high in pieces[index : index + per]:
+        for section, low, high in pieces[index:end]:
             if merged and merged[-1][0] == section:
                 merged[-1] = (section, merged[-1][1], high)
             else:
                 merged.append((section, low, high))
         wide = sum(high - low for _, low, high in merged)
-        groups.append((wide, merged, (index // per) % 2))
+        groups.append((wide, merged, len(groups) % 2))
     counts = [level[0].shape[0] for level in levels]
     rows = sum(counts)
     hidden = widths[1]
     many = len(groups)
     whole = [flow, gains, *attention, *tail, vecs]
-    args = whole + [weights] + [item for level in levels for item in level]
+    args = whole + [weights] + [item for level in levels for item in level if item is not None]
     return pl.pallas_call(
         functools.partial(finish_kernel, n, heads, devices, mp, group, counts, spans, groups),
         out_shape=(
@@ -1311,7 +1385,7 @@
             jax.ShapeDtypeStruct((depth, hidden), F32),
             jax.ShapeDtypeStruct((depth, hidden), F32),
             jax.ShapeDtypeStruct((depth, hidden), F32),
-            jax.ShapeDtypeStruct((depth, LANES), F32),
+            jax.ShapeDtypeStruct((8, depth), F32),
         ),
         in_specs=vmem(len(whole)) + [pl.BlockSpec(memory_space=pl.ANY)] * (len(args) - len(whole)),
         out_specs=tuple(vmem(9)),
@@ -1327,25 +1401,53 @@
             pltpu.SemaphoreType.DMA((devices,)),
             pltpu.VMEM((model, mix + 2 * HD), BF),
             pltpu.SemaphoreType.DMA(()),
+            pltpu.VMEM((2, model // mp // PIECES, 2 * hidden), BF),
+            pltpu.SemaphoreType.DMA((2,)),
+            pltpu.VMEM((n, model), F32),
+            *sum_scratch(mp, n, model),
             *sum_scratch(mp, n, model),
             pltpu.VMEM((2, rows, model), BF),
             pltpu.VMEM((2, model, rows), BF),
             pltpu.VMEM((rows, spans[3][1]), BF),
-            pltpu.VMEM((LANES, model), F32),
+            pltpu.VMEM((8, model), F32),
             pltpu.VMEM((SLOTS, 4, 4, 2, depth, GROUP), BF),
-            pltpu.VMEM((many, 4, 4, depth, GROUP), BF),
+            pltpu.VMEM((CORE_SLOTS, 4, 4, depth, GROUP), BF),
             pltpu.VMEM((many, 2, 2, depth, GROUP), BF),
             pltpu.VMEM((many, 2, 4, depth, GROUP), BF),
+            pltpu.VMEM((many, 4, depth, GROUP), BF),
             pltpu.VMEM((many, 3, depth, GROUP), BF),
             pltpu.SemaphoreType.DMA((len(levels), 8)),
             pltpu.SemaphoreType.DMA((many, 8)),
             pltpu.SemaphoreType.DMA((many, 8)),
+            pltpu.SemaphoreType.REGULAR,
         ],
         compiler_params=pltpu.CompilerParams(
             collective_id=ident, has_side_effects=True, vmem_limit_bytes=63 * 1024 * 1024
         ),
         name="finish",
     )(*args)
+
+
+def hand_over_kernel(count, *refs):
+    vectors, sources, targets = refs[0], refs[1 : 1 + count], refs[1 + count :]
+    for source, target in zip(sources, targets):
+        target[...] = source[...]
+    for i, target in enumerate(targets[count:]):
+        target[...] = vectors[i, :]
+
+
+def hand_over(items, vectors):
+    count = len(items)
+    return pl.pallas_call(
+        functools.partial(hand_over_kernel, count),
+        out_shape=tuple(
+            [jax.ShapeDtypeStruct(item.shape, F32) for item in items]
+            + [jax.ShapeDtypeStruct(vectors.shape[1:], F32)] * 3
+        ),
+        in_specs=vmem(1 + count),
+        out_specs=tuple(vmem(count + 3)),
+        name="hand_over",
+    )(vectors, *items)
 
 
 def rotary_tables(place):
@@ -1377,25 +1479,27 @@
         (w_query, w_key, w_value, w_out.T, w_gate, w_up, w_down.T),
         (row(norm_first), row(norm_second), row(router)), home, heads, devices, mp, 0,
     )
-    weights = kept["weights"].reshape(devices * depth, -1)
-    gains = kept["gains"]
+    weights = kept[K_WEIGHTS].reshape(devices * depth, -1)
+    gains = kept[K_GAINS]
     back = retreat(cotangent, kept, weights, heads, devices, mp, 1)
     terms = []
     for level in range(3):
         terms.append(
-            tuple(back.get(f"{base}_{level}", kept.get(f"{base}_{level}")) for base in (
-                "second", "parts_grad", "grad_ffn", "hidden", "grad_attn", "mixed", "normed", "grad_qkv"
-            )[: 8 if level else 7])
-        )
-    attention = [kept[f"{base}_0"] for base in ("place", "query", "packed", "mixed_t", "log")]
-    flow, query_grad, key_grad, value_grad, out_grad, gate_grad, up_grad, down_grad, vec = finish(
-        back["flow_out"], gains, (*attention, back["grad_mixed_0"], *home),
-        (kept["rows_0"], back["middle_0"], back["logit_0"]), back["vecs"], weights, terms,
+            tuple(back.get((base, level), kept.get((base, level))) for base in (
+                K_SECOND, K_PARTS_GRAD, K_GRAD_FFN, K_HIDDEN, K_GRAD_ATTN, K_MIXED, K_NORMED, K_GRAD_QKV
+            ))
+        )
+    attention = [kept[(base, 0)] for base in (K_PLACE, K_QUERY, K_PACKED, K_MIXED_T, K_LOG)]
+    results = finish(
+        back[K_FLOW_OUT], gains, (*attention, *home),
+        (kept[(K_ROWS, 0)], kept[(K_ATTN, 0)], back[(K_LOGIT, 0)]), back[K_VECS], weights, terms,
         heads, devices, mp, depth, 2,
     )
+    (state, flow, query_grad, key_grad, value_grad, out_grad, gate_grad, up_grad, down_grad,
+     first_grad, second_grad, router_grad) = hand_over((kept[K_STATE], *results[:-1]), results[-1])
     return (
-        kept["state"], flow, query_grad, key_grad, value_grad, out_grad.T, gate_grad, up_grad, down_grad.T,
-        vec[:, 0], vec[:, 1], vec[:, 2],
+        state, flow, query_grad, key_grad, value_grad, out_grad.T, gate_grad, up_grad, down_grad.T,
+        first_grad, second_grad, router_grad,
     )
 
 

time: 434 us -> 419 us (0.965)
  local copies, waits for them, and re-layouts: 9.67 us -> 0 us
  Pallas kernels: 414 us -> 408 us
    pallas_call x1, Pallas kernels: 120 us -> 102 us  [retreat(): pl.pallas_call(functools.partial(retreat_kernel, counts, heads, devices,...]
    pallas_call x1, Pallas kernels: 103 us -> 114 us  [finish(): pl.pallas_call(functools.partial(finish_kernel, n, heads, devices, mp, gr...]
    unnamed x25 -> x0, local copies, waits for them, and re-layouts: 8.04 us -> none
where the time goes in v7:
time: 419 us; the launch traced here: 411 us
  Pallas kernels  408 us (97%)
    pallas_call x1, Pallas kernels, advance(): pl.pallas_call(functools.partial(advance_kernel, counts, heads, devices,...  189 us
    pallas_call x1, Pallas kernels, finish(): pl.pallas_call(functools.partial(finish_kernel, n, heads, devices, mp, gr...  114 us
    pallas_call x1, Pallas kernels, retreat(): pl.pallas_call(functools.partial(retreat_kernel, counts, heads, devices,...  102 us

profile of v7, /device:TPU:0, one launch (start us, length us, event | category | flops | bytes accessed | tf_op | source)
XLA Modules:
  0.0 410.8 jit_solution(279511208439647510)
XLA Ops:
  0.7 0.3 fusion
  1.0 0.8 pad_maximum_fusion
  1.8 188.8 %advance.1 = (f32[128,2048]{1,0:T(8,128)}, bf16[4,4,2,64,5504]{4,3,2,1,0:T(8,128)(2,1)}, f32[8,2048]{1,0:T(8,128)}, f32[1,1024]{1,0:T(1,128)}, bf16[128,2048]{1,...) custom-call(bf16[128,2048]{1,0:T(8,128)(2,1)} %refs_0_.2, ...), custom_call_target="tpu_custom_call" | custom-call | tf_op jit(solution)/shard_map/advance/pallas_call | solution.py:915
  190.6 102.3 %retreat.1 = (f32[128,2048]{1,0:T(8,128)}, f32[8,2048]{1,0:T(8,128)}, bf16[128,2048]{1,0:T(8,128)(2,1)}, bf16[128,1408]{1,0:T(8,128)(2,1)}, bf16[128,2816]{1,0:T...) custom-call(f32[128,2048]{1,0:T(8,128)} %refs_0_.3, ...), custom_call_target="tpu_custom_call" | custom-call | tf_op jit(solution)/shard_map/retreat/pallas_call | solution.py:416
  292.9 113.6 %finish.1 = (f32[128,2048]{1,0:T(8,128)}, f32[64,512]{1,0:T(8,128)}, f32[64,64]{1,0:T(8,128)}, f32[64,64]{1,0:T(8,128)}, f32[64,512]{1,0:T(8,128)}, /*index=5*/f...) custom-call(f32[128,2048]{1,0:T(8,128)} %get-tuple-element.128.refs_0_, ...), custom_call_target="tpu_custom_call" | custom-call | tf_op jit(solution)/shard_map/finish/pallas_call | solution.py:1377
  406.5 3.8 hand_over.1
  (2 shorter events, 0.0 us)
